TPU v7x, 32 devices: a whole 2x2x4 slice. The times are simulated.
32 devices in a mesh: expert: 16 (over z, y, x), shard: 2 (over core).
Axes of the slice: x: 2, y: 2, z: 4, core: 2. Of those that a mesh axis runs over, the one named last changes fastest.
Arguments:
- tokens: bfloat16 [4096, 2048], P(('expert', 'shard')), may hold values from -6 to 6
- segment_ids: int32 [4096], P('expert'), may hold values from 0 to 2, as said below
- routes: int32 [4096, 6], P(('expert', 'shard')), may hold values from 0 to 15, all different within a row; in each aligned block of 128 rows (0 to 127, 128 to 255, ...) at most 64 rows name the same one
- cotangent: bfloat16 [4096, 2048], P(('expert', 'shard')), may hold values from -6 to 6
- gain_attn: bfloat16 [2048], P('shard'), may hold values from 0.5 to 1.5
- gain_query: bfloat16 [1536], P('shard'), may hold values from 0.5 to 1.5
- gain_latent: bfloat16 [512], P('shard'), may hold values from 0.5 to 1.5
- gain_ffn: bfloat16 [2048], P('shard'), may hold values from 0.5 to 1.5
- w_qa: bfloat16 [2048, 1536], P('shard'), may hold values from -0.125 to 0.125
- w_qb: bfloat16 [1536, 3072], P('shard'), may hold values from -0.15625 to 0.15625
- w_kva: bfloat16 [2048, 576], P('shard'), may hold values from -0.125 to 0.125
- w_kvb: bfloat16 [512, 4096], P('shard'), may hold values from -0.25 to 0.25
- w_out: bfloat16 [2048, 2048], P('shard'), may hold values from -0.5 to 0.5
- w_router: bfloat16 [2048, 16], P('shard'), may hold values from -0.06591797 to 0.06591797
- shared_gate: bfloat16 [2048, 2816], P(None, 'shard'), may hold values from -0.125 to 0.125
- shared_up: bfloat16 [2048, 2816], P(None, 'shard'), may hold values from -0.125 to 0.125
- shared_down: bfloat16 [2816, 2048], P('shard'), may hold values from -0.109375 to 0.109375
- expert_gate: bfloat16 [16, 2048, 1408], P('expert', None, 'shard'), may hold values from -0.125 to 0.125
- expert_up: bfloat16 [16, 2048, 1408], P('expert', None, 'shard'), may hold values from -0.125 to 0.125
- expert_down: bfloat16 [16, 1408, 2048], P('expert', 'shard'), may hold values from -0.15625 to 0.15625
Outputs:
- result: float32 [4096, 2048], P(('expert', 'shard'))
- grad_tokens: float32 [4096, 2048], P(('expert', 'shard'))
- grad_gain_attn: float32 [2048], P('shard')
- grad_gain_query: float32 [1536], P('shard')
- grad_gain_latent: float32 [512], P('shard')
- grad_gain_ffn: float32 [2048], P('shard')
- grad_w_qa: float32 [2048, 1536], P('shard')
- grad_w_qb: float32 [1536, 3072], P('shard')
- grad_w_kva: float32 [2048, 576], P('shard')
- grad_w_kvb: float32 [512, 4096], P('shard')
- grad_w_out: float32 [2048, 2048], P('shard')
- grad_w_router: float32 [2048, 16], P('shard')
- grad_shared_gate: float32 [2048, 2816], P(None, 'shard')
- grad_shared_up: float32 [2048, 2816], P(None, 'shard')
- grad_shared_down: float32 [2816, 2048], P('shard')
- grad_expert_gate: float32 [16, 2048, 1408], P('expert', None, 'shard')
- grad_expert_up: float32 [16, 2048, 1408], P('expert', None, 'shard')
- grad_expert_down: float32 [16, 1408, 2048], P('expert', 'shard')
Inputs may be any that keep to these rules, and one draw needn't show every extreme that they name: `segment_ids`: each group of 256 consecutive tokens holds three sequences numbered 0, 1, 2 in order; sequence 1 starts within the group's first 128 tokens and ends within its last 128. `routes`: each token names 6 different experts; among the 128 tokens of one device no expert is named by more than 64 tokens, a bound that some block reaches.
All inputs are finite; a program needn't handle non-finite values.
Results may differ from a plain program's by a relative error of at most 0.025.
Values may be sent and summed in bfloat16 or wider, within the bound.
No kernel may reach another device: no remote copies, remote signals or barrier semaphores. Data moves between devices by JAX's collectives and lax.ppermute only.
A program may use at most 448 MiB of HBM per device.

v0:
```python
import jax
import jax.numpy as jnp
from jax import lax
from jax.sharding import PartitionSpec as P

H = 16
DN = 128
DR = 64
DV = 128
KR = 512
TOP = 6


norm_eps = 1e-06
rope_base = 50000.0
route_scale = 2.446
masked_score = -1e30
highest = lax.Precision.HIGHEST
bfloat = jnp.bfloat16
single_layer = jnp.float32


def row_scale(values):
    return lax.rsqrt(jnp.mean(values * values, axis=-1, keepdims=True) + norm_eps)


def norm_back(grad_out, normed_rows, scale_rows, gain):
    grad_normed = grad_out * gain
    grad_input = scale_rows * (
        grad_normed - normed_rows * jnp.mean(grad_normed * normed_rows, axis=-1, keepdims=True)
    )
    return (grad_input, jnp.sum(grad_out * normed_rows, axis=0))


def seq_positions(segments):
    token_count = segments.shape[0]
    index = jnp.arange(token_count, dtype=jnp.int32)
    change = jnp.concatenate([jnp.ones((1,), bool), segments[1:] != segments[:-1]])
    starts = lax.cummax(jnp.where(change, index, 0), axis=0)
    return index - starts


def rope_tables(positions, half):
    freq = rope_base ** (-jnp.arange(half, dtype=jnp.float32) / half)
    angles = positions.astype(jnp.float32)[:, None] * freq[None, :]
    return (jnp.cos(angles), jnp.sin(angles))


def rotate(values, cosine, sine):
    half = values.shape[-1] // 2
    first = values[..., :half]
    second = values[..., half:]
    return jnp.concatenate(
        [first * cosine - second * sine, second * cosine + first * sine], axis=-1
    )


def rotate_back(grads, cosine, sine):
    half = grads.shape[-1] // 2
    first = grads[..., :half]
    second = grads[..., half:]
    return jnp.concatenate(
        [first * cosine + second * sine, second * cosine - first * sine], axis=-1
    )


def silu_grads(grad_hidden, pre_gate, pre_up):
    sigma = jax.nn.sigmoid(pre_gate)
    grad_gate = grad_hidden * pre_up * sigma * (1.0 + pre_gate * (1.0 - sigma))
    grad_up = grad_hidden * pre_gate * sigma
    return (grad_gate.astype(bfloat), grad_up.astype(bfloat))


def per_device(
    tokens,
    segment_ids,
    routes,
    cotangent,
    gain_attn,
    gain_query,
    gain_latent,
    gain_ffn,
    w_qa,
    w_qb,
    w_kva,
    w_kvb,
    w_out,
    w_router,
    shared_gate,
    shared_up,
    shared_down,
    expert_gate,
    expert_up,
    expert_down,
):
    shard_count = lax.axis_size("shard")
    shard_pos = lax.axis_index("shard")
    tok_rows = tokens.shape[0]
    model = tokens.shape[1]
    group_rows = tok_rows * shard_count
    score_scale = 1.0 / (DN + DR) ** 0.5
    (
        attention_norm_gain,
        query_norm_gain,
        latent_norm_gain,
        feedforward_norm_gain,
        query_down_weight,
        query_up_weight,
        key_value_down_weight,
        key_value_up_weight,
        output_projection_weight,
        router_weight_matrix,
    ) = (
        lax.all_gather(gain_attn, "shard", axis=0, tiled=True),
        lax.all_gather(gain_query, "shard", axis=0, tiled=True),
        lax.all_gather(gain_latent, "shard", axis=0, tiled=True),
        lax.all_gather(gain_ffn, "shard", axis=0, tiled=True),
        lax.all_gather(w_qa, "shard", axis=0, tiled=True),
        lax.all_gather(w_qb, "shard", axis=0, tiled=True),
        lax.all_gather(w_kva, "shard", axis=0, tiled=True),
        lax.all_gather(w_kvb, "shard", axis=0, tiled=True),
        lax.all_gather(w_out, "shard", axis=0, tiled=True),
        lax.all_gather(w_router, "shard", axis=0, tiled=True),
    )
    gain_attn_f = attention_norm_gain.astype(single_layer)
    gain_query_f = query_norm_gain.astype(single_layer)
    gain_latent_f = latent_norm_gain.astype(single_layer)
    gain_ffn_f = feedforward_norm_gain.astype(single_layer)
    resid = tokens.astype(single_layer)
    attn_scale = row_scale(resid)
    attn_normed = resid * attn_scale
    attn_in = (attn_normed * gain_attn_f).astype(bfloat)
    query_lat = jnp.dot(attn_in, query_down_weight, preferred_element_type=single_layer)
    query_scale = row_scale(query_lat)
    query_normed = query_lat * query_scale
    query_in = (query_normed * gain_query_f).astype(bfloat)
    query_all = jnp.dot(query_in, query_up_weight, preferred_element_type=single_layer).reshape(
        tok_rows, H, DN + DR
    )
    group_pos = seq_positions(segment_ids)
    own_start = shard_pos * tok_rows
    own_pos = lax.dynamic_slice_in_dim(group_pos, own_start, tok_rows, 0)
    own_seg = lax.dynamic_slice_in_dim(segment_ids, own_start, tok_rows, 0)
    cosine, sine = rope_tables(own_pos, DR // 2)
    query_nope = query_all[..., :DN].astype(bfloat)
    query_rope = rotate(query_all[..., DN:], cosine[:, None, :], sine[:, None, :]).astype(bfloat)
    latent_raw = jnp.dot(attn_in, key_value_down_weight, preferred_element_type=single_layer)
    latent_part = latent_raw[:, :KR]
    latent_scale = row_scale(latent_part)
    latent_normed = latent_part * latent_scale
    latent = (latent_normed * gain_latent_f).astype(bfloat)
    key_rope = rotate(latent_raw[:, KR:], cosine, sine).astype(bfloat)
    keys_latent, keys_rope = (
        lax.all_gather(latent, "shard", axis=0, tiled=True),
        lax.all_gather(key_rope, "shard", axis=0, tiled=True),
    )
    kvb_heads = key_value_up_weight.reshape(KR, H, DN + DV)
    w_uk = kvb_heads[..., :DN]
    w_uv = kvb_heads[..., DN:]
    query_abs = jnp.einsum(
        "thn,khn->thk", query_nope, w_uk, preferred_element_type=single_layer
    ).astype(bfloat)
    group_index = jnp.arange(group_rows, dtype=jnp.int32)
    own_index = own_start + jnp.arange(tok_rows, dtype=jnp.int32)
    visible = (own_seg[:, None] == segment_ids[None, :]) & (
        group_index[None, :] <= own_index[:, None]
    )

    def scores_of():
        raw = jnp.einsum("thk,gk->htg", query_abs, keys_latent, preferred_element_type=single_layer)
        raw = raw + jnp.einsum(
            "thr,gr->htg", query_rope, keys_rope, preferred_element_type=single_layer
        )
        return jnp.where(visible[None], raw * score_scale, masked_score)

    scores = scores_of()
    top_score = jnp.max(scores, axis=-1, keepdims=True)
    expd = jnp.exp(scores - top_score)
    total = jnp.sum(expd, axis=-1, keepdims=True)
    log_total = top_score + jnp.log(total)
    probs_low = (expd / total).astype(bfloat)
    attn_lat = jnp.einsum(
        "htg,gk->thk", probs_low, keys_latent, preferred_element_type=single_layer
    ).astype(bfloat)
    attn_heads = (
        jnp.einsum("thk,khv->thv", attn_lat, w_uv, preferred_element_type=single_layer)
        .astype(bfloat)
        .reshape(tok_rows, H * DV)
    )
    mid = resid + jnp.dot(attn_heads, output_projection_weight, preferred_element_type=single_layer)
    ffn_scale = row_scale(mid)
    ffn_normed = mid * ffn_scale
    ffn_in = (ffn_normed * gain_ffn_f).astype(bfloat)
    logits = jnp.dot(ffn_in, router_weight_matrix, preferred_element_type=single_layer)
    experts_all = router_weight_matrix.shape[1]
    local_experts = expert_gate.shape[0]
    chosen = jnp.sum(
        (routes[:, :, None] == jnp.arange(experts_all, dtype=jnp.int32)[None, None, :]).astype(
            single_layer
        ),
        axis=1,
    )
    sig = jax.nn.sigmoid(logits)
    denom = jnp.sum(chosen * sig, axis=-1, keepdims=True)
    routing_weights = route_scale * chosen * sig / denom
    capacity = min(tok_rows, 4 * tok_rows * TOP // (3 * experts_all))
    earlier = (jnp.arange(tok_rows)[:, None] > jnp.arange(tok_rows)[None, :]).astype(single_layer)
    slot = jnp.dot(earlier, chosen, precision=highest)
    placed = chosen[:, :, None] * (
        slot[:, :, None] == jnp.arange(capacity, dtype=single_layer)[None, None, :]
    ).astype(single_layer)
    placed_low = placed.astype(bfloat)
    place_flat = placed.reshape(tok_rows, experts_all * capacity)
    send_rows = jnp.einsum(
        "tm,td->md", place_flat.astype(bfloat), ffn_in, preferred_element_type=single_layer
    ).astype(bfloat)
    recv_rows = lax.all_to_all(send_rows, "expert", split_axis=0, concat_axis=0, tiled=True)
    gate_full, up_full, down_full = (
        lax.all_gather(expert_gate, "shard", axis=2, tiled=True),
        lax.all_gather(expert_up, "shard", axis=2, tiled=True),
        lax.all_gather(expert_down, "shard", axis=1, tiled=True),
    )
    rows_fourfold = recv_rows.reshape(-1, local_experts, capacity, model)
    pre_gate = jnp.einsum(
        "sxcd,xdf->sxcf", rows_fourfold, gate_full, preferred_element_type=single_layer
    )
    pre_up = jnp.einsum(
        "sxcd,xdf->sxcf", rows_fourfold, up_full, preferred_element_type=single_layer
    )
    hidden_exp = (jax.nn.silu(pre_gate) * pre_up).astype(bfloat)
    out_exp = (
        jnp.einsum("sxcf,xfd->sxcd", hidden_exp, down_full, preferred_element_type=single_layer)
        .astype(bfloat)
        .reshape(-1, model)
    )
    back_rows = lax.all_to_all(out_exp, "expert", split_axis=0, concat_axis=0, tiled=True)
    picked = jnp.einsum(
        "tec,ecd->ted",
        placed_low,
        back_rows.reshape(experts_all, capacity, model),
        preferred_element_type=single_layer,
    )
    routed_output = jnp.sum(routing_weights[:, :, None] * picked, axis=1)
    sgate_full, sup_full, sdown_full = (
        lax.all_gather(shared_gate, "shard", axis=1, tiled=True),
        lax.all_gather(shared_up, "shard", axis=1, tiled=True),
        lax.all_gather(shared_down, "shard", axis=0, tiled=True),
    )
    shared_pre_gate = jnp.dot(ffn_in, sgate_full, preferred_element_type=single_layer)
    shared_pre_up = jnp.dot(ffn_in, sup_full, preferred_element_type=single_layer)
    shared_hidden = (jax.nn.silu(shared_pre_gate) * shared_pre_up).astype(bfloat)
    shared_out = jnp.dot(shared_hidden, sdown_full, preferred_element_type=single_layer)
    result = mid + shared_out + routed_output
    grad_out = cotangent.astype(single_layer)
    grad_weights = jnp.sum(picked * grad_out[:, None, :], axis=-1)
    scaled_grads = (routing_weights[:, :, None] * grad_out[:, None, :]).astype(bfloat)
    ret_grads = (
        jnp.einsum("tec,ted->ecd", placed_low, scaled_grads, preferred_element_type=single_layer)
        .astype(bfloat)
        .reshape(-1, model)
    )
    recv_grads = lax.all_to_all(
        ret_grads, "expert", split_axis=0, concat_axis=0, tiled=True
    ).reshape(-1, local_experts, capacity, model)
    grad_edown = jnp.einsum(
        "sxcf,sxcd->xfd", hidden_exp, recv_grads, preferred_element_type=single_layer
    )
    grad_hidden = jnp.einsum(
        "sxcd,xfd->sxcf", recv_grads, down_full, preferred_element_type=single_layer
    )
    grad_pre_gate, pre_up_gradient = silu_grads(grad_hidden, pre_gate, pre_up)
    grad_egate = jnp.einsum(
        "eawq,eawv->aqv", rows_fourfold, grad_pre_gate, preferred_element_type=single_layer
    )
    expert_up_gradient = jnp.einsum(
        "eawq,eawv->aqv", rows_fourfold, pre_up_gradient, preferred_element_type=single_layer
    )
    grad_rows = jnp.einsum(
        "sxcf,xdf->sxcd", grad_pre_gate, gate_full, preferred_element_type=single_layer
    )
    grad_rows = (
        grad_rows
        + jnp.einsum(
            "sxcf,xdf->sxcd", pre_up_gradient, up_full, preferred_element_type=single_layer
        )
    ).reshape(-1, model)
    row_back = lax.all_to_all(
        grad_rows.astype(jnp.bfloat16), "expert", split_axis=0, concat_axis=0, tiled=True
    ).astype(grad_rows.dtype)
    local_gate_weight, local_up_weight, local_down_weight = (
        lax.psum_scatter(
            grad_egate.astype(jnp.bfloat16), "shard", scatter_dimension=2, tiled=True
        ).astype(jnp.float32),
        lax.psum_scatter(
            expert_up_gradient.astype(jnp.bfloat16), "shard", scatter_dimension=2, tiled=True
        ).astype(jnp.float32),
        lax.psum_scatter(
            grad_edown.astype(jnp.bfloat16), "shard", scatter_dimension=1, tiled=True
        ).astype(jnp.float32),
    )
    row_high = row_back.astype(bfloat)
    row_rest = (row_back - row_high.astype(single_layer)).astype(bfloat)
    flat_low = place_flat.astype(bfloat)
    grad_ffn_in = jnp.dot(flat_low, row_high, preferred_element_type=single_layer) + jnp.dot(
        flat_low, row_rest, preferred_element_type=single_layer
    )
    grad_sig = chosen * (
        route_scale * grad_weights / denom
        - jnp.sum(grad_weights * routing_weights, axis=-1, keepdims=True) / denom
    )
    grad_logits = grad_sig * sig * (1.0 - sig)
    grad_router = jnp.einsum(
        "td,te->de", ffn_in.astype(single_layer), grad_logits, precision=highest
    )
    grad_ffn_in = grad_ffn_in + jnp.einsum(
        "te,de->td", grad_logits, router_weight_matrix.astype(single_layer), precision=highest
    )
    grad_sdown_full = jnp.einsum(
        "tf,td->fd", shared_hidden, cotangent, preferred_element_type=single_layer
    )
    grad_shidden = jnp.einsum(
        "td,fd->tf", cotangent, sdown_full, preferred_element_type=single_layer
    )
    grad_sgate_pre, grad_sup_pre = silu_grads(grad_shidden, shared_pre_gate, shared_pre_up)
    grad_sgate_full = jnp.einsum(
        "td,tf->df", ffn_in, grad_sgate_pre, preferred_element_type=single_layer
    )
    grad_sup_full = jnp.einsum(
        "td,tf->df", ffn_in, grad_sup_pre, preferred_element_type=single_layer
    )
    grad_ffn_in = grad_ffn_in + jnp.einsum(
        "tf,df->td", grad_sgate_pre, sgate_full, preferred_element_type=single_layer
    )
    grad_ffn_in = grad_ffn_in + jnp.einsum(
        "tf,df->td", grad_sup_pre, sup_full, preferred_element_type=single_layer
    )
    grad_sgate, grad_sup, grad_sdown = (
        lax.psum_scatter(
            grad_sgate_full.astype(jnp.bfloat16), "shard", scatter_dimension=1, tiled=True
        ).astype(jnp.float32),
        lax.psum_scatter(
            grad_sup_full.astype(jnp.bfloat16), "shard", scatter_dimension=1, tiled=True
        ).astype(jnp.float32),
        lax.psum_scatter(
            grad_sdown_full.astype(jnp.bfloat16), "shard", scatter_dimension=0, tiled=True
        ).astype(jnp.float32),
    )
    grad_mid, grad_gffn = norm_back(grad_ffn_in, ffn_normed, ffn_scale, gain_ffn_f)
    grad_mid = grad_mid + grad_out
    grad_attn_out = grad_mid.astype(bfloat)
    grad_wout = jnp.einsum(
        "tv,td->vd", attn_heads, grad_attn_out, preferred_element_type=single_layer
    )
    grad_heads = (
        jnp.einsum(
            "td,vd->tv",
            grad_attn_out,
            output_projection_weight,
            preferred_element_type=single_layer,
        )
        .astype(bfloat)
        .reshape(tok_rows, H, DV)
    )
    grad_uv = jnp.einsum("thk,thv->khv", attn_lat, grad_heads, preferred_element_type=single_layer)
    grad_attn_lat = jnp.einsum(
        "thv,khv->thk", grad_heads, w_uv, preferred_element_type=single_layer
    ).astype(bfloat)
    probs = jnp.exp(scores_of() - log_total)
    grad_probs = jnp.einsum(
        "thk,gk->htg", grad_attn_lat, keys_latent, preferred_element_type=single_layer
    )
    delta = jnp.sum(probs * grad_probs, axis=-1, keepdims=True)
    grad_scores = (probs * (grad_probs - delta)).astype(bfloat)
    grad_qabs = (
        jnp.einsum("htg,gk->thk", grad_scores, keys_latent, preferred_element_type=single_layer)
        * score_scale
    ).astype(bfloat)
    grad_qrope = (
        jnp.einsum("htg,gr->thr", grad_scores, keys_rope, preferred_element_type=single_layer)
        * score_scale
    )
    key_terms = (
        jnp.einsum("htg,thk->gk", grad_scores, query_abs, preferred_element_type=single_layer)
        * score_scale
    )
    key_terms = key_terms + jnp.einsum(
        "htg,thk->gk", probs_low, grad_attn_lat, preferred_element_type=single_layer
    )
    rope_terms = (
        jnp.einsum("htg,thr->gr", grad_scores, query_rope, preferred_element_type=single_layer)
        * score_scale
    )
    grad_latent, grad_krope = (
        lax.psum_scatter(
            key_terms.astype(jnp.bfloat16), "shard", scatter_dimension=0, tiled=True
        ).astype(jnp.float32),
        lax.psum_scatter(
            rope_terms.astype(jnp.bfloat16), "shard", scatter_dimension=0, tiled=True
        ).astype(jnp.float32),
    )
    grad_uk = jnp.einsum("thn,thk->khn", query_nope, grad_qabs, preferred_element_type=single_layer)
    grad_qnope = jnp.einsum("thk,khn->thn", grad_qabs, w_uk, preferred_element_type=single_layer)
    grad_qrope_raw = rotate_back(grad_qrope, cosine[:, None, :], sine[:, None, :])
    grad_query = (
        jnp.concatenate([grad_qnope, grad_qrope_raw], axis=-1)
        .astype(bfloat)
        .reshape(tok_rows, H * (DN + DR))
    )
    grad_wqb = jnp.einsum("tq,tm->qm", query_in, grad_query, preferred_element_type=single_layer)
    grad_query_in = jnp.einsum(
        "tm,qm->tq", grad_query, query_up_weight, preferred_element_type=single_layer
    )
    grad_qlat, grad_gquery = norm_back(grad_query_in, query_normed, query_scale, gain_query_f)
    grad_qlat_low = grad_qlat.astype(bfloat)
    grad_wqa = jnp.einsum("td,tq->dq", attn_in, grad_qlat_low, preferred_element_type=single_layer)
    grad_kvpart, grad_glatent = norm_back(grad_latent, latent_normed, latent_scale, gain_latent_f)
    grad_kvrope = rotate_back(grad_krope, cosine, sine)
    grad_kv = jnp.concatenate([grad_kvpart, grad_kvrope], axis=-1).astype(bfloat)
    grad_wkva = jnp.einsum("td,tk->dk", attn_in, grad_kv, preferred_element_type=single_layer)
    grad_attn_in = jnp.einsum(
        "tq,dq->td", grad_qlat_low, query_down_weight, preferred_element_type=single_layer
    )
    grad_attn_in = grad_attn_in + jnp.einsum(
        "tk,dk->td", grad_kv, key_value_down_weight, preferred_element_type=single_layer
    )
    grad_resid, grad_gattn = norm_back(grad_attn_in, attn_normed, attn_scale, gain_attn_f)
    grad_tokens = grad_mid + grad_resid
    grad_wkvb = jnp.concatenate([grad_uk, grad_uv], axis=-1).reshape(KR, H * (DN + DV))
    reduced = (
        lax.psum_scatter(
            grad_gattn.astype(jnp.bfloat16), "shard", scatter_dimension=0, tiled=True
        ).astype(jnp.float32),
        lax.psum_scatter(
            grad_gquery.astype(jnp.bfloat16), "shard", scatter_dimension=0, tiled=True
        ).astype(jnp.float32),
        lax.psum_scatter(
            grad_glatent.astype(jnp.bfloat16), "shard", scatter_dimension=0, tiled=True
        ).astype(jnp.float32),
        lax.psum_scatter(
            grad_gffn.astype(jnp.bfloat16), "shard", scatter_dimension=0, tiled=True
        ).astype(jnp.float32),
        lax.psum_scatter(
            grad_wqa.astype(jnp.bfloat16), "shard", scatter_dimension=0, tiled=True
        ).astype(jnp.float32),
        lax.psum_scatter(
            grad_wqb.astype(jnp.bfloat16), "shard", scatter_dimension=0, tiled=True
        ).astype(jnp.float32),
        lax.psum_scatter(
            grad_wkva.astype(jnp.bfloat16), "shard", scatter_dimension=0, tiled=True
        ).astype(jnp.float32),
        lax.psum_scatter(
            grad_wkvb.astype(jnp.bfloat16), "shard", scatter_dimension=0, tiled=True
        ).astype(jnp.float32),
        lax.psum_scatter(
            grad_wout.astype(jnp.bfloat16), "shard", scatter_dimension=0, tiled=True
        ).astype(jnp.float32),
        lax.psum_scatter(
            grad_router.astype(jnp.bfloat16), "shard", scatter_dimension=0, tiled=True
        ).astype(jnp.float32),
    )
    summed = (
        lax.psum(reduced[0].astype(jnp.bfloat16), "expert").astype(jnp.float32),
        lax.psum(reduced[1].astype(jnp.bfloat16), "expert").astype(jnp.float32),
        lax.psum(reduced[2].astype(jnp.bfloat16), "expert").astype(jnp.float32),
        lax.psum(reduced[3].astype(jnp.bfloat16), "expert").astype(jnp.float32),
        lax.psum(reduced[4].astype(jnp.bfloat16), "expert").astype(jnp.float32),
        lax.psum(reduced[5].astype(jnp.bfloat16), "expert").astype(jnp.float32),
        lax.psum(reduced[6].astype(jnp.bfloat16), "expert").astype(jnp.float32),
        lax.psum(reduced[7].astype(jnp.bfloat16), "expert").astype(jnp.float32),
        lax.psum(reduced[8].astype(jnp.bfloat16), "expert").astype(jnp.float32),
        lax.psum(reduced[9].astype(jnp.bfloat16), "expert").astype(jnp.float32),
        lax.psum(grad_sgate.astype(jnp.bfloat16), "expert").astype(jnp.float32),
        lax.psum(grad_sup.astype(jnp.bfloat16), "expert").astype(jnp.float32),
        lax.psum(grad_sdown.astype(jnp.bfloat16), "expert").astype(jnp.float32),
    )
    return (
        result,
        grad_tokens,
        summed[0],
        summed[1],
        summed[2],
        summed[3],
        summed[4],
        summed[5],
        summed[6],
        summed[7],
        summed[8],
        summed[9],
        summed[10],
        summed[11],
        summed[12],
        local_gate_weight,
        local_up_weight,
        local_down_weight,
    )


def solution(mesh):
    in_specs = (
        P(("expert", "shard"), None),
        P("expert"),
        P(("expert", "shard"), None),
        P(("expert", "shard"), None),
        P("shard"),
        P("shard"),
        P("shard"),
        P("shard"),
        P("shard", None),
        P("shard", None),
        P("shard", None),
        P("shard", None),
        P("shard", None),
        P("shard", None),
        P(None, "shard"),
        P(None, "shard"),
        P("shard", None),
        P("expert", None, "shard"),
        P("expert", None, "shard"),
        P("expert", "shard", None),
    )
    out_specs = (
        P(("expert", "shard"), None),
        P(("expert", "shard"), None),
        P("shard"),
        P("shard"),
        P("shard"),
        P("shard"),
        P("shard", None),
        P("shard", None),
        P("shard", None),
        P("shard", None),
        P("shard", None),
        P("shard", None),
        P(None, "shard"),
        P(None, "shard"),
        P("shard", None),
        P("expert", None, "shard"),
        P("expert", None, "shard"),
        P("expert", "shard", None),
    )
    return jax.shard_map(
        per_device, mesh=mesh, in_specs=in_specs, out_specs=out_specs, check_vma=False
    )
```

profile of v0, /device:TPU:18, one launch (start us, length us, event | category | flops | bytes accessed | tf_op | source)
XLA Modules:
  0.0 1996.1 jit_solution(11241487128540587797)
XLA Ops:
  32.2 9.2 all-gather.16.cloned.1.call-done
  45.4 20.7 %all-gather.18.cloned.1.call-done = bf16[1536,3072]{1,0:T(8,128)(2,1)} async-done(((bf16[768,3072]{1,0:T(8,128)(2,1)}), bf16[1536,3072]{1,0:T(8,128)(2,1)}) %all-gather.18.cloned.1.call-update) | async-done | bytes 9437200 | tf_op jit(solution)/shard_map/all_gather | solution.py:119
  66.0 6.3 fusion.165
  72.4 9.8 all-gather.20.cloned.1.call-done
  90.9 13.8 all-gather.22.cloned.1.call-done
  112.9 7.1 all-to-all-start
  123.7 6.3 fusion.34
  129.9 85.2 %all-to-all-done = bf16[16,64,2048]{2,1,0:T(8,128)(2,1)} async-done(((bf16[16,64,2048]{2,1,0:T(8,128)(2,1)}), bf16[16,64,2048]{2,1,0:T(8,128)(2,1)}, u32[]{:S(2)}, u32[]{:S(2)}) %all-to-all-start) | async-done | bytes 4194336 | tf_op jit(solution)/shard_map/all_to_all | solution.py:217
  215.1 6.0 all-to-all-start.2
  221.7 12.0 fusion.10
  233.7 13.6 fusion.14
  247.3 66.3 %all-to-all-done.2 = bf16[16,64,2048]{2,1,0:T(8,128)(2,1)} async-done(((bf16[16,64,2048]{2,1,0:T(8,128)(2,1)}), bf16[16,64,2048]{2,1,0:T(8,128)(2,1)}, u32[]{:S(2)}, u32[]{:S(2)}) %all-to-all-start.2) | async-done | bytes 4194336 | tf_op jit(solution)/shard_map/all_to_all | solution.py:262
  313.6 16.0 fusion.18
  329.6 10.0 fusion.31
  346.2 9.7 fusion.8
  355.9 12.5 add_convert_fusion
  368.4 69.2 %all-to-all-done.1 = bf16[16,64,2048]{2,1,0:T(8,128)(2,1)} async-done(((bf16[16,64,2048]{2,1,0:T(8,128)(2,1)}), bf16[16,64,2048]{2,1,0:T(8,128)(2,1)}, u32[]{:S(2)}, u32[]{:S(2)}) %all-to-all-start.1) | async-done | bytes 4194336 | tf_op jit(solution)/shard_map/all_to_all | solution.py:236
  443.1 9.3 fusion.174
  452.4 7.0 fusion.173
  459.4 8.3 multiply_convert_fusion.6
  472.6 9.1 fusion.175
  481.7 8.3 fusion.1
  490.0 45.3 %all-to-all-done.3 = bf16[16,64,2048]{2,1,0:T(8,128)(2,1)} async-done(((bf16[16,64,2048]{2,1,0:T(8,128)(2,1)}), bf16[16,64,2048]{2,1,0:T(8,128)(2,1)}, u32[]{:S(2)}, u32[]{:S(2)}) %all-to-all-start.3) | async-done | bytes 4194336 | tf_op jit(solution)/shard_map/all_to_all | solution.py:287
  560.8 6.1 convolution_convert_fusion.1
  567.0 15.3 copy.178
  583.4 6.3 convolution_convert_fusion.2
  589.7 16.4 copy.176
  619.3 6.9 copy.156
  627.5 6.1 convolution_convert_fusion
  638.1 8.2 multiply_reduce_fusion.3
  660.3 6.4 convolution_convert_fusion.3
  668.6 12.4 fusion.6
  681.0 28.3 %copy.182 = bf16[1,2048,1408]{1,0,2:T(2,128)(2,1)} copy(bf16[1,2048,1408]{2,1,0:T(8,128)(2,1)} %fusion.6) | data formatting | bytes 11534336
  709.3 12.1 copy.190
  721.9 11.0 fusion.5
  732.9 28.3 %copy.180 = bf16[1,2048,1408]{1,0,2:T(2,128)(2,1)} copy(bf16[1,2048,1408]{2,1,0:T(8,128)(2,1)} %fusion.5) | data formatting | bytes 11534336
  761.2 11.4 copy.191
  772.7 10.5 fusion.7
  783.5 8.5 copy.179
  792.0 8.3 copy.177
  811.7 7.2 fusion.46
  823.3 67.3 %all-reduce.4 = (bf16[1024]{0:T(1024)(128)(2,1)S(1)}, bf16[768]{0:T(1024)(128)(2,1)S(1)}, bf16[256]{0:T(256)(128)(2,1)S(1)}, bf16[1024]{0:T(1024)(128)(2,1)S(1)}, bf16[1024,16]{0,1:T(8,128)(2,1)S(1)}) all-reduce(bf16[1024]{0:T(1024)(128)(2,1)S(1)} %dynamic-slice.1, ...), channel_id=1, replica_groups=mesh['expert'=16,'shard'=2] {'expert'}, use_global_device_ids=true, to_apply=%region_22.23 | all-reduce | flops 19456 | bytes 77824 | tf_op jit(solution)/shard_map/psum | solution.py:462
  894.9 6.9 reshape_bitcast_fusion
  901.8 13.3 copy.183
  918.5 6.9 reshape_bitcast_fusion.1
  925.4 13.4 copy.181
  947.3 1005.2 %all-reduce.9.cloned.1.call-done = (bf16[1024,1536]{1,0:T(8,128)(2,1)}, bf16[768,3072]{1,0:T(8,128)(2,1)}, bf16[1024,576]{0,1:T(8,128)(2,1)}, bf16[256,4096]{1,0...) async-done(((bf16[1024,1536]{1,0:T(8,128)(2,1)}, ...) | async-done | bytes 32636944 | tf_op jit(solution)/shard_map/psum | solution.py:466
  1983.4 6.0 convert_element_type.365
  (408 shorter events, 188.8 us)
Async XLA Ops:
  7.2 18.0 all-gather.14.cloned.1.call-start
  7.9 33.5 %all-gather.16.cloned.1.call-start = ((), (), s32[]{:S(2)}) async-start(), calls=%async_computation.19 | async-start | bytes 9437184 | tf_op jit(solution)/shard_map/all_gather | solution.py:118
  8.7 57.3 %all-gather.18.cloned.1.call-start = ((), (), s32[]{:S(2)}) async-start(), calls=%async_computation.20 | async-start | bytes 14155776 | tf_op jit(solution)/shard_map/all_gather | solution.py:119
  9.4 72.8 %all-gather.20.cloned.1.call-start = ((), (), s32[]{:S(2)}) async-start(), calls=%async_computation.21 | async-start | bytes 6291456 | tf_op jit(solution)/shard_map/all_gather | solution.py:121
  12.0 92.7 %all-gather.22.cloned.1.call-start = ((), (), s32[]{:S(2)}) async-start(), calls=%async_computation.22 | async-start | bytes 12582912 | tf_op jit(solution)/shard_map/all_gather | solution.py:122
  12.6 209.1 %all-gather.32.cloned.1.call-start = ((), (), s32[]{:S(2)}) async-start(), calls=%async_computation.27 | async-start | bytes 8650752 | tf_op jit(solution)/shard_map/all_gather | solution.py:220
  13.1 220.5 %all-gather.30.cloned.1.call-start = ((), (), s32[]{:S(2)}) async-start(), calls=%async_computation.26 | async-start | bytes 8650752 | tf_op jit(solution)/shard_map/all_gather | solution.py:219
  14.0 9.9 copy-start.81
  14.0 233.3 %all-gather.34.cloned.1.call-start = ((), (), s32[]{:S(2)}) async-start(), calls=%async_computation.28 | async-start | bytes 8650752 | tf_op jit(solution)/shard_map/all_gather | solution.py:221
  14.7 428.3 %all-gather.28.cloned.1.call-start = ((), (), s32[]{:S(2)}) async-start(), calls=%async_computation.25 | async-start | bytes 17301504 | tf_op jit(solution)/shard_map/all_gather | solution.py:247
  15.5 12.5 copy-start.85
  15.9 29.4 %copy-start.68 = (f32[128]{0:T(128)}, f32[128]{0:T(128)S(1)}, u32[]{:S(2)}) copy-start(f32[128]{0:T(128)S(1)} %add_rsqrt_fusion.3) | copy-start | bytes 1540
  16.6 11.4 copy-start.87
  18.5 26.9 %copy-start.66 = (f32[2,1,256]{2,1,0:T(1,128)}, f32[2,1,256]{2,1,0:T(1,128)S(1)}, u32[]{:S(2)}) copy-start(f32[2,1,256]{2,1,0:T(1,128)S(1)} %convert_element_type.375) | copy-start | bytes 6148
  20.3 45.7 %copy-start.52 = (f32[1536]{0:T(1024)}, f32[1536]{0:T(1024)S(1)}, u32[]{:S(2)}) copy-start(f32[1536]{0:T(1024)S(1)} %reshape.349) | copy-start | bytes 18436
  22.1 23.2 %copy-start.46 = (f32[2048]{0:T(1024)}, f32[2048]{0:T(1024)S(1)}, u32[]{:S(2)}) copy-start(f32[2048]{0:T(1024)S(1)} %convert_element_type.296) | copy-start | bytes 24580
  28.0 56.6 %copy-start.56 = (f32[128,32]{0,1:T(8,128)}, f32[128,32]{0,1:T(8,128)S(1)}, u32[]{:S(2)}) copy-start(f32[128,32]{0,1:T(8,128)S(1)} %get-tuple-element.149) | copy-start | bytes 49156
  28.0 56.6 %copy-start.58 = (f32[128,32]{0,1:T(8,128)}, f32[128,32]{0,1:T(8,128)S(1)}, u32[]{:S(2)}) copy-start(f32[128,32]{0,1:T(8,128)S(1)} %get-tuple-element.150) | copy-start | bytes 49156
  29.9 54.8 %copy-start.54 = (bf16[256,64]{0,1:T(8,128)(2,1)}, bf16[256,64]{0,1:T(8,128)(2,1)S(1)}, u32[]{:S(2)}) copy-start(bf16[256,64]{0,1:T(8,128)(2,1)S(1)} %all_gather.62) | copy-start | bytes 98308
  45.3 27.0 %copy-start.6 = (f32[128,1536]{1,0:T(8,128)}, f32[128,1536]{1,0:T(8,128)S(1)}, u32[]{:S(2)}) copy-start(f32[128,1536]{1,0:T(8,128)S(1)} %get-tuple-element.152) | copy-start | bytes 2359300
  45.4 27.0 %copy-start.74 = (f32[128]{0:T(128)}, f32[128]{0:T(128)S(1)}, u32[]{:S(2)}) copy-start(f32[128]{0:T(128)S(1)} %add_rsqrt_fusion.1) | copy-start | bytes 1540
  72.4 12.3 copy-start.13
  90.9 18.6 copy-start.24
  112.9 102.2 %all-to-all-start = ((bf16[16,64,2048]{2,1,0:T(8,128)(2,1)}), bf16[16,64,2048]{2,1,0:T(8,128)(2,1)}, u32[]{:S(2)}, u32[]{:S(2)}) async-start(bf16[16,64,2048]{2,1,0:T(8,128)(2,1)} %bitcast.316), calls=%async_computation | async-start | bytes 8388608 | tf_op jit(solution)/shard_map/all_to_all | solution.py:217
  215.1 98.5 %all-to-all-start.2 = ((bf16[16,64,2048]{2,1,0:T(8,128)(2,1)}), bf16[16,64,2048]{2,1,0:T(8,128)(2,1)}, u32[]{:S(2)}, u32[]{:S(2)}) async-start(bf16[16,64,2048]{2,1,0:T(8,128)(2,1)} %fusion.34), calls=%async_computation.2 | async-start | bytes 8388608 | tf_op jit(solution)/shard_map/all_to_all | solution.py:262
  221.1 231.3 %all-gather.26.cloned.1.call-start = ((), (), s32[]{:S(2)}) async-start(), calls=%async_computation.24 | async-start | bytes 17301504 | tf_op jit(solution)/shard_map/all_gather | solution.py:246
  313.6 16.0 copy-start.89
  339.6 97.9 %all-to-all-start.1 = ((bf16[16,64,2048]{2,1,0:T(8,128)(2,1)}), bf16[16,64,2048]{2,1,0:T(8,128)(2,1)}, u32[]{:S(2)}, u32[]{:S(2)}) async-start(bf16[16,64,2048]{2,1,0:T(8,128)(2,1)} %fusion.31), calls=%async_computation.1 | async-start | bytes 8388608 | tf_op jit(solution)/shard_map/all_to_all | solution.py:236
  345.5 113.9 %all-gather.24.cloned.1.call-start = ((), (), s32[]{:S(2)}) async-start(), calls=%async_computation.23 | async-start | bytes 17301504 | tf_op jit(solution)/shard_map/all_gather | solution.py:245
  437.6 97.7 %all-to-all-start.3 = ((bf16[16,64,2048]{2,1,0:T(8,128)(2,1)}), bf16[16,64,2048]{2,1,0:T(8,128)(2,1)}, u32[]{:S(2)}, u32[]{:S(2)}) async-start(bf16[16,64,2048]{2,1,0:T(8,128)(2,1)} %add_convert_fusion), calls=%async_computation.3 | async-start | bytes 8388608 | tf_op jit(solution)/shard_map/all_to_all | solution.py:287
  443.0 163.2 %reduce-scatter.45.cloned.1.call-start = ((), (), s32[]{:S(2)}) async-start(), calls=%async_computation.38 | async-start | bytes 98304
  490.0 51.7 %copy-start.64 = (f32[128,16]{0,1:T(8,128)}, f32[128,16]{0,1:T(8,128)S(1)}, u32[]{:S(2)}) copy-start(f32[128,16]{0,1:T(8,128)S(1)} %subtract_multiply_fusion) | copy-start | bytes 24580
  557.3 50.1 %reduce-scatter.43.cloned.1.call-start = ((), (), s32[]{:S(2)}) async-start(), calls=%async_computation.37 | async-start | bytes 393216
  560.8 222.7 %reduce-scatter.49.cloned.1.call-start = ((), (), s32[]{:S(2)}) async-start(), calls=%async_computation.40 | async-start | bytes 17301504
  582.3 209.7 %reduce-scatter.47.cloned.1.call-start = ((), (), s32[]{:S(2)}) async-start(), calls=%async_computation.39 | async-start | bytes 17301504
  606.2 194.2 %reduce-scatter.31.cloned.1.call-start = ((), (), s32[]{:S(2)}) async-start(), calls=%async_computation.31 | async-start | bytes 3538944 | tf_op jit(solution)/shard_map/reduce_scatter | solution.py:448
  611.8 188.5 %reduce-scatter.33.cloned.1.call-start = ((), (), s32[]{:S(2)}) async-start(), calls=%async_computation.32 | async-start | bytes 6291456 | tf_op jit(solution)/shard_map/reduce_scatter | solution.py:451
  626.2 174.2 %reduce-scatter.39.cloned.1.call-start = ((), (), s32[]{:S(2)}) async-start(), calls=%async_computation.35 | async-start | bytes 17301504 | tf_op jit(solution)/shard_map/reduce_scatter | solution.py:344
  633.6 166.8 %reduce-scatter.27.cloned.1.call-start = ((), (), s32[]{:S(2)}) async-start(), calls=%async_computation.29 | async-start | bytes 9437184 | tf_op jit(solution)/shard_map/reduce_scatter | solution.py:442
  652.2 148.2 %reduce-scatter.35.cloned.1.call-start = ((), (), s32[]{:S(2)}) async-start(), calls=%async_computation.33 | async-start | bytes 12582912 | tf_op jit(solution)/shard_map/reduce_scatter | solution.py:454
  659.7 140.7 %reduce-scatter.29.cloned.1.call-start = ((), (), s32[]{:S(2)}) async-start(), calls=%async_computation.30 | async-start | bytes 14155776 | tf_op jit(solution)/shard_map/reduce_scatter | solution.py:445
  666.6 156.6 %reduce-scatter.37.cloned.1.call-start = ((), (), s32[]{:S(2)}) async-start(), calls=%async_computation.34 | async-start | bytes 98304 | tf_op jit(solution)/shard_map/reduce_scatter | solution.py:457
  668.3 226.6 %reduce-scatter.53.cloned.1.call-start = ((), (), s32[]{:S(2)}) async-start(), calls=%async_computation.42 | async-start | bytes 8650752
  721.4 197.1 %reduce-scatter.51.cloned.1.call-start = ((), (), s32[]{:S(2)}) async-start(), calls=%async_computation.41 | async-start | bytes 8650752
  772.7 169.5 %reduce-scatter.41.cloned.1.call-start = ((), (), s32[]{:S(2)}) async-start(), calls=%async_computation.36 | async-start | bytes 8650752 | tf_op jit(solution)/shard_map/reduce_scatter | solution.py:297
  783.2 1169.3 %all-reduce.9.cloned.1.call-start = ((), (), s32[]{:S(2)}) async-start(), calls=%async_computation.43 | async-start | bytes 65273856 | tf_op jit(solution)/shard_map/psum | solution.py:466
  1967.4 10.8 slice-start.4
  1972.5 10.9 slice-start.2
  (85 other events, 314.6 us)
Sparse Core Ops, SparseCore 0:
  9.6 12.3 all-gather.13
  23.5 17.8 all-gather.15
  43.0 23.0 all-gather.17
  68.0 14.1 all-gather.19
  83.6 21.0 all-gather.21
  106.0 17.1 all-gather.31
  124.8 17.1 all-gather.29
  143.6 17.1 all-gather.33
  162.3 25.0 all-gather.27
  223.2 25.0 all-gather.25
  347.9 25.0 all-gather.23
  557.4 7.1 reduce-scatter.44
  566.8 8.8 reduce-scatter.42
  582.4 20.0 reduce-scatter.48
  606.3 20.5 reduce-scatter.46
  629.6 11.0 reduce-scatter.30
  643.4 13.3 reduce-scatter.32
  659.6 21.4 reduce-scatter.38
  684.1 15.6 reduce-scatter.26
  702.5 18.0 reduce-scatter.34
  723.6 18.9 reduce-scatter.28
  745.4 8.6 reduce-scatter.36
  757.1 15.0 reduce-scatter.52
  775.0 15.0 reduce-scatter.50
  792.4 15.1 reduce-scatter.40
  814.5 1138.0 all-reduce.8
where the time goes:
time: 2010 us; the launch traced here: 2000 us
  waiting for transfers between devices  1330 us (66%)
  matrix products  273 us (14%)
  local copies, waits for them, and re-layouts  210 us (10%)
  blocking collectives  84 us (4%)
  other arithmetic  53.3 us (3%)
  starting transfers between devices  27 us (1%)
    psum x1, waiting for transfers between devices, per_device(): lax.psum(reduced[4].astype(jnp.bfloat16), 'expert').astype(jnp.float32)  1010 us
    unnamed x231, local copies, waits for them, and re-layouts  197 us
    all_to_all x1, waiting for transfers between devices, per_device(): lax.all_to_all(send_rows, 'expert', split_axis=0, concat_axis=0, tiled=True)  85.2 us
    all_to_all x1, waiting for transfers between devices, per_device(): lax.all_to_all(out_exp, 'expert', split_axis=0, concat_axis=0, tiled=True)  69.2 us
    psum x1, blocking collectives, per_device(): lax.psum(reduced[0].astype(jnp.bfloat16), 'expert').astype(jnp.float32)  67.3 us
    all_to_all x1, waiting for transfers between devices, per_device(): lax.all_to_all(ret_grads, 'expert', split_axis=0, concat_axis=0, tiled=True)  66.3 us
    all_to_all x1, waiting for transfers between devices, per_device(): lax.all_to_all(grad_rows.astype(jnp.bfloat16), 'expert', split_axis=0, co...  45.3 us
  transfers between devices with their start and end apart: 30, of which 9 were waited for; matrix products, arithmetic and copies ran while one was open for 23% of the time, Pallas kernels for 0%

commit v1 on v0

v1 whole, which is shorter than its diff:
```python
import functools
import math

import jax
import jax.numpy as jnp
import numpy as np
from jax import lax
from jax.experimental import pallas as pl
from jax.experimental.pallas import tpu as pltpu
from jax.sharding import PartitionSpec as P

H = 16
DN = 128
DR = 64
DV = 128
KR = 512
TOP = 6


norm_eps = 1e-06
rope_base = 50000.0
route_scale = 2.446
masked_score = -1e30
highest = lax.Precision.HIGHEST
bfloat = jnp.bfloat16
single = jnp.float32


def row_scale(values):
    return lax.rsqrt(jnp.mean(values * values, axis=-1, keepdims=True) + norm_eps)


def norm_back(grad_out, normed_rows, scale_rows, gain):
    grad_normed = grad_out * gain
    grad_input = scale_rows * (
        grad_normed - normed_rows * jnp.mean(grad_normed * normed_rows, axis=-1, keepdims=True)
    )
    return (grad_input, jnp.sum(grad_out * normed_rows, axis=0))


def seq_positions(segments):
    token_count = segments.shape[0]
    index = jnp.arange(token_count, dtype=jnp.int32)
    change = jnp.concatenate([jnp.ones((1,), bool), segments[1:] != segments[:-1]])
    starts = lax.cummax(jnp.where(change, index, 0), axis=0)
    return index - starts


def rope_tables(positions, half):
    freq = rope_base ** (-jnp.arange(half, dtype=jnp.float32) / half)
    angles = positions.astype(jnp.float32)[:, None] * freq[None, :]
    return (jnp.cos(angles), jnp.sin(angles))


def rotate(values, cosine, sine):
    half = values.shape[-1] // 2
    first = values[..., :half]
    second = values[..., half:]
    return jnp.concatenate(
        [first * cosine - second * sine, second * cosine + first * sine], axis=-1
    )


def rotate_back(grads, cosine, sine):
    half = grads.shape[-1] // 2
    first = grads[..., :half]
    second = grads[..., half:]
    return jnp.concatenate(
        [first * cosine + second * sine, second * cosine - first * sine], axis=-1
    )


def silu_grads(grad_hidden, pre_gate, pre_up):
    sigma = jax.nn.sigmoid(pre_gate)
    grad_gate = grad_hidden * pre_up * sigma * (1.0 + pre_gate * (1.0 - sigma))
    grad_up = grad_hidden * pre_gate * sigma
    return (grad_gate.astype(bfloat), grad_up.astype(bfloat))


def dot(left, right):
    return jnp.dot(left, right, preferred_element_type=single)


def dot_t(left, right):
    return lax.dot_general(left, right, (((1,), (1,)), ((), ())), preferred_element_type=single)


def t_dot(left, right):
    return lax.dot_general(left, right, (((0,), (0,)), ((), ())), preferred_element_type=single)


def expert_kernel(count, pieces, capacity, experts, group, first, *refs):
    refs = list(refs)
    me_ref = refs.pop(0)
    blocks = [refs.pop(0) for _ in range(count)]
    cots = [refs.pop(0) for _ in range(count)]
    weights = [[refs.pop(0) for _ in range(pieces)] for _ in range(3)]
    if not first:
        refs = refs[4 + 3 * pieces:]
    backs = [refs.pop(0) for _ in range(count)]
    outs = [refs.pop(0) for _ in range(count)]
    kept = [refs.pop(0) for _ in range(4)]
    acts = [[refs.pop(0) for _ in range(pieces)] for _ in range(3)]
    full = [refs.pop(0) for _ in range(3)]
    rows, grads = refs.pop(0), refs.pop(0)
    act_scr = [[refs.pop(0) for _ in range(pieces)] for _ in range(3)]
    sem_w, sem_o = refs.pop(0), refs.pop(0)
    assert not refs
    model = cots[0].shape[1]
    tok = cots[0].shape[0]
    width = weights[0][0].shape[0]
    loads = []
    for k in range(3):
        loads.append([])
        for j in range(pieces):
            c = pltpu.make_async_copy(weights[k][j], full[k].at[pl.ds(j * width, width)], sem_w.at[k, j])
            c.start()
            loads[k].append(c)
    stores = []
    def store(src, dst, at):
        c = pltpu.make_async_copy(src, dst, sem_o.at[at])
        c.start()
        stores.append(c)
    me = me_ref[0]
    lane = lax.broadcasted_iota(jnp.int32, (tok, 128), 1)
    place = lax.broadcasted_iota(jnp.int32, (tok, capacity), 1).astype(single)
    picks, wcols = [], []
    for i in range(count):
        marks = blocks[i][:, model:model + 128].astype(single)
        code = jnp.sum(jnp.where(lane == me, marks, 0.0), axis=1, keepdims=True)
        weight = jnp.sum(jnp.where((lane == me + experts) | (lane == me + 2 * experts), marks, 0.0), axis=1, keepdims=True)
        pick = (code == place).astype(single).astype(bfloat)
        picks.append(pick)
        wcols.append(weight)
        here = pl.ds(i * capacity, capacity)
        rows[here] = t_dot(pick, blocks[i][:, :model]).astype(bfloat)
        scaled = (weight * cots[i][...].astype(single)).astype(bfloat)
        grads[here] = t_dot(pick, scaled).astype(bfloat)
    n = count * capacity
    store(rows, kept[0].at[pl.ds(group * n, n)], 0)
    store(grads, kept[1].at[pl.ds(group * n, n)], 1)
    for i in range(count):
        store(blocks[i].at[:, pl.ds(0, model)], kept[2].at[pl.ds((group * count + i) * tok, tok)], 2 + i)
        store(cots[i], kept[3].at[pl.ds((group * count + i) * tok, tok)], 2 + count + i)
    for c in loads[0]: c.wait()
    pre_gate = dot_t(rows[...], full[0][...])
    for c in loads[1]: c.wait()
    pre_up = dot_t(rows[...], full[1][...])
    sigma = jax.nn.sigmoid(pre_gate)
    silu = pre_gate * sigma
    hidden = (silu * pre_up).astype(bfloat)
    for c in loads[2]: c.wait()
    grad_hidden = dot_t(grads[...], full[2][...])
    grad_gate = (grad_hidden * pre_up * sigma * (1.0 + pre_gate * (1.0 - sigma))).astype(bfloat)
    grad_up = (grad_hidden * silu).astype(bfloat)
    at = 2 + 2 * count
    for k, v in enumerate((hidden, grad_gate, grad_up)):
        for j in range(pieces):
            act_scr[k][j][...] = v[:, j * width:(j + 1) * width]
            store(act_scr[k][j], acts[k][j].at[pl.ds(group * n, n)], at)
            at += 1
    back = (dot(grad_gate, full[0][...]) + dot(grad_up, full[1][...])).astype(bfloat)
    out = dot(hidden, full[2][...]).astype(bfloat)
    for i in range(count):
        here = slice(i * capacity, (i + 1) * capacity)
        got = dot(picks[i], out[here])
        dots = jnp.sum(got * cots[i][...].astype(single), axis=1, keepdims=True)
        outs[i][...] = (wcols[i] * got).astype(bfloat)
        backs[i][:, :model] = dot(picks[i], back[here]).astype(bfloat)
        high = dots.astype(bfloat).astype(single)
        tail = jnp.where(lane == me, high, 0.0) + jnp.where(lane == me + experts, dots - high, 0.0)
        backs[i][:, model:model + 128] = tail.astype(bfloat)
    for c in stores: c.wait()

def run_experts(me, blocks, cots, weights, capacity, experts, group, groups, carried):
    count, pieces = len(blocks), len(weights[0])
    tok, model = cots[0].shape
    width = weights[0][0].shape[0]
    n = count * capacity
    first = carried is None
    shape = jax.ShapeDtypeStruct
    kept = [shape((groups * n, model), bfloat)] * 2 + [shape((groups * count * tok, model), bfloat)] * 2
    kept += [shape((groups * n, width), bfloat)] * (3 * pieces)
    vm = pl.BlockSpec(memory_space=pltpu.VMEM)
    hbm = pl.BlockSpec(memory_space=pl.ANY)
    flat = [w for ws in weights for w in ws]
    operands = [me, *blocks, *cots, *flat]
    in_specs = [pl.BlockSpec(memory_space=pltpu.SMEM)] + [vm] * (2 * count) + [hbm] * len(flat)
    alias = {}
    if not first:
        base = len(operands)
        operands += list(carried)
        in_specs += [hbm] * len(kept)
        alias = {base + i: 2 * count + i for i in range(len(kept))}
    rows = n
    flops = 2 * rows * model * width * pieces * 6
    out = pl.pallas_call(
        functools.partial(expert_kernel, count, pieces, capacity, experts, group, first),
        out_shape=[shape(b.shape, bfloat) for b in blocks] + [shape((tok, model), bfloat)] * count + kept,
        in_specs=in_specs,
        out_specs=[vm] * (2 * count) + [hbm] * len(kept),
        input_output_aliases=alias,
        scratch_shapes=[pltpu.VMEM((pieces * width, model), bfloat)] * 3
        + [pltpu.VMEM((n, model), bfloat)] * 2
        + [pltpu.VMEM((n, width), bfloat)] * (3 * pieces)
        + [pltpu.SemaphoreType.DMA((3, pieces)), pltpu.SemaphoreType.DMA((2 + 2 * count + 3 * pieces,))],
        compiler_params=pltpu.CompilerParams(vmem_limit_bytes=58 << 20),
        cost_estimate=pl.CostEstimate(flops=flops, bytes_accessed=30 << 20, transcendentals=0),
    )(*operands)
    return out[:count], out[count:2 * count], out[2 * count:]


def shared_kernel(parts, tiles, start, width, first, *refs):
    refs = list(refs)
    xs = [refs.pop(0) for _ in range(parts)]
    cs = [refs.pop(0) for _ in range(parts)]
    weights = [refs.pop(0) for _ in range(3)]
    if not first:
        refs = refs[3:]
    outs = [refs.pop(0) for _ in range(3)]
    wgu, wd = (refs.pop(0) for _ in range(2))
    accs = [refs.pop(0) for _ in range(2)]
    sem_w, sem_o = refs
    step = pl.program_id(0)
    cols = pl.ds(start, width)
    loads = [
        pltpu.make_async_copy(weights[0].at[:, cols], wgu.at[:, pl.ds(0, width)], sem_w.at[0]),
        pltpu.make_async_copy(weights[1].at[:, cols], wgu.at[:, pl.ds(width, width)], sem_w.at[1]),
        pltpu.make_async_copy(weights[2].at[cols], wd, sem_w.at[2]),
    ]

    @pl.when(step == 0)
    def _():
        for c in loads:
            c.start()
        for a in accs:
            a[...] = jnp.zeros_like(a)
        for c in loads:
            c.wait()

    def work(x_ref, c_ref):
        x, c = x_ref[...], c_ref[...]
        pre = dot(x, wgu[...])
        pre_gate, pre_up = pre[:, :width], pre[:, width:]
        grad_hidden = dot_t(c, wd[...])
        sigma = jax.nn.sigmoid(pre_gate)
        silu = pre_gate * sigma
        hidden = (silu * pre_up).astype(bfloat)
        grad_gate = (grad_hidden * pre_up * sigma * (1.0 + pre_gate * (1.0 - sigma))).astype(bfloat)
        grad_up = (grad_hidden * silu).astype(bfloat)
        accs[0][...] += t_dot(x, jnp.concatenate([grad_gate, grad_up], axis=1))
        accs[1][...] += t_dot(hidden, c)

    if parts == 1:
        work(xs[0], cs[0])
    else:
        per = tiles // parts
        for p in range(parts):
            pl.when(step // per == p)(functools.partial(work, xs[p], cs[p]))

    @pl.when(step == tiles - 1)
    def _():
        puts = [
            pltpu.make_async_copy(accs[0].at[:, pl.ds(0, width)], outs[0].at[:, cols], sem_o.at[0]),
            pltpu.make_async_copy(accs[0].at[:, pl.ds(width, width)], outs[1].at[:, cols], sem_o.at[1]),
            pltpu.make_async_copy(accs[1], outs[2].at[cols], sem_o.at[2]),
        ]
        for c in puts:
            c.start()
        for c in puts:
            c.wait()

def run_shared(xs, cs, weights, start, width, carried, tile=512):
    parts = len(xs)
    rows, model = xs[0].shape
    per = rows // tile
    tiles = per * parts
    shape = jax.ShapeDtypeStruct
    hbm = pl.BlockSpec(memory_space=pl.ANY)
    specs = [
        pl.BlockSpec((tile, model), lambda i, p=p: (jnp.clip(i - p * per, 0, per - 1), 0))
        for p in range(parts)
    ]
    outs = [shape(w.shape, single) for w in weights]
    operands = [*xs, *cs, *weights]
    in_specs = specs + specs + [hbm] * 3
    alias = {}
    if carried is not None:
        alias = {len(operands) + i: i for i in range(3)}
        operands += list(carried)
        in_specs += [hbm] * 3
    return pl.pallas_call(
        functools.partial(shared_kernel, parts, tiles, start, width, carried is None),
        grid=(tiles,),
        out_shape=outs,
        in_specs=in_specs,
        out_specs=[hbm] * 3,
        input_output_aliases=alias,
        scratch_shapes=[
            pltpu.VMEM((model, 2 * width), bfloat),
            pltpu.VMEM((width, model), bfloat),
            pltpu.VMEM((model, 2 * width), single),
            pltpu.VMEM((width, model), single),
            pltpu.SemaphoreType.DMA((3,)),
            pltpu.SemaphoreType.DMA((3,)),
        ],
        compiler_params=pltpu.CompilerParams(vmem_limit_bytes=60 << 20),
        cost_estimate=pl.CostEstimate(flops=12 * tiles * tile * model * width, bytes_accessed=4 * tiles * tile * model, transcendentals=0),
    )(*operands)


def widths_of(total):
    if total % 128:
        return [total]
    out = []
    while total > 0:
        out.append(min(512, total))
        total -= out[-1]
    return out


def tie(value, *others):
    hbm = pl.BlockSpec(memory_space=pl.ANY)
    return pl.pallas_call(
        lambda *refs: None,
        out_shape=jax.ShapeDtypeStruct(value.shape, value.dtype),
        in_specs=[hbm] * (1 + len(others)),
        out_specs=hbm,
        input_output_aliases={0: 0},
    )(value, *others)


def grid_of(experts, shards):
    if shards == 2 and experts % 4 == 0:
        return (experts // 4, 2, 2)
    side = math.isqrt(experts)
    return (side, side) if side * side == experts else (experts,)


class Chips:
    def __init__(self, dims, names):
        self.dims = dims
        self.names = names
        self.size = int(np.prod(dims))
        self.plane = self.size // dims[0]
        self.places = [tuple(int(v) for v in np.unravel_index(i, dims)) for i in range(self.size)]
        self.offsets = [
            tuple(int(v) for v in np.unravel_index(i, dims[1:])) for i in range(self.plane)
        ]

    def index(self, place):
        return int(np.ravel_multi_index(place, self.dims))

    def own(self, axis):
        return lax.axis_index(self.names[axis])

    def me(self):
        return lax.axis_index(self.names)

    def pairs(self, axis_of, by):
        out = []
        for i, place in enumerate(self.places):
            axis = axis_of(place)
            to = list(place)
            to[axis] = (to[axis] + by) % self.dims[axis]
            out.append((i, self.index(to)))
        return out

    def turning(self, turn, second):
        return lambda place: 1 if ((place[0] + turn) % 2 == 0) != second else 2

    def along(self, value, axis, by):
        n = self.dims[axis]
        return lax.ppermute(value, self.names[axis], [(i, (i + by) % n) for i in range(n)])

    def in_plane(self, value, turn, second, by):
        return lax.ppermute(value, self.names, self.pairs(self.turning(turn, second), by))

    def offset_by(self, value, offset):
        out = []
        for i, place in enumerate(self.places):
            to = [place[0]] + [
                (p + o) % d for p, o, d in zip(place[1:], offset, self.dims[1:])
            ]
            out.append((i, self.index(to)))
        return lax.ppermute(value, self.names, out)

    def tree(self, block, along, in_plane):
        first = [block] + [along(block, 0, j) for j in range(1, self.dims[0])]
        out = []
        for j, b in enumerate(first):
            if len(self.dims) == 1:
                out.append(b)
            elif len(self.dims) == 2:
                out += [b] + [along(b, 1, s) for s in range(1, self.dims[1])]
            else:
                n = self.dims[1]
                hops = [b] + [in_plane(b, j, False, s) for s in range(1, n)]
                for h in hops:
                    out += [h] + [in_plane(h, j, True, s) for s in range(1, n)]
        return out

    def spread(self, block):
        return self.tree(block, self.along, self.in_plane)

    def sources(self):
        def apply(values, pairs):
            out = [0] * len(values)
            for i, to in pairs:
                out[to] = values[i]
            return out

        def along(values, axis, by):
            return apply(values, self.pairs(lambda place: axis, by))

        def in_plane(values, turn, second, by):
            return apply(values, self.pairs(self.turning(turn, second), by))

        table = self.tree(list(range(self.size)), along, in_plane)
        return jnp.asarray(np.array(table, np.int32).T)[self.me()]

    def collect(self, blocks, fillers=()):
        fillers = list(fillers)
        rest = self.plane
        total = None
        for j in range(self.dims[0] - 1, -1, -1):
            part = blocks[j * rest : (j + 1) * rest]
            if len(self.dims) == 1:
                acc = part[0].astype(single)
            elif len(self.dims) == 2:
                acc = part[0].astype(single)
                for s in range(1, self.dims[1]):
                    acc = acc + self.along(part[s], 1, -s).astype(single)
            else:
                n = self.dims[1]
                accs = []
                for h in range(n):
                    a = part[h * n].astype(single)
                    for s in range(1, n):
                        a = a + self.in_plane(part[h * n + s], j, True, -s).astype(single)
                    accs.append(a)
                acc = accs[0]
                for s in range(1, n):
                    acc = acc + self.in_plane(accs[s].astype(bfloat), j, False, -s).astype(single)
            if j > 0:
                acc = self.along(acc.astype(bfloat), 0, -j).astype(single)
            total = acc if total is None else total + acc
        return total

    def own_part(self):
        part = 0
        for axis in range(1, len(self.dims)):
            part = part * self.dims[axis] + self.own(axis)
        return part

    def swap_columns(self, value):
        size = value.shape[1] // self.plane
        out = []
        for offset in self.offsets:
            part = 0
            for axis, by in enumerate(offset):
                n = self.dims[axis + 1]
                part = part * n + (self.own(axis + 1) + by) % n
            piece = lax.dynamic_slice_in_dim(value, part * size, size, 1)
            out.append(self.offset_by(piece, offset) if any(offset) else piece)
        return jnp.concatenate(out, axis=0)

    def stack(self, value):
        if len(self.dims) != 3:
            rows = [self.offset_by(value, o) if any(o) else value for o in self.offsets]
            return [jnp.concatenate(rows, axis=0)]
        n = self.dims[1]
        cut = value.shape[1] // 256 * 128
        out = []
        for half, (one, two) in zip((value[:, :cut], value[:, cut:]), ((2, 1), (1, 2))):
            first = [half] + [self.along(half, one, s) for s in range(1, n)]
            first = jnp.concatenate(first, axis=0)
            second = [first] + [self.along(first, two, s) for s in range(1, n)]
            rows = half.shape[0]
            if one == 2:
                out.append(jnp.concatenate(second, axis=0))
            else:
                out.append(
                    jnp.concatenate(
                        [v[s * rows : (s + 1) * rows] for s in range(n) for v in second], axis=0
                    )
                )
        return out

    def plane_sums(self, value):
        if len(self.dims) != 3:
            return [self.scatter_axis(value, axis) for axis in range(1, len(self.dims))]
        cut = value.shape[1] // 2
        out = []
        for half, order in zip((value[:, :cut], value[:, cut:]), ((1, 2), (2, 1))):
            for axis in order:
                half = self.scatter_axis(half, axis)
            out.append(half)
        return out

    def plane_part(self, value):
        size = value.shape[0] // self.plane
        total = None
        for offset in self.offsets:
            part = 0
            for axis, by in enumerate(offset):
                n = self.dims[axis + 1]
                part = part * n + (self.own(axis + 1) + by) % n
            piece = lax.dynamic_slice_in_dim(value, part * size, size, 0)
            if any(offset):
                piece = self.offset_by(piece.astype(bfloat), offset).astype(single)
            total = piece if total is None else total + piece
        return total.astype(bfloat)

    def unstack(self, halves, swapped):
        if len(self.dims) != 3:
            out = halves[0]
            for axis in range(len(self.dims) - 1, 0, -1):
                out = self.gather_axis(out, axis)
            return out
        one = self.gather_axis(self.gather_axis(halves[0], 2), 1)
        two = self.gather_axis(self.gather_axis(halves[1], 1), 2)
        if swapped:
            n, m = self.dims[1], self.dims[2]
            rows = two.shape[0] // (n * m)
            two = two.reshape(m, n, rows, -1).swapaxes(0, 1).reshape(two.shape)
        return jnp.concatenate([one, two], axis=1)

    def line_sums(self, halves, before=()):
        halves = lax.optimization_barrier((*halves, *before))[: len(halves)]
        return lax.psum(tuple(halves), self.names[0])

    def scatter_axis(self, value, axis):
        n = self.dims[axis]
        rows = value.shape[0] // n
        own = self.own(axis)
        total = lax.dynamic_slice_in_dim(value, own * rows, rows, 0).astype(single)
        for j in range(1, n):
            piece = lax.dynamic_slice_in_dim(value, ((own + j) % n) * rows, rows, 0)
            total = total + self.along(piece, axis, j).astype(single)
        return total.astype(bfloat)

    def gather_axis(self, value, axis):
        n = self.dims[axis]
        pieces = [value] + [self.along(value, axis, j) for j in range(1, n)]
        return in_order(pieces, self.own(axis), 0)


def after(value, *others):
    return lax.optimization_barrier((value, *others))[0]


def in_order(pieces, own, axis):
    n = len(pieces)
    if n == 1:
        return pieces[0]
    if n == 2:
        return jnp.where(
            own == 0,
            jnp.concatenate(pieces, axis=axis),
            jnp.concatenate([pieces[1], pieces[0]], axis=axis),
        )
    turned = pieces[::-1]
    line = jnp.concatenate(turned + turned[:-1], axis=axis)
    extent = pieces[0].shape[axis]
    return lax.dynamic_slice_in_dim(line, (n - 1 - own) * extent, n * extent, axis)


class Cores:
    def __init__(self, count):
        self.count = count
        self.own = lax.axis_index("shard")

    def along(self, value, by):
        n = self.count
        return lax.ppermute(value, "shard", [(i, (i + by) % n) for i in range(n)])

    def spread(self, value):
        return [value] + [self.along(value, j) for j in range(1, self.count)]

    def whole(self, value, axis):
        return in_order(self.spread(value), self.own, axis)

    def chunk(self, value, j, axis):
        size = value.shape[axis] // self.count
        place = (self.own + j + self.count) % self.count
        return lax.dynamic_slice_in_dim(value, place * size, size, axis)

    def rows_times(self, left, pieces):
        out = None
        for j, piece in enumerate(pieces):
            term = dot(self.chunk(left, -j, 1), piece)
            out = term if out is None else out + term
        return out

    def times_rows_t(self, left, pieces):
        return in_order([dot_t(left, piece) for piece in pieces], self.own, 1)

    def swap_columns(self, value, axis=1):
        parts = [self.chunk(value, 0, axis)]
        parts += [self.along(self.chunk(value, j, axis), j) for j in range(1, self.count)]
        return jnp.concatenate(parts, axis=0)

    def stack(self, value):
        return jnp.concatenate(self.spread(value), axis=0)

    def give_back(self, value):
        rows = value.shape[0] // self.count
        total = value[:rows]
        for j in range(1, self.count):
            total = total + self.along(value[j * rows : (j + 1) * rows], -j)
        return total

    def scatter(self, value, axis):
        total = self.chunk(value, 0, axis).astype(single)
        for j in range(1, self.count):
            total = total + self.along(self.chunk(value, j, axis).astype(bfloat), j).astype(single)
        return total


def per_device(
    chips,
    shards,
    tokens,
    segment_ids,
    routes,
    cotangent,
    gain_attn,
    gain_query,
    gain_latent,
    gain_ffn,
    w_qa,
    w_qb,
    w_kva,
    w_kvb,
    w_out,
    w_router,
    shared_gate,
    shared_up,
    shared_down,
    expert_gate,
    expert_up,
    expert_down,
):
    cores = Cores(shards)
    me = chips.me()
    shard_pos = cores.own
    tok_rows = tokens.shape[0]
    model = tokens.shape[1]
    group_rows = tok_rows * shards
    score_scale = 1.0 / (DN + DR) ** 0.5
    query_rank = w_qa.shape[1]

    gains = jnp.concatenate([gain_attn, gain_query, gain_latent, gain_ffn])
    gain_pieces = cores.spread(gains)
    sizes = [v.shape[0] for v in (gain_attn, gain_query, gain_latent, gain_ffn)]
    full_gains = []
    start = 0
    for size in sizes:
        full_gains.append(
            in_order([g[start : start + size] for g in gain_pieces], shard_pos, 0).astype(single)
        )
        start += size
    gain_attn_f, gain_query_f, gain_latent_f, gain_ffn_f = full_gains
    qa_pieces = cores.spread(w_qa)
    kva_pieces = cores.spread(w_kva)
    qb_pieces = cores.spread(w_qb)
    kvb_full = cores.whole(w_kvb, 0)
    out_pieces = cores.spread(w_out)
    router_full = cores.whole(w_router, 0)
    expert_weights = [
        cores.spread(expert_gate[0].T),
        cores.spread(expert_up[0].T),
        cores.spread(expert_down[0]),
    ]
    cot_blocks = chips.spread(cotangent)

    resid = tokens.astype(single)
    attn_scale = row_scale(resid)
    attn_normed = resid * attn_scale
    attn_in = (attn_normed * gain_attn_f).astype(bfloat)
    query_lat = cores.rows_times(attn_in, qa_pieces)
    query_scale = row_scale(query_lat)
    query_normed = query_lat * query_scale
    query_in = (query_normed * gain_query_f).astype(bfloat)
    query_all = cores.rows_times(query_in, qb_pieces).reshape(tok_rows, H, DN + DR)
    group_pos = seq_positions(segment_ids)
    own_start = shard_pos * tok_rows
    own_pos = lax.dynamic_slice_in_dim(group_pos, own_start, tok_rows, 0)
    own_seg = lax.dynamic_slice_in_dim(segment_ids, own_start, tok_rows, 0)
    cosine, sine = rope_tables(own_pos, DR // 2)
    query_nope = query_all[..., :DN].astype(bfloat)
    query_rope = rotate(query_all[..., DN:], cosine[:, None, :], sine[:, None, :]).astype(bfloat)
    latent_raw = cores.rows_times(attn_in, kva_pieces)
    latent_part = latent_raw[:, :KR]
    latent_scale = row_scale(latent_part)
    latent_normed = latent_part * latent_scale
    latent = (latent_normed * gain_latent_f).astype(bfloat)
    key_rope = rotate(latent_raw[:, KR:], cosine, sine).astype(bfloat)
    keys = cores.whole(jnp.concatenate([latent, key_rope], axis=1), 0)
    keys_latent, keys_rope = keys[:, :KR], keys[:, KR:]
    kvb_heads = kvb_full.reshape(KR, H, DN + DV)
    w_uk = kvb_heads[..., :DN]
    w_uv = kvb_heads[..., DN:]
    query_abs = jnp.einsum(
        "thn,khn->thk", query_nope, w_uk, preferred_element_type=single
    ).astype(bfloat)
    group_index = jnp.arange(group_rows, dtype=jnp.int32)
    own_index = own_start + jnp.arange(tok_rows, dtype=jnp.int32)
    visible = (own_seg[:, None] == segment_ids[None, :]) & (
        group_index[None, :] <= own_index[:, None]
    )

    def scores_of():
        raw = jnp.einsum("thk,gk->htg", query_abs, keys_latent, preferred_element_type=single)
        raw = raw + jnp.einsum("thr,gr->htg", query_rope, keys_rope, preferred_element_type=single)
        return jnp.where(visible[None], raw * score_scale, masked_score)

    scores = scores_of()
    top_score = jnp.max(scores, axis=-1, keepdims=True)
    expd = jnp.exp(scores - top_score)
    total = jnp.sum(expd, axis=-1, keepdims=True)
    probs = expd / total
    probs_low = probs.astype(bfloat)
    attn_lat = jnp.einsum(
        "htg,gk->thk", probs_low, keys_latent, preferred_element_type=single
    ).astype(bfloat)
    attn_heads = (
        jnp.einsum("thk,khv->thv", attn_lat, w_uv, preferred_element_type=single)
        .astype(bfloat)
        .reshape(tok_rows, H * DV)
    )
    mid = resid + cores.rows_times(attn_heads, out_pieces)
    ffn_scale = row_scale(mid)
    ffn_normed = mid * ffn_scale
    ffn_in = (ffn_normed * gain_ffn_f).astype(bfloat)

    experts_all = router_full.shape[1]
    lanes = -(-4 * experts_all // 128) * 128
    logits = dot(ffn_in, router_full)
    chosen = jnp.sum(
        (routes[:, :, None] == jnp.arange(experts_all, dtype=jnp.int32)[None, None, :]).astype(
            single
        ),
        axis=1,
    )
    sig = jax.nn.sigmoid(logits)
    denom = jnp.sum(chosen * sig, axis=-1, keepdims=True)
    routing_weights = route_scale * chosen * sig / denom
    capacity = min(tok_rows, 4 * tok_rows * TOP // (3 * experts_all))
    earlier = (jnp.arange(tok_rows)[:, None] > jnp.arange(tok_rows)[None, :]).astype(bfloat)
    slot = dot(earlier, chosen.astype(bfloat))
    code = jnp.where(chosen > 0, slot, -1.0)
    weight_high = routing_weights.astype(bfloat)
    weight_rest = (routing_weights - weight_high.astype(single)).astype(bfloat)
    marks = jnp.concatenate(
        [
            code.astype(bfloat),
            weight_high,
            weight_rest,
            jnp.zeros((tok_rows, lanes - 3 * experts_all), bfloat),
        ],
        axis=1,
    )
    blocks = chips.spread(jnp.concatenate([ffn_in, marks], axis=1))

    stack_ffn = cores.stack(ffn_in)
    stack_cot = cores.stack(cotangent)

    def feed_forward(rows, grads, gate, up, down):
        pre_gate = dot(rows, gate)
        pre_up = dot(rows, up)
        hidden = (jax.nn.silu(pre_gate) * pre_up).astype(bfloat)
        grad_gate, grad_up = silu_grads(dot_t(grads, down), pre_gate, pre_up)
        return hidden, grad_gate, grad_up

    sh_hidden, sh_gate, sh_up = feed_forward(
        stack_ffn, stack_cot, shared_gate, shared_up, shared_down
    )
    shared_out = cores.give_back(dot(sh_hidden, shared_down))
    shared_back = cores.give_back(dot_t(sh_gate, shared_gate) + dot_t(sh_up, shared_up))

    back_blocks, out_blocks, kept = [], [], None
    turns = chips.dims[0]
    per_turn = chips.plane
    who = me.astype(jnp.int32).reshape(1)
    for turn in range(turns):
        here = slice(turn * per_turn, (turn + 1) * per_turn)
        backs, outs, kept = run_experts(
            who,
            blocks[here],
            cot_blocks[here],
            expert_weights,
            capacity,
            experts_all,
            turn,
            turns,
            kept,
        )
        back_blocks += backs
        out_blocks += outs
    rows, row_grads, chip_ffn, chip_cot = kept[:4]
    acts = [kept[4 + k * shards : 4 + (k + 1) * shards] for k in range(3)]
    hiddens, gate_grads, up_grads = acts
    routed_back = chips.collect(back_blocks)
    routed_out = chips.collect(out_blocks)
    result = mid + shared_out + routed_out

    def over_cores(lefts, right):
        sent = [t_dot(lefts[j], right).astype(bfloat) for j in range(1, shards)]
        got = [cores.along(v, -j - 1).astype(single) for j, v in enumerate(sent)]
        return sum(got, t_dot(lefts[0], right))

    grad_egate = over_cores(gate_grads, rows).T[None]
    grad_eup = over_cores(up_grads, rows).T[None]
    grad_edown = over_cores(hiddens, row_grads)[None]

    if shards == 2:
        xs, cs = cores.spread(chip_ffn), cores.spread(chip_cot)
        shared_weights = (shared_gate, shared_up, shared_down)
        shared_grads = None
        start = 0
        for width in widths_of(shared_gate.shape[1]):
            shared_grads = run_shared(xs, cs, shared_weights, start, width, shared_grads)
            start += width
        grad_sgate, grad_sup, grad_sdown = shared_grads
    else:
        grad_sgate = grad_sup = grad_sdown = 0.0
        all_ffn, all_cot = chip_ffn, chip_cot
        for turn in range(shards):
            if turn > 0:
                tied = lax.optimization_barrier(
                    (all_ffn, all_cot, grad_sgate, grad_sup, grad_sdown)
                )
                grad_sgate, grad_sup, grad_sdown = tied[2:]
                all_ffn, all_cot = cores.along(tied[0], 1), cores.along(tied[1], 1)
            all_hidden, all_gate, all_up = feed_forward(
                all_ffn, all_cot, shared_gate, shared_up, shared_down
            )
            grad_sgate = grad_sgate + t_dot(all_ffn, all_gate)
            grad_sup = grad_sup + t_dot(all_ffn, all_up)
            grad_sdown = grad_sdown + t_dot(all_hidden, all_cot)

    grad_out = cotangent.astype(single)
    grad_weights = (
        routed_back[:, model : model + experts_all]
        + routed_back[:, model + experts_all : model + 2 * experts_all]
    )
    grad_sig = chosen * (
        route_scale * grad_weights / denom
        - jnp.sum(grad_weights * routing_weights, axis=-1, keepdims=True) / denom
    )
    grad_logits = grad_sig * sig * (1.0 - sig)
    grad_router = jnp.einsum("te,td->ed", grad_logits, ffn_in.astype(single), precision=highest)
    grad_ffn_in = (
        routed_back[:, :model]
        + shared_back
        + jnp.einsum("te,de->td", grad_logits, router_full.astype(single), precision=highest)
    )
    grad_mid, grad_gffn = norm_back(grad_ffn_in, ffn_normed, ffn_scale, gain_ffn_f)
    grad_mid = grad_mid + grad_out

    def over_plane(rows, grads, extra=None):
        left = chips.swap_columns(cores.swap_columns(rows))
        halves = [t_dot(left, right).astype(bfloat) for right in chips.stack(cores.stack(grads))]
        if extra is not None:
            halves[-1] = jnp.concatenate([halves[-1], extra], axis=1)
        sums = chips.line_sums(halves, done)
        done[:] = sums
        return chips.unstack(sums, True)

    done = []

    grad_attn_out = grad_mid.astype(bfloat)
    grad_wout = over_plane(attn_heads, grad_attn_out)
    grad_heads = (
        cores.times_rows_t(grad_attn_out, out_pieces).astype(bfloat).reshape(tok_rows, H, DV)
    )
    grad_uv = jnp.einsum("thk,thv->khv", attn_lat, grad_heads, preferred_element_type=single)
    grad_attn_lat = jnp.einsum(
        "thv,khv->thk", grad_heads, w_uv, preferred_element_type=single
    ).astype(bfloat)
    grad_probs = jnp.einsum(
        "thk,gk->htg", grad_attn_lat, keys_latent, preferred_element_type=single
    )
    delta = jnp.sum(probs * grad_probs, axis=-1, keepdims=True)
    grad_scores = (probs * (grad_probs - delta)).astype(bfloat)
    grad_qabs = (
        jnp.einsum("htg,gk->thk", grad_scores, keys_latent, preferred_element_type=single)
        * score_scale
    ).astype(bfloat)
    grad_qrope = (
        jnp.einsum("htg,gr->thr", grad_scores, keys_rope, preferred_element_type=single)
        * score_scale
    )
    key_terms = (
        jnp.einsum("htg,thk->gk", grad_scores, query_abs, preferred_element_type=single)
        * score_scale
    )
    key_terms = key_terms + jnp.einsum(
        "htg,thk->gk", probs_low, grad_attn_lat, preferred_element_type=single
    )
    rope_terms = (
        jnp.einsum("htg,thr->gr", grad_scores, query_rope, preferred_element_type=single)
        * score_scale
    )
    grad_keys = cores.scatter(jnp.concatenate([key_terms, rope_terms], axis=1), 0)
    grad_latent, grad_krope = grad_keys[:, :KR], grad_keys[:, KR:]
    grad_uk = jnp.einsum("thn,thk->khn", query_nope, grad_qabs, preferred_element_type=single)
    kvb_terms = jnp.concatenate([grad_uk, grad_uv], axis=-1).reshape(KR, H * (DN + DV))
    kvb_sums = chips.line_sums(
        chips.plane_sums(cores.scatter(kvb_terms, 0).astype(bfloat)), done
    )
    done[:] = kvb_sums
    grad_wkvb = chips.unstack(kvb_sums, False)
    grad_qnope = jnp.einsum("thk,khn->thn", grad_qabs, w_uk, preferred_element_type=single)
    grad_qrope_raw = rotate_back(grad_qrope, cosine[:, None, :], sine[:, None, :])
    grad_query = (
        jnp.concatenate([grad_qnope, grad_qrope_raw], axis=-1)
        .astype(bfloat)
        .reshape(tok_rows, H * (DN + DR))
    )
    grad_wqb = over_plane(query_in, grad_query)
    grad_query_in = cores.times_rows_t(grad_query, qb_pieces)
    grad_qlat, grad_gquery = norm_back(grad_query_in, query_normed, query_scale, gain_query_f)
    grad_kvpart, grad_glatent = norm_back(grad_latent, latent_normed, latent_scale, gain_latent_f)
    grad_kvrope = rotate_back(grad_krope, cosine, sine)
    grad_low = jnp.concatenate([grad_qlat, grad_kvpart, grad_kvrope], axis=-1).astype(bfloat)
    grad_attn_in = in_order(
        [
            dot_t(grad_low[:, :query_rank], qa) + dot_t(grad_low[:, query_rank:], kva)
            for qa, kva in zip(qa_pieces, kva_pieces)
        ],
        shard_pos,
        1,
    )
    grad_resid, grad_gattn = norm_back(grad_attn_in, attn_normed, attn_scale, gain_attn_f)
    grad_tokens = grad_mid + grad_resid

    mixed = jnp.concatenate(
        [grad_gquery.reshape(shards, -1), grad_glatent.reshape(shards, -1)], axis=1
    ).reshape(-1)
    small = jnp.concatenate(
        [grad_gattn[None], grad_gffn[None], mixed[None], grad_router], axis=0
    )
    small = cores.scatter(small, 1)
    grad_wlow = over_plane(attn_in, grad_low, chips.plane_part(small.T))
    low_cols = grad_low.shape[1]
    small = grad_wlow[:, low_cols : low_cols + small.shape[0]].astype(single)
    query_part = gain_query.shape[0]
    return (
        result,
        grad_tokens,
        small[:, 0],
        small[:query_part, 2],
        small[query_part:, 2],
        small[:, 1],
        grad_wlow[:, :query_rank].astype(single),
        grad_wqb.astype(single),
        grad_wlow[:, query_rank:low_cols].astype(single),
        grad_wkvb.astype(single),
        grad_wout.astype(single),
        small[:, 3:],
        grad_sgate,
        grad_sup,
        grad_sdown,
        grad_egate,
        grad_eup,
        grad_edown,
    )


def solution(mesh):
    shards = mesh.shape["shard"]
    dims = grid_of(mesh.shape["expert"], shards)
    names = tuple(f"line{i}" for i in range(len(dims)))
    grid = jax.sharding.Mesh(mesh.devices.reshape(dims + (shards,)), names + ("shard",))
    chips = Chips(dims, names)
    both = names + ("shard",)
    in_specs = (
        P(both, None),
        P(names),
        P(both, None),
        P(both, None),
        P("shard"),
        P("shard"),
        P("shard"),
        P("shard"),
        P("shard", None),
        P("shard", None),
        P("shard", None),
        P("shard", None),
        P("shard", None),
        P("shard", None),
        P(None, "shard"),
        P(None, "shard"),
        P("shard", None),
        P(names, None, "shard"),
        P(names, None, "shard"),
        P(names, "shard", None),
    )
    out_specs = (
        P(both, None),
        P(both, None),
        P("shard"),
        P("shard"),
        P("shard"),
        P("shard"),
        P("shard", None),
        P("shard", None),
        P("shard", None),
        P("shard", None),
        P("shard", None),
        P("shard", None),
        P(None, "shard"),
        P(None, "shard"),
        P("shard", None),
        P(names, None, "shard"),
        P(names, None, "shard"),
        P(names, "shard", None),
    )

    def body(*args):
        return per_device(chips, shards, *args)

    return jax.shard_map(
        body, mesh=grid, in_specs=in_specs, out_specs=out_specs, check_vma=False
    )
```

time: 2010 us -> 1310 us (0.65)
  waiting for transfers between devices: 1330 us -> 495 us
  Pallas kernels: 0 us -> 282 us
  starting transfers between devices: 27 us -> 148 us
  local copies, waits for them, and re-layouts: 210 us -> 90.4 us
  matrix products: 273 us -> 158 us
  blocking collectives: 84 us -> 0 us
  other arithmetic: 53.3 us -> 104 us
    psum x1 -> x4, waiting for transfers between devices: 1010 us -> 79.1 us  [line_sums(): return lax.psum(tuple(halves), self.names[0])]
    ppermute x0 -> x133, waiting for transfers between devices: none -> 416 us  [the longest x44 236 us: along(): lax.ppermute(value, self.names[axis], [(i, (i + by) % n) for i in range(n)])]
    pallas_call x0 -> x7, Pallas kernels: none -> 282 us  [the longest x3 191 us: run_shared(): pl.pallas_call(functools.partial(shared_kernel, parts, tiles, start, widt...]
    all_to_all x4 -> x0, waiting for transfers between devices: 266 us -> none  [the longest x1 85.2 us: per_device(): lax.all_to_all(send_rows, 'expert', split_axis=0, concat_axis=0, tiled=True)]
    unnamed x231 -> x373, local copies, waits for them, and re-layouts: 197 us -> 37.7 us
    ppermute x0 -> x133, starting transfers between devices: none -> 147 us  [the longest x44 73.8 us: along(): lax.ppermute(value, self.names[axis], [(i, (i + by) % n) for i in range(n)])]
    dot_general x43 -> x40, matrix products: 262 us -> 130 us  [the longest x12 54.2 us: t_dot(): lax.dot_general(left, right, (((0,), (0,)), ((), ())), preferred_element_...]
    psum x1 -> x0, blocking collectives: 67.3 us -> none  [per_device(): lax.psum(reduced[0].astype(jnp.bfloat16), 'expert').astype(jnp.float32)]
  transfers between devices with their start and end apart: 30 -> 137, of which waited for: 9 -> 48; matrix products, arithmetic and copies ran while one was open for 23% -> 24% of each run, Pallas kernels for 0% -> 22%
where the time goes in v1:
time: 1310 us; the launch traced here: 1290 us
  waiting for transfers between devices  495 us (38%)
  Pallas kernels  282 us (22%)
  matrix products  158 us (12%)
  starting transfers between devices  148 us (11%)
  other arithmetic  104 us (8%)
  local copies, waits for them, and re-layouts  90.4 us (7%)
  between operations  16.6 us (1%)
    ppermute x44, waiting for transfers between devices, along(): lax.ppermute(value, self.names[axis], [(i, (i + by) % n) for i in range(n)])  236 us
    pallas_call x3, Pallas kernels, run_shared(): pl.pallas_call(functools.partial(shared_kernel, parts, tiles, start, widt...  191 us
    ppermute x48, waiting for transfers between devices, in_plane(): lax.ppermute(value, self.names, self.pairs(self.turning(turn, second), by))  153 us
    pallas_call x4, Pallas kernels, run_experts(): pl.pallas_call(functools.partial(expert_kernel, count, pieces, capacity,...  91.2 us
    psum x4, waiting for transfers between devices, line_sums(): return lax.psum(tuple(halves), self.names[0])  79.1 us
    ppermute x44, starting transfers between devices, along(): lax.ppermute(value, self.names[axis], [(i, (i + by) % n) for i in range(n)])  73.8 us
    dot_general x12, matrix products, t_dot(): lax.dot_general(left, right, (((0,), (0,)), ((), ())), preferred_element_...  54.2 us
    ppermute x48, starting transfers between devices, in_plane(): lax.ppermute(value, self.names, self.pairs(self.turning(turn, second), by))  49.2 us
  transfers between devices with their start and end apart: 137, of which 48 were waited for; matrix products, arithmetic and copies ran while one was open for 24% of the time, Pallas kernels for 22%

profile of v1, /device:TPU:18, one launch (start us, length us, event | category | flops | bytes accessed | tf_op | source)
XLA Modules:
  0.0 1294.0 jit_solution(8012973688996983114)
XLA Ops:
  88.9 14.9 %collective-permute-done.25.refs_5_ = bf16[128,2048]{1,0:T(8,128)(2,1)} collective-permute-done((bf16[128,2048]{1,0:T(8,128)(2,1)}, bf16[128,2048]{1,0:T(8,128)(2,1)}, u32[]{:S(2)}, u32[]{:S(2)}) %collective-permute-start.25) | collective-permute-done | bytes 524320 | tf_op jit(solution)/shard_map/ppermute | solution.py:374
  126.9 6.8 collective-permute-done.37.refs_2_
  133.8 11.8 collective-permute-done.39.refs_4_
  149.2 22.7 %shard_map.331 = (bf16[128,2176]{1,0:T(8,128)(2,1)}, bf16[128,2176]{1,0:T(8,128)(2,1)}, bf16[128,2176]{1,0:T(8,128)(2,1)}, bf16[128,2176]{1,0:T(8,128)(2,1)}, bf...) custom-call(s32[1]{0:T(128)} %bitcast.13.refs_0_, ...), custom_call_target="tpu_custom_call" | custom-call | flops 8858370048 | bytes 31457280 | tf_op jit(solution)/shard_map/pallas_call | solution.py:197
  176.2 6.8 convolution_add_fusion.1
  187.0 7.9 collective-permute-done.21.refs_1_
  214.8 7.9 collective-permute-done.23.refs_3_
  222.9 8.8 collective-permute-done.32.refs_4_
  233.7 23.1 %shard_map.332 = (bf16[128,2176]{1,0:T(8,128)(2,1)}, bf16[128,2176]{1,0:T(8,128)(2,1)}, bf16[128,2176]{1,0:T(8,128)(2,1)}, bf16[128,2176]{1,0:T(8,128)(2,1)}, bf...) custom-call(s32[1]{0:T(128)} %bitcast.13.refs_0_, ...), custom_call_target="tpu_custom_call", output_to_operand_aliasing={{8}: (15, {}), {9}: (16, {}), {10}: (17, {}), {11}: (18, {}... | custom-call | flops 8858370048 | bytes 31457280 | tf_op jit(solution)/shard_map/pallas_call | solution.py:197
  263.0 9.8 collective-permute-done.24.refs_4_
  272.7 22.8 %shard_map.333 = (bf16[128,2176]{1,0:T(8,128)(2,1)}, bf16[128,2176]{1,0:T(8,128)(2,1)}, bf16[128,2176]{1,0:T(8,128)(2,1)}, bf16[128,2176]{1,0:T(8,128)(2,1)}, bf...) custom-call(s32[1]{0:T(128)} %bitcast.13.refs_0_, ...), custom_call_target="tpu_custom_call", output_to_operand_aliasing={{8}: (15, {}), {9}: (16, {}), {10}: (17, {}), {11}: (18, {}... | custom-call | flops 8858370048 | bytes 31457280 | tf_op jit(solution)/shard_map/pallas_call | solution.py:197
  297.4 7.6 collective-permute-done.13.refs_4_
  305.0 22.6 %shard_map.334 = (bf16[128,2176]{1,0:T(8,128)(2,1)}, bf16[128,2176]{1,0:T(8,128)(2,1)}, bf16[128,2176]{1,0:T(8,128)(2,1)}, bf16[128,2176]{1,0:T(8,128)(2,1)}, bf...) custom-call(s32[1]{0:T(128)} %bitcast.13.refs_0_, ...), custom_call_target="tpu_custom_call", output_to_operand_aliasing={{8}: (15, {}), {9}: (16, {}), {10}: (17, {}), {11}: (18, {}... | custom-call | flops 8858370048 | bytes 31457280 | tf_op jit(solution)/shard_map/pallas_call | solution.py:197
  330.8 7.8 convolution_convert_fusion.2
  356.4 8.8 collective-permute-done.52
  366.4 19.9 %collective-permute-done.59 = bf16[128,2176]{1,0:T(8,128)(2,1)S(1)} collective-permute-done((bf16[128,2176]{1,0:T(8,128)(2,1)S(1)}, bf16[128,2176]{1,0:T(8,128)(2,1)S(1)}, u32[]{:S(2)}, u32[]{:S(2)}) %collective-permute-start.59) | collective-permute-done | bytes 557088 | tf_op jit(solution)/shard_map/ppermute | solution.py:377
  388.1 9.9 collective-permute-done.67
  402.6 10.9 collective-permute-done.60
  414.0 18.3 %collective-permute-done.62 = bf16[128,2176]{1,0:T(8,128)(2,1)S(1)} collective-permute-done((bf16[128,2176]{1,0:T(8,128)(2,1)S(1)}, bf16[128,2176]{1,0:T(8,128)(2,1)S(1)}, u32[]{:S(2)}, u32[]{:S(2)}) %collective-permute-start.62) | collective-permute-done | bytes 557088 | tf_op jit(solution)/shard_map/ppermute | solution.py:377
  436.2 11.7 collective-permute-done.66
  451.4 16.6 %collective-permute-start.61 = (bf16[128,2176]{1,0:T(8,128)(2,1)S(1)}, bf16[128,2176]{1,0:T(8,128)(2,1)S(1)}, u32[]{:S(2)}, u32[]{:S(2)}) collective-permute-start(bf16[128,2176]{1,0:T(8,128)(2,1)S(1)} %add_convert_fusion.6), channel_id=1, source_target_pairs={{0,8},{8,16},{16,24},{24,0},{1,9},{9,17},{17,25},{25,1},{2,10},{10... | collective-permute-start | bytes 1671176 | tf_op jit(solution)/shard_map/ppermute | solution.py:374
  468.0 13.7 %collective-permute-start.69 = (bf16[128,2176]{1,0:T(8,128)(2,1)S(1)}, bf16[128,2176]{1,0:T(8,128)(2,1)S(1)}, u32[]{:S(2)}, u32[]{:S(2)}) collective-permute-start(bf16[128,2176]{1,0:T(8,128)(2,1)S(1)} %add_convert_fusion.2), channel_id=1, source_target_pairs={{0,24},{8,0},{16,8},{24,16},{1,25},{9,1},{17,9},{25,17},{2,26},{10... | collective-permute-start | bytes 1671176 | tf_op jit(solution)/shard_map/ppermute | solution.py:374
  482.9 18.2 %collective-permute-done.61 = bf16[128,2176]{1,0:T(8,128)(2,1)S(1)} collective-permute-done((bf16[128,2176]{1,0:T(8,128)(2,1)S(1)}, bf16[128,2176]{1,0:T(8,128)(2,1)S(1)}, u32[]{:S(2)}, u32[]{:S(2)}) %collective-permute-start.61) | collective-permute-done | bytes 557088 | tf_op jit(solution)/shard_map/ppermute | solution.py:374
  501.6 17.5 %collective-permute-done.69 = bf16[128,2176]{1,0:T(8,128)(2,1)S(1)} collective-permute-done((bf16[128,2176]{1,0:T(8,128)(2,1)S(1)}, bf16[128,2176]{1,0:T(8,128)(2,1)S(1)}, u32[]{:S(2)}, u32[]{:S(2)}) %collective-permute-start.69) | collective-permute-done | bytes 557088 | tf_op jit(solution)/shard_map/ppermute | solution.py:374
  527.9 6.9 collective-permute-done.46
  534.7 12.5 collective-permute-done.50
  547.2 10.3 collective-permute-done.54
  656.2 8.4 collective-permute-done.108
  671.4 6.5 add_bitcast_fusion
  679.3 6.5 add_bitcast_fusion.1
  686.7 6.4 add_bitcast_fusion.2
  699.5 6.9 collective-permute-done.94
  709.3 19.6 %collective-permute-done.104 = bf16[256,256]{0,1:T(8,128)(2,1)S(1)} collective-permute-done((bf16[256,256]{0,1:T(8,128)(2,1)}, bf16[256,256]{0,1:T(8,128)(2,1)S(1)}, u32[]{:S(2)}, u32[]{:S(2)}) %collective-permute-start.104) | collective-permute-done | bytes 131104 | tf_op jit(solution)/shard_map/ppermute | solution.py:386
  756.3 9.5 collective-permute-done.82
  769.8 6.4 collective-permute-done.84
  781.9 28.6 %collective-permute-done.99 = bf16[128,2048]{1,0:T(8,128)(2,1)} collective-permute-done((bf16[128,2048]{1,0:T(8,128)(2,1)}, bf16[128,2048]{1,0:T(8,128)(2,1)}, u32[]{:S(2)}, u32[]{:S(2)}) %collective-permute-start.99) | collective-permute-done | bytes 524320 | tf_op jit(solution)/shard_map/ppermute | solution.py:374
  813.3 9.4 collective-permute-done.101
  856.8 29.7 %all-reduce.13.cloned.1.call-done = (bf16[64,2048]{1,0:T(8,128)(2,1)}, bf16[64,2048]{1,0:T(8,128)(2,1)}) async-done(((bf16[64,2048]{1,0:T(8,128)(2,1)}, bf16[64,2048]{1,0:T(8,128)(2,1)}), (bf16[64,2048]{1,0:T(8,128)(2,1)}, bf16[64,2048]{1,0:T(8,128)(2,1)})) %all-reduce.13.cloned.1.call-update) | async-done | bytes 524304 | tf_op jit(solution)/shard_map/psum | solution.py:531
  895.1 15.7 %collective-permute-done.120 = bf16[64,2048]{1,0:T(8,128)(2,1)S(1)} collective-permute-done((bf16[64,2048]{1,0:T(8,128)(2,1)S(1)}, bf16[64,2048]{1,0:T(8,128)(2,1)S(1)}, u32[]{:S(2)}, u32[]{:S(2)}) %collective-permute-start.120) | collective-permute-done | bytes 262176 | tf_op jit(solution)/shard_map/ppermute | solution.py:374
  916.1 30.2 %all-reduce.11.cloned.1.call-done = (bf16[192,1536]{1,0:T(8,128)(2,1)}, bf16[192,1536]{1,0:T(8,128)(2,1)}) async-done(((bf16[192,1536]{1,0:T(8,128)(2,1)}, bf16[192,1536]{1,0:T(8,128)(2,1)}), (bf16[192,1536]{1,0:T(8,128)(2,1)}, bf16[192,1536]{1,0:T(8,128)(2,1)})) %all-reduce.11.cloned.1.call-update) | async-done | bytes 1179664 | tf_op jit(solution)/shard_map/psum | solution.py:531
  958.2 25.8 %collective-permute-done.118 = bf16[192,1536]{1,0:T(8,128)(2,1)} collective-permute-done((bf16[192,1536]{1,0:T(8,128)(2,1)S(1)}, bf16[192,1536]{1,0:T(8,128)(2,1)}, u32[]{:S(2)}, u32[]{:S(2)}) %collective-permute-start.118) | collective-permute-done | bytes 589856 | tf_op jit(solution)/shard_map/ppermute | solution.py:374
  984.1 19.3 %all-reduce.9.cloned.1.call-done = (bf16[256,1107]{0,1:T(8,128)(2,1)}, bf16[256,1024]{1,0:T(8,128)(2,1)}) async-done(((bf16[256,1107]{0,1:T(8,128)(2,1)}, bf16[256,1024]{1,0:T(8,128)(2,1)}), (bf16[256,1107]{0,1:T(8,128)(2,1)}, bf16[256,1024]{1,0:T(8,128)(2,1)})) %all-reduce.9.cloned.1.call-update) | async-done | bytes 1091088 | tf_op jit(solution)/shard_map/psum | solution.py:531
  1025.8 23.0 %collective-permute-done.112 = bf16[256,1107]{0,1:T(8,128)(2,1)S(1)} collective-permute-done((bf16[256,1107]{0,1:T(8,128)(2,1)S(1)}, bf16[256,1107]{0,1:T(8,128)(2,1)S(1)}, u32[]{:S(2)}, u32[]{:S(2)}) %collective-permute-start.112) | collective-permute-done | bytes 566816 | tf_op jit(solution)/shard_map/ppermute | solution.py:374
  1058.7 68.2 %shard_map.335 = (f32[2048,1408]{1,0:T(8,128)}, f32[2048,1408]{1,0:T(8,128)}, f32[1408,2048]{1,0:T(8,128)}) custom-call(bf16[2048,2048]{1,0:T(8,128)(2,1)} %get-tuple-element.177.refs_0_, bf16[2048,2048]{1,0:T(8,128)(2,1)} %collective-permute-done.128.refs_1_, bf16[2048,2048]{1,0:T(8,128)(2,1)} %get-tuple-element.178.refs_2_, ...), custom_call_target="tpu_custom_call" | custom-call | flops 51539607552 | bytes 33554432 | tf_op jit(solution)/shard_map/pallas_call | solution.py:292
  1126.9 68.5 %shard_map.336 = (f32[2048,1408]{1,0:T(8,128)}, f32[2048,1408]{1,0:T(8,128)}, f32[1408,2048]{1,0:T(8,128)}) custom-call(bf16[2048,2048]{1,0:T(8,128)(2,1)} %get-tuple-element.177.refs_0_, bf16[2048,2048]{1,0:T(8,128)(2,1)} %collective-permute-done.128.refs_1_, ...), custom_call_target="tpu_custom_call", output_to_operand_aliasing={{0}: (7, {}), {1}: (8, {}), {2}: (9, {})} | custom-call | flops 51539607552 | bytes 33554432 | tf_op jit(solution)/shard_map/pallas_call | solution.py:292
  1195.4 54.1 %shard_map.337 = (f32[2048,1408]{1,0:T(8,128)}, f32[2048,1408]{1,0:T(8,128)}, f32[1408,2048]{1,0:T(8,128)}) custom-call(bf16[2048,2048]{1,0:T(8,128)(2,1)} %get-tuple-element.177.refs_0_, bf16[2048,2048]{1,0:T(8,128)(2,1)} %collective-permute-done.128.refs_1_, ...), custom_call_target="tpu_custom_call", output_to_operand_aliasing={{0}: (7, {}), {1}: (8, {}), {2}: (9, {})} | custom-call | flops 38654705664 | bytes 33554432 | tf_op jit(solution)/shard_map/pallas_call | solution.py:292
  1261.6 6.3 copy.301
  1280.7 6.6 copy.305
  (833 shorter events, 465.5 us)
Async XLA Ops:
  7.2 830.7 %all-reduce.15.cloned.1.call-start = ((), (), s32[]{:S(2)}) async-start(), calls=%async_computation.3 | async-start | bytes 2097152 | tf_op jit(solution)/shard_map/psum | solution.py:531
  12.4 41.2 %collective-permute-start.5 = (bf16[768,3072]{1,0:T(8,128)(2,1)}, bf16[768,3072]{1,0:T(8,128)(2,1)}, u32[]{:S(2)}, u32[]{:S(2)}) collective-permute-start(bf16[768,3072]{1,0:T(8,128)(2,1)} %param.29), channel_id=1, source_target_pairs={{0,1},{1,0},{2,3},{3,2},{4,5},{5,4},{6,7},{7,6},{8,9},{9,8},{10,11... | collective-permute-start | bytes 14155784 | tf_op jit(solution)/shard_map/ppermute | solution.py:576
  24.4 54.3 %collective-permute-start.41 = (bf16[128,2048]{1,0:T(8,128)(2,1)}, bf16[128,2048]{1,0:T(8,128)(2,1)}, u32[]{:S(2)}, u32[]{:S(2)}) collective-permute-start(bf16[128,2048]{1,0:T(8,128)(2,1)} %refs_5_.4), channel_id=1, source_target_pairs={{0,4},{2,6},{4,0},{6,2},{8,10},{10,8},{12,14},{14,12},{16,20},{18,... | collective-permute-start | bytes 1572872 | tf_op jit(solution)/shard_map/ppermute | solution.py:377
  34.5 44.5 %collective-permute-start.40 = (bf16[128,2048]{1,0:T(8,128)(2,1)}, bf16[128,2048]{1,0:T(8,128)(2,1)}, u32[]{:S(2)}, u32[]{:S(2)}) collective-permute-start(bf16[128,2048]{1,0:T(8,128)(2,1)} %refs_5_.4), channel_id=1, source_target_pairs={{0,2},{2,0},{4,6},{6,4},{8,12},{10,14},{12,8},{14,10},{16,18},{18,... | collective-permute-start | bytes 1572872 | tf_op jit(solution)/shard_map/ppermute | solution.py:377
  35.3 39.7 %collective-permute-start.6 = (bf16[1024,2048]{1,0:T(8,128)(2,1)}, bf16[1024,2048]{1,0:T(8,128)(2,1)}, u32[]{:S(2)}, u32[]{:S(2)}) collective-permute-start(bf16[1024,2048]{1,0:T(8,128)(2,1)} %param.32), channel_id=1, source_target_pairs={{0,1},{1,0},{2,3},{3,2},{4,5},{5,4},{6,7},{7,6},{8,9},{9,8},{10,11... | collective-permute-start | bytes 12582920 | tf_op jit(solution)/shard_map/ppermute | solution.py:576
  74.9 48.7 %collective-permute-start.18 = (bf16[704,2048]{1,0:T(8,128)(2,1)}, bf16[704,2048]{1,0:T(8,128)(2,1)}, u32[]{:S(2)}, u32[]{:S(2)}) collective-permute-start(bf16[704,2048]{1,0:T(8,128)(2,1)} %bitcast.15.refs_9_), channel_id=1, source_target_pairs={{0,1},{1,0},{2,3},{3,2},{4,5},{5,4},{6,7},{7,6},{8,9},{9,8},{10,11... | collective-permute-start | bytes 8650760 | tf_op jit(solution)/shard_map/ppermute | solution.py:576
  78.5 45.6 %collective-permute-start.19 = (bf16[704,2048]{1,0:T(8,128)(2,1)}, bf16[704,2048]{1,0:T(8,128)(2,1)}, u32[]{:S(2)}, u32[]{:S(2)}) collective-permute-start(bf16[704,2048]{1,0:T(8,128)(2,1)} %bitcast.18.refs_11_), channel_id=1, source_target_pairs={{0,1},{1,0},{2,3},{3,2},{4,5},{5,4},{6,7},{7,6},{8,9},{9,8},{10,11... | collective-permute-start | bytes 8650760 | tf_op jit(solution)/shard_map/ppermute | solution.py:576
  78.7 46.4 %collective-permute-start.20 = (bf16[704,2048]{1,0:T(8,128)(2,1)}, bf16[704,2048]{1,0:T(8,128)(2,1)}, u32[]{:S(2)}, u32[]{:S(2)}) collective-permute-start(bf16[704,2048]{1,0:T(8,128)(2,1)} %bitcast.20.refs_13_), channel_id=1, source_target_pairs={{0,1},{1,0},{2,3},{3,2},{4,5},{5,4},{6,7},{7,6},{8,9},{9,8},{10,11... | collective-permute-start | bytes 8650760 | tf_op jit(solution)/shard_map/ppermute | solution.py:576
  123.6 48.3 %collective-permute-start.14 = (bf16[128,2048]{1,0:T(8,128)(2,1)}, bf16[128,2048]{1,0:T(8,128)(2,1)}, u32[]{:S(2)}, u32[]{:S(2)}) collective-permute-start(bf16[128,2048]{1,0:T(8,128)(2,1)} %refs_5_.4), channel_id=1, source_target_pairs={{0,24},{8,0},{16,8},{24,16},{1,25},{9,1},{17,9},{25,17},{2,26},{10... | collective-permute-start | bytes 1572872 | tf_op jit(solution)/shard_map/ppermute | solution.py:374
  124.1 48.9 %collective-permute-start.35 = (bf16[128,2048]{1,0:T(8,128)(2,1)}, bf16[128,2048]{1,0:T(8,128)(2,1)S(1)}, u32[]{:S(2)}, u32[]{:S(2)}) collective-permute-start(bf16[128,2048]{1,0:T(8,128)(2,1)} %collective-permute-done.33.refs_5_), channel_id=1, source_target_pairs={{0,2},{2,0},{4,6},{6,4},{8,12},{10,14},{12,8},{14,10},{16,18},{18,... | collective-permute-start | bytes 1572872 | tf_op jit(solution)/shard_map/ppermute | solution.py:377
  125.1 50.0 %collective-permute-start.34 = (bf16[128,2048]{1,0:T(8,128)(2,1)}, bf16[128,2048]{1,0:T(8,128)(2,1)S(1)}, u32[]{:S(2)}, u32[]{:S(2)}) collective-permute-start(bf16[128,2048]{1,0:T(8,128)(2,1)} %collective-permute-done.33.refs_5_), channel_id=1, source_target_pairs={{0,4},{2,6},{4,0},{6,2},{8,10},{10,8},{12,14},{14,12},{16,20},{18,... | collective-permute-start | bytes 1572872 | tf_op jit(solution)/shard_map/ppermute | solution.py:377
  133.7 49.3 %collective-permute-start.27 = (bf16[128,2048]{1,0:T(8,128)(2,1)}, bf16[128,2048]{1,0:T(8,128)(2,1)}, u32[]{:S(2)}, u32[]{:S(2)}) collective-permute-start(bf16[128,2048]{1,0:T(8,128)(2,1)} %collective-permute-done.25.refs_5_), channel_id=1, source_target_pairs={{0,4},{2,6},{4,0},{6,2},{8,10},{10,8},{12,14},{14,12},{16,20},{18,... | collective-permute-start | bytes 1572872 | tf_op jit(solution)/shard_map/ppermute | solution.py:377
  210.9 45.8 %collective-permute-start.16 = (bf16[128,2048]{1,0:T(8,128)(2,1)}, bf16[128,2048]{1,0:T(8,128)(2,1)}, u32[]{:S(2)}, u32[]{:S(2)}) collective-permute-start(bf16[128,2048]{1,0:T(8,128)(2,1)} %collective-permute-done.14.refs_5_), channel_id=1, source_target_pairs={{0,2},{2,0},{4,6},{6,4},{8,12},{10,14},{12,8},{14,10},{16,18},{18,... | collective-permute-start | bytes 1572872 | tf_op jit(solution)/shard_map/ppermute | solution.py:377
  212.7 44.4 %collective-permute-start.28 = (bf16[128,2048]{1,0:T(8,128)(2,1)}, bf16[128,2048]{1,0:T(8,128)(2,1)}, u32[]{:S(2)}, u32[]{:S(2)}) collective-permute-start(bf16[128,2048]{1,0:T(8,128)(2,1)} %collective-permute-done.27.refs_7_), channel_id=1, source_target_pairs={{0,2},{2,0},{4,6},{6,4},{8,12},{10,14},{12,8},{14,10},{16,18},{18,... | collective-permute-start | bytes 1572872 | tf_op jit(solution)/shard_map/ppermute | solution.py:377
  213.0 45.9 %collective-permute-start.22 = (bf16[128,2176]{1,0:T(8,128)(2,1)S(1)}, bf16[128,2176]{1,0:T(8,128)(2,1)}, u32[]{:S(2)}, u32[]{:S(2)}) collective-permute-start(bf16[128,2176]{1,0:T(8,128)(2,1)S(1)} %collective-permute-done.21.refs_1_), channel_id=1, source_target_pairs={{0,2},{2,0},{4,6},{6,4},{8,12},{10,14},{12,8},{14,10},{16,18},{18,... | collective-permute-start | bytes 1671176 | tf_op jit(solution)/shard_map/ppermute | solution.py:377
  231.7 41.1 %collective-permute-start.24 = (bf16[128,2176]{1,0:T(8,128)(2,1)}, bf16[128,2176]{1,0:T(8,128)(2,1)}, u32[]{:S(2)}, u32[]{:S(2)}) collective-permute-start(bf16[128,2176]{1,0:T(8,128)(2,1)} %collective-permute-done.23.refs_3_), channel_id=1, source_target_pairs={{0,2},{2,0},{4,6},{6,4},{8,12},{10,14},{12,8},{14,10},{16,18},{18,... | collective-permute-start | bytes 1671176 | tf_op jit(solution)/shard_map/ppermute | solution.py:377
  257.1 40.3 %collective-permute-start.17 = (bf16[128,2048]{1,0:T(8,128)(2,1)}, bf16[128,2048]{1,0:T(8,128)(2,1)}, u32[]{:S(2)}, u32[]{:S(2)}) collective-permute-start(bf16[128,2048]{1,0:T(8,128)(2,1)} %collective-permute-done.16.refs_7_), channel_id=1, source_target_pairs={{0,4},{2,6},{4,0},{6,2},{8,10},{10,8},{12,14},{14,12},{16,20},{18,... | collective-permute-start | bytes 1572872 | tf_op jit(solution)/shard_map/ppermute | solution.py:377
  261.2 174.6 %collective-permute-start.70 = (bf16[128,2176]{1,0:T(8,128)(2,1)}, bf16[128,2176]{1,0:T(8,128)(2,1)S(1)}, u32[]{:S(2)}, u32[]{:S(2)}) collective-permute-start(bf16[128,2176]{1,0:T(8,128)(2,1)} %get-tuple-element.166), channel_id=1, source_target_pairs={{0,2},{2,0},{4,6},{6,4},{8,12},{10,14},{12,8},{14,10},{16,18},{18,... | collective-permute-start | bytes 1671176 | tf_op jit(solution)/shard_map/ppermute | solution.py:377
  295.5 52.2 %collective-permute-start.71 = (bf16[128,2176]{1,0:T(8,128)(2,1)}, bf16[128,2176]{1,0:T(8,128)(2,1)}, u32[]{:S(2)}, u32[]{:S(2)}) collective-permute-start(bf16[128,2176]{1,0:T(8,128)(2,1)} %get-tuple-element.168), channel_id=1, source_target_pairs={{0,2},{2,0},{4,6},{6,4},{8,12},{10,14},{12,8},{14,10},{16,18},{18,... | collective-permute-start | bytes 1671176 | tf_op jit(solution)/shard_map/ppermute | solution.py:377
  327.6 71.8 %collective-permute-start.43 = (bf16[128,2048]{1,0:T(8,128)(2,1)}, bf16[128,2048]{1,0:T(8,128)(2,1)S(1)}, u32[]{:S(2)}, u32[]{:S(2)}) collective-permute-start(bf16[128,2048]{1,0:T(8,128)(2,1)} %get-tuple-element.138), channel_id=1, source_target_pairs={{0,4},{2,6},{4,0},{6,2},{8,10},{10,8},{12,14},{14,12},{16,20},{18,... | collective-permute-start | bytes 1572872 | tf_op jit(solution)/shard_map/ppermute | solution.py:377
  354.0 46.8 %collective-permute-start.58 = (bf16[128,2176]{1,0:T(8,128)(2,1)S(1)}, bf16[128,2176]{1,0:T(8,128)(2,1)S(1)}, u32[]{:S(2)}, u32[]{:S(2)}) collective-permute-start(bf16[128,2176]{1,0:T(8,128)(2,1)S(1)} %copy-done.159), channel_id=1, source_target_pairs={{0,4},{2,6},{4,0},{6,2},{8,10},{10,8},{12,14},{14,12},{16,20},{18,... | collective-permute-start | bytes 1671176 | tf_op jit(solution)/shard_map/ppermute | solution.py:377
  399.5 51.9 %collective-permute-start.47 = (bf16[128,2048]{1,0:T(8,128)(2,1)S(1)}, bf16[128,2048]{1,0:T(8,128)(2,1)S(1)}, u32[]{:S(2)}, u32[]{:S(2)}) collective-permute-start(bf16[128,2048]{1,0:T(8,128)(2,1)S(1)} %copy-done.166), channel_id=1, source_target_pairs={{0,2},{2,0},{4,6},{6,4},{8,12},{10,14},{12,8},{14,10},{16,18},{18,... | collective-permute-start | bytes 1572872 | tf_op jit(solution)/shard_map/ppermute | solution.py:377
  400.2 67.8 %collective-permute-start.51 = (bf16[128,2048]{1,0:T(8,128)(2,1)S(1)}, bf16[128,2048]{1,0:T(8,128)(2,1)S(1)}, u32[]{:S(2)}, u32[]{:S(2)}) collective-permute-start(bf16[128,2048]{1,0:T(8,128)(2,1)S(1)} %copy-done.165), channel_id=1, source_target_pairs={{0,4},{2,6},{4,0},{6,2},{8,10},{10,8},{12,14},{14,12},{16,20},{18,... | collective-permute-start | bytes 1572872 | tf_op jit(solution)/shard_map/ppermute | solution.py:377
  435.8 46.2 %collective-permute-start.72 = (bf16[128,2176]{1,0:T(8,128)(2,1)S(1)}, bf16[128,2176]{1,0:T(8,128)(2,1)S(1)}, u32[]{:S(2)}, u32[]{:S(2)}) collective-permute-start(bf16[128,2176]{1,0:T(8,128)(2,1)S(1)} %add_convert_fusion.1), channel_id=1, source_target_pairs={{0,4},{2,6},{4,0},{6,2},{8,10},{10,8},{12,14},{14,12},{16,20},{18,... | collective-permute-start | bytes 1671176 | tf_op jit(solution)/shard_map/ppermute | solution.py:377
  451.4 49.6 %collective-permute-start.61 = (bf16[128,2176]{1,0:T(8,128)(2,1)S(1)}, bf16[128,2176]{1,0:T(8,128)(2,1)S(1)}, u32[]{:S(2)}, u32[]{:S(2)}) collective-permute-start(bf16[128,2176]{1,0:T(8,128)(2,1)S(1)} %add_convert_fusion.6), channel_id=1, source_target_pairs={{0,8},{8,16},{16,24},{24,0},{1,9},{9,17},{17,25},{25,1},{2,10},{10... | collective-permute-start | bytes 1671176 | tf_op jit(solution)/shard_map/ppermute | solution.py:374
  468.0 51.2 %collective-permute-start.69 = (bf16[128,2176]{1,0:T(8,128)(2,1)S(1)}, bf16[128,2176]{1,0:T(8,128)(2,1)S(1)}, u32[]{:S(2)}, u32[]{:S(2)}) collective-permute-start(bf16[128,2176]{1,0:T(8,128)(2,1)S(1)} %add_convert_fusion.2), channel_id=1, source_target_pairs={{0,24},{8,0},{16,8},{24,16},{1,25},{9,1},{17,9},{25,17},{2,26},{10... | collective-permute-start | bytes 1671176 | tf_op jit(solution)/shard_map/ppermute | solution.py:374
  482.1 42.1 %collective-permute-start.74 = (f32[128,2048]{1,0:T(8,128)S(1)}, f32[128,2048]{1,0:T(8,128)S(1)}, u32[]{:S(2)}, u32[]{:S(2)}) collective-permute-start(f32[128,2048]{1,0:T(8,128)S(1)} %copy-done.56), channel_id=1, source_target_pairs={{0,1},{1,0},{2,3},{3,2},{4,5},{5,4},{6,7},{7,6},{8,9},{9,8},{10,11... | collective-permute-start | bytes 3145736 | tf_op jit(solution)/shard_map/ppermute | solution.py:576
  527.3 143.5 %collective-permute-start.132 = (bf16[704,2048]{1,0:T(8,128)(2,1)}, bf16[704,2048]{1,0:T(8,128)(2,1)}, u32[]{:S(2)}, u32[]{:S(2)}) collective-permute-start(bf16[704,2048]{1,0:T(8,128)(2,1)} %convolution_convert_fusion), channel_id=1, source_target_pairs={{0,1},{1,0},{2,3},{3,2},{4,5},{5,4},{6,7},{7,6},{8,9},{9,8},{10,11... | collective-permute-start | bytes 8650760 | tf_op jit(solution)/shard_map/ppermute | solution.py:576
  527.4 150.5 %collective-permute-start.131 = (bf16[704,2048]{1,0:T(8,128)(2,1)}, bf16[704,2048]{1,0:T(8,128)(2,1)}, u32[]{:S(2)}, u32[]{:S(2)}) collective-permute-start(bf16[704,2048]{1,0:T(8,128)(2,1)} %convolution_convert_fusion.1), channel_id=1, source_target_pairs={{0,1},{1,0},{2,3},{3,2},{4,5},{5,4},{6,7},{7,6},{8,9},{9,8},{10,11... | collective-permute-start | bytes 8650760 | tf_op jit(solution)/shard_map/ppermute | solution.py:576
  664.6 83.8 %collective-permute-start.98 = (bf16[256,4096]{1,0:T(8,128)(2,1)}, bf16[256,4096]{1,0:T(8,128)(2,1)}, u32[]{:S(2)}, u32[]{:S(2)}) collective-permute-start(bf16[256,4096]{1,0:T(8,128)(2,1)} %copy.333), channel_id=1, source_target_pairs={{0,1},{1,0},{2,3},{3,2},{4,5},{5,4},{6,7},{7,6},{8,9},{9,8},{10,11... | collective-permute-start | bytes 6291464 | tf_op jit(solution)/shard_map/ppermute | solution.py:576
  677.9 51.6 %collective-permute-start.96 = (bf16[256,1536]{0,1:T(8,128)(2,1)}, bf16[256,1536]{0,1:T(8,128)(2,1)}, u32[]{:S(2)}, u32[]{:S(2)}) collective-permute-start(bf16[256,1536]{0,1:T(8,128)(2,1)} %get-tuple-element.311), channel_id=1, source_target_pairs={{0,4},{4,0},{1,5},{5,1},{2,6},{6,2},{3,7},{7,3},{8,12},{12,8},{9,1... | collective-permute-start | bytes 2359304 | tf_op jit(solution)/shard_map/ppermute | solution.py:374
  686.3 50.7 %collective-permute-start.109 = (bf16[512,1024]{1,0:T(8,128)(2,1)}, bf16[512,1024]{1,0:T(8,128)(2,1)}, u32[]{:S(2)}, u32[]{:S(2)}) collective-permute-start(bf16[512,1024]{1,0:T(8,128)(2,1)} %pad_maximum_fusion.7), channel_id=1, source_target_pairs={{0,4},{4,0},{1,5},{5,1},{2,6},{6,2},{3,7},{7,3},{8,12},{12,8},{9,1... | collective-permute-start | bytes 3145736 | tf_op jit(solution)/shard_map/ppermute | solution.py:374
  694.9 47.6 %collective-permute-start.111 = (bf16[512,1024]{1,0:T(8,128)(2,1)}, bf16[512,1024]{1,0:T(8,128)(2,1)}, u32[]{:S(2)}, u32[]{:S(2)}) collective-permute-start(bf16[512,1024]{1,0:T(8,128)(2,1)} %pad_maximum_fusion.8), channel_id=1, source_target_pairs={{0,2},{2,0},{1,3},{3,1},{4,6},{6,4},{5,7},{7,5},{8,10},{10,8},{9,1... | collective-permute-start | bytes 3145736 | tf_op jit(solution)/shard_map/ppermute | solution.py:374
  748.0 138.5 %all-reduce.13.cloned.1.call-start = ((), (), s32[]{:S(2)}) async-start(), calls=%async_computation.2 | async-start | bytes 1048576 | tf_op jit(solution)/shard_map/psum | solution.py:531
  753.8 304.9 %collective-permute-start.128 = (bf16[2048,2048]{1,0:T(8,128)(2,1)}, bf16[2048,2048]{1,0:T(8,128)(2,1)}, u32[]{:S(2)}, u32[]{:S(2)}) collective-permute-start(bf16[2048,2048]{1,0:T(8,128)(2,1)} %get-tuple-element.177.refs_0_), channel_id=1, source_target_pairs={{0,1},{1,0},{2,3},{3,2},{4,5},{5,4},{6,7},{7,6},{8,9},{9,8},{10,11... | collective-permute-start | bytes 25165832 | tf_op jit(solution)/shard_map/ppermute | solution.py:576
  753.8 304.9 %collective-permute-start.129 = (bf16[2048,2048]{1,0:T(8,128)(2,1)}, bf16[2048,2048]{1,0:T(8,128)(2,1)}, u32[]{:S(2)}, u32[]{:S(2)}) collective-permute-start(bf16[2048,2048]{1,0:T(8,128)(2,1)} %get-tuple-element.178.refs_2_), channel_id=1, source_target_pairs={{0,1},{1,0},{2,3},{3,2},{4,5},{5,4},{6,7},{7,6},{8,9},{9,8},{10,11... | collective-permute-start | bytes 25165832 | tf_op jit(solution)/shard_map/ppermute | solution.py:576
  754.3 87.1 %collective-permute-start.97 = (bf16[512,1536]{0,1:T(8,128)(2,1)}, bf16[512,1536]{0,1:T(8,128)(2,1)}, u32[]{:S(2)}, u32[]{:S(2)}) collective-permute-start(bf16[512,1536]{0,1:T(8,128)(2,1)} %pad_maximum_fusion.3), channel_id=1, source_target_pairs={{0,2},{2,0},{1,3},{3,1},{4,6},{6,4},{5,7},{7,5},{8,10},{10,8},{9,1... | collective-permute-start | bytes 4718600 | tf_op jit(solution)/shard_map/ppermute | solution.py:374
  765.8 87.1 %collective-permute-start.95 = (bf16[512,1536]{0,1:T(8,128)(2,1)}, bf16[512,1536]{0,1:T(8,128)(2,1)}, u32[]{:S(2)}, u32[]{:S(2)}) collective-permute-start(bf16[512,1536]{0,1:T(8,128)(2,1)} %pad_maximum_fusion.2), channel_id=1, source_target_pairs={{0,4},{4,0},{1,5},{5,1},{2,6},{6,2},{3,7},{7,3},{8,12},{12,8},{9,1... | collective-permute-start | bytes 4718600 | tf_op jit(solution)/shard_map/ppermute | solution.py:374
  837.9 108.4 %all-reduce.11.cloned.1.call-start = ((), (), s32[]{:S(2)}) async-start(), calls=%async_computation.1 | async-start | bytes 2359296 | tf_op jit(solution)/shard_map/psum | solution.py:531
  848.6 42.3 %collective-permute-start.126 = (bf16[256,1024]{1,0:T(8,128)(2,1)}, bf16[256,1024]{1,0:T(8,128)(2,1)}, u32[]{:S(2)}, u32[]{:S(2)}) collective-permute-start(bf16[256,1024]{1,0:T(8,128)(2,1)} %get-tuple-element.301), channel_id=1, source_target_pairs={{0,4},{4,0},{1,5},{5,1},{2,6},{6,2},{3,7},{7,3},{8,12},{12,8},{9,1... | collective-permute-start | bytes 1572872 | tf_op jit(solution)/shard_map/ppermute | solution.py:374
  888.0 115.4 %all-reduce.9.cloned.1.call-start = ((), (), s32[]{:S(2)}) async-start(), calls=%async_computation | async-start | bytes 2187264 | tf_op jit(solution)/shard_map/psum | solution.py:531
  894.3 58.2 %collective-permute-start.127 = (bf16[512,1024]{1,0:T(8,128)(2,1)S(1)}, bf16[512,1024]{1,0:T(8,128)(2,1)}, u32[]{:S(2)}, u32[]{:S(2)}) collective-permute-start(bf16[512,1024]{1,0:T(8,128)(2,1)S(1)} %maximum_select_fusion.16), channel_id=1, source_target_pairs={{0,2},{2,0},{1,3},{3,1},{4,6},{6,4},{5,7},{7,5},{8,10},{10,8},{9,1... | collective-permute-start | bytes 3145736 | tf_op jit(solution)/shard_map/ppermute | solution.py:374
  946.3 63.0 %collective-permute-start.125 = (bf16[512,1024]{1,0:T(8,128)(2,1)S(1)}, bf16[512,1024]{1,0:T(8,128)(2,1)}, u32[]{:S(2)}, u32[]{:S(2)}) collective-permute-start(bf16[512,1024]{1,0:T(8,128)(2,1)S(1)} %maximum_select_fusion.15), channel_id=1, source_target_pairs={{0,4},{4,0},{1,5},{5,1},{2,6},{6,2},{3,7},{7,3},{8,12},{12,8},{9,1... | collective-permute-start | bytes 3145736 | tf_op jit(solution)/shard_map/ppermute | solution.py:374
  951.9 53.9 %collective-permute-start.116 = (bf16[192,1536]{1,0:T(8,128)(2,1)}, bf16[192,1536]{1,0:T(8,128)(2,1)}, u32[]{:S(2)}, u32[]{:S(2)}) collective-permute-start(bf16[192,1536]{1,0:T(8,128)(2,1)} %get-tuple-element.296), channel_id=1, source_target_pairs={{0,2},{2,0},{1,3},{3,1},{4,6},{6,4},{5,7},{7,5},{8,10},{10,8},{9,1... | collective-permute-start | bytes 1769480 | tf_op jit(solution)/shard_map/ppermute | solution.py:374
  1005.8 45.8 %collective-permute-start.119 = (bf16[384,1536]{1,0:T(8,128)(2,1)S(1)}, bf16[384,1536]{1,0:T(8,128)(2,1)S(1)}, u32[]{:S(2)}, u32[]{:S(2)}) collective-permute-start(bf16[384,1536]{1,0:T(8,128)(2,1)S(1)} %maximum_select_fusion.8), channel_id=1, source_target_pairs={{0,2},{2,0},{1,3},{3,1},{4,6},{6,4},{5,7},{7,5},{8,10},{10,8},{9,1... | collective-permute-start | bytes 3538952 | tf_op jit(solution)/shard_map/ppermute | solution.py:374
  1009.4 43.6 %collective-permute-start.117 = (bf16[384,1536]{1,0:T(8,128)(2,1)S(1)}, bf16[384,1536]{1,0:T(8,128)(2,1)S(1)}, u32[]{:S(2)}, u32[]{:S(2)}) collective-permute-start(bf16[384,1536]{1,0:T(8,128)(2,1)S(1)} %maximum_select_fusion.7), channel_id=1, source_target_pairs={{0,4},{4,0},{1,5},{5,1},{2,6},{6,2},{3,7},{7,3},{8,12},{12,8},{9,1... | collective-permute-start | bytes 3538952 | tf_op jit(solution)/shard_map/ppermute | solution.py:374
  1048.8 200.7 %collective-permute-start.115 = (bf16[512,1024]{1,0:T(8,128)(2,1)}, bf16[512,1024]{1,0:T(8,128)(2,1)}, u32[]{:S(2)}, u32[]{:S(2)}) collective-permute-start(bf16[512,1024]{1,0:T(8,128)(2,1)} %maximum_select_fusion.12), channel_id=1, source_target_pairs={{0,4},{4,0},{1,5},{5,1},{2,6},{6,2},{3,7},{7,3},{8,12},{12,8},{9,1... | collective-permute-start | bytes 3145736 | tf_op jit(solution)/shard_map/ppermute | solution.py:374
  1051.6 204.1 %collective-permute-start.113 = (bf16[512,1107]{0,1:T(8,128)(2,1)}, bf16[512,1107]{0,1:T(8,128)(2,1)}, u32[]{:S(2)}, u32[]{:S(2)}) collective-permute-start(bf16[512,1107]{0,1:T(8,128)(2,1)} %maximum_select_fusion.9), channel_id=1, source_target_pairs={{0,2},{2,0},{1,3},{3,1},{4,6},{6,4},{5,7},{7,5},{8,10},{10,8},{9,1... | collective-permute-start | bytes 3400712 | tf_op jit(solution)/shard_map/ppermute | solution.py:374
  (272 other events, 4367.0 us)
Sparse Core Ops, SparseCore 0:
  748.1 61.4 all-reduce.14
  838.0 48.3 all-reduce.12
  890.1 56.1 all-reduce.10
  949.9 53.4 all-reduce.8

commit v2 on v1

v2 whole, which is shorter than its diff:
```python
import functools
import math

import jax
import jax.numpy as jnp
import numpy as np
from jax import lax
from jax.experimental import pallas as pl
from jax.experimental.pallas import tpu as pltpu
from jax.sharding import PartitionSpec as P

H = 16
DN = 128
DR = 64
DV = 128
KR = 512
TOP = 6


norm_eps = 1e-06
rope_base = 50000.0
route_scale = 2.446
masked_score = -1e30
highest = lax.Precision.HIGHEST
bfloat = jnp.bfloat16
single = jnp.float32


def row_scale(values):
    return lax.rsqrt(jnp.mean(values * values, axis=-1, keepdims=True) + norm_eps)


def norm_back(grad_out, normed_rows, scale_rows, gain):
    grad_normed = grad_out * gain
    grad_input = scale_rows * (
        grad_normed - normed_rows * jnp.mean(grad_normed * normed_rows, axis=-1, keepdims=True)
    )
    return (grad_input, jnp.sum(grad_out * normed_rows, axis=0))


def seq_positions(segments):
    token_count = segments.shape[0]
    index = jnp.arange(token_count, dtype=jnp.int32)
    change = jnp.concatenate([jnp.ones((1,), bool), segments[1:] != segments[:-1]])
    starts = lax.cummax(jnp.where(change, index, 0), axis=0)
    return index - starts


def rope_tables(positions, half):
    freq = rope_base ** (-jnp.arange(half, dtype=jnp.float32) / half)
    angles = positions.astype(jnp.float32)[:, None] * freq[None, :]
    return (jnp.cos(angles), jnp.sin(angles))


def rotate(values, cosine, sine):
    half = values.shape[-1] // 2
    first = values[..., :half]
    second = values[..., half:]
    return jnp.concatenate(
        [first * cosine - second * sine, second * cosine + first * sine], axis=-1
    )


def rotate_back(grads, cosine, sine):
    half = grads.shape[-1] // 2
    first = grads[..., :half]
    second = grads[..., half:]
    return jnp.concatenate(
        [first * cosine + second * sine, second * cosine - first * sine], axis=-1
    )


def silu_grads(grad_hidden, pre_gate, pre_up):
    sigma = jax.nn.sigmoid(pre_gate)
    grad_gate = grad_hidden * pre_up * sigma * (1.0 + pre_gate * (1.0 - sigma))
    grad_up = grad_hidden * pre_gate * sigma
    return (grad_gate.astype(bfloat), grad_up.astype(bfloat))


def dot(left, right):
    return jnp.dot(left, right, preferred_element_type=single)


def dot_t(left, right):
    return lax.dot_general(left, right, (((1,), (1,)), ((), ())), preferred_element_type=single)


def t_dot(left, right):
    return lax.dot_general(left, right, (((0,), (0,)), ((), ())), preferred_element_type=single)


def expert_kernel(count, pieces, capacity, experts, group, first, waits, *refs):
    refs = list(refs)
    me_ref = refs.pop(0)
    blocks = [refs.pop(0) for _ in range(count)]
    all_cots = refs.pop(0)
    weights = [[refs.pop(0) for _ in range(pieces)] for _ in range(3)]
    refs = refs[waits:]
    if not first:
        refs = refs[4 + 3 * pieces:]
    backs = [refs.pop(0) for _ in range(count)]
    outs = [refs.pop(0) for _ in range(count)]
    kept = [refs.pop(0) for _ in range(4)]
    acts = [[refs.pop(0) for _ in range(pieces)] for _ in range(3)]
    full = [refs.pop(0) for _ in range(3)]
    rows, grads, cot_scr = refs.pop(0), refs.pop(0), refs.pop(0)
    act_scr = [[refs.pop(0) for _ in range(pieces)] for _ in range(3)]
    sem_w, sem_o, sem_c = refs.pop(0), refs.pop(0), refs.pop(0)
    assert not refs
    tok = blocks[0].shape[0]
    model = all_cots.shape[1]
    width = weights[0][0].shape[0]
    fetches = []
    for i in range(count):
        source = pl.multiple_of(me_ref[1 + group * count + i] * tok, tok)
        c = pltpu.make_async_copy(all_cots.at[pl.ds(source, tok)], cot_scr.at[i], sem_c.at[i])
        c.start()
        fetches.append(c)
    cots = [cot_scr.at[i] for i in range(count)]
    loads = []
    for k in range(3):
        loads.append([])
        for j in range(pieces):
            c = pltpu.make_async_copy(weights[k][j], full[k].at[pl.ds(j * width, width)], sem_w.at[k, j])
            c.start()
            loads[k].append(c)
    stores = []
    def store(src, dst, at):
        c = pltpu.make_async_copy(src, dst, sem_o.at[at])
        c.start()
        stores.append(c)
    me = me_ref[0]
    lane = lax.broadcasted_iota(jnp.int32, (tok, 128), 1)
    place = lax.broadcasted_iota(jnp.int32, (tok, capacity), 1).astype(single)
    picks, wcols = [], []
    for c in fetches:
        c.wait()
    for i in range(count):
        marks = blocks[i][:, model:model + 128].astype(single)
        code = jnp.sum(jnp.where(lane == me, marks, 0.0), axis=1, keepdims=True)
        weight = jnp.sum(jnp.where((lane == me + experts) | (lane == me + 2 * experts), marks, 0.0), axis=1, keepdims=True)
        pick = (code == place).astype(single).astype(bfloat)
        picks.append(pick)
        wcols.append(weight)
        here = pl.ds(i * capacity, capacity)
        rows[here] = t_dot(pick, blocks[i][:, :model]).astype(bfloat)
        scaled = (weight * cots[i][...].astype(single)).astype(bfloat)
        grads[here] = t_dot(pick, scaled).astype(bfloat)
    n = count * capacity
    store(rows, kept[0].at[pl.ds(group * n, n)], 0)
    store(grads, kept[1].at[pl.ds(group * n, n)], 1)
    for i in range(count):
        store(blocks[i].at[:, pl.ds(0, model)], kept[2].at[pl.ds((group * count + i) * tok, tok)], 2 + i)
        store(cots[i], kept[3].at[pl.ds((group * count + i) * tok, tok)], 2 + count + i)
    for c in loads[0]: c.wait()
    pre_gate = dot_t(rows[...], full[0][...])
    for c in loads[1]: c.wait()
    pre_up = dot_t(rows[...], full[1][...])
    sigma = jax.nn.sigmoid(pre_gate)
    silu = pre_gate * sigma
    hidden = (silu * pre_up).astype(bfloat)
    for c in loads[2]: c.wait()
    grad_hidden = dot_t(grads[...], full[2][...])
    grad_gate = (grad_hidden * pre_up * sigma * (1.0 + pre_gate * (1.0 - sigma))).astype(bfloat)
    grad_up = (grad_hidden * silu).astype(bfloat)
    at = 2 + 2 * count
    for k, v in enumerate((hidden, grad_gate, grad_up)):
        for j in range(pieces):
            act_scr[k][j][...] = v[:, j * width:(j + 1) * width]
            store(act_scr[k][j], acts[k][j].at[pl.ds(group * n, n)], at)
            at += 1
    back = (dot(grad_gate, full[0][...]) + dot(grad_up, full[1][...])).astype(bfloat)
    out = dot(hidden, full[2][...]).astype(bfloat)
    for i in range(count):
        here = slice(i * capacity, (i + 1) * capacity)
        got = dot(picks[i], out[here])
        dots = jnp.sum(got * cots[i][...].astype(single), axis=1, keepdims=True)
        outs[i][...] = (wcols[i] * got).astype(bfloat)
        backs[i][:, :model] = dot(picks[i], back[here]).astype(bfloat)
        high = dots.astype(bfloat).astype(single)
        tail = jnp.where(lane == me, high, 0.0) + jnp.where(lane == me + experts, dots - high, 0.0)
        backs[i][:, model:model + 128] = tail.astype(bfloat)
    for c in stores: c.wait()

def run_experts(me, blocks, all_cots, weights, capacity, experts, group, groups, carried, others):
    count, pieces = len(blocks), len(weights[0])
    tok, model = blocks[0].shape[0], weights[0][0].shape[1]
    width = weights[0][0].shape[0]
    n = count * capacity
    first = carried is None
    shape = jax.ShapeDtypeStruct
    kept = [shape((groups * n, model), bfloat)] * 2 + [shape((groups * count * tok, model), bfloat)] * 2
    kept += [shape((groups * n, width), bfloat)] * (3 * pieces)
    vm = pl.BlockSpec(memory_space=pltpu.VMEM)
    hbm = pl.BlockSpec(memory_space=pl.ANY)
    flat = [w for ws in weights for w in ws]
    operands = [me, *blocks, all_cots, *flat, *others]
    in_specs = [pl.BlockSpec(memory_space=pltpu.SMEM)] + [vm] * count
    in_specs += [hbm] * (1 + len(flat) + len(others))
    alias = {}
    if not first:
        base = len(operands)
        operands += list(carried)
        in_specs += [hbm] * len(kept)
        alias = {base + i: 2 * count + i for i in range(len(kept))}
    rows = n
    flops = 2 * rows * model * width * pieces * 6
    out = pl.pallas_call(
        functools.partial(expert_kernel, count, pieces, capacity, experts, group, first, len(others)),
        out_shape=[shape(b.shape, bfloat) for b in blocks] + [shape((tok, model), bfloat)] * count + kept,
        in_specs=in_specs,
        out_specs=[vm] * (2 * count) + [hbm] * len(kept),
        input_output_aliases=alias,
        scratch_shapes=[pltpu.VMEM((pieces * width, model), bfloat)] * 3
        + [pltpu.VMEM((n, model), bfloat)] * 2
        + [pltpu.VMEM((count, tok, model), bfloat)]
        + [pltpu.VMEM((n, width), bfloat)] * (3 * pieces)
        + [pltpu.SemaphoreType.DMA((3, pieces)), pltpu.SemaphoreType.DMA((2 + 2 * count + 3 * pieces,))]
        + [pltpu.SemaphoreType.DMA((count,))],
        compiler_params=pltpu.CompilerParams(vmem_limit_bytes=58 << 20),
        cost_estimate=pl.CostEstimate(flops=flops, bytes_accessed=30 << 20, transcendentals=0),
    )(*operands)
    return out[:count], out[count:2 * count], out[2 * count:]


def shared_kernel(parts, tiles, start, width, first, waits, *refs):
    refs = list(refs)
    xs = [refs.pop(0) for _ in range(parts)]
    cs = [refs.pop(0) for _ in range(parts)]
    weights = [refs.pop(0) for _ in range(3)]
    refs = refs[waits:]
    if not first:
        refs = refs[3:]
    outs = [refs.pop(0) for _ in range(3)]
    wgu, wd = (refs.pop(0) for _ in range(2))
    accs = [refs.pop(0) for _ in range(2)]
    sem_w, sem_o = refs
    step = pl.program_id(0)
    cols = pl.ds(start, width)
    loads = [
        pltpu.make_async_copy(weights[0].at[:, cols], wgu.at[:, pl.ds(0, width)], sem_w.at[0]),
        pltpu.make_async_copy(weights[1].at[:, cols], wgu.at[:, pl.ds(width, width)], sem_w.at[1]),
        pltpu.make_async_copy(weights[2].at[cols], wd, sem_w.at[2]),
    ]

    @pl.when(step == 0)
    def _():
        for c in loads:
            c.start()
        for a in accs:
            a[...] = jnp.zeros_like(a)
        for c in loads:
            c.wait()

    def work(x_ref, c_ref):
        x, c = x_ref[...], c_ref[...]
        pre = dot(x, wgu[...])
        pre_gate, pre_up = pre[:, :width], pre[:, width:]
        grad_hidden = dot_t(c, wd[...])
        sigma = jax.nn.sigmoid(pre_gate)
        silu = pre_gate * sigma
        hidden = (silu * pre_up).astype(bfloat)
        grad_gate = (grad_hidden * pre_up * sigma * (1.0 + pre_gate * (1.0 - sigma))).astype(bfloat)
        grad_up = (grad_hidden * silu).astype(bfloat)
        accs[0][...] += t_dot(x, jnp.concatenate([grad_gate, grad_up], axis=1))
        accs[1][...] += t_dot(hidden, c)

    if parts == 1:
        work(xs[0], cs[0])
    else:
        per = tiles // parts
        for p in range(parts):
            pl.when(step // per == p)(functools.partial(work, xs[p], cs[p]))

    @pl.when(step == tiles - 1)
    def _():
        puts = [
            pltpu.make_async_copy(accs[0].at[:, pl.ds(0, width)], outs[0].at[:, cols], sem_o.at[0]),
            pltpu.make_async_copy(accs[0].at[:, pl.ds(width, width)], outs[1].at[:, cols], sem_o.at[1]),
            pltpu.make_async_copy(accs[1], outs[2].at[cols], sem_o.at[2]),
        ]
        for c in puts:
            c.start()
        for c in puts:
            c.wait()

def run_shared(xs, cs, weights, start, width, carried, others=(), tile=512):
    parts = len(xs)
    rows, model = xs[0].shape
    per = rows // tile
    tiles = per * parts
    shape = jax.ShapeDtypeStruct
    hbm = pl.BlockSpec(memory_space=pl.ANY)
    specs = [
        pl.BlockSpec((tile, model), lambda i, p=p: (jnp.clip(i - p * per, 0, per - 1), 0))
        for p in range(parts)
    ]
    outs = [shape(w.shape, single) for w in weights]
    operands = [*xs, *cs, *weights, *others]
    in_specs = specs + specs + [hbm] * (3 + len(others))
    alias = {}
    if carried is not None:
        alias = {len(operands) + i: i for i in range(3)}
        operands += list(carried)
        in_specs += [hbm] * 3
    return pl.pallas_call(
        functools.partial(shared_kernel, parts, tiles, start, width, carried is None, len(others)),
        grid=(tiles,),
        out_shape=outs,
        in_specs=in_specs,
        out_specs=[hbm] * 3,
        input_output_aliases=alias,
        scratch_shapes=[
            pltpu.VMEM((model, 2 * width), bfloat),
            pltpu.VMEM((width, model), bfloat),
            pltpu.VMEM((model, 2 * width), single),
            pltpu.VMEM((width, model), single),
            pltpu.SemaphoreType.DMA((3,)),
            pltpu.SemaphoreType.DMA((3,)),
        ],
        compiler_params=pltpu.CompilerParams(vmem_limit_bytes=60 << 20),
        cost_estimate=pl.CostEstimate(flops=12 * tiles * tile * model * width, bytes_accessed=4 * tiles * tile * model, transcendentals=0),
    )(*operands)


def turned(values, cosine, sine, way):
    half = values.shape[-1] // 2
    first, second = values[:, :half], values[:, half:]
    return jnp.concatenate(
        [first * cosine - way * second * sine, second * cosine + way * first * sine], axis=1
    )


def heads_kernel(pieces, score_scale, *refs):
    refs = list(refs)
    q_ref = refs.pop(0)
    kvbs = [refs.pop(0) for _ in range(pieces)]
    latent, rope, shown, cosine, sine = (refs.pop(0) for _ in range(5))
    heads_ref, nope_ref, qrope_ref, abs_ref, probs_ref, lat_ref = refs
    latents, ropes = latent[...], rope[...]
    visible = shown[...] > 0
    q = q_ref[...]
    rank = latents.shape[1]
    for h in range(2):
        nope = q[:, h * (DN + DR) : h * (DN + DR) + DN].astype(bfloat)
        tail = q[:, h * (DN + DR) + DN : (h + 1) * (DN + DR)]
        qrope = turned(tail, cosine[...], sine[...], 1.0).astype(bfloat)
        at = h * (DN + DV)
        w_uk = jnp.concatenate([w[:, at : at + DN] for w in kvbs], axis=0)
        w_uv = jnp.concatenate([w[:, at + DN : at + DN + DV] for w in kvbs], axis=0)
        query = dot_t(nope, w_uk).astype(bfloat)
        raw = dot_t(query, latents) + dot_t(qrope, ropes)
        scores = jnp.where(visible, raw * score_scale, masked_score)
        expd = jnp.exp(scores - jnp.max(scores, axis=1, keepdims=True))
        probs = expd / jnp.sum(expd, axis=1, keepdims=True)
        lat = dot(probs.astype(bfloat), latents).astype(bfloat)
        heads_ref[:, h * DV : (h + 1) * DV] = dot(lat, w_uv).astype(bfloat)
        nope_ref[:, h * DN : (h + 1) * DN] = nope
        qrope_ref[:, h * DR : (h + 1) * DR] = qrope
        abs_ref[:, h * rank : (h + 1) * rank] = query
        keys = probs.shape[1]
        probs_ref[:, h * keys : (h + 1) * keys] = probs
        lat_ref[:, h * rank : (h + 1) * rank] = lat


def heads_back_kernel(pieces, score_scale, *refs):
    refs = list(refs)
    g_ref = refs.pop(0)
    kvbs = [refs.pop(0) for _ in range(pieces)]
    latent, rope, cosine, sine = (refs.pop(0) for _ in range(4))
    nope_ref, qrope_ref, abs_ref, probs_ref, lat_ref = (refs.pop(0) for _ in range(5))
    gq_ref = refs.pop(0)
    gkvbs = [refs.pop(0) for _ in range(pieces)]
    key_ref, rope_out = refs
    latents, ropes = latent[...], rope[...]
    rank, keys = latents.shape[1], latents.shape[0]

    @pl.when(pl.program_id(0) == 0)
    def _():
        key_ref[...] = jnp.zeros_like(key_ref)
        rope_out[...] = jnp.zeros_like(rope_out)

    parts = []
    key_sum = key_ref[...]
    rope_sum = rope_out[...]
    for h in range(2):
        at = h * (DN + DV)
        w_uk = jnp.concatenate([w[:, at : at + DN] for w in kvbs], axis=0)
        w_uv = jnp.concatenate([w[:, at + DN : at + DN + DV] for w in kvbs], axis=0)
        grad = g_ref[:, h * DV : (h + 1) * DV]
        lat = lat_ref[:, h * rank : (h + 1) * rank]
        query = abs_ref[:, h * rank : (h + 1) * rank]
        nope = nope_ref[:, h * DN : (h + 1) * DN]
        qrope = qrope_ref[:, h * DR : (h + 1) * DR]
        probs = probs_ref[:, h * keys : (h + 1) * keys]
        grad_uv = t_dot(lat, grad).astype(bfloat)
        grad_lat = dot_t(grad, w_uv).astype(bfloat)
        grad_probs = dot_t(grad_lat, latents)
        delta = jnp.sum(probs * grad_probs, axis=1, keepdims=True)
        grad_scores = (probs * (grad_probs - delta)).astype(bfloat)
        grad_abs = (dot(grad_scores, latents) * score_scale).astype(bfloat)
        grad_rope = dot(grad_scores, ropes) * score_scale
        key_sum = key_sum + t_dot(grad_scores, query) * score_scale
        key_sum = key_sum + t_dot(probs.astype(bfloat), grad_lat)
        rope_sum = rope_sum + t_dot(grad_scores, qrope) * score_scale
        grad_uk = t_dot(grad_abs, nope).astype(bfloat)
        rows = rank // pieces
        for j in range(pieces):
            gkvbs[j][:, at : at + DN] = grad_uk[j * rows : (j + 1) * rows]
            gkvbs[j][:, at + DN : at + DN + DV] = grad_uv[j * rows : (j + 1) * rows]
        parts.append(dot(grad_abs, w_uk))
        parts.append(turned(grad_rope, cosine[...], sine[...], -1.0))
    gq_ref[...] = jnp.concatenate(parts, axis=1).astype(bfloat)
    key_ref[...] = key_sum
    rope_out[...] = rope_sum


def run_heads(q, kvbs, latent, rope, shown, cosine, sine, heads, score_scale):
    rows, pieces = q.shape[0], len(kvbs)
    keys, rank = latent.shape
    shape = jax.ShapeDtypeStruct
    own = lambda width: pl.BlockSpec((rows, width), lambda g: (0, g))
    still = lambda v: pl.BlockSpec(v.shape, lambda g: (0, 0))
    kvb = [pl.BlockSpec((w.shape[0], 2 * (DN + DV)), lambda g: (0, g)) for w in kvbs]
    widths = (DV, DN, DR, rank, keys, rank)
    kinds = (bfloat, bfloat, bfloat, bfloat, single, bfloat)
    return pl.pallas_call(
        functools.partial(heads_kernel, pieces, score_scale),
        grid=(heads // 2,),
        out_shape=[shape((rows, heads * w), k) for w, k in zip(widths, kinds)],
        in_specs=[own(2 * (DN + DR)), *kvb] + [still(v) for v in (latent, rope, shown, cosine, sine)],
        out_specs=[own(2 * w) for w in widths],
        compiler_params=pltpu.CompilerParams(vmem_limit_bytes=40 << 20),
        cost_estimate=pl.CostEstimate(flops=3 << 30, bytes_accessed=14 << 20, transcendentals=heads * rows * keys),
    )(q, *kvbs, latent, rope, shown, cosine, sine)


def run_heads_back(grad, kvbs, latent, rope, cosine, sine, saved, heads, score_scale, others):
    rows, pieces = grad.shape[0], len(kvbs)
    keys, rank = latent.shape
    shape = jax.ShapeDtypeStruct
    own = lambda width: pl.BlockSpec((rows, width), lambda g: (0, g))
    still = lambda v: pl.BlockSpec(v.shape, lambda g: (0, 0))
    kvb = [pl.BlockSpec((w.shape[0], 2 * (DN + DV)), lambda g: (0, g)) for w in kvbs]
    widths = (DN, DR, rank, keys, rank)

    def body(*refs):
        cut = 1 + pieces + 4 + 5
        heads_back_kernel(pieces, score_scale, *refs[:cut], *refs[cut + len(others) :])

    out = pl.pallas_call(
        body,
        grid=(heads // 2,),
        out_shape=[shape((rows, heads * (DN + DR)), bfloat)]
        + [shape(w.shape, bfloat) for w in kvbs]
        + [shape((keys, rank), single), shape((keys, DR), single)],
        in_specs=[own(2 * DV), *kvb]
        + [still(v) for v in (latent, rope, cosine, sine)]
        + [own(2 * w) for w in widths]
        + [pl.BlockSpec(memory_space=pl.ANY)] * len(others),
        out_specs=[own(2 * (DN + DR)), *kvb]
        + [pl.BlockSpec((keys, rank), lambda g: (0, 0)), pl.BlockSpec((keys, DR), lambda g: (0, 0))],
        compiler_params=pltpu.CompilerParams(vmem_limit_bytes=40 << 20),
        cost_estimate=pl.CostEstimate(flops=6 << 30, bytes_accessed=20 << 20, transcendentals=0),
    )(grad, *kvbs, latent, rope, cosine, sine, *saved, *others)
    return out[0], out[1 : 1 + pieces], out[1 + pieces], out[2 + pieces]


def assemble_kernel(parts, cuts, fold, *refs):
    where, one_0, one_1, two_0, two_1, *outs = refs
    step = pl.program_id(0)
    _, m = parts
    row = jnp.where(step // m == where[0], one_0[...], one_1[...])
    column = jnp.where(step % m == where[1], two_0[...], two_1[...])
    value = jnp.concatenate([row, column], axis=1).astype(single)
    start = 0
    for i, (width, out) in enumerate(zip(cuts, outs)):
        piece = value[:, start : start + width]
        start += width
        if i == 0 and fold > 1:
            rows = piece.shape[0] // fold
            piece = jnp.concatenate(
                [piece[k * rows : (k + 1) * rows] for k in range(fold)], axis=1
            )
        if out.shape[0] == width and out.shape[0] != piece.shape[0]:
            piece = piece.T
        out[...] = piece


def assemble(chips, lines, cuts, fold, turned):
    n, m = chips.dims[1:]
    parts = n * m
    rows = lines[0][0].shape[0] * n // parts
    where = jnp.stack([chips.own(1), chips.own(2)]).astype(jnp.int32)
    one = pl.BlockSpec((rows, lines[0][0].shape[1]), lambda p: (p % m, 0))
    two = pl.BlockSpec((rows, lines[1][0].shape[1]), lambda p: (p // m, 0))
    shapes, specs = [], []
    for i, width in enumerate(cuts):
        if i == 0 and fold > 1:
            shapes.append((rows * parts // fold, width * fold))
            specs.append(pl.BlockSpec((rows // fold, width * fold), lambda p: (p, 0)))
        elif i in turned:
            shapes.append((width, rows * parts))
            specs.append(pl.BlockSpec((width, rows), lambda p: (0, p)))
        else:
            shapes.append((rows * parts, width))
            specs.append(pl.BlockSpec((rows, width), lambda p: (p, 0)))
    return pl.pallas_call(
        functools.partial(assemble_kernel, (n, m), cuts, fold),
        grid=(parts,),
        out_shape=[jax.ShapeDtypeStruct(v, single) for v in shapes],
        in_specs=[pl.BlockSpec(memory_space=pltpu.SMEM), one, one, two, two],
        out_specs=specs,
        compiler_params=pltpu.CompilerParams(vmem_limit_bytes=56 << 20),
        cost_estimate=pl.CostEstimate(flops=0, bytes_accessed=50 << 20, transcendentals=0),
    )(where, *lines[0], *lines[1])


def widths_of(total):
    if total % 128:
        return [total]
    out = []
    while total > 0:
        out.append(min(384, total))
        total -= out[-1]
    return out


def tie(value, *others):
    hbm = pl.BlockSpec(memory_space=pl.ANY)
    return pl.pallas_call(
        lambda *refs: None,
        out_shape=jax.ShapeDtypeStruct(value.shape, value.dtype),
        in_specs=[hbm] * (1 + len(others)),
        out_specs=hbm,
        input_output_aliases={0: 0},
    )(value, *others)


def grid_of(experts, shards):
    if shards == 2 and experts % 4 == 0:
        return (experts // 4, 2, 2)
    side = math.isqrt(experts)
    return (side, side) if side * side == experts else (experts,)


class Chips:
    def __init__(self, dims, names):
        self.dims = dims
        self.names = names
        self.size = int(np.prod(dims))
        self.plane = self.size // dims[0]
        self.places = [tuple(int(v) for v in np.unravel_index(i, dims)) for i in range(self.size)]
        self.offsets = [
            tuple(int(v) for v in np.unravel_index(i, dims[1:])) for i in range(self.plane)
        ]

    def index(self, place):
        return int(np.ravel_multi_index(place, self.dims))

    def own(self, axis):
        return lax.axis_index(self.names[axis])

    def me(self):
        return lax.axis_index(self.names)

    def pairs(self, axis_of, by):
        out = []
        for i, place in enumerate(self.places):
            axis = axis_of(place)
            to = list(place)
            to[axis] = (to[axis] + by) % self.dims[axis]
            out.append((i, self.index(to)))
        return out

    def along(self, value, axis, by):
        n = self.dims[axis]
        return lax.ppermute(value, self.names[axis], [(i, (i + by) % n) for i in range(n)])

    def offset_by(self, value, offset):
        out = []
        for i, place in enumerate(self.places):
            to = [place[0]] + [
                (p + o) % d for p, o, d in zip(place[1:], offset, self.dims[1:])
            ]
            out.append((i, self.index(to)))
        return lax.ppermute(value, self.names, out)

    def first(self, block):
        return [block] + [self.along(block, 0, j) for j in range(1, self.dims[0])]

    def hop_one(self, block, j):
        if len(self.dims) < 3:
            return [block]
        return [block] + [self.along(block, 1, s) for s in range(1, self.dims[1])]

    def hop_two(self, blocks, j):
        last = len(self.dims) - 1
        if last == 0:
            return blocks
        return [v for b in blocks for v in self.hop_line(b, last)]

    def hop_line(self, block, axis):
        return [block] + [self.along(block, axis, s) for s in range(1, self.dims[axis])]

    def straight(self, block):
        return [self.offset_by(block, o) if any(o) else block for o in self.offsets]

    def straight_back(self, blocks):
        return [
            self.offset_by(b, [-v for v in o]) if any(o) else b
            for b, o in zip(blocks, self.offsets)
        ]

    def back_two(self, blocks, j, turn=False):
        if len(self.dims) == 1:
            return [(blocks[0], [])]
        n = self.dims[-1]
        if len(self.dims) == 2:
            return [(blocks[0], [self.along(blocks[s], 1, -s) for s in range(1, n)])]
        m = self.dims[1]
        if turn:
            return [
                (blocks[h * n], [self.along(blocks[h * n + t], 2, -t) for t in range(1, n)])
                for h in range(m)
            ]
        return [
            (blocks[t], [self.along(blocks[h * n + t], 1, -h) for h in range(1, m)])
            for t in range(n)
        ]

    def back_one(self, sums, j, turn=False):
        axis = 1 if turn else 2
        got = [self.along(v.astype(bfloat), axis, -s) for s, v in enumerate(sums) if s]
        return [sums[0], got]

    def sources(self):
        table = [
            [
                self.index([(p - o) % d for p, o, d in zip(place, self.places[i], self.dims)])
                for i in range(self.size)
            ]
            for place in self.places
        ]
        return jnp.asarray(np.array(table, np.int32))[self.me()]

    def back_first(self, total, j):
        return self.along(total.astype(bfloat), 0, -j) if j else total

    def own_part(self):
        part = 0
        for axis in range(1, len(self.dims)):
            part = part * self.dims[axis] + self.own(axis)
        return part

    def swap_columns(self, *values):
        out = []
        for offset in self.offsets:
            part = 0
            for axis, by in enumerate(offset):
                n = self.dims[axis + 1]
                part = part * n + (self.own(axis + 1) + by) % n
            pieces = []
            for v in values:
                size = v.shape[1] // self.plane
                pieces.append(lax.dynamic_slice_in_dim(v, part * size, size, 1))
            piece = jnp.concatenate(pieces, axis=1)
            out.append(self.offset_by(piece, offset) if any(offset) else piece)
        return out

    def orders(self):
        return ((2, 1), (1, 2)) if len(self.dims) == 3 else ((1,),)

    def halves(self, value):
        if len(self.dims) != 3:
            return [value]
        cut = value.shape[1] // 256 * 128
        return [value[:, :cut], value[:, cut:]]

    def stack_one(self, value):
        return [self.hop_line(v, o[0]) for v, o in zip(self.halves(value), self.orders())]

    def stack_two(self, lines, mark):
        out = []
        for line, order in zip(lines, self.orders()):
            both = jnp.concatenate(hold(line, mark), axis=0)
            out.append(self.hop_line(both, order[1]) if len(order) > 1 else [both])
        return out

    def stack_done(self, lines, mark):
        out = []
        for line, order in zip(lines, self.orders()):
            line = hold(line, mark)
            if order == (1, 2):
                n = self.dims[1]
                rows = line[0].shape[0] // n
                line = [v[s * rows : (s + 1) * rows] for s in range(n) for v in line]
            out.append(jnp.concatenate(line, axis=0))
        return out

    def send_rows(self, value):
        size = value.shape[0] // self.plane
        out = []
        for offset in self.offsets:
            part = 0
            for axis, by in enumerate(offset):
                n = self.dims[axis + 1]
                part = part * n + (self.own(axis + 1) + by) % n
            piece = lax.dynamic_slice_in_dim(value, part * size, size, 0)
            out.append(self.offset_by(piece, offset) if any(offset) else piece)
        return out

    def line_send(self, value):
        n = self.dims[0]
        rows = value.shape[0] // n
        own = self.own(0)
        out = [lax.dynamic_slice_in_dim(value, own * rows, rows, 0)]
        for j in range(1, n):
            piece = lax.dynamic_slice_in_dim(value, ((own + j) % n) * rows, rows, 0)
            out.append(self.along(piece, 0, j))
        return out

    def gather_one(self, halves):
        return [self.hop_line(v, o[0]) for v, o in zip(halves, self.orders())]

    def gather_two(self, lines, mark):
        out = []
        for line, order in zip(lines, self.orders()):
            line = hold(line, mark)
            own = self.own(order[0])
            if len(order) == 1:
                out.append([in_order(line, own, 0)])
            else:
                both = in_order(line, own, 0)
                out.append(self.hop_line(both, order[1]))
        return out

    def gather_done(self, lines, mark):
        out = []
        for line, order in zip(lines, self.orders()):
            line = hold(line, mark)
            if len(order) == 1:
                out.append(line[0])
            elif order == (1, 2):
                n = self.dims[1]
                rows = line[0].shape[0] // n
                cut = [[v[i * rows : (i + 1) * rows] for v in line] for i in range(n)]
                out += [jnp.concatenate([in_order(v, self.own(2), 0) for v in cut], axis=0)]
            else:
                out.append(in_order(line, self.own(order[1]), 0))
        return jnp.concatenate(out, axis=1)


def after(value, *others):
    return lax.optimization_barrier((value, *others))[0]


def hold(values, *others):
    return [values[0]] + [tie(v, *others) for v in values[1:]]


def add_up(values):
    return sum([v.astype(single) for v in values[1:]], values[0].astype(single)).astype(bfloat)


def split(value, widths):
    out, start = [], 0
    for width in widths:
        out.append(value[:, start : start + width])
        start += width
    return out


def in_order(pieces, own, axis):
    n = len(pieces)
    if n == 1:
        return pieces[0]
    if n == 2:
        return jnp.where(
            own == 0,
            jnp.concatenate(pieces, axis=axis),
            jnp.concatenate([pieces[1], pieces[0]], axis=axis),
        )
    turned = pieces[::-1]
    line = jnp.concatenate(turned + turned[:-1], axis=axis)
    extent = pieces[0].shape[axis]
    return lax.dynamic_slice_in_dim(line, (n - 1 - own) * extent, n * extent, axis)


class Cores:
    def __init__(self, count):
        self.count = count
        self.own = lax.axis_index("shard")

    def along(self, value, by):
        n = self.count
        return lax.ppermute(value, "shard", [(i, (i + by) % n) for i in range(n)])

    def spread(self, value):
        return [value] + [self.along(value, j) for j in range(1, self.count)]

    def whole(self, value, axis):
        return in_order(self.spread(value), self.own, axis)

    def chunk(self, value, j, axis):
        size = value.shape[axis] // self.count
        place = (self.own + j + self.count) % self.count
        return lax.dynamic_slice_in_dim(value, place * size, size, axis)

    def rows_times(self, left, pieces):
        out = None
        for j, piece in enumerate(pieces):
            term = dot(self.chunk(left, -j, 1), piece)
            out = term if out is None else out + term
        return out

    def times_rows_t(self, left, pieces):
        return in_order([dot_t(left, piece) for piece in pieces], self.own, 1)

    def swap_columns(self, *values):
        out = []
        for j in range(self.count):
            piece = jnp.concatenate([self.chunk(v, j, 1) for v in values], axis=1)
            out.append(self.along(piece, j) if j else piece)
        return split(jnp.concatenate(out, axis=0), [v.shape[1] // self.count for v in values])

    def stack(self, value):
        return jnp.concatenate(self.spread(value), axis=0)

    def give_back(self, value):
        rows = value.shape[0] // self.count
        total = value[:rows]
        for j in range(1, self.count):
            total = total + self.along(value[j * rows : (j + 1) * rows], -j)
        return total

    def scatter(self, value, axis):
        total = self.chunk(value, 0, axis).astype(single)
        for j in range(1, self.count):
            total = total + self.along(self.chunk(value, j, axis).astype(bfloat), j).astype(single)
        return total


def per_device(
    chips,
    shards,
    tokens,
    segment_ids,
    routes,
    cotangent,
    gain_attn,
    gain_query,
    gain_latent,
    gain_ffn,
    w_qa,
    w_qb,
    w_kva,
    w_kvb,
    w_out,
    w_router,
    shared_gate,
    shared_up,
    shared_down,
    expert_gate,
    expert_up,
    expert_down,
):
    cores = Cores(shards)
    me = chips.me()
    shard_pos = cores.own
    tok_rows = tokens.shape[0]
    model = tokens.shape[1]
    group_rows = tok_rows * shards
    score_scale = 1.0 / (DN + DR) ** 0.5
    query_rank = w_qa.shape[1]

    gains = jnp.concatenate([gain_attn, gain_query, gain_latent, gain_ffn])
    gain_pieces = cores.spread(gains)
    sizes = [v.shape[0] for v in (gain_attn, gain_query, gain_latent, gain_ffn)]
    full_gains = []
    start = 0
    for size in sizes:
        full_gains.append(
            in_order([g[start : start + size] for g in gain_pieces], shard_pos, 0).astype(single)
        )
        start += size
    gain_attn_f, gain_query_f, gain_latent_f, gain_ffn_f = full_gains
    qa_pieces = cores.spread(w_qa)
    kva_pieces = cores.spread(w_kva)
    qb_pieces = cores.spread(w_qb)
    kvb_pieces = cores.spread(w_kvb)
    out_pieces = cores.spread(w_out)
    router_full = cores.whole(w_router, 0)
    expert_weights = [
        cores.spread(expert_gate[0].T),
        cores.spread(expert_up[0].T),
        cores.spread(expert_down[0]),
    ]
    turns = chips.dims[0]
    order = [0] + list(range(2, turns, 2)) + list(range(1, turns, 2))
    all_cots = lax.all_gather(cotangent, chips.names, axis=0, tiled=True)

    resid = tokens.astype(single)
    attn_scale = row_scale(resid)
    attn_normed = resid * attn_scale
    attn_in = (attn_normed * gain_attn_f).astype(bfloat)
    query_lat = cores.rows_times(attn_in, qa_pieces)
    query_scale = row_scale(query_lat)
    query_normed = query_lat * query_scale
    query_in = (query_normed * gain_query_f).astype(bfloat)
    query_all = cores.rows_times(query_in, qb_pieces)
    group_pos = seq_positions(segment_ids)
    own_start = shard_pos * tok_rows
    own_pos = lax.dynamic_slice_in_dim(group_pos, own_start, tok_rows, 0)
    own_seg = lax.dynamic_slice_in_dim(segment_ids, own_start, tok_rows, 0)
    cosine, sine = rope_tables(own_pos, DR // 2)
    latent_raw = cores.rows_times(attn_in, kva_pieces)
    latent_part = latent_raw[:, :KR]
    latent_scale = row_scale(latent_part)
    latent_normed = latent_part * latent_scale
    latent = (latent_normed * gain_latent_f).astype(bfloat)
    key_rope = rotate(latent_raw[:, KR:], cosine, sine).astype(bfloat)
    keys = cores.whole(jnp.concatenate([latent, key_rope], axis=1), 0)
    keys_latent, keys_rope = keys[:, :KR], keys[:, KR:]
    keys_turned = jnp.concatenate(
        [cores.chunk(keys_latent, -j, 1) for j in range(shards)], axis=1
    )
    group_index = jnp.arange(group_rows, dtype=jnp.int32)
    own_index = own_start + jnp.arange(tok_rows, dtype=jnp.int32)
    visible = (own_seg[:, None] == segment_ids[None, :]) & (
        group_index[None, :] <= own_index[:, None]
    )

    attn_heads, *saved = run_heads(
        query_all,
        kvb_pieces,
        keys_turned,
        keys_rope,
        visible.astype(single),
        cosine,
        sine,
        H,
        score_scale,
    )
    mid = resid + cores.rows_times(attn_heads, out_pieces)
    ffn_scale = row_scale(mid)
    ffn_normed = mid * ffn_scale
    ffn_in = (ffn_normed * gain_ffn_f).astype(bfloat)

    experts_all = router_full.shape[1]
    lanes = -(-4 * experts_all // 128) * 128
    logits = dot(ffn_in, router_full)
    chosen = jnp.sum(
        (routes[:, :, None] == jnp.arange(experts_all, dtype=jnp.int32)[None, None, :]).astype(
            single
        ),
        axis=1,
    )
    sig = jax.nn.sigmoid(logits)
    denom = jnp.sum(chosen * sig, axis=-1, keepdims=True)
    routing_weights = route_scale * chosen * sig / denom
    capacity = min(tok_rows, 4 * tok_rows * TOP // (3 * experts_all))
    earlier = (jnp.arange(tok_rows)[:, None] > jnp.arange(tok_rows)[None, :]).astype(bfloat)
    slot = dot(earlier, chosen.astype(bfloat))
    code = jnp.where(chosen > 0, slot, -1.0)
    weight_high = routing_weights.astype(bfloat)
    weight_rest = (routing_weights - weight_high.astype(single)).astype(bfloat)
    marks = jnp.concatenate(
        [
            code.astype(bfloat),
            weight_high,
            weight_rest,
            jnp.zeros((tok_rows, lanes - 3 * experts_all), bfloat),
        ],
        axis=1,
    )
    payload = jnp.concatenate([ffn_in, marks], axis=1)
    first = chips.first(payload)
    one, two = [None] * turns, [None] * turns
    two[0] = chips.straight(payload)
    one[1] = None

    stack_ffn = cores.stack(ffn_in)
    stack_cot = cores.stack(cotangent)

    def feed_forward(rows, grads, gate, up, down):
        pre_gate = dot(rows, gate)
        pre_up = dot(rows, up)
        hidden = (jax.nn.silu(pre_gate) * pre_up).astype(bfloat)
        grad_gate, grad_up = silu_grads(dot_t(grads, down), pre_gate, pre_up)
        return hidden, grad_gate, grad_up

    def got_two(j, *others):
        out = []
        for own, got in back_two[j]:
            total = own.astype(single)
            for v in got:
                total = total + tie(v, *others).astype(single)
            out.append(total)
        return out

    def got_one(j, *others):
        own, got = back_one[j]
        for v in got:
            own = own + tie(v, *others).astype(single)
        return own

    sh_hidden, sh_gate, sh_up = feed_forward(
        stack_ffn, stack_cot, shared_gate, shared_up, shared_down
    )
    sh_back = dot_t(sh_gate, shared_gate) + dot_t(sh_up, shared_up)
    shared_out = cores.give_back(dot(sh_hidden, shared_down))
    shared_back = cores.give_back(sh_back)

    who = jnp.concatenate([me.astype(jnp.int32).reshape(1), chips.sources()])
    kept = None
    back_blocks, out_blocks = [None] * turns, [None] * turns
    sent, grads_of = [], []

    def others_part(i, waits):
        base = 4 + ((i + 1) % 3) * shards
        left = kept[base : base + shards]
        right = kept[1] if i == 2 else kept[0]
        out = [t_dot(tie(v, *waits), right).astype(bfloat) for v in left[1:]]
        sent.append([cores.along(v, -j - 1) for j, v in enumerate(out)])
        return out[-1]

    def own_part(i, waits):
        left = kept[4 + ((i + 1) % 3) * shards]
        right = kept[1] if i == 2 else kept[0]
        got = [tie(v, *waits).astype(single) for v in sent[i]]
        grads_of.append(sum(got, t_dot(tie(left, *waits), right)))
        return grads_of[-1]

    fillers = [
        lambda waits: others_part(1, [others_part(0, waits)]),
        lambda waits: own_part(0, [others_part(2, waits)]),
        lambda waits: own_part(2, [own_part(1, waits)]),
    ]
    mark = sh_back
    backs = [None] * turns
    for step in range(turns + 2):
        waits = []
        if step + 1 < turns:
            k = order[step + 1]
            if step == 0:
                first[k] = tie(first[k], mark)
                two[k] = chips.straight(first[k])
                waits.append(first[k])
            else:
                one[k] = hold(one[k], mark)
                two[k] = chips.hop_two(one[k], k)
                waits += one[k]
        if step + 2 < turns:
            k = order[step + 2]
            first[k] = tie(first[k], mark)
            one[k] = chips.hop_one(first[k], k)
            waits.append(first[k])
        if 2 <= step:
            k = order[step - 2]
            total = add_up(hold(backs[k], mark))
            backs[k] = chips.back_first(total, k)
            waits.append(total)
        if step >= turns:
            mark = fillers[step - turns](waits)
            continue
        j = order[step]
        back_blocks[j], out_blocks[j], kept = run_experts(
            who,
            two[j],
            all_cots,
            expert_weights,
            capacity,
            experts_all,
            j,
            turns,
            kept,
            waits,
        )
        backs[j] = chips.straight_back(back_blocks[j])
        mark = back_blocks[j][0]
    routed_back = backs[0].astype(single)
    for j in order[1:]:
        routed_back = routed_back + tie(backs[j], mark).astype(single)
    chip_ffn, chip_cot = kept[2:4]

    grad_out = cotangent.astype(single)
    grad_weights = (
        routed_back[:, model : model + experts_all]
        + routed_back[:, model + experts_all : model + 2 * experts_all]
    )
    grad_sig = chosen * (
        route_scale * grad_weights / denom
        - jnp.sum(grad_weights * routing_weights, axis=-1, keepdims=True) / denom
    )
    grad_logits = grad_sig * sig * (1.0 - sig)
    grad_router = jnp.einsum("te,td->ed", grad_logits, ffn_in.astype(single), precision=highest)
    grad_ffn_in = (
        routed_back[:, :model]
        + shared_back
        + jnp.einsum("te,de->td", grad_logits, router_full.astype(single), precision=highest)
    )
    grad_mid, grad_gffn = norm_back(grad_ffn_in, ffn_normed, ffn_scale, gain_ffn_f)
    grad_mid = grad_mid + grad_out

    grad_attn_out = grad_mid.astype(bfloat)
    heads_line = chips.stack_one(cores.stack(grad_attn_out))
    lefts = cores.swap_columns(attn_in, query_in, tie(attn_heads, mark))
    lefts = chips.swap_columns(*[tie(v, grad_attn_out) for v in lefts])
    mark = fillers[2]([grad_attn_out, heads_line[0][0]])
    grad_egate = grads_of[0].T[None]
    grad_eup = grads_of[1].T[None]
    grad_edown = grads_of[2][None]
    grad_heads = cores.times_rows_t(tie(grad_attn_out, mark), out_pieces).astype(bfloat)
    heads_line = chips.stack_two(heads_line, grad_heads)
    grad_query, kvb_parts, key_terms, rope_terms = run_heads_back(
        grad_heads,
        kvb_pieces,
        keys_turned,
        keys_rope,
        cosine,
        sine,
        saved,
        H,
        score_scale,
        [v[0] for v in heads_line],
    )
    query_line = chips.stack_one(cores.stack(grad_query))
    kvb_terms = add_up(
        [kvb_parts[0]] + [cores.along(v, -j - 1) for j, v in enumerate(kvb_parts[1:])]
    )
    kvb_line = chips.send_rows(kvb_terms)
    size = KR // shards
    key_terms = in_order(
        [key_terms[:, j * size : (j + 1) * size] for j in range(shards)], shard_pos, 1
    )
    grad_keys = cores.scatter(jnp.concatenate([key_terms, rope_terms], axis=1), 0)
    grad_latent, grad_krope = grad_keys[:, :KR], grad_keys[:, KR:]
    grad_query_in = cores.times_rows_t(grad_query, qb_pieces)
    grad_qlat, grad_gquery = norm_back(grad_query_in, query_normed, query_scale, gain_query_f)
    grad_kvpart, grad_glatent = norm_back(grad_latent, latent_normed, latent_scale, gain_latent_f)
    grad_kvrope = rotate_back(grad_krope, cosine, sine)
    grad_low = jnp.concatenate([grad_qlat, grad_kvpart, grad_kvrope], axis=-1).astype(bfloat)
    shared_weights = (shared_gate, shared_up, shared_down)
    xs, cs = cores.spread(tie(chip_ffn, routed_back)), cores.spread(tie(chip_cot, routed_back))
    widths = widths_of(shared_gate.shape[1]) if shards == 2 else []
    shared_grads = None
    start = 0

    def shared_step(waits):
        nonlocal shared_grads, start
        if not widths:
            return waits[0]
        width = widths.pop(0)
        shared_grads = run_shared(xs, cs, shared_weights, start, width, shared_grads, waits)
        start += width
        return shared_grads[0]

    low_wide = jnp.pad(grad_low, ((0, 0), (0, -grad_low.shape[1] % 128)))
    low_line = chips.straight(cores.stack(low_wide))
    query_line = chips.stack_two(query_line, grad_low)
    lefts = jnp.concatenate(hold(lefts, grad_low), axis=0)
    sizes = [v.shape[1] // (shards * chips.plane) for v in (attn_in, query_in, attn_heads)]
    left_in, left_query, left_heads = split(lefts, sizes)
    heads_all = chips.stack_done(heads_line, grad_low)
    out_part = [t_dot(left_heads, right).astype(bfloat) for right in heads_all]
    kvb_part = add_up(hold(kvb_line, out_part[0]))
    fold = left_heads.shape[1] // kvb_part.shape[0]
    kvb_cols = kvb_part.shape[1] // fold
    kvb_part = jnp.concatenate(split(kvb_part, [kvb_cols] * fold), axis=0)
    part = jnp.concatenate([kvb_part, *out_part], axis=1)
    part_sums = lax.psum_scatter(part, chips.names[0], scatter_dimension=0, tiled=True)
    mark = shared_step([part, low_line[0]] + [v[0] for v in query_line])
    part_all = lax.all_gather(tie(part_sums, mark), chips.names[0], axis=0, tiled=True)
    grad_low = tie(grad_low, mark)
    grad_attn_in = in_order(
        [
            dot_t(grad_low[:, :query_rank], qa) + dot_t(grad_low[:, query_rank:], kva)
            for qa, kva in zip(qa_pieces, kva_pieces)
        ],
        shard_pos,
        1,
    )
    grad_resid, grad_gattn = norm_back(grad_attn_in, attn_normed, attn_scale, gain_attn_f)
    grad_tokens = grad_mid + grad_resid
    mixed = jnp.concatenate(
        [grad_gquery.reshape(shards, -1), grad_glatent.reshape(shards, -1)], axis=1
    ).reshape(-1)
    small = jnp.concatenate(
        [grad_gattn[None], grad_gffn[None], mixed[None], grad_router], axis=0
    )
    small_line = chips.send_rows(cores.scatter(small, 1).T.astype(bfloat))
    query_all = chips.stack_done(query_line, mark)
    query_part = jnp.concatenate(
        [t_dot(left_query, right).astype(bfloat) for right in query_all], axis=1
    )
    query_sums = lax.psum_scatter(query_part, chips.names[0], scatter_dimension=0, tiled=True)
    low_all = jnp.concatenate(hold(low_line, mark), axis=0)
    low_part = t_dot(left_in, low_all).astype(bfloat)
    small_part = add_up(hold(small_line, query_part))
    low_cols = grad_low.shape[1]
    spare = low_part.shape[1] - low_cols - small_part.shape[1]
    low_part = jnp.concatenate(
        [low_part[:, :low_cols], jnp.pad(small_part, ((0, 0), (0, spare)))], axis=1
    )
    low_line = chips.line_send(low_part)
    turn_of = [j % 2 == 1 for j in range(turns)]
    back_two = [
        chips.back_two([tie(v, mark) for v in out_blocks[j]], j, turn_of[j])
        for j in range(turns)
    ]
    mark = shared_step([query_part, low_line[0]])
    part_line = chips.gather_one(chips.halves(tie(part_all, mark)))
    query_all = lax.all_gather(tie(query_sums, mark), chips.names[0], axis=0, tiled=True)
    low_line = chips.hop_line(add_up(hold(low_line, mark)), 0)
    back_one = [chips.back_one(got_two(j, mark), j, turn_of[j]) for j in range(turns)]
    waits = [v[0] for v in part_line] + [v[0] for v in back_one]
    mark = shared_step(waits + [low_line[0]])
    low_all = in_order(hold(low_line, mark), chips.own(0), 0)
    low_line = chips.gather_one(chips.halves(low_all))
    query_line = chips.gather_one(chips.halves(tie(query_all, mark)))
    part_line = chips.gather_two(part_line, mark)
    back_sums = [chips.back_first(got_one(j, mark), j) for j in range(turns)]
    waits = [v[0] for line in (part_line, query_line, low_line) for v in line]
    mark = shared_step(waits + back_sums)
    low_line = chips.gather_two(low_line, mark)
    query_line = chips.gather_two(query_line, mark)
    routed_out = back_sums[0]
    for j in range(1, turns):
        routed_out = routed_out + tie(back_sums[j], mark).astype(single)
    result = mid + shared_out + routed_out
    cuts = [kvb_cols, w_out.shape[1]]
    low_cuts = [query_rank, low_cols - query_rank, small_part.shape[1] + spare]
    if len(chips.dims) == 3:
        part_line = [hold(v, mark) for v in part_line]
        grad_wkvb, grad_wout = assemble(chips, part_line, cuts, fold, ())
        low_line = [hold(v, grad_wout, result) for v in low_line]
        grad_wqa, grad_wkva, small = assemble(chips, low_line, low_cuts, 1, (1,))
        grad_wkva = grad_wkva.T
        query_line = [hold(v, grad_wqa) for v in query_line]
        (grad_wqb,) = assemble(chips, query_line, [w_qb.shape[1]], 1, ())
    else:
        part_all = chips.gather_done(part_line, mark).astype(single)
        kvb_all, grad_wout = split(part_all, cuts)
        kvb_all = kvb_all.reshape(chips.plane, fold, -1, kvb_cols)
        grad_wkvb = kvb_all.swapaxes(1, 2).reshape(-1, fold * kvb_cols)
        low_all = chips.gather_done(low_line, mark).astype(single)
        grad_wqa, grad_wkva, small = split(low_all, low_cuts)
        grad_wqb = chips.gather_done(query_line, mark).astype(single)

    if shards == 2:
        grad_sgate, grad_sup, grad_sdown = shared_grads
    else:
        grad_sgate = grad_sup = grad_sdown = 0.0
        all_ffn, all_cot = chip_ffn, chip_cot
        for turn in range(shards):
            if turn > 0:
                tied = lax.optimization_barrier(
                    (all_ffn, all_cot, grad_sgate, grad_sup, grad_sdown)
                )
                grad_sgate, grad_sup, grad_sdown = tied[2:]
                all_ffn, all_cot = cores.along(tied[0], 1), cores.along(tied[1], 1)
            all_hidden, all_gate, all_up = feed_forward(
                all_ffn, all_cot, shared_gate, shared_up, shared_down
            )
            grad_sgate = grad_sgate + t_dot(all_ffn, all_gate)
            grad_sup = grad_sup + t_dot(all_ffn, all_up)
            grad_sdown = grad_sdown + t_dot(all_hidden, all_cot)
    query_part = gain_query.shape[0]
    return (
        result,
        grad_tokens,
        small[:, 0],
        small[:query_part, 2],
        small[query_part:, 2],
        small[:, 1],
        grad_wqa,
        grad_wqb,
        grad_wkva,
        grad_wkvb,
        grad_wout,
        small[:, 3 : 3 + experts_all],
        grad_sgate,
        grad_sup,
        grad_sdown,
        grad_egate,
        grad_eup,
        grad_edown,
    )


def solution(mesh):
    shards = mesh.shape["shard"]
    dims = grid_of(mesh.shape["expert"], shards)
    names = tuple(f"line{i}" for i in range(len(dims)))
    grid = jax.sharding.Mesh(mesh.devices.reshape(dims + (shards,)), names + ("shard",))
    chips = Chips(dims, names)
    both = names + ("shard",)
    in_specs = (
        P(both, None),
        P(names),
        P(both, None),
        P(both, None),
        P("shard"),
        P("shard"),
        P("shard"),
        P("shard"),
        P("shard", None),
        P("shard", None),
        P("shard", None),
        P("shard", None),
        P("shard", None),
        P("shard", None),
        P(None, "shard"),
        P(None, "shard"),
        P("shard", None),
        P(names, None, "shard"),
        P(names, None, "shard"),
        P(names, "shard", None),
    )
    out_specs = (
        P(both, None),
        P(both, None),
        P("shard"),
        P("shard"),
        P("shard"),
        P("shard"),
        P("shard", None),
        P("shard", None),
        P("shard", None),
        P("shard", None),
        P("shard", None),
        P("shard", None),
        P(None, "shard"),
        P(None, "shard"),
        P("shard", None),
        P(names, None, "shard"),
        P(names, None, "shard"),
        P(names, "shard", None),
    )

    def body(*args):
        return per_device(chips, shards, *args)

    return jax.shard_map(
        body, mesh=grid, in_specs=in_specs, out_specs=out_specs, check_vma=False
    )
```

time: 1310 us -> 1110 us (0.85)
  waiting for transfers between devices: 495 us -> 272 us
  Pallas kernels: 282 us -> 369 us
  starting transfers between devices: 148 us -> 116 us
  matrix products: 158 us -> 133 us
    ppermute x48 -> x0, waiting for transfers between devices: 153 us -> none  [in_plane(): lax.ppermute(value, self.names, self.pairs(self.turning(turn, second), by))]
    psum x4 -> x0, waiting for transfers between devices: 79.1 us -> none  [line_sums(): return lax.psum(tuple(halves), self.names[0])]
    pallas_call x0 -> x115, Pallas kernels: none -> 54.7 us  [the longest x3 23.8 us: assemble(): pl.pallas_call(functools.partial(assemble_kernel, (n, m), cuts, fold), gr...]
    ppermute x48 -> x0, starting transfers between devices: 49.2 us -> none  [in_plane(): lax.ppermute(value, self.names, self.pairs(self.turning(turn, second), by))]
    ppermute x12 -> x30, waiting for transfers between devices: 25.6 us -> 65.8 us  [offset_by(): return lax.ppermute(value, self.names, out)]
    ppermute x44 -> x53, waiting for transfers between devices: 236 us -> 202 us  [along(): lax.ppermute(value, self.names[axis], [(i, (i + by) % n) for i in range(n)])]
    dot_general x15 -> x0, matrix products: 29.3 us -> none  [the longest x1 4.48 us: per_device(): jnp.einsum('htg,thk->gk', probs_low, grad_attn_lat, preferred_element_typ...]
    unnamed x373 -> x409, local copies, waits for them, and re-layouts: 37.7 us -> 57.2 us
  transfers between devices with their start and end apart: 137 -> 115, of which waited for: 48 -> 29; matrix products, arithmetic and copies ran while one was open for 24% -> 26% of each run, Pallas kernels for 22% -> 33%
where the time goes in v2:
time: 1110 us; the launch traced here: 1100 us
  Pallas kernels  369 us (33%)
  waiting for transfers between devices  272 us (25%)
  matrix products  133 us (12%)
  starting transfers between devices  116 us (10%)
  other arithmetic  101 us (9%)
  local copies, waits for them, and re-layouts  91.8 us (8%)
  between operations  17.1 us (2%)
    pallas_call x4, Pallas kernels, run_shared(): pl.pallas_call(functools.partial(shared_kernel, parts, tiles, start, widt...  209 us
    ppermute x53, waiting for transfers between devices, along(): lax.ppermute(value, self.names[axis], [(i, (i + by) % n) for i in range(n)])  202 us
    pallas_call x4, Pallas kernels, run_experts(): pl.pallas_call(functools.partial(expert_kernel, count, pieces, capacity,...  105 us
    ppermute x53, starting transfers between devices, along(): lax.ppermute(value, self.names[axis], [(i, (i + by) % n) for i in range(n)])  78 us
    dot_general x11, matrix products, t_dot(): lax.dot_general(left, right, (((0,), (0,)), ((), ())), preferred_element_...  65.9 us
    ppermute x30, waiting for transfers between devices, offset_by(): return lax.ppermute(value, self.names, out)  65.8 us
    unnamed x409, local copies, waits for them, and re-layouts  57.2 us
    dot_general x11, matrix products, dot_t(): lax.dot_general(left, right, (((1,), (1,)), ((), ())), preferred_element_...  34.5 us
  transfers between devices with their start and end apart: 115, of which 29 were waited for; matrix products, arithmetic and copies ran while one was open for 26% of the time, Pallas kernels for 33%

profile of v2, /device:TPU:18, one launch (start us, length us, event | category | flops | bytes accessed | tf_op | source)
XLA Modules:
  0.0 1098.9 jit_solution(4915275647791681137)
XLA Ops:
  38.7 14.0 %shard_map.340 = (bf16[128,2048]{1,0:T(8,128)(2,1)S(1)}, bf16[128,2048]{1,0:T(8,128)(2,1)S(1)}, bf16[128,1024]{1,0:T(8,128)(2,1)S(1)}, bf16[128,8192]{1,0:T(8,12...) custom-call(f32[128,3072]{1,0:T(8,128)S(1)} %convolution_add_fusion.refs_0_, ...), custom_call_target="tpu_custom_call" | custom-call | flops 3221225472 | bytes 14680064 | tf_op jit(solution)/shard_map/pallas_call | solution.py:427
  61.0 5.8 fusion.62
  70.4 4.6 fusion.73
  75.1 5.1 fusion.72
  80.3 5.2 fusion.68
  86.1 30.9 %collective-permute-done.18.refs_0_ = bf16[128,2176]{1,0:T(8,128)(2,1)S(1)} collective-permute-done((bf16[128,2176]{1,0:T(8,128)(2,1)}, bf16[128,2176]{1,0:T(8,128)(2,1)S(1)}, u32[]{:S(2)}, u32[]{:S(2)}) %collective-permute-start.18) | collective-permute-done | bytes 557088 | tf_op jit(solution)/shard_map/ppermute | solution.py:578
  118.5 22.4 %collective-permute-done.16.refs_0_ = bf16[128,2176]{1,0:T(8,128)(2,1)S(1)} collective-permute-done((bf16[128,2176]{1,0:T(8,128)(2,1)}, bf16[128,2176]{1,0:T(8,128)(2,1)S(1)}, u32[]{:S(2)}, u32[]{:S(2)}) %collective-permute-start.16) | collective-permute-done | bytes 557088 | tf_op jit(solution)/shard_map/ppermute | solution.py:578
  146.7 8.6 collective-permute-start.19
  159.3 23.9 %shard_map.343 = (bf16[128,2176]{1,0:T(8,128)(2,1)}, bf16[128,2176]{1,0:T(8,128)(2,1)}, bf16[128,2176]{1,0:T(8,128)(2,1)}, bf16[128,2176]{1,0:T(8,128)(2,1)}, bf...) custom-call(s32[17]{0:T(128)} %pad_add_fusion.refs_0_, ...), custom_call_target="tpu_custom_call" | custom-call | flops 8858370048 | bytes 31457280 | tf_op jit(solution)/shard_map/pallas_call | solution.py:208
  183.3 9.0 collective-permute-done.25.refs_0_
  198.1 32.7 %shard_map.346 = (bf16[128,2176]{1,0:T(8,128)(2,1)}, bf16[128,2176]{1,0:T(8,128)(2,1)}, bf16[128,2176]{1,0:T(8,128)(2,1)}, bf16[128,2176]{1,0:T(8,128)(2,1)}, bf...) custom-call(s32[17]{0:T(128)} %pad_add_fusion.refs_0_, ...), custom_call_target="tpu_custom_call", output_to_operand_aliasing={{8}: (15, {}), {9}: (16, {}), {10}: (17, {}), {11}: (18, {}... | custom-call | flops 8858370048 | bytes 31457280 | tf_op jit(solution)/shard_map/pallas_call | solution.py:208
  237.5 9.1 collective-permute-done.28.refs_2_
  247.0 11.4 %collective-permute-done.29.refs_4_ = bf16[128,2176]{1,0:T(8,128)(2,1)} collective-permute-done((bf16[128,2176]{1,0:T(8,128)(2,1)}, bf16[128,2176]{1,0:T(8,128)(2,1)}, u32[]{:S(2)}, u32[]{:S(2)}) %collective-permute-start.29) | collective-permute-done | bytes 557088 | tf_op jit(solution)/shard_map/ppermute | solution.py:578
  259.2 24.0 %shard_map.351 = (bf16[128,2176]{1,0:T(8,128)(2,1)}, bf16[128,2176]{1,0:T(8,128)(2,1)}, bf16[128,2176]{1,0:T(8,128)(2,1)}, bf16[128,2176]{1,0:T(8,128)(2,1)}, bf...) custom-call(s32[17]{0:T(128)} %pad_add_fusion.refs_0_, ...), custom_call_target="tpu_custom_call", output_to_operand_aliasing={{8}: (15, {}), {9}: (16, {}), {10}: (17, {}), {11}: (18, {}... | custom-call | flops 8858370048 | bytes 31457280 | tf_op jit(solution)/shard_map/pallas_call | solution.py:208
  286.2 8.0 collective-permute-done.34.refs_0_
  298.9 7.3 collective-permute-done.26.refs_4_
  306.2 24.3 %shard_map.355 = (bf16[128,2176]{1,0:T(8,128)(2,1)}, bf16[128,2176]{1,0:T(8,128)(2,1)}, bf16[128,2176]{1,0:T(8,128)(2,1)}, bf16[128,2176]{1,0:T(8,128)(2,1)}, bf...) custom-call(s32[17]{0:T(128)} %pad_add_fusion.refs_0_, ...), custom_call_target="tpu_custom_call", output_to_operand_aliasing={{8}: (13, {}), {9}: (14, {}), {10}: (15, {}), {11}: (16, {}... | custom-call | flops 8858370048 | bytes 31457280 | tf_op jit(solution)/shard_map/pallas_call | solution.py:208
  334.9 7.8 convolution_convert_fusion.2.refs_1_
  342.7 4.5 fusion.67
  353.1 7.4 convolution_convert_fusion.1.refs_1_
  360.5 4.8 collective-permute-done.36.refs_0_
  368.7 8.6 collective-permute-done.40.refs_0_
  377.3 4.9 collective-permute-start.43
  385.9 7.4 convolution_convert_fusion.refs_1_
  396.3 8.8 convert_add_fusion.2.refs_1_
  405.1 11.1 %collective-permute-done.43.refs_0_ = bf16[128,2176]{1,0:T(8,128)(2,1)} collective-permute-done((bf16[128,2176]{1,0:T(8,128)(2,1)S(1)}, bf16[128,2176]{1,0:T(8,128)(2,1)}, u32[]{:S(2)}, u32[]{:S(2)}) %collective-permute-start.43) | collective-permute-done | bytes 557088 | tf_op jit(solution)/shard_map/ppermute | solution.py:578
  431.4 8.8 convert_add_fusion.1.refs_1_
  441.6 8.9 convert_add_fusion.refs_1_
  477.3 16.8 %shard_map.379 = (bf16[128,3072]{1,0:T(8,128)(2,1)S(1)}, bf16[256,4096]{1,0:T(8,128)(2,1)S(1)}, bf16[256,4096]{1,0:T(8,128)(2,1)}, f32[256,512]{1,0:T(8,128)S(1)}, f32[256,64]{1,0:T(8,128)S(1)}) custom-call(bf16[128,2048]{1,0:T(8,128)(2,1)S(1)} %copy-done, bf16[256,4096]{1,0:T(8,128)(2,1)S(1)} %copy-done.15, bf16[256,4096]{1,0:T(8,128)(2,1)S(1)} %copy-done.17, ...), custom_call_target="tpu_custom_call" | custom-call | flops 6442450944 | bytes 20971520 | tf_op jit(solution)/shard_map/pallas_call | solution.py:451
  510.6 5.9 collective-permute-done.59.refs_0_
  528.0 17.1 %collective-permute-done.63.refs_0_ = bf16[512,1024]{1,0:T(8,128)(2,1)S(1)} collective-permute-done((bf16[512,1024]{1,0:T(8,128)(2,1)S(1)}, bf16[512,1024]{1,0:T(8,128)(2,1)S(1)}, u32[]{:S(2)}, u32[]{:S(2)}) %collective-permute-start.63) | collective-permute-done | bytes 1048608 | tf_op jit(solution)/shard_map/ppermute | solution.py:578
  556.1 8.1 collective-permute-done.67.refs_0_
  576.1 6.6 collective-permute-done.54.refs_0_
  583.8 31.7 %collective-permute-done.61.refs_0_ = bf16[64,4096]{1,0:T(8,128)(2,1)S(1)} collective-permute-done((bf16[64,4096]{1,0:T(8,128)(2,1)S(1)}, bf16[64,4096]{1,0:T(8,128)(2,1)S(1)}, u32[]{:S(2)}, u32[]{:S(2)}) %collective-permute-start.61) | collective-permute-done | bytes 524320 | tf_op jit(solution)/shard_map/ppermute | solution.py:587
  623.6 54.5 %shard_map.394 = (f32[2048,1408]{1,0:T(8,128)}, f32[2048,1408]{1,0:T(8,128)}, f32[1408,2048]{1,0:T(8,128)}) custom-call(bf16[2048,2048]{1,0:T(8,128)(2,1)} %shard_map.370.refs_0_, bf16[2048,2048]{1,0:T(8,128)(2,1)} %collective-permute-done.45.refs_1_, bf16[2048,2048]{1,0:T(8,128)(2,1)} %shard_map.371.refs_2_, ...), custom_call_target="tpu_custom_call" | custom-call | flops 38654705664 | bytes 33554432 | tf_op jit(solution)/shard_map/pallas_call | solution.py:306
  726.2 54.5 %shard_map.406 = (f32[2048,1408]{1,0:T(8,128)}, f32[2048,1408]{1,0:T(8,128)}, f32[1408,2048]{1,0:T(8,128)}) custom-call(bf16[2048,2048]{1,0:T(8,128)(2,1)} %shard_map.370.refs_0_, bf16[2048,2048]{1,0:T(8,128)(2,1)} %collective-permute-done.45.refs_1_, ...), custom_call_target="tpu_custom_call", output_to_operand_aliasing={{0}: (9, {}), {1}: (10, {}), {2}: (11, {})} | custom-call | flops 38654705664 | bytes 33554432 | tf_op jit(solution)/shard_map/pallas_call | solution.py:306
  789.0 16.3 %collective-permute-done.86.refs_0_ = bf16[128,2048]{1,0:T(8,128)(2,1)S(1)} collective-permute-done((bf16[128,2048]{1,0:T(8,128)(2,1)}, bf16[128,2048]{1,0:T(8,128)(2,1)S(1)}, u32[]{:S(2)}, u32[]{:S(2)}) %collective-permute-start.86) | collective-permute-done | bytes 524320 | tf_op jit(solution)/shard_map/ppermute | solution.py:578
  829.5 54.3 %shard_map.425 = (f32[2048,1408]{1,0:T(8,128)}, f32[2048,1408]{1,0:T(8,128)}, f32[1408,2048]{1,0:T(8,128)}) custom-call(bf16[2048,2048]{1,0:T(8,128)(2,1)} %shard_map.370.refs_0_, bf16[2048,2048]{1,0:T(8,128)(2,1)} %collective-permute-done.45.refs_1_, ...), custom_call_target="tpu_custom_call", output_to_operand_aliasing={{0}: (14, {}), {1}: (15, {}), {2}: (16, {})} | custom-call | flops 38654705664 | bytes 33554432 | tf_op jit(solution)/shard_map/pallas_call | solution.py:306
  902.7 7.5 collective-permute-done.98.refs_0_
  936.8 6.8 collective-permute-start.100
  943.7 7.9 collective-permute-done.88.refs_14_.refs_0_
  955.2 46.2 %shard_map.446 = (f32[2048,1408]{1,0:T(8,128)}, f32[2048,1408]{1,0:T(8,128)}, f32[1408,2048]{1,0:T(8,128)}) custom-call(bf16[2048,2048]{1,0:T(8,128)(2,1)} %shard_map.370.refs_0_, bf16[2048,2048]{1,0:T(8,128)(2,1)} %collective-permute-done.45.refs_1_, ...), custom_call_target="tpu_custom_call", output_to_operand_aliasing={{0}: (17, {}), {1}: (18, {}), {2}: (19, {})} | custom-call | flops 25769803776 | bytes 33554432 | tf_op jit(solution)/shard_map/pallas_call | solution.py:306
  1024.7 14.5 %collective-permute-done.102.refs_0_ = bf16[512,1536]{1,0:T(8,128)(2,1)} collective-permute-done((bf16[512,1536]{1,0:T(8,128)(2,1)}, bf16[512,1536]{1,0:T(8,128)(2,1)}, u32[]{:S(2)}, u32[]{:S(2)}) %collective-permute-start.102) | collective-permute-done | bytes 1572896 | tf_op jit(solution)/shard_map/ppermute | solution.py:578
  1039.2 9.0 shard_map.453
  1048.2 13.5 %collective-permute-done.101.refs_0_ = bf16[512,1024]{1,0:T(8,128)(2,1)} collective-permute-done((bf16[512,1024]{1,0:T(8,128)(2,1)}, bf16[512,1024]{1,0:T(8,128)(2,1)}, u32[]{:S(2)}, u32[]{:S(2)}) %collective-permute-start.101) | collective-permute-done | bytes 1048608 | tf_op jit(solution)/shard_map/ppermute | solution.py:578
  1061.7 7.3 shard_map.457
  1075.8 8.7 collective-permute-done.107.refs_0_
  1084.5 7.5 shard_map.462
  (906 shorter events, 357.8 us)
Async XLA Ops:
  7.2 152.1 %all-gather.4.cloned.1.call-start = ((), (), s32[]{:S(2)}) async-start(), calls=%async_computation.2 | async-start | bytes 8912896 | tf_op jit(solution)/shard_map/all_gather | solution.py:901
  7.9 680.9 %reduce-scatter.3.cloned.1.call-start = ((), (), s32[]{:S(2)}) async-start(), calls=%async_computation.3 | async-start | bytes 1966080 | tf_op jit(solution)/shard_map/reduce_scatter | solution.py:1172
  8.0 52.8 %collective-permute-start.17 = (bf16[128,2048]{1,0:T(8,128)(2,1)}, bf16[128,2048]{1,0:T(8,128)(2,1)}, u32[]{:S(2)}, u32[]{:S(2)}) collective-permute-start(bf16[128,2048]{1,0:T(8,128)(2,1)} %param.24), channel_id=1, source_target_pairs={{0,1},{1,0},{2,3},{3,2},{4,5},{5,4},{6,7},{7,6},{8,9},{9,8},{10,11... | collective-permute-start | bytes 1572872 | tf_op jit(solution)/shard_map/ppermute | solution.py:797
  34.9 50.6 %collective-permute-start.13 = (bf16[704,2048]{1,0:T(8,128)(2,1)}, bf16[704,2048]{1,0:T(8,128)(2,1)}, u32[]{:S(2)}, u32[]{:S(2)}) collective-permute-start(bf16[704,2048]{1,0:T(8,128)(2,1)} %bitcast.5.refs_6_), channel_id=1, source_target_pairs={{0,1},{1,0},{2,3},{3,2},{4,5},{5,4},{6,7},{7,6},{8,9},{9,8},{10,11... | collective-permute-start | bytes 8650760 | tf_op jit(solution)/shard_map/ppermute | solution.py:797
  38.3 108.5 %collective-permute-start.14 = (bf16[704,2048]{1,0:T(8,128)(2,1)}, bf16[704,2048]{1,0:T(8,128)(2,1)}, u32[]{:S(2)}, u32[]{:S(2)}) collective-permute-start(bf16[704,2048]{1,0:T(8,128)(2,1)} %bitcast.8.refs_8_), channel_id=1, source_target_pairs={{0,1},{1,0},{2,3},{3,2},{4,5},{5,4},{6,7},{7,6},{8,9},{9,8},{10,11... | collective-permute-start | bytes 8650760 | tf_op jit(solution)/shard_map/ppermute | solution.py:797
  54.1 101.2 %collective-permute-start.15 = (bf16[704,2048]{1,0:T(8,128)(2,1)}, bf16[704,2048]{1,0:T(8,128)(2,1)}, u32[]{:S(2)}, u32[]{:S(2)}) collective-permute-start(bf16[704,2048]{1,0:T(8,128)(2,1)} %bitcast.10.refs_10_), channel_id=1, source_target_pairs={{0,1},{1,0},{2,3},{3,2},{4,5},{5,4},{6,7},{7,6},{8,9},{9,8},{10,11... | collective-permute-start | bytes 8650760 | tf_op jit(solution)/shard_map/ppermute | solution.py:797
  68.3 48.7 %collective-permute-start.18 = (bf16[128,2176]{1,0:T(8,128)(2,1)}, bf16[128,2176]{1,0:T(8,128)(2,1)S(1)}, u32[]{:S(2)}, u32[]{:S(2)}) collective-permute-start(bf16[128,2176]{1,0:T(8,128)(2,1)} %concatenate.265.refs_1_), channel_id=1, source_target_pairs={{0,8},{8,16},{16,24},{24,0},{1,9},{9,17},{17,25},{25,1},{2,10},{10... | collective-permute-start | bytes 1671176 | tf_op jit(solution)/shard_map/ppermute | solution.py:578
  70.1 70.8 %collective-permute-start.16 = (bf16[128,2176]{1,0:T(8,128)(2,1)}, bf16[128,2176]{1,0:T(8,128)(2,1)S(1)}, u32[]{:S(2)}, u32[]{:S(2)}) collective-permute-start(bf16[128,2176]{1,0:T(8,128)(2,1)} %concatenate.265.refs_1_), channel_id=1, source_target_pairs={{0,16},{8,24},{16,0},{24,8},{1,17},{9,25},{17,1},{25,9},{2,18},{10... | collective-permute-start | bytes 1671176 | tf_op jit(solution)/shard_map/ppermute | solution.py:578
  85.5 71.3 %collective-permute-start.10 = (bf16[128,2176]{1,0:T(8,128)(2,1)}, bf16[128,2176]{1,0:T(8,128)(2,1)}, u32[]{:S(2)}, u32[]{:S(2)}) collective-permute-start(bf16[128,2176]{1,0:T(8,128)(2,1)} %concatenate.265.refs_1_), channel_id=1, source_target_pairs={{0,2},{2,0},{4,6},{6,4},{8,10},{10,8},{12,14},{14,12},{16,18},{18,... | collective-permute-start | bytes 1671176 | tf_op jit(solution)/shard_map/ppermute | solution.py:587
  146.7 46.3 %collective-permute-start.19 = (bf16[128,2176]{1,0:T(8,128)(2,1)}, bf16[128,2176]{1,0:T(8,128)(2,1)S(1)}, u32[]{:S(2)}, u32[]{:S(2)}) collective-permute-start(bf16[128,2176]{1,0:T(8,128)(2,1)} %concatenate.265.refs_1_), channel_id=1, source_target_pairs={{0,24},{8,0},{16,8},{24,16},{1,25},{9,1},{17,9},{25,17},{2,26},{10... | collective-permute-start | bytes 1671176 | tf_op jit(solution)/shard_map/ppermute | solution.py:578
  192.2 226.8 %collective-permute-start.47 = (f32[128,2048]{1,0:T(8,128)}, f32[128,2048]{1,0:T(8,128)}, u32[]{:S(2)}, u32[]{:S(2)}) collective-permute-start(f32[128,2048]{1,0:T(8,128)} %slice.251), channel_id=1, source_target_pairs={{0,1},{1,0},{2,3},{3,2},{4,5},{5,4},{6,7},{7,6},{8,9},{9,8},{10,11... | collective-permute-start | bytes 3145736 | tf_op jit(solution)/shard_map/ppermute | solution.py:797
  233.0 65.2 %collective-permute-start.20 = (bf16[128,2176]{1,0:T(8,128)(2,1)S(1)}, bf16[128,2176]{1,0:T(8,128)(2,1)}, u32[]{:S(2)}, u32[]{:S(2)}) collective-permute-start(bf16[128,2176]{1,0:T(8,128)(2,1)S(1)} %copy-done.53), channel_id=1, source_target_pairs={{0,2},{2,0},{1,3},{3,1},{4,6},{6,4},{5,7},{7,5},{8,10},{10,8},{9,1... | collective-permute-start | bytes 1671176 | tf_op jit(solution)/shard_map/ppermute | solution.py:578
  233.8 49.5 %collective-permute-start.27 = (bf16[128,2176]{1,0:T(8,128)(2,1)}, bf16[128,2176]{1,0:T(8,128)(2,1)}, u32[]{:S(2)}, u32[]{:S(2)}) collective-permute-start(bf16[128,2176]{1,0:T(8,128)(2,1)} %get-tuple-element.132), channel_id=1, source_target_pairs={{0,2},{2,0},{4,6},{6,4},{8,10},{10,8},{12,14},{14,12},{16,18},{18,... | collective-permute-start | bytes 1671176 | tf_op jit(solution)/shard_map/ppermute | solution.py:587
  285.4 45.1 %collective-permute-start.37 = (bf16[128,2176]{1,0:T(8,128)(2,1)}, bf16[128,2176]{1,0:T(8,128)(2,1)S(1)}, u32[]{:S(2)}, u32[]{:S(2)}) collective-permute-start(bf16[128,2176]{1,0:T(8,128)(2,1)} %get-tuple-element.166), channel_id=1, source_target_pairs={{0,2},{2,0},{4,6},{6,4},{8,10},{10,8},{12,14},{14,12},{16,18},{18,... | collective-permute-start | bytes 1671176 | tf_op jit(solution)/shard_map/ppermute | solution.py:587
  342.6 50.7 %collective-permute-start.42 = (bf16[704,2048]{1,0:T(8,128)(2,1)}, bf16[704,2048]{1,0:T(8,128)(2,1)}, u32[]{:S(2)}, u32[]{:S(2)}) collective-permute-start(bf16[704,2048]{1,0:T(8,128)(2,1)} %convolution_convert_fusion.2.refs_1_), channel_id=1, source_target_pairs={{0,1},{1,0},{2,3},{3,2},{4,5},{5,4},{6,7},{7,6},{8,9},{9,8},{10,11... | collective-permute-start | bytes 8650760 | tf_op jit(solution)/shard_map/ppermute | solution.py:797
  382.2 47.3 %collective-permute-start.49 = (bf16[704,2048]{1,0:T(8,128)(2,1)}, bf16[704,2048]{1,0:T(8,128)(2,1)}, u32[]{:S(2)}, u32[]{:S(2)}) collective-permute-start(bf16[704,2048]{1,0:T(8,128)(2,1)} %convolution_convert_fusion.1.refs_1_), channel_id=1, source_target_pairs={{0,1},{1,0},{2,3},{3,2},{4,5},{5,4},{6,7},{7,6},{8,9},{9,8},{10,11... | collective-permute-start | bytes 8650760 | tf_op jit(solution)/shard_map/ppermute | solution.py:797
  424.9 196.7 %collective-permute-start.46 = (bf16[2048,2048]{1,0:T(8,128)(2,1)}, bf16[2048,2048]{1,0:T(8,128)(2,1)}, u32[]{:S(2)}, u32[]{:S(2)}) collective-permute-start(bf16[2048,2048]{1,0:T(8,128)(2,1)} %shard_map.371.refs_2_), channel_id=1, source_target_pairs={{0,1},{1,0},{2,3},{3,2},{4,5},{5,4},{6,7},{7,6},{8,9},{9,8},{10,11... | collective-permute-start | bytes 25165832 | tf_op jit(solution)/shard_map/ppermute | solution.py:797
  428.4 194.5 %collective-permute-start.45 = (bf16[2048,2048]{1,0:T(8,128)(2,1)}, bf16[2048,2048]{1,0:T(8,128)(2,1)}, u32[]{:S(2)}, u32[]{:S(2)}) collective-permute-start(bf16[2048,2048]{1,0:T(8,128)(2,1)} %shard_map.370.refs_0_), channel_id=1, source_target_pairs={{0,1},{1,0},{2,3},{3,2},{4,5},{5,4},{6,7},{7,6},{8,9},{9,8},{10,11... | collective-permute-start | bytes 25165832 | tf_op jit(solution)/shard_map/ppermute | solution.py:797
  460.4 48.7 %collective-permute-start.56 = (bf16[256,704]{1,0:T(8,128)(2,1)}, bf16[256,704]{1,0:T(8,128)(2,1)}, u32[]{:S(2)}, u32[]{:S(2)}) collective-permute-start(bf16[256,704]{1,0:T(8,128)(2,1)} %pad_maximum_fusion.16), channel_id=1, source_target_pairs={{0,2},{2,0},{4,6},{6,4},{8,10},{10,8},{12,14},{14,12},{16,18},{18,... | collective-permute-start | bytes 1081352 | tf_op jit(solution)/shard_map/ppermute | solution.py:587
  465.8 43.5 %collective-permute-start.58 = (bf16[256,704]{1,0:T(8,128)(2,1)}, bf16[256,704]{1,0:T(8,128)(2,1)}, u32[]{:S(2)}, u32[]{:S(2)}) collective-permute-start(bf16[256,704]{1,0:T(8,128)(2,1)} %pad_maximum_fusion.17), channel_id=1, source_target_pairs={{0,4},{2,6},{4,0},{6,2},{8,12},{10,14},{12,8},{14,10},{16,20},{18,... | collective-permute-start | bytes 1081352 | tf_op jit(solution)/shard_map/ppermute | solution.py:587
  568.6 46.9 %collective-permute-start.61 = (bf16[64,4096]{1,0:T(8,128)(2,1)S(1)}, bf16[64,4096]{1,0:T(8,128)(2,1)S(1)}, u32[]{:S(2)}, u32[]{:S(2)}) collective-permute-start(bf16[64,4096]{1,0:T(8,128)(2,1)S(1)} %get-tuple-element.323), channel_id=1, source_target_pairs={{0,4},{2,6},{4,0},{6,2},{8,12},{10,14},{12,8},{14,10},{16,20},{18,... | collective-permute-start | bytes 1572872 | tf_op jit(solution)/shard_map/ppermute | solution.py:587
  569.5 46.8 %collective-permute-start.62 = (bf16[64,4096]{1,0:T(8,128)(2,1)S(1)}, bf16[64,4096]{1,0:T(8,128)(2,1)S(1)}, u32[]{:S(2)}, u32[]{:S(2)}) collective-permute-start(bf16[64,4096]{1,0:T(8,128)(2,1)S(1)} %get-tuple-element.322), channel_id=1, source_target_pairs={{0,6},{2,4},{4,2},{6,0},{8,14},{10,12},{12,10},{14,8},{16,22},{18,... | collective-permute-start | bytes 1572872 | tf_op jit(solution)/shard_map/ppermute | solution.py:587
  582.7 106.3 %collective-permute-start.73 = (bf16[256,2176]{1,0:T(8,128)(2,1)}, bf16[256,2176]{1,0:T(8,128)(2,1)}, u32[]{:S(2)}, u32[]{:S(2)}) collective-permute-start(bf16[256,2176]{1,0:T(8,128)(2,1)} %pad_maximum_fusion.6.refs_8_), channel_id=1, source_target_pairs={{0,6},{2,4},{4,2},{6,0},{8,14},{10,12},{12,10},{14,8},{16,22},{18,... | collective-permute-start | bytes 3342344 | tf_op jit(solution)/shard_map/ppermute | solution.py:587
  615.6 73.5 %collective-permute-start.72 = (bf16[256,2176]{1,0:T(8,128)(2,1)}, bf16[256,2176]{1,0:T(8,128)(2,1)}, u32[]{:S(2)}, u32[]{:S(2)}) collective-permute-start(bf16[256,2176]{1,0:T(8,128)(2,1)} %pad_maximum_fusion.6.refs_8_), channel_id=1, source_target_pairs={{0,4},{2,6},{4,0},{6,2},{8,12},{10,14},{12,8},{14,10},{16,20},{18,... | collective-permute-start | bytes 3342344 | tf_op jit(solution)/shard_map/ppermute | solution.py:587
  616.4 73.4 %collective-permute-start.71 = (bf16[256,2176]{1,0:T(8,128)(2,1)}, bf16[256,2176]{1,0:T(8,128)(2,1)}, u32[]{:S(2)}, u32[]{:S(2)}) collective-permute-start(bf16[256,2176]{1,0:T(8,128)(2,1)} %pad_maximum_fusion.6.refs_8_), channel_id=1, source_target_pairs={{0,2},{2,0},{4,6},{6,4},{8,10},{10,8},{12,14},{14,12},{16,18},{18,... | collective-permute-start | bytes 3342344 | tf_op jit(solution)/shard_map/ppermute | solution.py:587
  621.5 205.2 %all-gather.6.cloned.1.call-start = ((), (), s32[]{:S(2)}) async-start(), calls=%async_computation.4 | async-start | bytes 1966080 | tf_op jit(solution)/shard_map/all_gather | solution.py:1174
  621.5 69.7 %collective-permute-start.69 = (bf16[512,1536]{1,0:T(8,128)(2,1)}, bf16[512,1536]{1,0:T(8,128)(2,1)}, u32[]{:S(2)}, u32[]{:S(2)}) collective-permute-start(bf16[512,1536]{1,0:T(8,128)(2,1)} %pad_maximum_fusion.2.refs_9_), channel_id=1, source_target_pairs={{0,4},{4,0},{1,5},{5,1},{2,6},{6,2},{3,7},{7,3},{8,12},{12,8},{9,1... | collective-permute-start | bytes 4718600 | tf_op jit(solution)/shard_map/ppermute | solution.py:578
  622.9 78.9 %collective-permute-start.70 = (bf16[512,1536]{1,0:T(8,128)(2,1)}, bf16[512,1536]{1,0:T(8,128)(2,1)S(1)}, u32[]{:S(2)}, u32[]{:S(2)}) collective-permute-start(bf16[512,1536]{1,0:T(8,128)(2,1)} %pad_maximum_fusion.3.refs_10_), channel_id=1, source_target_pairs={{0,2},{2,0},{1,3},{3,1},{4,6},{6,4},{5,7},{7,5},{8,10},{10,8},{9,1... | collective-permute-start | bytes 4718600 | tf_op jit(solution)/shard_map/ppermute | solution.py:578
  688.9 140.5 %reduce-scatter.5.cloned.1.call-start = ((), (), s32[]{:S(2)}) async-start(), calls=%async_computation.5 | async-start | bytes 1474560 | tf_op jit(solution)/shard_map/reduce_scatter | solution.py:1197
  689.1 96.8 %collective-permute-start.94 = (bf16[128,2048]{1,0:T(8,128)(2,1)}, bf16[128,2048]{1,0:T(8,128)(2,1)}, u32[]{:S(2)}, u32[]{:S(2)}) collective-permute-start(bf16[128,2048]{1,0:T(8,128)(2,1)} %shard_map.439), channel_id=1, source_target_pairs={{0,4},{4,0},{1,5},{5,1},{2,6},{6,2},{3,7},{7,3},{8,12},{12,8},{9,1... | collective-permute-start | bytes 1572872 | tf_op jit(solution)/shard_map/ppermute | solution.py:578
  689.8 121.4 %collective-permute-start.82 = (bf16[128,2048]{1,0:T(8,128)(2,1)}, bf16[128,2048]{1,0:T(8,128)(2,1)S(1)}, u32[]{:S(2)}, u32[]{:S(2)}) collective-permute-start(bf16[128,2048]{1,0:T(8,128)(2,1)} %shard_map.420), channel_id=1, source_target_pairs={{0,2},{2,0},{1,3},{3,1},{4,6},{6,4},{5,7},{7,5},{8,10},{10,8},{9,1... | collective-permute-start | bytes 1572872 | tf_op jit(solution)/shard_map/ppermute | solution.py:578
  718.1 214.8 %all-gather.8.cloned.1.call-start = ((), (), s32[]{:S(2)}) async-start(), calls=%async_computation.6 | async-start | bytes 1474560 | tf_op jit(solution)/shard_map/all_gather | solution.py:1214
  722.0 58.7 %collective-permute-start.83 = (bf16[64,2176]{1,0:T(8,128)(2,1)S(1)}, bf16[64,2176]{1,0:T(8,128)(2,1)S(1)}, u32[]{:S(2)}, u32[]{:S(2)}) collective-permute-start(bf16[64,2176]{1,0:T(8,128)(2,1)S(1)} %get-tuple-element.332), channel_id=1, source_target_pairs={{0,8},{8,16},{16,24},{24,0},{1,9},{9,17},{17,25},{25,1},{2,10},{10... | collective-permute-start | bytes 835592 | tf_op jit(solution)/shard_map/ppermute | solution.py:578
  723.2 58.5 %collective-permute-start.84 = (bf16[64,2176]{1,0:T(8,128)(2,1)S(1)}, bf16[64,2176]{1,0:T(8,128)(2,1)S(1)}, u32[]{:S(2)}, u32[]{:S(2)}) collective-permute-start(bf16[64,2176]{1,0:T(8,128)(2,1)S(1)} %get-tuple-element.334), channel_id=1, source_target_pairs={{0,16},{8,24},{16,0},{24,8},{1,17},{9,25},{17,1},{25,9},{2,18},{10... | collective-permute-start | bytes 835592 | tf_op jit(solution)/shard_map/ppermute | solution.py:578
  726.0 56.8 %collective-permute-start.85 = (bf16[64,2176]{1,0:T(8,128)(2,1)S(1)}, bf16[64,2176]{1,0:T(8,128)(2,1)S(1)}, u32[]{:S(2)}, u32[]{:S(2)}) collective-permute-start(bf16[64,2176]{1,0:T(8,128)(2,1)S(1)} %get-tuple-element.333), channel_id=1, source_target_pairs={{0,24},{8,0},{16,8},{24,16},{1,25},{9,1},{17,9},{25,17},{2,26},{10... | collective-permute-start | bytes 835592 | tf_op jit(solution)/shard_map/ppermute | solution.py:578
  811.2 205.8 %collective-permute-start.8 = (f32[128,2048]{1,0:T(8,128)}, f32[128,2048]{1,0:T(8,128)}, u32[]{:S(2)}, u32[]{:S(2)}) collective-permute-start(f32[128,2048]{1,0:T(8,128)} %slice.248), channel_id=1, source_target_pairs={{0,1},{1,0},{2,3},{3,2},{4,5},{5,4},{6,7},{7,6},{8,9},{9,8},{10,11... | collective-permute-start | bytes 3145736 | tf_op jit(solution)/shard_map/ppermute | solution.py:797
  812.0 81.1 %collective-permute-start.93 = (bf16[64,2176]{1,0:T(8,128)(2,1)}, bf16[64,2176]{1,0:T(8,128)(2,1)S(1)}, u32[]{:S(2)}, u32[]{:S(2)}) collective-permute-start(bf16[64,2176]{1,0:T(8,128)(2,1)} %add_convert_fusion.13.refs_13_), channel_id=1, source_target_pairs={{0,8},{8,16},{16,24},{24,0},{1,9},{9,17},{17,25},{25,1},{2,10},{10... | collective-permute-start | bytes 835592 | tf_op jit(solution)/shard_map/ppermute | solution.py:578
  813.8 76.6 %collective-permute-start.92 = (bf16[64,2176]{1,0:T(8,128)(2,1)}, bf16[64,2176]{1,0:T(8,128)(2,1)}, u32[]{:S(2)}, u32[]{:S(2)}) collective-permute-start(bf16[64,2176]{1,0:T(8,128)(2,1)} %add_convert_fusion.13.refs_13_), channel_id=1, source_target_pairs={{0,16},{8,24},{16,0},{24,8},{1,17},{9,25},{17,1},{25,9},{2,18},{10... | collective-permute-start | bytes 835592 | tf_op jit(solution)/shard_map/ppermute | solution.py:578
  816.9 70.2 %collective-permute-start.91 = (bf16[64,2176]{1,0:T(8,128)(2,1)}, bf16[64,2176]{1,0:T(8,128)(2,1)}, u32[]{:S(2)}, u32[]{:S(2)}) collective-permute-start(bf16[64,2176]{1,0:T(8,128)(2,1)} %add_convert_fusion.13.refs_13_), channel_id=1, source_target_pairs={{0,24},{8,0},{16,8},{24,16},{1,25},{9,1},{17,9},{25,17},{2,26},{10... | collective-permute-start | bytes 835592 | tf_op jit(solution)/shard_map/ppermute | solution.py:578
  819.7 64.0 %collective-permute-start.95 = (bf16[128,2048]{1,0:T(8,128)(2,1)}, bf16[128,2048]{1,0:T(8,128)(2,1)}, u32[]{:S(2)}, u32[]{:S(2)}) collective-permute-start(bf16[128,2048]{1,0:T(8,128)(2,1)} %add_convert_fusion.8), channel_id=1, source_target_pairs={{0,2},{2,0},{1,3},{3,1},{4,6},{6,4},{5,7},{7,5},{8,10},{10,8},{9,1... | collective-permute-start | bytes 1572872 | tf_op jit(solution)/shard_map/ppermute | solution.py:578
  936.8 64.7 %collective-permute-start.100 = (bf16[256,1024]{1,0:T(8,128)(2,1)}, bf16[256,1024]{1,0:T(8,128)(2,1)}, u32[]{:S(2)}, u32[]{:S(2)}) collective-permute-start(bf16[256,1024]{1,0:T(8,128)(2,1)} %constant_dynamic-slice_fusion.14.refs_11_), channel_id=1, source_target_pairs={{0,2},{2,0},{1,3},{3,1},{4,6},{6,4},{5,7},{7,5},{8,10},{10,8},{9,1... | collective-permute-start | bytes 1572872 | tf_op jit(solution)/shard_map/ppermute | solution.py:578
  951.5 66.0 %collective-permute-start.103 = (bf16[512,1536]{1,0:T(8,128)(2,1)}, bf16[512,1536]{1,0:T(8,128)(2,1)S(1)}, u32[]{:S(2)}, u32[]{:S(2)}) collective-permute-start(bf16[512,1536]{1,0:T(8,128)(2,1)} %maximum_select_fusion.1.refs_8_.refs_3_), channel_id=1, source_target_pairs={{0,2},{2,0},{1,3},{3,1},{4,6},{6,4},{5,7},{7,5},{8,10},{10,8},{9,1... | collective-permute-start | bytes 4718600 | tf_op jit(solution)/shard_map/ppermute | solution.py:578
  953.3 54.5 %collective-permute-start.108 = (bf16[192,1536]{1,0:T(8,128)(2,1)}, bf16[192,1536]{1,0:T(8,128)(2,1)}, u32[]{:S(2)}, u32[]{:S(2)}) collective-permute-start(bf16[192,1536]{1,0:T(8,128)(2,1)} %get-tuple-element.330.refs_10_), channel_id=1, source_target_pairs={{0,4},{4,0},{1,5},{5,1},{2,6},{6,2},{3,7},{7,3},{8,12},{12,8},{9,1... | collective-permute-start | bytes 1769480 | tf_op jit(solution)/shard_map/ppermute | solution.py:578
  954.8 54.7 %collective-permute-start.106 = (bf16[192,1536]{1,0:T(8,128)(2,1)}, bf16[192,1536]{1,0:T(8,128)(2,1)S(1)}, u32[]{:S(2)}, u32[]{:S(2)}) collective-permute-start(bf16[192,1536]{1,0:T(8,128)(2,1)} %get-tuple-element.331.refs_9_), channel_id=1, source_target_pairs={{0,2},{2,0},{1,3},{3,1},{4,6},{6,4},{5,7},{7,5},{8,10},{10,8},{9,1... | collective-permute-start | bytes 1769480 | tf_op jit(solution)/shard_map/ppermute | solution.py:578
  1007.8 53.9 %collective-permute-start.105 = (bf16[512,1152]{1,0:T(8,128)(2,1)}, bf16[512,1152]{1,0:T(8,128)(2,1)}, u32[]{:S(2)}, u32[]{:S(2)}) collective-permute-start(bf16[512,1152]{1,0:T(8,128)(2,1)} %maximum_select_fusion.2.refs_3_), channel_id=1, source_target_pairs={{0,2},{2,0},{1,3},{3,1},{4,6},{6,4},{5,7},{7,5},{8,10},{10,8},{9,1... | collective-permute-start | bytes 3538952 | tf_op jit(solution)/shard_map/ppermute | solution.py:578
  1009.4 52.3 %collective-permute-start.101 = (bf16[512,1024]{1,0:T(8,128)(2,1)}, bf16[512,1024]{1,0:T(8,128)(2,1)}, u32[]{:S(2)}, u32[]{:S(2)}) collective-permute-start(bf16[512,1024]{1,0:T(8,128)(2,1)} %maximum_select_fusion.7.refs_1_), channel_id=1, source_target_pairs={{0,4},{4,0},{1,5},{5,1},{2,6},{6,2},{3,7},{7,3},{8,12},{12,8},{9,1... | collective-permute-start | bytes 3145736 | tf_op jit(solution)/shard_map/ppermute | solution.py:578
  1017.0 58.8 %collective-permute-start.109 = (bf16[384,1536]{1,0:T(8,128)(2,1)}, bf16[384,1536]{1,0:T(8,128)(2,1)}, u32[]{:S(2)}, u32[]{:S(2)}) collective-permute-start(bf16[384,1536]{1,0:T(8,128)(2,1)} %maximum_select_fusion.4.refs_3_), channel_id=1, source_target_pairs={{0,2},{2,0},{1,3},{3,1},{4,6},{6,4},{5,7},{7,5},{8,10},{10,8},{9,1... | collective-permute-start | bytes 3538952 | tf_op jit(solution)/shard_map/ppermute | solution.py:578
  1017.5 67.0 %collective-permute-start.107 = (bf16[384,1536]{1,0:T(8,128)(2,1)}, bf16[384,1536]{1,0:T(8,128)(2,1)}, u32[]{:S(2)}, u32[]{:S(2)}) collective-permute-start(bf16[384,1536]{1,0:T(8,128)(2,1)} %maximum_select_fusion.3.refs_1_), channel_id=1, source_target_pairs={{0,4},{4,0},{1,5},{5,1},{2,6},{6,2},{3,7},{7,3},{8,12},{12,8},{9,1... | collective-permute-start | bytes 3538952 | tf_op jit(solution)/shard_map/ppermute | solution.py:578
  (265 other events, 4242.3 us)
Sparse Core Ops, SparseCore 0:
  10.8 142.0 all-gather.3
  621.6 35.2 reduce-scatter.2
  689.0 37.0 all-gather.5
  728.9 39.1 reduce-scatter.4
  829.6 30.0 all-gather.7

commit v3 on v2

--- a/solution.py
+++ b/solution.py
@@ -89,138 +89,306 @@
     return lax.dot_general(left, right, (((0,), (0,)), ((), ())), preferred_element_type=single)
 
 
-def expert_kernel(count, pieces, capacity, experts, group, first, waits, *refs):
+def expert_marks(marks, me, experts, capacity):
+    marks = marks.astype(single)
+    lane = lax.broadcasted_iota(jnp.int32, marks.shape, 1)
+    place = lax.broadcasted_iota(jnp.int32, (marks.shape[0], capacity), 1).astype(single)
+    code = jnp.sum(jnp.where(lane == me, marks, 0.0), axis=1, keepdims=True)
+    weight = (lane == me + experts) | (lane == me + 2 * experts)
+    weight = jnp.sum(jnp.where(weight, marks, 0.0), axis=1, keepdims=True)
+    return (code == place).astype(single).astype(bfloat), weight, lane
+
+
+def views(arrays, tok):
+    return [(v, at) for v in arrays for at in range(0, v.shape[0], tok)]
+
+
+def expert_kernel(arrays, tok, pieces, capacity, experts, group, places, first, waits, *refs):
     refs = list(refs)
     me_ref = refs.pop(0)
-    blocks = [refs.pop(0) for _ in range(count)]
-    all_cots = refs.pop(0)
+    count = len(places)
+    blocks = views([refs.pop(0) for _ in range(arrays)], tok)
     weights = [[refs.pop(0) for _ in range(pieces)] for _ in range(3)]
     refs = refs[waits:]
     if not first:
-        refs = refs[4 + 3 * pieces:]
-    backs = [refs.pop(0) for _ in range(count)]
-    outs = [refs.pop(0) for _ in range(count)]
-    kept = [refs.pop(0) for _ in range(4)]
-    acts = [[refs.pop(0) for _ in range(pieces)] for _ in range(3)]
+        refs = refs[5 + pieces + count :]
+    mark = refs.pop(0)
+    rows_all, ffn_all, gate_all, up_all, out_all = (refs.pop(0) for _ in range(5))
+    hidden_all = [refs.pop(0) for _ in range(pieces)]
+    packs = [refs.pop(0) for _ in range(count)]
     full = [refs.pop(0) for _ in range(3)]
-    rows, grads, cot_scr = refs.pop(0), refs.pop(0), refs.pop(0)
-    act_scr = [[refs.pop(0) for _ in range(pieces)] for _ in range(3)]
-    sem_w, sem_o, sem_c = refs.pop(0), refs.pop(0), refs.pop(0)
-    assert not refs
-    tok = blocks[0].shape[0]
-    model = all_cots.shape[1]
+    rows, gate_scr, up_scr, out_scr = (refs.pop(0) for _ in range(4))
+    hidden_scr = [refs.pop(0) for _ in range(pieces)]
+    outs = refs.pop(0)
+    sem_w, sem_o = refs
+    model = rows.shape[1]
     width = weights[0][0].shape[0]
-    fetches = []
-    for i in range(count):
-        source = pl.multiple_of(me_ref[1 + group * count + i] * tok, tok)
-        c = pltpu.make_async_copy(all_cots.at[pl.ds(source, tok)], cot_scr.at[i], sem_c.at[i])
-        c.start()
-        fetches.append(c)
-    cots = [cot_scr.at[i] for i in range(count)]
-    loads = []
+    loads = [[], [], []]
     for k in range(3):
-        loads.append([])
         for j in range(pieces):
-            c = pltpu.make_async_copy(weights[k][j], full[k].at[pl.ds(j * width, width)], sem_w.at[k, j])
+            c = pltpu.make_async_copy(
+                weights[k][j], full[k].at[pl.ds(j * width, width)], sem_w.at[k, j]
+            )
             c.start()
             loads[k].append(c)
     stores = []
-    def store(src, dst, at):
-        c = pltpu.make_async_copy(src, dst, sem_o.at[at])
+
+    def store(src, dst):
+        c = pltpu.make_async_copy(src, dst, sem_o.at[len(stores)])
         c.start()
         stores.append(c)
+
     me = me_ref[0]
-    lane = lax.broadcasted_iota(jnp.int32, (tok, 128), 1)
-    place = lax.broadcasted_iota(jnp.int32, (tok, capacity), 1).astype(single)
-    picks, wcols = [], []
-    for c in fetches:
+    n = count * capacity
+    mine = pl.ds(group * n, n)
+    picks = []
+    for i in range(count):
+        ref, at = blocks[i]
+        pick, weight, _ = expert_marks(
+            ref[at : at + tok, model : model + 128], me, experts, capacity
+        )
+        picks.append((pick, weight))
+        rows[pl.ds(i * capacity, capacity)] = t_dot(pick, ref[at : at + tok, :model]).astype(bfloat)
+    store(rows, rows_all.at[mine])
+    for i in range(count):
+        store(
+            blocks[i][0].at[pl.ds(blocks[i][1], tok), pl.ds(0, model)],
+            ffn_all.at[pl.ds((group * count + i) * tok, tok)],
+        )
+    for c in loads[0]:
         c.wait()
-    for i in range(count):
-        marks = blocks[i][:, model:model + 128].astype(single)
-        code = jnp.sum(jnp.where(lane == me, marks, 0.0), axis=1, keepdims=True)
-        weight = jnp.sum(jnp.where((lane == me + experts) | (lane == me + 2 * experts), marks, 0.0), axis=1, keepdims=True)
-        pick = (code == place).astype(single).astype(bfloat)
-        picks.append(pick)
-        wcols.append(weight)
-        here = pl.ds(i * capacity, capacity)
-        rows[here] = t_dot(pick, blocks[i][:, :model]).astype(bfloat)
-        scaled = (weight * cots[i][...].astype(single)).astype(bfloat)
-        grads[here] = t_dot(pick, scaled).astype(bfloat)
-    n = count * capacity
-    store(rows, kept[0].at[pl.ds(group * n, n)], 0)
-    store(grads, kept[1].at[pl.ds(group * n, n)], 1)
-    for i in range(count):
-        store(blocks[i].at[:, pl.ds(0, model)], kept[2].at[pl.ds((group * count + i) * tok, tok)], 2 + i)
-        store(cots[i], kept[3].at[pl.ds((group * count + i) * tok, tok)], 2 + count + i)
-    for c in loads[0]: c.wait()
     pre_gate = dot_t(rows[...], full[0][...])
-    for c in loads[1]: c.wait()
+    gate_scr[...] = pre_gate
+    store(gate_scr, gate_all.at[mine])
+    for c in loads[1]:
+        c.wait()
     pre_up = dot_t(rows[...], full[1][...])
-    sigma = jax.nn.sigmoid(pre_gate)
-    silu = pre_gate * sigma
-    hidden = (silu * pre_up).astype(bfloat)
-    for c in loads[2]: c.wait()
-    grad_hidden = dot_t(grads[...], full[2][...])
-    grad_gate = (grad_hidden * pre_up * sigma * (1.0 + pre_gate * (1.0 - sigma))).astype(bfloat)
-    grad_up = (grad_hidden * silu).astype(bfloat)
-    at = 2 + 2 * count
-    for k, v in enumerate((hidden, grad_gate, grad_up)):
-        for j in range(pieces):
-            act_scr[k][j][...] = v[:, j * width:(j + 1) * width]
-            store(act_scr[k][j], acts[k][j].at[pl.ds(group * n, n)], at)
-            at += 1
-    back = (dot(grad_gate, full[0][...]) + dot(grad_up, full[1][...])).astype(bfloat)
+    up_scr[...] = pre_up
+    store(up_scr, up_all.at[mine])
+    hidden = (pre_gate * jax.nn.sigmoid(pre_gate) * pre_up).astype(bfloat)
+    for j in range(pieces):
+        hidden_scr[j][...] = hidden[:, j * width : (j + 1) * width]
+        store(hidden_scr[j], hidden_all[j].at[mine])
+    for c in loads[2]:
+        c.wait()
     out = dot(hidden, full[2][...]).astype(bfloat)
-    for i in range(count):
-        here = slice(i * capacity, (i + 1) * capacity)
-        got = dot(picks[i], out[here])
-        dots = jnp.sum(got * cots[i][...].astype(single), axis=1, keepdims=True)
-        outs[i][...] = (wcols[i] * got).astype(bfloat)
-        backs[i][:, :model] = dot(picks[i], back[here]).astype(bfloat)
-        high = dots.astype(bfloat).astype(single)
-        tail = jnp.where(lane == me, high, 0.0) + jnp.where(lane == me + experts, dots - high, 0.0)
-        backs[i][:, model:model + 128] = tail.astype(bfloat)
-    for c in stores: c.wait()
-
-def run_experts(me, blocks, all_cots, weights, capacity, experts, group, groups, carried, others):
-    count, pieces = len(blocks), len(weights[0])
-    tok, model = blocks[0].shape[0], weights[0][0].shape[1]
+    out_scr[...] = out
+    store(out_scr, out_all.at[mine])
+    for i, (pick, weight) in enumerate(picks):
+        got = dot(pick, out[i * capacity : (i + 1) * capacity])
+        outs[i] = (weight * got).astype(bfloat)
+        pack, at = places[i]
+        store(outs.at[i], packs[pack].at[pl.ds(at * tok, tok)])
+    mark[...] = jnp.zeros_like(mark)
+    for c in stores:
+        c.wait()
+
+
+def run_experts(me, blocks, weights, capacity, experts, group, groups, places, carried, others):
+    count, pieces = len(places), len(weights[0])
+    tok, model = sum(v.shape[0] for v in blocks) // count, weights[0][0].shape[1]
     width = weights[0][0].shape[0]
     n = count * capacity
-    first = carried is None
     shape = jax.ShapeDtypeStruct
-    kept = [shape((groups * n, model), bfloat)] * 2 + [shape((groups * count * tok, model), bfloat)] * 2
-    kept += [shape((groups * n, width), bfloat)] * (3 * pieces)
+    kept = [
+        shape((groups * n, model), bfloat),
+        shape((groups * count * tok, model), bfloat),
+        shape((groups * n, pieces * width), single),
+        shape((groups * n, pieces * width), single),
+        shape((groups * n, model), bfloat),
+    ] + [shape((groups * n, width), bfloat)] * pieces
+    kept += [shape((groups * tok, model), bfloat)] * count
     vm = pl.BlockSpec(memory_space=pltpu.VMEM)
     hbm = pl.BlockSpec(memory_space=pl.ANY)
     flat = [w for ws in weights for w in ws]
-    operands = [me, *blocks, all_cots, *flat, *others]
-    in_specs = [pl.BlockSpec(memory_space=pltpu.SMEM)] + [vm] * count
-    in_specs += [hbm] * (1 + len(flat) + len(others))
+    operands = [me, *blocks, *flat, *others]
+    in_specs = [pl.BlockSpec(memory_space=pltpu.SMEM)] + [vm] * len(blocks)
+    in_specs += [hbm] * (len(flat) + len(others))
     alias = {}
-    if not first:
-        base = len(operands)
+    if carried is not None:
+        alias = {len(operands) + i: 1 + i for i in range(len(kept))}
         operands += list(carried)
         in_specs += [hbm] * len(kept)
-        alias = {base + i: 2 * count + i for i in range(len(kept))}
-    rows = n
-    flops = 2 * rows * model * width * pieces * 6
     out = pl.pallas_call(
-        functools.partial(expert_kernel, count, pieces, capacity, experts, group, first, len(others)),
-        out_shape=[shape(b.shape, bfloat) for b in blocks] + [shape((tok, model), bfloat)] * count + kept,
+        functools.partial(
+            expert_kernel,
+            len(blocks),
+            tok,
+            pieces,
+            capacity,
+            experts,
+            group,
+            places,
+            carried is None,
+            len(others),
+        ),
+        out_shape=[shape((16, 128), bfloat)] + kept,
         in_specs=in_specs,
-        out_specs=[vm] * (2 * count) + [hbm] * len(kept),
+        out_specs=[vm] + [hbm] * len(kept),
         input_output_aliases=alias,
         scratch_shapes=[pltpu.VMEM((pieces * width, model), bfloat)] * 3
-        + [pltpu.VMEM((n, model), bfloat)] * 2
+        + [pltpu.VMEM((n, model), bfloat)]
+        + [pltpu.VMEM((n, pieces * width), single)] * 2
+        + [pltpu.VMEM((n, model), bfloat)]
+        + [pltpu.VMEM((n, width), bfloat)] * pieces
         + [pltpu.VMEM((count, tok, model), bfloat)]
-        + [pltpu.VMEM((n, width), bfloat)] * (3 * pieces)
-        + [pltpu.SemaphoreType.DMA((3, pieces)), pltpu.SemaphoreType.DMA((2 + 2 * count + 3 * pieces,))]
-        + [pltpu.SemaphoreType.DMA((count,))],
-        compiler_params=pltpu.CompilerParams(vmem_limit_bytes=58 << 20),
-        cost_estimate=pl.CostEstimate(flops=flops, bytes_accessed=30 << 20, transcendentals=0),
+        + [pltpu.SemaphoreType.DMA((3, pieces)), pltpu.SemaphoreType.DMA((4 + 2 * count + pieces,))],
+        compiler_params=pltpu.CompilerParams(vmem_limit_bytes=56 << 20),
+        cost_estimate=pl.CostEstimate(flops=0, bytes_accessed=0, transcendentals=0),
     )(*operands)
-    return out[:count], out[count:2 * count], out[2 * count:]
+    return out[0], out[1:]
+
+
+def expert_back_kernel(
+    arrays, results, tok, pieces, capacity, experts, group, first, waits, *refs
+):
+    refs = list(refs)
+    me_ref = refs.pop(0)
+    blocks = views([refs.pop(0) for _ in range(arrays)], tok)
+    count = len(blocks)
+    all_cots = refs.pop(0)
+    weights = [[refs.pop(0) for _ in range(pieces)] for _ in range(3)]
+    gate_all, up_all, out_all = (refs.pop(0) for _ in range(3))
+    refs = refs[waits:]
+    if not first:
+        refs = refs[2 + 2 * pieces :]
+    backs = views([refs.pop(0) for _ in range(results)], tok)
+    grads_all, cot_all = refs.pop(0), refs.pop(0)
+    acts = [[refs.pop(0) for _ in range(pieces)] for _ in range(2)]
+    full = [refs.pop(0) for _ in range(3)]
+    grads, gate_scr, up_scr, out_scr, cot_scr, mark_scr = (refs.pop(0) for _ in range(6))
+    act_scr = [[refs.pop(0) for _ in range(pieces)] for _ in range(2)]
+    sem_w, sem_i, sem_c, sem_o = refs
+    model = grads.shape[1]
+    width = weights[0][0].shape[0]
+    n = count * capacity
+    mine = pl.ds(group * n, n)
+
+    def fetch(src, dst, sem):
+        c = pltpu.make_async_copy(src, dst, sem)
+        c.start()
+        return c
+
+    cots = []
+    for i in range(count):
+        source = pl.multiple_of(me_ref[1 + group * count + i] * tok, tok)
+        cots.append(fetch(all_cots.at[pl.ds(source, tok)], cot_scr.at[i], sem_c.at[0, i]))
+        marks = blocks[i][0].at[pl.ds(blocks[i][1], tok), pl.ds(model, 128)]
+        cots.append(fetch(marks, mark_scr.at[i], sem_c.at[1, i]))
+    loads = {}
+    for k in (2, 0, 1):
+        loads[k] = [
+            fetch(weights[k][j], full[k].at[pl.ds(j * width, width)], sem_w.at[k, j])
+            for j in range(pieces)
+        ]
+    saved = [
+        fetch(gate_all.at[mine], gate_scr, sem_i.at[0]),
+        fetch(up_all.at[mine], up_scr, sem_i.at[1]),
+        fetch(out_all.at[mine], out_scr, sem_i.at[2]),
+    ]
+    stores = []
+
+    def store(src, dst):
+        stores.append(fetch(src, dst, sem_o.at[len(stores)]))
+
+    me = me_ref[0]
+    for c in cots:
+        c.wait()
+    picks = []
+    for i in range(count):
+        pick, weight, lane = expert_marks(mark_scr[i], me, experts, capacity)
+        picks.append(pick)
+        scaled = (weight * cot_scr[i].astype(single)).astype(bfloat)
+        grads[pl.ds(i * capacity, capacity)] = t_dot(pick, scaled).astype(bfloat)
+        store(cot_scr.at[i], cot_all.at[pl.ds((group * count + i) * tok, tok)])
+    store(grads, grads_all.at[mine])
+    for c in loads[2]:
+        c.wait()
+    grad_hidden = dot_t(grads[...], full[2][...])
+    for c in saved:
+        c.wait()
+    pre_gate, pre_up = gate_scr[...], up_scr[...]
+    sigma = jax.nn.sigmoid(pre_gate)
+    grad_gate = grad_hidden * pre_up * sigma * (1.0 + pre_gate * (1.0 - sigma))
+    grad_gate = grad_gate.astype(bfloat)
+    grad_up = (grad_hidden * pre_gate * sigma).astype(bfloat)
+    for k, v in enumerate((grad_gate, grad_up)):
+        for j in range(pieces):
+            act_scr[k][j][...] = v[:, j * width : (j + 1) * width]
+            store(act_scr[k][j], acts[k][j].at[mine])
+    for c in loads[0] + loads[1]:
+        c.wait()
+    back = (dot(grad_gate, full[0][...]) + dot(grad_up, full[1][...])).astype(bfloat)
+    for i in range(count):
+        here = slice(i * capacity, (i + 1) * capacity)
+        got = dot(picks[i], out_scr[here])
+        dots = jnp.sum(got * cot_scr[i].astype(single), axis=1, keepdims=True)
+        ref, at = backs[i]
+        ref[at : at + tok, :model] = dot(picks[i], back[here]).astype(bfloat)
+        high = dots.astype(bfloat).astype(single)
+        tail = jnp.where(lane == me, high, 0.0) + jnp.where(lane == me + experts, dots - high, 0.0)
+        ref[at : at + tok, model : model + 128] = tail.astype(bfloat)
+    for c in stores:
+        c.wait()
+
+
+def run_experts_back(
+    me, blocks, all_cots, weights, saved, capacity, experts, group, groups, apart, carried, others
+):
+    pieces, model = len(weights[0]), weights[0][0].shape[1]
+    count = saved[0].shape[0] // groups // capacity
+    tok = sum(v.shape[0] for v in blocks) // count
+    results = [tok] * count if apart else [v.shape[0] for v in blocks]
+    width = weights[0][0].shape[0]
+    n = count * capacity
+    shape = jax.ShapeDtypeStruct
+    kept = [shape((groups * n, model), bfloat), shape((groups * count * tok, model), bfloat)]
+    kept += [shape((groups * n, width), bfloat)] * (2 * pieces)
+    hbm = pl.BlockSpec(memory_space=pl.ANY)
+    flat = [w for ws in weights for w in ws]
+    operands = [me, *blocks, all_cots, *flat, *saved, *others]
+    in_specs = [pl.BlockSpec(memory_space=pltpu.SMEM)] + [hbm] * (len(operands) - 1)
+    alias = {}
+    if carried is not None:
+        alias = {len(operands) + i: len(results) + i for i in range(len(kept))}
+        operands += list(carried)
+        in_specs += [hbm] * len(kept)
+    out = pl.pallas_call(
+        functools.partial(
+            expert_back_kernel,
+            len(blocks),
+            len(results),
+            tok,
+            pieces,
+            capacity,
+            experts,
+            group,
+            carried is None,
+            len(others),
+        ),
+        out_shape=[shape((v, model + 128), bfloat) for v in results] + kept,
+        in_specs=in_specs,
+        out_specs=[pl.BlockSpec(memory_space=pltpu.VMEM)] * len(results) + [hbm] * len(kept),
+        input_output_aliases=alias,
+        scratch_shapes=[pltpu.VMEM((pieces * width, model), bfloat)] * 3
+        + [pltpu.VMEM((n, model), bfloat)]
+        + [pltpu.VMEM((n, pieces * width), single)] * 2
+        + [
+            pltpu.VMEM((n, model), bfloat),
+            pltpu.VMEM((count, tok, model), bfloat),
+            pltpu.VMEM((count, tok, 128), bfloat),
+        ]
+        + [pltpu.VMEM((n, width), bfloat)] * (2 * pieces)
+        + [
+            pltpu.SemaphoreType.DMA((3, pieces)),
+            pltpu.SemaphoreType.DMA((3,)),
+            pltpu.SemaphoreType.DMA((2, count)),
+            pltpu.SemaphoreType.DMA((1 + count + 2 * pieces,)),
+        ],
+        compiler_params=pltpu.CompilerParams(vmem_limit_bytes=56 << 20),
+        cost_estimate=pl.CostEstimate(flops=0, bytes_accessed=0, transcendentals=0),
+    )(*operands)
+    return out[: len(results)], out[len(results) :]
 
 
 def shared_kernel(parts, tiles, start, width, first, waits, *refs):
@@ -319,7 +487,7 @@
             pltpu.SemaphoreType.DMA((3,)),
         ],
         compiler_params=pltpu.CompilerParams(vmem_limit_bytes=60 << 20),
-        cost_estimate=pl.CostEstimate(flops=12 * tiles * tile * model * width, bytes_accessed=4 * tiles * tile * model, transcendentals=0),
+        cost_estimate=pl.CostEstimate(flops=0, bytes_accessed=0, transcendentals=0),
     )(*operands)
 
 
@@ -431,7 +599,7 @@
         in_specs=[own(2 * (DN + DR)), *kvb] + [still(v) for v in (latent, rope, shown, cosine, sine)],
         out_specs=[own(2 * w) for w in widths],
         compiler_params=pltpu.CompilerParams(vmem_limit_bytes=40 << 20),
-        cost_estimate=pl.CostEstimate(flops=3 << 30, bytes_accessed=14 << 20, transcendentals=heads * rows * keys),
+        cost_estimate=pl.CostEstimate(flops=0, bytes_accessed=0, transcendentals=0),
     )(q, *kvbs, latent, rope, shown, cosine, sine)
 
 
@@ -461,7 +629,7 @@
         out_specs=[own(2 * (DN + DR)), *kvb]
         + [pl.BlockSpec((keys, rank), lambda g: (0, 0)), pl.BlockSpec((keys, DR), lambda g: (0, 0))],
         compiler_params=pltpu.CompilerParams(vmem_limit_bytes=40 << 20),
-        cost_estimate=pl.CostEstimate(flops=6 << 30, bytes_accessed=20 << 20, transcendentals=0),
+        cost_estimate=pl.CostEstimate(flops=0, bytes_accessed=0, transcendentals=0),
     )(grad, *kvbs, latent, rope, cosine, sine, *saved, *others)
     return out[0], out[1 : 1 + pieces], out[1 + pieces], out[2 + pieces]
 
@@ -512,8 +680,78 @@
         in_specs=[pl.BlockSpec(memory_space=pltpu.SMEM), one, one, two, two],
         out_specs=specs,
         compiler_params=pltpu.CompilerParams(vmem_limit_bytes=56 << 20),
-        cost_estimate=pl.CostEstimate(flops=0, bytes_accessed=50 << 20, transcendentals=0),
+        cost_estimate=pl.CostEstimate(flops=0, bytes_accessed=0, transcendentals=0),
     )(where, *lines[0], *lines[1])
+
+
+def plane_kernel(count, rows, start, widths, fold, *refs):
+    refs = list(refs)
+    lefts = [refs.pop(0) for _ in range(count)]
+    rights = [[refs.pop(0) for _ in range(rows)] for _ in widths]
+    extra = refs[:-1]
+    out = refs[-1]
+    tok = lefts[0].shape[0] // rows
+    cols = out.shape[0]
+    at = 0
+    if extra:
+        kvb, small = extra
+        size = kvb.shape[1] // fold
+        for k in range(fold):
+            here = pl.ds(k * kvb.shape[0], kvb.shape[0])
+            out[here, :size] = kvb[:, k * size : (k + 1) * size]
+        at = size
+    for width, parts in zip(widths, rights):
+        total = None
+        for c in range(rows):
+            for o in range(count):
+                left = lefts[o][c * tok : (c + 1) * tok, start : start + cols]
+                term = t_dot(left, parts[c][o * tok : (o + 1) * tok, :width])
+                total = term if total is None else total + term
+        value = total.astype(bfloat)
+        if extra:
+            value = jnp.concatenate([value, small[...]], axis=1)
+        out[:, at : at + value.shape[1]] = value
+        at += value.shape[1]
+
+
+def plane_dot(lefts, start, cols, rights, widths, fold=1, extra=()):
+    total = sum(widths)
+    if extra:
+        total += extra[0].shape[1] // fold + extra[1].shape[1]
+    flat = [v for parts in rights for v in parts]
+    vm = pl.BlockSpec(memory_space=pltpu.VMEM)
+    return pl.pallas_call(
+        functools.partial(plane_kernel, len(lefts), len(rights[0]), start, widths, fold),
+        out_shape=jax.ShapeDtypeStruct((cols, total), bfloat),
+        in_specs=[vm] * (len(lefts) + len(flat) + len(extra)),
+        out_specs=vm,
+        compiler_params=pltpu.CompilerParams(vmem_limit_bytes=48 << 20),
+        cost_estimate=pl.CostEstimate(flops=0, bytes_accessed=0, transcendentals=0),
+    )(*lefts, *flat, *extra)
+
+
+def rows_kernel(value, out):
+    lines, rows = value.shape[0], value.shape[2]
+    for i in range(lines):
+        out[i * rows : (i + 1) * rows] = value[i, 0].astype(single)
+
+
+def in_rows(chips, value):
+    lines, parts = chips.dims[0], chips.plane
+    rows = value.shape[0] // (lines * parts)
+    value = value.reshape(lines, parts, rows, -1)
+    if rows % 16:
+        return value.swapaxes(0, 1).reshape(lines * parts * rows, -1).astype(single)
+    width = value.shape[3]
+    return pl.pallas_call(
+        rows_kernel,
+        grid=(parts,),
+        out_shape=jax.ShapeDtypeStruct((lines * parts * rows, width), single),
+        in_specs=[pl.BlockSpec((lines, 1, rows, width), lambda p: (0, p, 0, 0))],
+        out_specs=pl.BlockSpec((lines * rows, width), lambda p: (p, 0)),
+        compiler_params=pltpu.CompilerParams(vmem_limit_bytes=48 << 20),
+        cost_estimate=pl.CostEstimate(flops=0, bytes_accessed=0, transcendentals=0),
+    )(value)
 
 
 def widths_of(total):
@@ -589,16 +827,29 @@
     def first(self, block):
         return [block] + [self.along(block, 0, j) for j in range(1, self.dims[0])]
 
+    def axes(self, j):
+        if len(self.dims) < 3:
+            return (0, len(self.dims) - 1)
+        return (1, 2) if j % 2 == 0 else (2, 1)
+
     def hop_one(self, block, j):
-        if len(self.dims) < 3:
-            return [block]
-        return [block] + [self.along(block, 1, s) for s in range(1, self.dims[1])]
+        axis, _ = self.axes(j)
+        return self.hop_line(block, axis) if axis else [block]
 
     def hop_two(self, blocks, j):
-        last = len(self.dims) - 1
-        if last == 0:
-            return blocks
-        return [v for b in blocks for v in self.hop_line(b, last)]
+        _, axis = self.axes(j)
+        both = jnp.concatenate(blocks, axis=0) if len(blocks) > 1 else blocks[0]
+        return self.hop_line(both, axis) if axis else [both]
+
+    def places_of(self, j):
+        one, two = self.axes(j)
+        if not one:
+            return list(range(self.plane))
+        out = []
+        for t in range(self.dims[two]):
+            for h in range(self.dims[one]):
+                out.append(self.offsets.index((h, t) if one == 1 else (t, h)))
+        return out
 
     def hop_line(self, block, axis):
         return [block] + [self.along(block, axis, s) for s in range(1, self.dims[axis])]
@@ -612,36 +863,40 @@
             for b, o in zip(blocks, self.offsets)
         ]
 
-    def back_two(self, blocks, j, turn=False):
-        if len(self.dims) == 1:
-            return [(blocks[0], [])]
-        n = self.dims[-1]
-        if len(self.dims) == 2:
-            return [(blocks[0], [self.along(blocks[s], 1, -s) for s in range(1, n)])]
-        m = self.dims[1]
-        if turn:
-            return [
-                (blocks[h * n], [self.along(blocks[h * n + t], 2, -t) for t in range(1, n)])
-                for h in range(m)
-            ]
+    def pack_of(self, j, p):
+        if len(self.dims) != 3:
+            return (p, j)
+        half = self.dims[0] // 2
+        y, x = self.offsets[p]
+        part, rest = (x, y) if j < half else (y, x)
+        return (j // half * 2 + part, rest * half + j % half)
+
+    def packs_one(self, packs):
+        if len(self.dims) != 3:
+            return [self.straight_back(packs)]
         return [
-            (blocks[t], [self.along(blocks[h * n + t], 1, -h) for h in range(1, m)])
-            for t in range(n)
+            [packs[0], self.along(packs[1], 2, -1)],
+            [packs[2], self.along(packs[3], 1, -1)],
         ]
 
-    def back_one(self, sums, j, turn=False):
-        axis = 1 if turn else 2
-        got = [self.along(v.astype(bfloat), axis, -s) for s, v in enumerate(sums) if s]
-        return [sums[0], got]
-
-    def sources(self):
-        table = [
-            [
-                self.index([(p - o) % d for p, o, d in zip(place, self.places[i], self.dims)])
-                for i in range(self.size)
-            ]
-            for place in self.places
-        ]
+    def packs_two(self, totals):
+        if len(self.dims) != 3:
+            return [[v] for v in totals]
+        out = []
+        for v, axis in zip(totals, (1, 2)):
+            rows = v.shape[0] // 2
+            out.append([v[:rows], self.along(v[rows:], axis, -1)])
+        return out
+
+    def sources(self, at_once):
+        table = []
+        for place in self.places:
+            row = []
+            for j in range(self.dims[0]):
+                for p in range(self.plane) if j in at_once else self.places_of(j):
+                    offset = (j, *self.offsets[p])
+                    row.append(self.index([(q - o) % d for q, o, d in zip(place, offset, self.dims)]))
+            table.append(row)
         return jnp.asarray(np.array(table, np.int32))[self.me()]
 
     def back_first(self, total, j):
@@ -751,12 +1006,16 @@
         return jnp.concatenate(out, axis=1)
 
 
-def after(value, *others):
-    return lax.optimization_barrier((value, *others))[0]
-
-
 def hold(values, *others):
     return [values[0]] + [tie(v, *others) for v in values[1:]]
+
+
+def visit(mark, lines, singles=()):
+    lines = [[v[0]] + [tie(x, mark) for x in v[1:]] for v in lines]
+    singles = [tie(v, mark) for v in singles]
+    mark = tie(lines[0][0], mark, *[x for v in lines for x in v[1:]], *singles)
+    lines = [[mark] + lines[0][1:]] + [[tie(v[0], mark)] + v[1:] for v in lines[1:]]
+    return mark, lines, [tie(v, mark) for v in singles]
 
 
 def add_up(values):
@@ -897,7 +1156,7 @@
         cores.spread(expert_down[0]),
     ]
     turns = chips.dims[0]
-    order = [0] + list(range(2, turns, 2)) + list(range(1, turns, 2))
+    order = [0] + list(range(1, turns, 2)) + list(range(2, turns, 2))
     all_cots = lax.all_gather(cotangent, chips.names, axis=0, tiled=True)
 
     resid = tokens.astype(single)
@@ -978,7 +1237,6 @@
     first = chips.first(payload)
     one, two = [None] * turns, [None] * turns
     two[0] = chips.straight(payload)
-    one[1] = None
 
     stack_ffn = cores.stack(ffn_in)
     stack_cot = cores.stack(cotangent)
@@ -990,21 +1248,6 @@
         grad_gate, grad_up = silu_grads(dot_t(grads, down), pre_gate, pre_up)
         return hidden, grad_gate, grad_up
 
-    def got_two(j, *others):
-        out = []
-        for own, got in back_two[j]:
-            total = own.astype(single)
-            for v in got:
-                total = total + tie(v, *others).astype(single)
-            out.append(total)
-        return out
-
-    def got_one(j, *others):
-        own, got = back_one[j]
-        for v in got:
-            own = own + tie(v, *others).astype(single)
-        return own
-
     sh_hidden, sh_gate, sh_up = feed_forward(
         stack_ffn, stack_cot, shared_gate, shared_up, shared_down
     )
@@ -1012,77 +1255,114 @@
     shared_out = cores.give_back(dot(sh_hidden, shared_down))
     shared_back = cores.give_back(sh_back)
 
-    who = jnp.concatenate([me.astype(jnp.int32).reshape(1), chips.sources()])
-    kept = None
-    back_blocks, out_blocks = [None] * turns, [None] * turns
+    at_once = order[:2]
+    who = jnp.concatenate([me.astype(jnp.int32).reshape(1), chips.sources(at_once)])
+    kept, kept_back = None, None
     sent, grads_of = [], []
 
+    def parts_of(i):
+        if i == 2:
+            return kept[5 : 5 + shards], kept_back[0]
+        return kept_back[2 + i * shards : 2 + (i + 1) * shards], kept[0]
+
     def others_part(i, waits):
-        base = 4 + ((i + 1) % 3) * shards
-        left = kept[base : base + shards]
-        right = kept[1] if i == 2 else kept[0]
+        left, right = parts_of(i)
         out = [t_dot(tie(v, *waits), right).astype(bfloat) for v in left[1:]]
         sent.append([cores.along(v, -j - 1) for j, v in enumerate(out)])
         return out[-1]
 
     def own_part(i, waits):
-        left = kept[4 + ((i + 1) % 3) * shards]
-        right = kept[1] if i == 2 else kept[0]
+        left, right = parts_of(i)
         got = [tie(v, *waits).astype(single) for v in sent[i]]
-        grads_of.append(sum(got, t_dot(tie(left, *waits), right)))
+        grads_of.append(sum(got, t_dot(tie(left[0], *waits), right)))
         return grads_of[-1]
 
     fillers = [
         lambda waits: others_part(1, [others_part(0, waits)]),
-        lambda waits: own_part(0, [others_part(2, waits)]),
-        lambda waits: own_part(2, [own_part(1, waits)]),
+        lambda waits: others_part(2, waits),
+        lambda waits: own_part(1, [own_part(0, waits)]),
     ]
     mark = sh_back
     backs = [None] * turns
-    for step in range(turns + 2):
-        waits = []
+
+    def places_of(j):
+        return list(range(chips.plane)) if j in at_once else chips.places_of(j)
+
+    def forward_step(step):
+        nonlocal kept, mark
+        waits = [mark]
         if step + 1 < turns:
             k = order[step + 1]
-            if step == 0:
+            if k in at_once:
                 first[k] = tie(first[k], mark)
                 two[k] = chips.straight(first[k])
                 waits.append(first[k])
             else:
                 one[k] = hold(one[k], mark)
                 two[k] = chips.hop_two(one[k], k)
-                waits += one[k]
+                waits.append(one[k][0])
         if step + 2 < turns:
             k = order[step + 2]
             first[k] = tie(first[k], mark)
             one[k] = chips.hop_one(first[k], k)
             waits.append(first[k])
+        j = order[step]
+        mark, kept = run_experts(
+            who,
+            two[j],
+            expert_weights,
+            capacity,
+            experts_all,
+            j,
+            turns,
+            [chips.pack_of(j, p) for p in places_of(j)],
+            kept,
+            waits,
+        )
+
+    def backward_step(step):
+        nonlocal kept_back, mark
+        waits = [mark]
         if 2 <= step:
-            k = order[step - 2]
+            k = step - 2
             total = add_up(hold(backs[k], mark))
             backs[k] = chips.back_first(total, k)
             waits.append(total)
         if step >= turns:
             mark = fillers[step - turns](waits)
-            continue
-        j = order[step]
-        back_blocks[j], out_blocks[j], kept = run_experts(
+            return
+        j = step
+        back_blocks, kept_back = run_experts_back(
             who,
             two[j],
             all_cots,
             expert_weights,
+            kept[2:5],
             capacity,
             experts_all,
             j,
             turns,
-            kept,
+            True,
+            kept_back,
             waits,
         )
-        backs[j] = chips.straight_back(back_blocks[j])
-        mark = back_blocks[j][0]
+        places = places_of(j)
+        back_blocks = [back_blocks[places.index(p)] for p in range(chips.plane)]
+        backs[j] = chips.straight_back(back_blocks)
+        mark = back_blocks[0]
+
+    ahead = min(3, turns)
+    for step in range(ahead):
+        forward_step(step)
+    for step in range(turns + 2):
+        backward_step(step)
+        if step + ahead < turns:
+            forward_step(step + ahead)
+    out_packs = kept[5 + shards :]
     routed_back = backs[0].astype(single)
     for j in order[1:]:
         routed_back = routed_back + tie(backs[j], mark).astype(single)
-    chip_ffn, chip_cot = kept[2:4]
+    chip_ffn, chip_cot = kept[1], kept_back[1]
 
     grad_out = cotangent.astype(single)
     grad_weights = (
@@ -1104,14 +1384,12 @@
     grad_mid = grad_mid + grad_out
 
     grad_attn_out = grad_mid.astype(bfloat)
-    heads_line = chips.stack_one(cores.stack(grad_attn_out))
-    lefts = cores.swap_columns(attn_in, query_in, tie(attn_heads, mark))
-    lefts = chips.swap_columns(*[tie(v, grad_attn_out) for v in lefts])
-    mark = fillers[2]([grad_attn_out, heads_line[0][0]])
-    grad_egate = grads_of[0].T[None]
-    grad_eup = grads_of[1].T[None]
-    grad_edown = grads_of[2][None]
-    grad_heads = cores.times_rows_t(tie(grad_attn_out, mark), out_pieces).astype(bfloat)
+    heads_line = chips.stack_one(grad_attn_out)
+    lefts = cores.swap_columns(attn_in, query_in, tie(attn_heads, sh_back))
+    lefts = chips.swap_columns(*[tie(v, mark) for v in lefts])
+    sent[:] = [[tie(v, grad_attn_out) for v in line] for line in sent]
+    grad_attn_out = tie(grad_attn_out, *[v for line in sent for v in line])
+    grad_heads = cores.times_rows_t(grad_attn_out, out_pieces).astype(bfloat)
     heads_line = chips.stack_two(heads_line, grad_heads)
     grad_query, kvb_parts, key_terms, rope_terms = run_heads_back(
         grad_heads,
@@ -1125,7 +1403,12 @@
         score_scale,
         [v[0] for v in heads_line],
     )
-    query_line = chips.stack_one(cores.stack(grad_query))
+    heads_line = [hold(v, grad_query) for v in heads_line]
+    lefts = hold(lefts, grad_query)
+    there = [v for line in [*heads_line, lefts] for v in line[1:]]
+    grad_query = tie(grad_query, *there)
+    heads_all = [cores.spread(v) for v in chips.stack_done(heads_line, grad_query)]
+    query_line = chips.stack_one(grad_query)
     kvb_terms = add_up(
         [kvb_parts[0]] + [cores.along(v, -j - 1) for j, v in enumerate(kvb_parts[1:])]
     )
@@ -1157,22 +1440,24 @@
         return shared_grads[0]
 
     low_wide = jnp.pad(grad_low, ((0, 0), (0, -grad_low.shape[1] % 128)))
-    low_line = chips.straight(cores.stack(low_wide))
-    query_line = chips.stack_two(query_line, grad_low)
-    lefts = jnp.concatenate(hold(lefts, grad_low), axis=0)
+    low_line = chips.straight(low_wide)
+    mark = fillers[2]([grad_low, kvb_line[0], *[v[0] for v in query_line]])
+    query_line = chips.stack_two(query_line, mark)
     sizes = [v.shape[1] // (shards * chips.plane) for v in (attn_in, query_in, attn_heads)]
-    left_in, left_query, left_heads = split(lefts, sizes)
-    heads_all = chips.stack_done(heads_line, grad_low)
-    out_part = [t_dot(left_heads, right).astype(bfloat) for right in heads_all]
-    kvb_part = add_up(hold(kvb_line, out_part[0]))
-    fold = left_heads.shape[1] // kvb_part.shape[0]
-    kvb_cols = kvb_part.shape[1] // fold
-    kvb_part = jnp.concatenate(split(kvb_part, [kvb_cols] * fold), axis=0)
-    part = jnp.concatenate([kvb_part, *out_part], axis=1)
+    kvb_line = hold(kvb_line, mark)
+    part = plane_dot(
+        lefts, sizes[0] + sizes[1], sizes[2], heads_all, [v[0].shape[1] for v in heads_all]
+    )
     part_sums = lax.psum_scatter(part, chips.names[0], scatter_dimension=0, tiled=True)
-    mark = shared_step([part, low_line[0]] + [v[0] for v in query_line])
-    part_all = lax.all_gather(tie(part_sums, mark), chips.names[0], axis=0, tiled=True)
-    grad_low = tie(grad_low, mark)
+    kvb_part = add_up(kvb_line)
+    mark = shared_step([part, low_line[0], kvb_part] + [v[0] for v in query_line])
+    mark, lines, (part_sums,) = visit(
+        mark, [low_line, *query_line], [part_sums]
+    )
+    low_line, *query_line = lines
+    part_all = lax.all_gather(part_sums, chips.names, axis=0, tiled=True)
+    mark = tie(grad_low, mark)
+    grad_low = mark
     grad_attn_in = in_order(
         [
             dot_t(grad_low[:, :query_rank], qa) + dot_t(grad_low[:, query_rank:], kva)
@@ -1190,63 +1475,62 @@
         [grad_gattn[None], grad_gffn[None], mixed[None], grad_router], axis=0
     )
     small_line = chips.send_rows(cores.scatter(small, 1).T.astype(bfloat))
-    query_all = chips.stack_done(query_line, mark)
-    query_part = jnp.concatenate(
-        [t_dot(left_query, right).astype(bfloat) for right in query_all], axis=1
+    query_all = [cores.spread(v) for v in chips.stack_done(query_line, mark)]
+    query_part = plane_dot(
+        lefts, sizes[0], sizes[1], query_all, [v[0].shape[1] for v in query_all]
     )
     query_sums = lax.psum_scatter(query_part, chips.names[0], scatter_dimension=0, tiled=True)
-    low_all = jnp.concatenate(hold(low_line, mark), axis=0)
-    low_part = t_dot(left_in, low_all).astype(bfloat)
+    low_all = cores.spread(jnp.concatenate(low_line, axis=0))
     small_part = add_up(hold(small_line, query_part))
     low_cols = grad_low.shape[1]
-    spare = low_part.shape[1] - low_cols - small_part.shape[1]
-    low_part = jnp.concatenate(
-        [low_part[:, :low_cols], jnp.pad(small_part, ((0, 0), (0, spare)))], axis=1
+    spare = low_wide.shape[1] - low_cols - small_part.shape[1]
+    fold = sizes[2] // kvb_part.shape[0]
+    kvb_cols = kvb_part.shape[1] // fold
+    small_wide = jnp.pad(small_part, ((0, 0), (0, spare)))
+    low_part = plane_dot(
+        lefts, 0, sizes[0], [low_all], [low_cols], fold, (kvb_part, small_wide)
     )
     low_line = chips.line_send(low_part)
-    turn_of = [j % 2 == 1 for j in range(turns)]
-    back_two = [
-        chips.back_two([tie(v, mark) for v in out_blocks[j]], j, turn_of[j])
-        for j in range(turns)
+    out_lines = chips.packs_one([tie(v, small_part) for v in out_packs])
+    mark = shared_step([query_part, low_line[0]])
+    mark, lines, (query_sums,) = visit(mark, [low_line, *out_lines], [query_sums])
+    low_line, *out_lines = lines
+    query_all = lax.all_gather(query_sums, chips.names, axis=0, tiled=True)
+    low_line = chips.hop_line(add_up(low_line), 0)
+    out_lines = chips.packs_two([add_up(v) for v in out_lines])
+    waits = [v[0] for v in out_lines]
+    mark = shared_step(waits + [low_line[0]])
+    mark, lines, (part_all,) = visit(mark, [low_line, *out_lines], [part_all])
+    low_line, *out_lines = lines
+    low_all = in_order(low_line, chips.own(0), 0)
+    low_line = chips.gather_one(chips.halves(low_all))
+    totals = jnp.concatenate([add_up(v) for v in out_lines], axis=0)
+    back_sums = [
+        chips.back_first(totals[j * tok_rows : (j + 1) * tok_rows], j) for j in range(turns)
     ]
-    mark = shared_step([query_part, low_line[0]])
-    part_line = chips.gather_one(chips.halves(tie(part_all, mark)))
-    query_all = lax.all_gather(tie(query_sums, mark), chips.names[0], axis=0, tiled=True)
-    low_line = chips.hop_line(add_up(hold(low_line, mark)), 0)
-    back_one = [chips.back_one(got_two(j, mark), j, turn_of[j]) for j in range(turns)]
-    waits = [v[0] for v in part_line] + [v[0] for v in back_one]
-    mark = shared_step(waits + [low_line[0]])
-    low_all = in_order(hold(low_line, mark), chips.own(0), 0)
-    low_line = chips.gather_one(chips.halves(low_all))
-    query_line = chips.gather_one(chips.halves(tie(query_all, mark)))
-    part_line = chips.gather_two(part_line, mark)
-    back_sums = [chips.back_first(got_one(j, mark), j) for j in range(turns)]
-    waits = [v[0] for line in (part_line, query_line, low_line) for v in line]
-    mark = shared_step(waits + back_sums)
+    mark = shared_step([v[0] for v in low_line] + back_sums[:1])
+    mark, low_line, back_sums[1:] = visit(mark, low_line, back_sums[1:])
     low_line = chips.gather_two(low_line, mark)
-    query_line = chips.gather_two(query_line, mark)
-    routed_out = back_sums[0]
+    routed_out = back_sums[0].astype(single)
     for j in range(1, turns):
         routed_out = routed_out + tie(back_sums[j], mark).astype(single)
     result = mid + shared_out + routed_out
-    cuts = [kvb_cols, w_out.shape[1]]
-    low_cuts = [query_rank, low_cols - query_rank, small_part.shape[1] + spare]
+    mark = own_part(2, [mark])
+    grad_egate = grads_of[0].T[None]
+    grad_eup = grads_of[1].T[None]
+    grad_edown = grads_of[2][None]
+    grad_wout = in_rows(chips, tie(part_all, result))
+    grad_wqb = in_rows(chips, tie(query_all, grad_wout))
+    low_cuts = [kvb_cols, query_rank, low_cols - query_rank, small_part.shape[1] + spare]
     if len(chips.dims) == 3:
-        part_line = [hold(v, mark) for v in part_line]
-        grad_wkvb, grad_wout = assemble(chips, part_line, cuts, fold, ())
-        low_line = [hold(v, grad_wout, result) for v in low_line]
-        grad_wqa, grad_wkva, small = assemble(chips, low_line, low_cuts, 1, (1,))
+        low_line = [hold(v, grad_wqb, mark) for v in low_line]
+        grad_wkvb, grad_wqa, grad_wkva, small = assemble(chips, low_line, low_cuts, fold, (2,))
         grad_wkva = grad_wkva.T
-        query_line = [hold(v, grad_wqa) for v in query_line]
-        (grad_wqb,) = assemble(chips, query_line, [w_qb.shape[1]], 1, ())
     else:
-        part_all = chips.gather_done(part_line, mark).astype(single)
-        kvb_all, grad_wout = split(part_all, cuts)
+        low_all = chips.gather_done(low_line, mark).astype(single)
+        kvb_all, grad_wqa, grad_wkva, small = split(low_all, low_cuts)
         kvb_all = kvb_all.reshape(chips.plane, fold, -1, kvb_cols)
         grad_wkvb = kvb_all.swapaxes(1, 2).reshape(-1, fold * kvb_cols)
-        low_all = chips.gather_done(low_line, mark).astype(single)
-        grad_wqa, grad_wkva, small = split(low_all, low_cuts)
-        grad_wqb = chips.gather_done(query_line, mark).astype(single)
 
     if shards == 2:
         grad_sgate, grad_sup, grad_sdown = shared_grads

time: 1110 us -> 942 us (0.85)
  waiting for transfers between devices: 272 us -> 141 us
  starting transfers between devices: 116 us -> 87.7 us
  Pallas kernels: 369 us -> 397 us
  matrix products: 133 us -> 111 us
  other arithmetic: 101 us -> 82.8 us
    ppermute x53 -> x35, waiting for transfers between devices: 202 us -> 109 us  [along(): lax.ppermute(value, self.names[axis], [(i, (i + by) % n) for i in range(n)])]
    ppermute x30, waiting for transfers between devices: 65.8 us -> 23 us  [offset_by(): return lax.ppermute(value, self.names, out)]
    pallas_call x4 -> x13, Pallas kernels: 105 us -> 147 us  [the longest x4 68.4 us: run_experts_back(): pl.pallas_call(functools.partial(expert_back_kernel, len(blocks), len(res...]
    ppermute x53 -> x35, starting transfers between devices: 78 us -> 46.8 us  [along(): lax.ppermute(value, self.names[axis], [(i, (i + by) % n) for i in range(n)])]
    dot_general x11 -> x6, matrix products: 65.9 us -> 47.9 us  [t_dot(): lax.dot_general(left, right, (((0,), (0,)), ((), ())), preferred_element_...]
    convert_element_type x8 -> x1, other arithmetic: 15.3 us -> 0.93 us  [per_device(): grad_heads = cores.times_rows_t(grad_attn_out, out_pieces).astype(bfloat)]
    pallas_call x3 -> x1, Pallas kernels: 23.8 us -> 9.68 us  [assemble(): pl.pallas_call(functools.partial(assemble_kernel, (n, m), cuts, fold), gr...]
    select_n x8 -> x4, other arithmetic: 17.9 us -> 5.02 us  [in_order(): jnp.where(own == 0, jnp.concatenate(pieces, axis=axis), jnp.concatenate([...]
  transfers between devices with their start and end apart: 115 -> 99, of which waited for: 29 -> 22; matrix products, arithmetic and copies ran while one was open for 26% -> 24% of each run, Pallas kernels for 33% -> 41%
where the time goes in v3:
time: 942 us; the launch traced here: 932 us
  Pallas kernels  397 us (42%)
  waiting for transfers between devices  141 us (15%)
  matrix products  111 us (12%)
  local copies, waits for them, and re-layouts  95.7 us (10%)
  starting transfers between devices  87.7 us (9%)
  other arithmetic  82.8 us (9%)
  between operations  16.7 us (2%)
    pallas_call x4, Pallas kernels, run_shared(): pl.pallas_call(functools.partial(shared_kernel, parts, tiles, start, widt...  210 us
    ppermute x35, waiting for transfers between devices, along(): lax.ppermute(value, self.names[axis], [(i, (i + by) % n) for i in range(n)])  109 us
    pallas_call x4, Pallas kernels, run_experts_back(): pl.pallas_call(functools.partial(expert_back_kernel, len(blocks), len(res...  68.4 us
    unnamed x438, local copies, waits for them, and re-layouts  61.8 us
    pallas_call x4, Pallas kernels, run_experts(): pl.pallas_call(functools.partial(expert_kernel, len(blocks), tok, pieces,...  54.2 us
    dot_general x6, matrix products, t_dot(): lax.dot_general(left, right, (((0,), (0,)), ((), ())), preferred_element_...  47.9 us
    ppermute x35, starting transfers between devices, along(): lax.ppermute(value, self.names[axis], [(i, (i + by) % n) for i in range(n)])  46.8 us
    ppermute x30, starting transfers between devices, offset_by(): return lax.ppermute(value, self.names, out)  34.2 us
  transfers between devices with their start and end apart: 99, of which 22 were waited for; matrix products, arithmetic and copies ran while one was open for 24% of the time, Pallas kernels for 41%

profile of v3, /device:TPU:18, one launch (start us, length us, event | category | flops | bytes accessed | tf_op | source)
XLA Modules:
  0.0 931.7 jit_solution(8572823438813420127)
XLA Ops:
  25.8 3.6 collective-permute-done.5
  34.8 3.2 convolution_add_fusion.refs_0_
  38.4 14.0 %shard_map.340 = (bf16[128,2048]{1,0:T(8,128)(2,1)S(1)}, bf16[128,2048]{1,0:T(8,128)(2,1)S(1)}, bf16[128,1024]{1,0:T(8,128)(2,1)S(1)}, bf16[128,8192]{1,0:T(8,12...) custom-call(f32[128,3072]{1,0:T(8,128)S(1)} %convolution_add_fusion.refs_0_, ...), custom_call_target="tpu_custom_call" | custom-call | tf_op jit(solution)/shard_map/pallas_call | solution.py:595
  57.5 4.0 multiply_reduce_fusion.2
  63.0 4.0 fusion.20
  73.2 5.8 fusion.31
  79.1 5.3 fusion.30
  84.4 5.2 fusion.26
  93.2 23.5 %collective-permute-done.19.refs_0_ = bf16[128,2176]{1,0:T(8,128)(2,1)} collective-permute-done((bf16[128,2176]{1,0:T(8,128)(2,1)}, bf16[128,2176]{1,0:T(8,128)(2,1)}, u32[]{:S(2)}, u32[]{:S(2)}) %collective-permute-start.19) | collective-permute-done | bytes 557088 | tf_op jit(solution)/shard_map/ppermute | solution.py:816
  120.3 3.5 collective-permute-done.18.refs_0_
  131.4 13.6 %shard_map.343 = (bf16[16,128]{1,0:T(8,128)(2,1)}, bf16[1024,2048]{1,0:T(8,128)(2,1)}, bf16[2048,2048]{1,0:T(8,128)(2,1)}, f32[1024,1408]{1,0:T(8,128)}, f32[102...) custom-call(s32[17]{0:T(128)} %pad_add_fusion.refs_0_, ...), custom_call_target="tpu_custom_call" | custom-call | tf_op jit(solution)/shard_map/pallas_call | solution.py:212
  145.0 20.0 %collective-permute-done.10.refs_0_ = bf16[128,2176]{1,0:T(8,128)(2,1)S(1)} collective-permute-done((bf16[128,2176]{1,0:T(8,128)(2,1)}, bf16[128,2176]{1,0:T(8,128)(2,1)S(1)}, u32[]{:S(2)}, u32[]{:S(2)}) %collective-permute-start.10) | collective-permute-done | bytes 557088 | tf_op jit(solution)/shard_map/ppermute | solution.py:816
  171.0 13.7 %shard_map.345 = (bf16[16,128]{1,0:T(8,128)(2,1)}, bf16[1024,2048]{1,0:T(8,128)(2,1)}, bf16[2048,2048]{1,0:T(8,128)(2,1)}, f32[1024,1408]{1,0:T(8,128)}, f32[102...) custom-call(s32[17]{0:T(128)} %pad_add_fusion.refs_0_, ...), custom_call_target="tpu_custom_call", output_to_operand_aliasing={{1}: (14, {}), {2}: (15, {}), {3}: (16, {}), {4}: (17, {}),... | custom-call | tf_op jit(solution)/shard_map/pallas_call | solution.py:212
  188.7 15.3 %collective-permute-done.26.refs_2_ = bf16[256,2176]{1,0:T(8,128)(2,1)} collective-permute-done((bf16[256,2176]{1,0:T(8,128)(2,1)S(1)}, bf16[256,2176]{1,0:T(8,128)(2,1)}, u32[]{:S(2)}, u32[]{:S(2)}) %collective-permute-start.26) | collective-permute-done | bytes 1114144 | tf_op jit(solution)/shard_map/ppermute | solution.py:816
  204.0 13.5 %shard_map.348 = (bf16[16,128]{1,0:T(8,128)(2,1)}, bf16[1024,2048]{1,0:T(8,128)(2,1)}, bf16[2048,2048]{1,0:T(8,128)(2,1)}, f32[1024,1408]{1,0:T(8,128)}, f32[102...) custom-call(s32[17]{0:T(128)} %pad_add_fusion.refs_0_, ...), custom_call_target="tpu_custom_call", output_to_operand_aliasing={{1}: (11, {}), {2}: (12, {}), {3}: (13, {}), {4}: (14, {}),... | custom-call | tf_op jit(solution)/shard_map/pallas_call | solution.py:212
  217.6 17.3 %shard_map.349 = (bf16[128,2176]{1,0:T(8,128)(2,1)}, bf16[128,2176]{1,0:T(8,128)(2,1)}, bf16[128,2176]{1,0:T(8,128)(2,1)}, bf16[128,2176]{1,0:T(8,128)(2,1)}, bf...) custom-call(s32[17]{0:T(128)} %pad_add_fusion.refs_0_, ...), custom_call_target="tpu_custom_call" | custom-call | tf_op jit(solution)/shard_map/pallas_call | solution.py:356
  244.0 13.5 %shard_map.350 = (bf16[16,128]{1,0:T(8,128)(2,1)}, bf16[1024,2048]{1,0:T(8,128)(2,1)}, bf16[2048,2048]{1,0:T(8,128)(2,1)}, f32[1024,1408]{1,0:T(8,128)}, f32[102...) custom-call(s32[17]{0:T(128)} %pad_add_fusion.refs_0_, ...), custom_call_target="tpu_custom_call", output_to_operand_aliasing={{1}: (10, {}), {2}: (11, {}), {3}: (12, {}), {4}: (13, {}),... | custom-call | tf_op jit(solution)/shard_map/pallas_call | solution.py:212
  257.5 17.0 %shard_map.351 = (bf16[128,2176]{1,0:T(8,128)(2,1)}, bf16[128,2176]{1,0:T(8,128)(2,1)}, bf16[128,2176]{1,0:T(8,128)(2,1)}, bf16[128,2176]{1,0:T(8,128)(2,1)}, bf...) custom-call(s32[17]{0:T(128)} %pad_add_fusion.refs_0_, ...), custom_call_target="tpu_custom_call", output_to_operand_aliasing={{4}: (16, {}), {5}: (17, {}), {6}: (18, {}), {7}: (19, {}),... | custom-call | tf_op jit(solution)/shard_map/pallas_call | solution.py:356
  282.4 17.2 %shard_map.355 = (bf16[128,2176]{1,0:T(8,128)(2,1)}, bf16[128,2176]{1,0:T(8,128)(2,1)}, bf16[128,2176]{1,0:T(8,128)(2,1)}, bf16[128,2176]{1,0:T(8,128)(2,1)}, bf...) custom-call(s32[17]{0:T(128)} %pad_add_fusion.refs_0_, ...), custom_call_target="tpu_custom_call", output_to_operand_aliasing={{4}: (15, {}), {5}: (16, {}), {6}: (17, {}), {7}: (18, {}),... | custom-call | tf_op jit(solution)/shard_map/pallas_call | solution.py:356
  309.2 16.8 %shard_map.359 = (bf16[128,2176]{1,0:T(8,128)(2,1)}, bf16[128,2176]{1,0:T(8,128)(2,1)}, bf16[128,2176]{1,0:T(8,128)(2,1)}, bf16[128,2176]{1,0:T(8,128)(2,1)}, bf...) custom-call(s32[17]{0:T(128)} %pad_add_fusion.refs_0_, ...), custom_call_target="tpu_custom_call", output_to_operand_aliasing={{4}: (15, {}), {5}: (16, {}), {6}: (17, {}), {7}: (18, {}),... | custom-call | tf_op jit(solution)/shard_map/pallas_call | solution.py:356
  332.2 7.4 convolution_convert_fusion.2.refs_1_
  339.7 7.9 convolution_convert_fusion.1.refs_1_
  354.5 7.4 convolution_convert_fusion.refs_1_
  372.8 19.0 %collective-permute-done.41.refs_0_ = bf16[128,2176]{1,0:T(8,128)(2,1)} collective-permute-done((bf16[128,2176]{1,0:T(8,128)(2,1)}, bf16[128,2176]{1,0:T(8,128)(2,1)}, u32[]{:S(2)}, u32[]{:S(2)}) %collective-permute-start.41) | collective-permute-done | bytes 557088 | tf_op jit(solution)/shard_map/ppermute | solution.py:816
  405.3 4.0 fusion.106
  411.8 6.3 collective-permute-done.47.refs_0_
  426.3 16.3 %shard_map.378 = (bf16[128,3072]{1,0:T(8,128)(2,1)S(1)}, bf16[256,4096]{1,0:T(8,128)(2,1)S(1)}, bf16[256,4096]{1,0:T(8,128)(2,1)S(1)}, f32[256,512]{1,0:T(8,128)S(1)}, f32[256,64]{1,0:T(8,128)S(1)}) custom-call(bf16[128,2048]{1,0:T(8,128)(2,1)S(1)} %copy-done.14, bf16[256,4096]{1,0:T(8,128)(2,1)S(1)} %copy-done.11, bf16[256,4096]{1,0:T(8,128)(2,1)S(1)} %copy-done.13, ...), custom_call_target="tpu_custom_call" | custom-call | tf_op jit(solution)/shard_map/pallas_call | solution.py:619
  455.1 6.4 collective-permute-done.49.refs_0_
  468.2 4.0 fusion.108
  472.2 4.1 fusion.109
  484.9 5.3 shard_map.393.refs_7_
  494.8 9.5 %convert_add_fusion.2.refs_1_ = f32[704,2048]{1,0:T(8,128)} fusion(bf16[704,2048]{1,0:T(8,128)(2,1)} %shard_map.395, bf16[1024,704]{1,0:T(8,128)(2,1)} %shard_map.394, bf16[1024,2048]{1,0:T(8,128)(2,1)} %get-tuple-element.209), kind=kOutput, calls=%fused_computation.2 | convolution fusion | flops 2955673600 | bytes 14286848 | tf_op jit(solution)/shard_map/dot_general | solution.py:89
  508.6 9.3 %convert_add_fusion.1.refs_1_ = f32[704,2048]{1,0:T(8,128)} fusion(bf16[704,2048]{1,0:T(8,128)(2,1)} %shard_map.397, bf16[1024,704]{1,0:T(8,128)(2,1)} %shard_map.396, bf16[1024,2048]{1,0:T(8,128)(2,1)} %get-tuple-element.209), kind=kOutput, calls=%fused_computation.1 | convolution fusion | flops 2955673600 | bytes 14286848 | tf_op jit(solution)/shard_map/dot_general | solution.py:89
  523.2 18.9 %collective-permute-done.61.refs_0_ = bf16[64,4096]{1,0:T(8,128)(2,1)S(1)} collective-permute-done((bf16[64,4096]{1,0:T(8,128)(2,1)}, bf16[64,4096]{1,0:T(8,128)(2,1)S(1)}, u32[]{:S(2)}, u32[]{:S(2)}) %collective-permute-start.61) | collective-permute-done | bytes 524320 | tf_op jit(solution)/shard_map/ppermute | solution.py:825
  548.7 54.7 %shard_map.403 = (f32[2048,1408]{1,0:T(8,128)}, f32[2048,1408]{1,0:T(8,128)}, f32[1408,2048]{1,0:T(8,128)}) custom-call(bf16[2048,2048]{1,0:T(8,128)(2,1)} %shard_map.389.refs_0_, bf16[2048,2048]{1,0:T(8,128)(2,1)} %collective-permute-done.55.refs_1_, bf16[2048,2048]{1,0:T(8,128)(2,1)} %shard_map.390.refs_2_, ...), custom_call_target="tpu_custom_call" | custom-call | tf_op jit(solution)/shard_map/pallas_call | solution.py:474
  611.9 5.5 shard_map.416.refs_1_.refs_7_
  642.4 4.9 shard_map.421
  649.0 4.5 collective-permute-start.78
  654.1 54.5 %shard_map.422 = (f32[2048,1408]{1,0:T(8,128)}, f32[2048,1408]{1,0:T(8,128)}, f32[1408,2048]{1,0:T(8,128)}) custom-call(bf16[2048,2048]{1,0:T(8,128)(2,1)} %shard_map.389.refs_0_, bf16[2048,2048]{1,0:T(8,128)(2,1)} %collective-permute-done.55.refs_1_, ...), custom_call_target="tpu_custom_call", output_to_operand_aliasing={{0}: (9, {}), {1}: (10, {}), {2}: (11, {})} | custom-call | tf_op jit(solution)/shard_map/pallas_call | solution.py:474
  728.4 54.5 %shard_map.435 = (f32[2048,1408]{1,0:T(8,128)}, f32[2048,1408]{1,0:T(8,128)}, f32[1408,2048]{1,0:T(8,128)}) custom-call(bf16[2048,2048]{1,0:T(8,128)(2,1)} %shard_map.389.refs_0_, bf16[2048,2048]{1,0:T(8,128)(2,1)} %collective-permute-done.55.refs_1_, ...), custom_call_target="tpu_custom_call", output_to_operand_aliasing={{0}: (10, {}), {1}: (11, {}), {2}: (12, {})} | custom-call | tf_op jit(solution)/shard_map/pallas_call | solution.py:474
  807.9 46.2 %shard_map.445 = (f32[2048,1408]{1,0:T(8,128)}, f32[2048,1408]{1,0:T(8,128)}, f32[1408,2048]{1,0:T(8,128)}) custom-call(bf16[2048,2048]{1,0:T(8,128)(2,1)} %shard_map.389.refs_0_, bf16[2048,2048]{1,0:T(8,128)(2,1)} %collective-permute-done.55.refs_1_, ...), custom_call_target="tpu_custom_call", output_to_operand_aliasing={{0}: (10, {}), {1}: (11, {}), {2}: (12, {})} | custom-call | tf_op jit(solution)/shard_map/pallas_call | solution.py:474
  856.6 5.9 collective-permute-done.91.refs_0_
  866.7 3.8 collective-permute-start.93
  882.7 4.4 shard_map.463.refs_1_
  888.2 6.3 convert_add_fusion.refs_2_
  896.9 4.1 shard_map.465.refs_1_
  901.0 6.6 collective-permute-done.93.refs_0_
  909.3 9.7 %shard_map.472 = (f32[256,4096]{1,0:T(8,128)}, f32[1024,1536]{1,0:T(8,128)}, f32[576,1024]{1,0:T(8,128)}, f32[1024,64]{1,0:T(8,128)}) custom-call(s32[2]{0:T(128)} %pad_add_fusion.1.refs_0_, bf16[512,1536]{1,0:T(8,128)(2,1)} %maximum_select_fusion.1.refs_1_, bf16[512,1536]{1,0:T(8,128)(2,1)} %shard_map.468.refs_2_, ...), custom_call_target="tpu_custom_call" | custom-call | tf_op jit(solution)/shard_map/pallas_call | solution.py:676
  (902 shorter events, 293.5 us)
Async XLA Ops:
  7.2 210.3 %all-gather.4.cloned.1.call-start = ((), (), s32[]{:S(2)}) async-start(), calls=%async_computation.2 | async-start | bytes 8912896 | tf_op jit(solution)/shard_map/all_gather | solution.py:1160
  7.9 595.6 %reduce-scatter.3.cloned.1.call-start = ((), (), s32[]{:S(2)}) async-start(), calls=%async_computation.3 | async-start | bytes 1310720 | tf_op jit(solution)/shard_map/reduce_scatter | solution.py:1451
  8.0 54.7 %collective-permute-start.17 = (bf16[128,2048]{1,0:T(8,128)(2,1)}, bf16[128,2048]{1,0:T(8,128)(2,1)}, u32[]{:S(2)}, u32[]{:S(2)}) collective-permute-start(bf16[128,2048]{1,0:T(8,128)(2,1)} %param.24), channel_id=1, source_target_pairs={{0,1},{1,0},{2,3},{3,2},{4,5},{5,4},{6,7},{7,6},{8,9},{9,8},{10,11... | collective-permute-start | bytes 1572872 | tf_op jit(solution)/shard_map/ppermute | solution.py:1056
  34.7 55.0 %collective-permute-start.14 = (bf16[704,2048]{1,0:T(8,128)(2,1)S(1)}, bf16[704,2048]{1,0:T(8,128)(2,1)}, u32[]{:S(2)}, u32[]{:S(2)}) collective-permute-start(bf16[704,2048]{1,0:T(8,128)(2,1)S(1)} %bitcast.102), channel_id=1, source_target_pairs={{0,1},{1,0},{2,3},{3,2},{4,5},{5,4},{6,7},{7,6},{8,9},{9,8},{10,11... | collective-permute-start | bytes 8650760 | tf_op jit(solution)/shard_map/ppermute | solution.py:1056
  38.0 52.3 %collective-permute-start.15 = (bf16[704,2048]{1,0:T(8,128)(2,1)}, bf16[704,2048]{1,0:T(8,128)(2,1)}, u32[]{:S(2)}, u32[]{:S(2)}) collective-permute-start(bf16[704,2048]{1,0:T(8,128)(2,1)} %bitcast.8.refs_7_.refs_5_.refs_8_.refs_6_), channel_id=1, source_target_pairs={{0,1},{1,0},{2,3},{3,2},{4,5},{5,4},{6,7},{7,6},{8,9},{9,8},{10,11... | collective-permute-start | bytes 8650760 | tf_op jit(solution)/shard_map/ppermute | solution.py:1056
  71.0 45.7 %collective-permute-start.19 = (bf16[128,2176]{1,0:T(8,128)(2,1)}, bf16[128,2176]{1,0:T(8,128)(2,1)}, u32[]{:S(2)}, u32[]{:S(2)}) collective-permute-start(bf16[128,2176]{1,0:T(8,128)(2,1)} %concatenate.221.refs_1_), channel_id=1, source_target_pairs={{0,24},{8,0},{16,8},{24,16},{1,25},{9,1},{17,9},{25,17},{2,26},{10... | collective-permute-start | bytes 1671176 | tf_op jit(solution)/shard_map/ppermute | solution.py:816
  71.5 52.3 %collective-permute-start.18 = (bf16[128,2176]{1,0:T(8,128)(2,1)}, bf16[128,2176]{1,0:T(8,128)(2,1)}, u32[]{:S(2)}, u32[]{:S(2)}) collective-permute-start(bf16[128,2176]{1,0:T(8,128)(2,1)} %concatenate.221.refs_1_), channel_id=1, source_target_pairs={{0,8},{8,16},{16,24},{24,0},{1,9},{9,17},{17,25},{25,1},{2,10},{10... | collective-permute-start | bytes 1671176 | tf_op jit(solution)/shard_map/ppermute | solution.py:816
  116.7 48.3 %collective-permute-start.10 = (bf16[128,2176]{1,0:T(8,128)(2,1)}, bf16[128,2176]{1,0:T(8,128)(2,1)S(1)}, u32[]{:S(2)}, u32[]{:S(2)}) collective-permute-start(bf16[128,2176]{1,0:T(8,128)(2,1)} %concatenate.221.refs_1_), channel_id=1, source_target_pairs={{0,16},{8,24},{16,0},{24,8},{1,17},{9,25},{17,1},{25,9},{2,18},{10... | collective-permute-start | bytes 1671176 | tf_op jit(solution)/shard_map/ppermute | solution.py:816
  123.8 43.5 %collective-permute-start.25 = (bf16[128,2176]{1,0:T(8,128)(2,1)}, bf16[128,2176]{1,0:T(8,128)(2,1)S(1)}, u32[]{:S(2)}, u32[]{:S(2)}) collective-permute-start(bf16[128,2176]{1,0:T(8,128)(2,1)} %shard_map.342.refs_13_.refs_12_), channel_id=1, source_target_pairs={{0,2},{2,0},{1,3},{3,1},{4,6},{6,4},{5,7},{7,5},{8,10},{10,8},{9,1... | collective-permute-start | bytes 1671176 | tf_op jit(solution)/shard_map/ppermute | solution.py:816
  127.3 43.7 %collective-permute-start.21 = (bf16[128,2176]{1,0:T(8,128)(2,1)}, bf16[128,2176]{1,0:T(8,128)(2,1)}, u32[]{:S(2)}, u32[]{:S(2)}) collective-permute-start(bf16[128,2176]{1,0:T(8,128)(2,1)} %shard_map.341.refs_12_.refs_1_), channel_id=1, source_target_pairs={{0,2},{2,0},{4,6},{6,4},{8,10},{10,8},{12,14},{14,12},{16,18},{18,... | collective-permute-start | bytes 1671176 | tf_op jit(solution)/shard_map/ppermute | solution.py:825
  129.1 41.8 %collective-permute-start.22 = (bf16[128,2176]{1,0:T(8,128)(2,1)}, bf16[128,2176]{1,0:T(8,128)(2,1)}, u32[]{:S(2)}, u32[]{:S(2)}) collective-permute-start(bf16[128,2176]{1,0:T(8,128)(2,1)} %shard_map.341.refs_12_.refs_1_), channel_id=1, source_target_pairs={{0,4},{2,6},{4,0},{6,2},{8,12},{10,14},{12,8},{14,10},{16,20},{18,... | collective-permute-start | bytes 1671176 | tf_op jit(solution)/shard_map/ppermute | solution.py:825
  170.9 67.5 %collective-permute-start.50 = (bf16[128,2816]{1,0:T(8,128)(2,1)}, bf16[128,2816]{1,0:T(8,128)(2,1)}, u32[]{:S(2)}, u32[]{:S(2)}) collective-permute-start(bf16[128,2816]{1,0:T(8,128)(2,1)} %pad_maximum_fusion.11), channel_id=1, source_target_pairs={{0,1},{1,0},{2,3},{3,2},{4,5},{5,4},{6,7},{7,6},{8,9},{9,8},{10,11... | collective-permute-start | bytes 2162696 | tf_op jit(solution)/shard_map/ppermute | solution.py:1056
  187.2 56.9 %collective-permute-start.24 = (bf16[256,2176]{1,0:T(8,128)(2,1)}, bf16[256,2176]{1,0:T(8,128)(2,1)}, u32[]{:S(2)}, u32[]{:S(2)}) collective-permute-start(bf16[256,2176]{1,0:T(8,128)(2,1)} %pad_maximum_fusion.4.refs_1_), channel_id=1, source_target_pairs={{0,2},{2,0},{1,3},{3,1},{4,6},{6,4},{5,7},{7,5},{8,10},{10,8},{9,1... | collective-permute-start | bytes 3342344 | tf_op jit(solution)/shard_map/ppermute | solution.py:816
  234.9 41.8 %collective-permute-start.27 = (bf16[128,2176]{1,0:T(8,128)(2,1)}, bf16[128,2176]{1,0:T(8,128)(2,1)}, u32[]{:S(2)}, u32[]{:S(2)}) collective-permute-start(bf16[128,2176]{1,0:T(8,128)(2,1)} %get-tuple-element.172), channel_id=1, source_target_pairs={{0,2},{2,0},{4,6},{6,4},{8,10},{10,8},{12,14},{14,12},{16,18},{18,... | collective-permute-start | bytes 1671176 | tf_op jit(solution)/shard_map/ppermute | solution.py:825
  235.7 42.5 %collective-permute-start.28 = (bf16[128,2176]{1,0:T(8,128)(2,1)}, bf16[128,2176]{1,0:T(8,128)(2,1)S(1)}, u32[]{:S(2)}, u32[]{:S(2)}) collective-permute-start(bf16[128,2176]{1,0:T(8,128)(2,1)} %get-tuple-element.184), channel_id=1, source_target_pairs={{0,4},{2,6},{4,0},{6,2},{8,12},{10,14},{12,8},{14,10},{16,20},{18,... | collective-permute-start | bytes 1671176 | tf_op jit(solution)/shard_map/ppermute | solution.py:825
  237.0 42.0 %collective-permute-start.29 = (bf16[128,2176]{1,0:T(8,128)(2,1)}, bf16[128,2176]{1,0:T(8,128)(2,1)S(1)}, u32[]{:S(2)}, u32[]{:S(2)}) collective-permute-start(bf16[128,2176]{1,0:T(8,128)(2,1)} %get-tuple-element.185), channel_id=1, source_target_pairs={{0,6},{2,4},{4,2},{6,0},{8,14},{10,12},{12,10},{14,8},{16,22},{18,... | collective-permute-start | bytes 1671176 | tf_op jit(solution)/shard_map/ppermute | solution.py:825
  306.7 57.1 %collective-permute-start.33 = (bf16[128,2176]{1,0:T(8,128)(2,1)}, bf16[128,2176]{1,0:T(8,128)(2,1)}, u32[]{:S(2)}, u32[]{:S(2)}) collective-permute-start(bf16[128,2176]{1,0:T(8,128)(2,1)} %add_convert_fusion.7.refs_14_), channel_id=1, source_target_pairs={{0,24},{8,0},{16,8},{24,16},{1,25},{9,1},{17,9},{25,17},{2,26},{10... | collective-permute-start | bytes 1671176 | tf_op jit(solution)/shard_map/ppermute | solution.py:816
  339.7 64.7 %collective-permute-start.43 = (bf16[704,2048]{1,0:T(8,128)(2,1)}, bf16[704,2048]{1,0:T(8,128)(2,1)}, u32[]{:S(2)}, u32[]{:S(2)}) collective-permute-start(bf16[704,2048]{1,0:T(8,128)(2,1)} %convolution_convert_fusion.2.refs_1_), channel_id=1, source_target_pairs={{0,1},{1,0},{2,3},{3,2},{4,5},{5,4},{6,7},{7,6},{8,9},{9,8},{10,11... | collective-permute-start | bytes 8650760 | tf_op jit(solution)/shard_map/ppermute | solution.py:1056
  347.5 55.5 %collective-permute-start.44 = (bf16[704,2048]{1,0:T(8,128)(2,1)}, bf16[704,2048]{1,0:T(8,128)(2,1)}, u32[]{:S(2)}, u32[]{:S(2)}) collective-permute-start(bf16[704,2048]{1,0:T(8,128)(2,1)} %convolution_convert_fusion.1.refs_1_), channel_id=1, source_target_pairs={{0,1},{1,0},{2,3},{3,2},{4,5},{5,4},{6,7},{7,6},{8,9},{9,8},{10,11... | collective-permute-start | bytes 8650760 | tf_op jit(solution)/shard_map/ppermute | solution.py:1056
  391.8 53.9 %collective-permute-start.53 = (bf16[256,704]{1,0:T(8,128)(2,1)}, bf16[256,704]{1,0:T(8,128)(2,1)S(1)}, u32[]{:S(2)}, u32[]{:S(2)}) collective-permute-start(bf16[256,704]{1,0:T(8,128)(2,1)} %pad_maximum_fusion.20), channel_id=1, source_target_pairs={{0,6},{2,4},{4,2},{6,0},{8,14},{10,12},{12,10},{14,8},{16,22},{18,... | collective-permute-start | bytes 1081352 | tf_op jit(solution)/shard_map/ppermute | solution.py:825
  397.1 50.1 %collective-permute-start.52 = (bf16[256,704]{1,0:T(8,128)(2,1)}, bf16[256,704]{1,0:T(8,128)(2,1)S(1)}, u32[]{:S(2)}, u32[]{:S(2)}) collective-permute-start(bf16[256,704]{1,0:T(8,128)(2,1)} %pad_maximum_fusion.19), channel_id=1, source_target_pairs={{0,4},{2,6},{4,0},{6,2},{8,12},{10,14},{12,8},{14,10},{16,20},{18,... | collective-permute-start | bytes 1081352 | tf_op jit(solution)/shard_map/ppermute | solution.py:825
  402.0 46.6 %collective-permute-start.51 = (bf16[256,704]{1,0:T(8,128)(2,1)}, bf16[256,704]{1,0:T(8,128)(2,1)S(1)}, u32[]{:S(2)}, u32[]{:S(2)}) collective-permute-start(bf16[256,704]{1,0:T(8,128)(2,1)} %pad_maximum_fusion.18), channel_id=1, source_target_pairs={{0,2},{2,0},{4,6},{6,4},{8,10},{10,8},{12,14},{14,12},{16,18},{18,... | collective-permute-start | bytes 1081352 | tf_op jit(solution)/shard_map/ppermute | solution.py:825
  418.1 125.6 %collective-permute-start.56 = (bf16[2048,2048]{1,0:T(8,128)(2,1)}, bf16[2048,2048]{1,0:T(8,128)(2,1)}, u32[]{:S(2)}, u32[]{:S(2)}) collective-permute-start(bf16[2048,2048]{1,0:T(8,128)(2,1)} %shard_map.390.refs_2_), channel_id=1, source_target_pairs={{0,1},{1,0},{2,3},{3,2},{4,5},{5,4},{6,7},{7,6},{8,9},{9,8},{10,11... | collective-permute-start | bytes 25165832 | tf_op jit(solution)/shard_map/ppermute | solution.py:1056
  419.8 125.2 %collective-permute-start.55 = (bf16[2048,2048]{1,0:T(8,128)(2,1)}, bf16[2048,2048]{1,0:T(8,128)(2,1)}, u32[]{:S(2)}, u32[]{:S(2)}) collective-permute-start(bf16[2048,2048]{1,0:T(8,128)(2,1)} %shard_map.389.refs_0_), channel_id=1, source_target_pairs={{0,1},{1,0},{2,3},{3,2},{4,5},{5,4},{6,7},{7,6},{8,9},{9,8},{10,11... | collective-permute-start | bytes 25165832 | tf_op jit(solution)/shard_map/ppermute | solution.py:1056
  449.6 40.9 %collective-permute-start.59 = (bf16[256,4096]{1,0:T(8,128)(2,1)}, bf16[256,4096]{1,0:T(8,128)(2,1)}, u32[]{:S(2)}, u32[]{:S(2)}) collective-permute-start(bf16[256,4096]{1,0:T(8,128)(2,1)} %copy-done.33), channel_id=1, source_target_pairs={{0,1},{1,0},{2,3},{3,2},{4,5},{5,4},{6,7},{7,6},{8,9},{9,8},{10,11... | collective-permute-start | bytes 6291464 | tf_op jit(solution)/shard_map/ppermute | solution.py:1056
  490.2 220.7 %reduce-scatter.5.cloned.1.call-start = ((), (), s32[]{:S(2)}) async-start(), calls=%async_computation.4 | async-start | bytes 1474560 | tf_op jit(solution)/shard_map/reduce_scatter | solution.py:1482
  522.0 82.3 %collective-permute-start.67 = (bf16[128,2176]{1,0:T(8,128)(2,1)S(1)}, bf16[128,2176]{1,0:T(8,128)(2,1)}, u32[]{:S(2)}, u32[]{:S(2)}) collective-permute-start(bf16[128,2176]{1,0:T(8,128)(2,1)S(1)} %copy-done.46), channel_id=1, source_target_pairs={{0,6},{2,4},{4,2},{6,0},{8,14},{10,12},{12,10},{14,8},{16,22},{18,... | collective-permute-start | bytes 1671176 | tf_op jit(solution)/shard_map/ppermute | solution.py:825
  542.1 62.3 %collective-permute-start.66 = (bf16[128,2176]{1,0:T(8,128)(2,1)S(1)}, bf16[128,2176]{1,0:T(8,128)(2,1)}, u32[]{:S(2)}, u32[]{:S(2)}) collective-permute-start(bf16[128,2176]{1,0:T(8,128)(2,1)S(1)} %copy-done.46), channel_id=1, source_target_pairs={{0,4},{2,6},{4,0},{6,2},{8,12},{10,14},{12,8},{14,10},{16,20},{18,... | collective-permute-start | bytes 1671176 | tf_op jit(solution)/shard_map/ppermute | solution.py:825
  542.9 61.5 %collective-permute-start.65 = (bf16[128,2176]{1,0:T(8,128)(2,1)S(1)}, bf16[128,2176]{1,0:T(8,128)(2,1)}, u32[]{:S(2)}, u32[]{:S(2)}) collective-permute-start(bf16[128,2176]{1,0:T(8,128)(2,1)S(1)} %copy-done.46), channel_id=1, source_target_pairs={{0,2},{2,0},{4,6},{6,4},{8,10},{10,8},{12,14},{14,12},{16,18},{18,... | collective-permute-start | bytes 1671176 | tf_op jit(solution)/shard_map/ppermute | solution.py:825
  543.7 59.8 %collective-permute-start.69 = (bf16[256,1536]{1,0:T(8,128)(2,1)}, bf16[256,1536]{1,0:T(8,128)(2,1)S(1)}, u32[]{:S(2)}, u32[]{:S(2)}) collective-permute-start(bf16[256,1536]{1,0:T(8,128)(2,1)} %pad_maximum_fusion.10.refs_11_.refs_0_), channel_id=1, source_target_pairs={{0,2},{2,0},{1,3},{3,1},{4,6},{6,4},{5,7},{7,5},{8,10},{10,8},{9,1... | collective-permute-start | bytes 2359304 | tf_op jit(solution)/shard_map/ppermute | solution.py:816
  545.0 59.4 %collective-permute-start.68 = (bf16[256,1536]{1,0:T(8,128)(2,1)}, bf16[256,1536]{1,0:T(8,128)(2,1)}, u32[]{:S(2)}, u32[]{:S(2)}) collective-permute-start(bf16[256,1536]{1,0:T(8,128)(2,1)} %pad_maximum_fusion.9.refs_10_.refs_0_), channel_id=1, source_target_pairs={{0,4},{4,0},{1,5},{5,1},{2,6},{6,2},{3,7},{7,3},{8,12},{12,8},{9,1... | collective-permute-start | bytes 2359304 | tf_op jit(solution)/shard_map/ppermute | solution.py:816
  617.4 173.8 %all-gather.6.cloned.1.call-start = ((), (), s32[]{:S(2)}) async-start(), calls=%async_computation.5 | async-start | bytes 4456448 | tf_op jit(solution)/shard_map/all_gather | solution.py:1458
  619.2 275.3 %all-gather.8.cloned.1.call-start = ((), (), s32[]{:S(2)}) async-start(), calls=%async_computation.6 | async-start | bytes 5013504 | tf_op jit(solution)/shard_map/all_gather | solution.py:1498
  639.8 71.0 %collective-permute-start.80 = (bf16[512,2048]{1,0:T(8,128)(2,1)}, bf16[512,2048]{1,0:T(8,128)(2,1)}, u32[]{:S(2)}, u32[]{:S(2)}) collective-permute-start(bf16[512,2048]{1,0:T(8,128)(2,1)} %shard_map.426), channel_id=1, source_target_pairs={{0,2},{2,0},{1,3},{3,1},{4,6},{6,4},{5,7},{7,5},{8,10},{10,8},{9,1... | collective-permute-start | bytes 6291464 | tf_op jit(solution)/shard_map/ppermute | solution.py:816
  641.1 69.8 %collective-permute-start.81 = (bf16[512,2048]{1,0:T(8,128)(2,1)}, bf16[512,2048]{1,0:T(8,128)(2,1)}, u32[]{:S(2)}, u32[]{:S(2)}) collective-permute-start(bf16[512,2048]{1,0:T(8,128)(2,1)} %shard_map.428), channel_id=1, source_target_pairs={{0,4},{4,0},{1,5},{5,1},{2,6},{6,2},{3,7},{7,3},{8,12},{12,8},{9,1... | collective-permute-start | bytes 6291464 | tf_op jit(solution)/shard_map/ppermute | solution.py:816
  648.2 60.4 %collective-permute-start.79 = (bf16[64,3200]{1,0:T(8,128)(2,1)S(1)}, bf16[64,3200]{1,0:T(8,128)(2,1)S(1)}, u32[]{:S(2)}, u32[]{:S(2)}) collective-permute-start(bf16[64,3200]{1,0:T(8,128)(2,1)S(1)} %get-tuple-element.359), channel_id=1, source_target_pairs={{0,24},{8,0},{16,8},{24,16},{1,25},{9,1},{17,9},{25,17},{2,26},{10... | collective-permute-start | bytes 1228808 | tf_op jit(solution)/shard_map/ppermute | solution.py:816
  649.0 60.3 %collective-permute-start.78 = (bf16[64,3200]{1,0:T(8,128)(2,1)S(1)}, bf16[64,3200]{1,0:T(8,128)(2,1)S(1)}, u32[]{:S(2)}, u32[]{:S(2)}) collective-permute-start(bf16[64,3200]{1,0:T(8,128)(2,1)S(1)} %get-tuple-element.360), channel_id=1, source_target_pairs={{0,16},{8,24},{16,0},{24,8},{1,17},{9,25},{17,1},{25,9},{2,18},{10... | collective-permute-start | bytes 1228808 | tf_op jit(solution)/shard_map/ppermute | solution.py:816
  653.5 56.6 %collective-permute-start.77 = (bf16[64,3200]{1,0:T(8,128)(2,1)S(1)}, bf16[64,3200]{1,0:T(8,128)(2,1)S(1)}, u32[]{:S(2)}, u32[]{:S(2)}) collective-permute-start(bf16[64,3200]{1,0:T(8,128)(2,1)S(1)} %get-tuple-element.361), channel_id=1, source_target_pairs={{0,8},{8,16},{16,24},{24,0},{1,9},{9,17},{17,25},{25,1},{2,10},{10... | collective-permute-start | bytes 1228808 | tf_op jit(solution)/shard_map/ppermute | solution.py:816
  713.4 69.6 %collective-permute-start.84 = (bf16[64,3200]{1,0:T(8,128)(2,1)S(1)}, bf16[64,3200]{1,0:T(8,128)(2,1)}, u32[]{:S(2)}, u32[]{:S(2)}) collective-permute-start(bf16[64,3200]{1,0:T(8,128)(2,1)S(1)} %add_convert_fusion.10.refs_9_.refs_0_), channel_id=1, source_target_pairs={{0,24},{8,0},{16,8},{24,16},{1,25},{9,1},{17,9},{25,17},{2,26},{10... | collective-permute-start | bytes 1228808 | tf_op jit(solution)/shard_map/ppermute | solution.py:816
  715.5 69.3 %collective-permute-start.83 = (bf16[64,3200]{1,0:T(8,128)(2,1)S(1)}, bf16[64,3200]{1,0:T(8,128)(2,1)S(1)}, u32[]{:S(2)}, u32[]{:S(2)}) collective-permute-start(bf16[64,3200]{1,0:T(8,128)(2,1)S(1)} %add_convert_fusion.10.refs_9_.refs_0_), channel_id=1, source_target_pairs={{0,16},{8,24},{16,0},{24,8},{1,17},{9,25},{17,1},{25,9},{2,18},{10... | collective-permute-start | bytes 1228808 | tf_op jit(solution)/shard_map/ppermute | solution.py:816
  717.3 68.3 %collective-permute-start.82 = (bf16[64,3200]{1,0:T(8,128)(2,1)S(1)}, bf16[64,3200]{1,0:T(8,128)(2,1)S(1)}, u32[]{:S(2)}, u32[]{:S(2)}) collective-permute-start(bf16[64,3200]{1,0:T(8,128)(2,1)S(1)} %add_convert_fusion.10.refs_9_.refs_0_), channel_id=1, source_target_pairs={{0,8},{8,16},{16,24},{24,0},{1,9},{9,17},{17,25},{25,1},{2,10},{10... | collective-permute-start | bytes 1228808 | tf_op jit(solution)/shard_map/ppermute | solution.py:816
  722.7 66.5 %collective-permute-start.85 = (bf16[256,2048]{1,0:T(8,128)(2,1)}, bf16[256,2048]{1,0:T(8,128)(2,1)S(1)}, u32[]{:S(2)}, u32[]{:S(2)}) collective-permute-start(bf16[256,2048]{1,0:T(8,128)(2,1)} %get-tuple-element.351), channel_id=1, source_target_pairs={{0,4},{4,0},{1,5},{5,1},{2,6},{6,2},{3,7},{7,3},{8,12},{12,8},{9,1... | collective-permute-start | bytes 3145736 | tf_op jit(solution)/shard_map/ppermute | solution.py:816
  727.5 62.7 %collective-permute-start.86 = (bf16[256,2048]{1,0:T(8,128)(2,1)}, bf16[256,2048]{1,0:T(8,128)(2,1)S(1)}, u32[]{:S(2)}, u32[]{:S(2)}) collective-permute-start(bf16[256,2048]{1,0:T(8,128)(2,1)} %get-tuple-element.354), channel_id=1, source_target_pairs={{0,2},{2,0},{1,3},{3,1},{4,6},{6,4},{5,7},{7,5},{8,10},{10,8},{9,1... | collective-permute-start | bytes 3145736 | tf_op jit(solution)/shard_map/ppermute | solution.py:816
  795.1 59.1 %collective-permute-start.90 = (bf16[128,2048]{1,0:T(8,128)(2,1)S(1)}, bf16[128,2048]{1,0:T(8,128)(2,1)S(1)}, u32[]{:S(2)}, u32[]{:S(2)}) collective-permute-start(bf16[128,2048]{1,0:T(8,128)(2,1)S(1)} %get-tuple-element.363), channel_id=1, source_target_pairs={{0,16},{8,24},{16,0},{24,8},{1,17},{9,25},{17,1},{25,9},{2,18},{10... | collective-permute-start | bytes 1572872 | tf_op jit(solution)/shard_map/ppermute | solution.py:816
  797.8 58.0 %collective-permute-start.87 = (bf16[128,2048]{1,0:T(8,128)(2,1)}, bf16[128,2048]{1,0:T(8,128)(2,1)S(1)}, u32[]{:S(2)}, u32[]{:S(2)}) collective-permute-start(bf16[128,2048]{1,0:T(8,128)(2,1)} %get-tuple-element.365), channel_id=1, source_target_pairs={{0,24},{8,0},{16,8},{24,16},{1,25},{9,1},{17,9},{25,17},{2,26},{10... | collective-permute-start | bytes 1572872 | tf_op jit(solution)/shard_map/ppermute | solution.py:816
  801.9 60.6 %collective-permute-start.89 = (bf16[256,1664]{1,0:T(8,128)(2,1)S(1)}, bf16[256,1664]{1,0:T(8,128)(2,1)S(1)}, u32[]{:S(2)}, u32[]{:S(2)}) collective-permute-start(bf16[256,1664]{1,0:T(8,128)(2,1)S(1)} %dynamic-slice.14.refs_8_.refs_0_), channel_id=1, source_target_pairs={{0,4},{4,0},{1,5},{5,1},{2,6},{6,2},{3,7},{7,3},{8,12},{12,8},{9,1... | collective-permute-start | bytes 2555912 | tf_op jit(solution)/shard_map/ppermute | solution.py:816
  803.2 59.3 %collective-permute-start.88 = (bf16[256,1536]{1,0:T(8,128)(2,1)S(1)}, bf16[256,1536]{1,0:T(8,128)(2,1)}, u32[]{:S(2)}, u32[]{:S(2)}) collective-permute-start(bf16[256,1536]{1,0:T(8,128)(2,1)S(1)} %constant_dynamic-slice_fusion.13.refs_7_.refs_0_), channel_id=1, source_target_pairs={{0,2},{2,0},{1,3},{3,1},{4,6},{6,4},{5,7},{7,5},{8,10},{10,8},{9,1... | collective-permute-start | bytes 2359304 | tf_op jit(solution)/shard_map/ppermute | solution.py:816
  804.3 58.2 %collective-permute-start.91 = (bf16[128,2048]{1,0:T(8,128)(2,1)}, bf16[128,2048]{1,0:T(8,128)(2,1)}, u32[]{:S(2)}, u32[]{:S(2)}) collective-permute-start(bf16[128,2048]{1,0:T(8,128)(2,1)} %get-tuple-element.364), channel_id=1, source_target_pairs={{0,8},{8,16},{16,24},{24,0},{1,9},{9,17},{17,25},{25,1},{2,10},{10... | collective-permute-start | bytes 1572872 | tf_op jit(solution)/shard_map/ppermute | solution.py:816
  (265 other events, 2104.2 us)
Sparse Core Ops, SparseCore 0:
  10.8 153.8 all-gather.3
  490.3 26.7 reduce-scatter.2
  617.5 29.6 reduce-scatter.4
  650.3 115.2 all-gather.5
  768.6 112.1 all-gather.7

commit v4 on v3

--- a/solution.py
+++ b/solution.py
@@ -1157,6 +1157,7 @@
     ]
     turns = chips.dims[0]
     order = [0] + list(range(1, turns, 2)) + list(range(2, turns, 2))
+    order_back = [0] + list(range(2, turns, 2)) + list(range(1, turns, 2))
     all_cots = lax.all_gather(cotangent, chips.names, axis=0, tiled=True)
 
     resid = tokens.astype(single)
@@ -1324,14 +1325,14 @@
         nonlocal kept_back, mark
         waits = [mark]
         if 2 <= step:
-            k = step - 2
+            k = order_back[step - 2]
             total = add_up(hold(backs[k], mark))
             backs[k] = chips.back_first(total, k)
             waits.append(total)
         if step >= turns:
             mark = fillers[step - turns](waits)
             return
-        j = step
+        j = order_back[step]
         back_blocks, kept_back = run_experts_back(
             who,
             two[j],
@@ -1351,13 +1352,14 @@
         backs[j] = chips.straight_back(back_blocks)
         mark = back_blocks[0]
 
-    ahead = min(3, turns)
+    ahead = min(2, turns)
     for step in range(ahead):
         forward_step(step)
-    for step in range(turns + 2):
+    backward_step(0)
+    for step in range(ahead, turns):
+        forward_step(step)
+    for step in range(1, turns + 2):
         backward_step(step)
-        if step + ahead < turns:
-            forward_step(step + ahead)
     out_packs = kept[5 + shards :]
     routed_back = backs[0].astype(single)
     for j in order[1:]:
@@ -1412,7 +1414,7 @@
     kvb_terms = add_up(
         [kvb_parts[0]] + [cores.along(v, -j - 1) for j, v in enumerate(kvb_parts[1:])]
     )
-    kvb_line = chips.send_rows(kvb_terms)
+    kvb_part = lax.psum_scatter(kvb_terms, chips.names[1:], scatter_dimension=0, tiled=True)
     size = KR // shards
     key_terms = in_order(
         [key_terms[:, j * size : (j + 1) * size] for j in range(shards)], shard_pos, 1
@@ -1441,18 +1443,16 @@
 
     low_wide = jnp.pad(grad_low, ((0, 0), (0, -grad_low.shape[1] % 128)))
     low_line = chips.straight(low_wide)
-    mark = fillers[2]([grad_low, kvb_line[0], *[v[0] for v in query_line]])
+    mark = fillers[2]([grad_low, kvb_terms, *[v[0] for v in query_line]])
     query_line = chips.stack_two(query_line, mark)
     sizes = [v.shape[1] // (shards * chips.plane) for v in (attn_in, query_in, attn_heads)]
-    kvb_line = hold(kvb_line, mark)
     part = plane_dot(
         lefts, sizes[0] + sizes[1], sizes[2], heads_all, [v[0].shape[1] for v in heads_all]
     )
     part_sums = lax.psum_scatter(part, chips.names[0], scatter_dimension=0, tiled=True)
-    kvb_part = add_up(kvb_line)
-    mark = shared_step([part, low_line[0], kvb_part] + [v[0] for v in query_line])
-    mark, lines, (part_sums,) = visit(
-        mark, [low_line, *query_line], [part_sums]
+    mark = shared_step([part, low_line[0]] + [v[0] for v in query_line])
+    mark, lines, (part_sums, kvb_part) = visit(
+        mark, [low_line, *query_line], [part_sums, kvb_part]
     )
     low_line, *query_line = lines
     part_all = lax.all_gather(part_sums, chips.names, axis=0, tiled=True)

time: 942 us -> 913 us (0.969)
  waiting for transfers between devices: 141 us -> 107 us
    ppermute x35, waiting for transfers between devices: 109 us -> 90.1 us  [along(): lax.ppermute(value, self.names[axis], [(i, (i + by) % n) for i in range(n)])]
    ppermute x30 -> x27, waiting for transfers between devices: 23 us -> 6.33 us  [offset_by(): return lax.ppermute(value, self.names, out)]
    unnamed x438 -> x450, local copies, waits for them, and re-layouts: 61.8 us -> 63.3 us
    convert_element_type x12 -> x11, other arithmetic: 24.3 us -> 23.2 us  [add_up(): sum([v.astype(single) for v in values[1:]], values[0].astype(single))]
    ppermute x30 -> x27, starting transfers between devices: 34.2 us -> 34.1 us  [offset_by(): return lax.ppermute(value, self.names, out)]
  transfers between devices with their start and end apart: 99 -> 97, of which waited for: 22 -> 20; matrix products, arithmetic and copies ran while one was open for 24% -> 26% of each run, Pallas kernels for 41% -> 42%
where the time goes in v4:
time: 913 us; the launch traced here: 898 us
  Pallas kernels  397 us (43%)
  matrix products  116 us (13%)
  waiting for transfers between devices  107 us (12%)
  local copies, waits for them, and re-layouts  95 us (10%)
  starting transfers between devices  83.2 us (9%)
  other arithmetic  82.7 us (9%)
  between operations  17.7 us (2%)
    pallas_call x4, Pallas kernels, run_shared(): pl.pallas_call(functools.partial(shared_kernel, parts, tiles, start, widt...  210 us
    ppermute x35, waiting for transfers between devices, along(): lax.ppermute(value, self.names[axis], [(i, (i + by) % n) for i in range(n)])  90.1 us
    pallas_call x4, Pallas kernels, run_experts_back(): pl.pallas_call(functools.partial(expert_back_kernel, len(blocks), len(res...  68.4 us
    unnamed x450, local copies, waits for them, and re-layouts  63.3 us
    pallas_call x4, Pallas kernels, run_experts(): pl.pallas_call(functools.partial(expert_kernel, len(blocks), tok, pieces,...  54 us
    dot_general x6, matrix products, t_dot(): lax.dot_general(left, right, (((0,), (0,)), ((), ())), preferred_element_...  47.2 us
    ppermute x35, starting transfers between devices, along(): lax.ppermute(value, self.names[axis], [(i, (i + by) % n) for i in range(n)])  43.7 us
    ppermute x27, starting transfers between devices, offset_by(): return lax.ppermute(value, self.names, out)  34.1 us
  transfers between devices with their start and end apart: 97, of which 20 were waited for; matrix products, arithmetic and copies ran while one was open for 26% of the time, Pallas kernels for 42%

profile of v4, /device:TPU:18, one launch (start us, length us, event | category | flops | bytes accessed | tf_op | source)
XLA Modules:
  0.0 898.5 jit_solution(16599571791255281156)
XLA Ops:
  25.1 4.6 collective-permute-done.5
  40.3 14.0 %shard_map.340 = (bf16[128,2048]{1,0:T(8,128)(2,1)S(1)}, bf16[128,2048]{1,0:T(8,128)(2,1)S(1)}, bf16[128,1024]{1,0:T(8,128)(2,1)S(1)}, bf16[128,8192]{1,0:T(8,12...) custom-call(f32[128,3072]{1,0:T(8,128)S(1)} %convolution_add_fusion.refs_0_, ...), custom_call_target="tpu_custom_call" | custom-call | tf_op jit(solution)/shard_map/pallas_call | solution.py:595
  57.8 4.0 fusion.38
  67.1 4.0 fusion.20
  78.1 4.8 fusion.31
  82.9 5.3 fusion.30
  88.3 5.2 fusion.26
  97.0 25.2 %collective-permute-done.19.refs_0_ = bf16[128,2176]{1,0:T(8,128)(2,1)S(1)} collective-permute-done((bf16[128,2176]{1,0:T(8,128)(2,1)}, bf16[128,2176]{1,0:T(8,128)(2,1)S(1)}, u32[]{:S(2)}, u32[]{:S(2)}) %collective-permute-start.19) | collective-permute-done | bytes 557088 | tf_op jit(solution)/shard_map/ppermute | solution.py:816
  122.2 5.5 collective-permute-start.10
  137.9 13.6 %shard_map.343 = (bf16[16,128]{1,0:T(8,128)(2,1)}, bf16[1024,2048]{1,0:T(8,128)(2,1)}, bf16[2048,2048]{1,0:T(8,128)(2,1)}, f32[1024,1408]{1,0:T(8,128)}, f32[102...) custom-call(s32[17]{0:T(128)} %pad_add_fusion.refs_0_, ...), custom_call_target="tpu_custom_call" | custom-call | tf_op jit(solution)/shard_map/pallas_call | solution.py:212
  151.5 14.8 %collective-permute-done.10.refs_0_ = bf16[128,2176]{1,0:T(8,128)(2,1)S(1)} collective-permute-done((bf16[128,2176]{1,0:T(8,128)(2,1)}, bf16[128,2176]{1,0:T(8,128)(2,1)S(1)}, u32[]{:S(2)}, u32[]{:S(2)}) %collective-permute-start.10) | collective-permute-done | bytes 557088 | tf_op jit(solution)/shard_map/ppermute | solution.py:816
  174.2 13.5 %shard_map.345 = (bf16[16,128]{1,0:T(8,128)(2,1)}, bf16[1024,2048]{1,0:T(8,128)(2,1)}, bf16[2048,2048]{1,0:T(8,128)(2,1)}, f32[1024,1408]{1,0:T(8,128)}, f32[102...) custom-call(s32[17]{0:T(128)} %pad_add_fusion.refs_0_, ...), custom_call_target="tpu_custom_call", output_to_operand_aliasing={{1}: (14, {}), {2}: (15, {}), {3}: (16, {}), {4}: (17, {}),... | custom-call | tf_op jit(solution)/shard_map/pallas_call | solution.py:212
  187.7 17.0 %shard_map.346 = (bf16[128,2176]{1,0:T(8,128)(2,1)}, bf16[128,2176]{1,0:T(8,128)(2,1)}, bf16[128,2176]{1,0:T(8,128)(2,1)}, bf16[128,2176]{1,0:T(8,128)(2,1)}, bf...) custom-call(s32[17]{0:T(128)} %pad_add_fusion.refs_0_, ...), custom_call_target="tpu_custom_call" | custom-call | tf_op jit(solution)/shard_map/pallas_call | solution.py:356
  218.0 13.5 %shard_map.349 = (bf16[16,128]{1,0:T(8,128)(2,1)}, bf16[1024,2048]{1,0:T(8,128)(2,1)}, bf16[2048,2048]{1,0:T(8,128)(2,1)}, f32[1024,1408]{1,0:T(8,128)}, f32[102...) custom-call(s32[17]{0:T(128)} %pad_add_fusion.refs_0_, ...), custom_call_target="tpu_custom_call", output_to_operand_aliasing={{1}: (11, {}), {2}: (12, {}), {3}: (13, {}), {4}: (14, {}),... | custom-call | tf_op jit(solution)/shard_map/pallas_call | solution.py:212
  231.4 3.5 collective-permute-done.24.refs_2_
  234.9 13.5 %shard_map.350 = (bf16[16,128]{1,0:T(8,128)(2,1)}, bf16[1024,2048]{1,0:T(8,128)(2,1)}, bf16[2048,2048]{1,0:T(8,128)(2,1)}, f32[1024,1408]{1,0:T(8,128)}, f32[102...) custom-call(s32[17]{0:T(128)} %pad_add_fusion.refs_0_, ...), custom_call_target="tpu_custom_call", output_to_operand_aliasing={{1}: (10, {}), {2}: (11, {}), {3}: (12, {}), {4}: (13, {}),... | custom-call | tf_op jit(solution)/shard_map/pallas_call | solution.py:212
  248.4 17.2 %shard_map.351 = (bf16[128,2176]{1,0:T(8,128)(2,1)}, bf16[128,2176]{1,0:T(8,128)(2,1)}, bf16[128,2176]{1,0:T(8,128)(2,1)}, bf16[128,2176]{1,0:T(8,128)(2,1)}, bf...) custom-call(s32[17]{0:T(128)} %pad_add_fusion.refs_0_, ...), custom_call_target="tpu_custom_call", output_to_operand_aliasing={{4}: (14, {}), {5}: (15, {}), {6}: (16, {}), {7}: (17, {}),... | custom-call | tf_op jit(solution)/shard_map/pallas_call | solution.py:356
  272.9 17.2 %shard_map.355 = (bf16[128,2176]{1,0:T(8,128)(2,1)}, bf16[128,2176]{1,0:T(8,128)(2,1)}, bf16[128,2176]{1,0:T(8,128)(2,1)}, bf16[128,2176]{1,0:T(8,128)(2,1)}, bf...) custom-call(s32[17]{0:T(128)} %pad_add_fusion.refs_0_, ...), custom_call_target="tpu_custom_call", output_to_operand_aliasing={{4}: (17, {}), {5}: (18, {}), {6}: (19, {}), {7}: (20, {}),... | custom-call | tf_op jit(solution)/shard_map/pallas_call | solution.py:356
  297.2 3.3 collective-permute-start.41
  300.5 17.0 %shard_map.359 = (bf16[128,2176]{1,0:T(8,128)(2,1)}, bf16[128,2176]{1,0:T(8,128)(2,1)}, bf16[128,2176]{1,0:T(8,128)(2,1)}, bf16[128,2176]{1,0:T(8,128)(2,1)}, bf...) custom-call(s32[17]{0:T(128)} %pad_add_fusion.refs_0_, ...), custom_call_target="tpu_custom_call", output_to_operand_aliasing={{4}: (15, {}), {5}: (16, {}), {6}: (17, {}), {7}: (18, {}),... | custom-call | tf_op jit(solution)/shard_map/pallas_call | solution.py:356
  325.0 7.4 convolution_convert_fusion.2.refs_1_
  332.5 7.4 convolution_convert_fusion.1.refs_1_
  346.8 7.4 convolution_convert_fusion.refs_1_
  364.4 7.3 collective-permute-done.40.refs_0_
  384.8 4.0 fusion.106
  390.4 7.8 collective-permute-done.47.refs_0_
  410.7 16.8 %shard_map.378 = (bf16[128,3072]{1,0:T(8,128)(2,1)S(1)}, bf16[256,4096]{1,0:T(8,128)(2,1)S(1)}, bf16[256,4096]{1,0:T(8,128)(2,1)}, f32[256,512]{1,0:T(8,128)S(1)}, f32[256,64]{1,0:T(8,128)S(1)}) custom-call(bf16[128,2048]{1,0:T(8,128)(2,1)S(1)} %copy-done.15, bf16[256,4096]{1,0:T(8,128)(2,1)S(1)} %copy-done.11, bf16[256,4096]{1,0:T(8,128)(2,1)S(1)} %copy-done.13, ...), custom_call_target="tpu_custom_call" | custom-call | tf_op jit(solution)/shard_map/pallas_call | solution.py:619
  434.3 10.2 %collective-permute-done.49.refs_0_ = bf16[256,1024]{1,0:T(8,128)(2,1)} collective-permute-done((bf16[256,1024]{1,0:T(8,128)(2,1)S(1)}, bf16[256,1024]{1,0:T(8,128)(2,1)}, u32[]{:S(2)}, u32[]{:S(2)}) %collective-permute-start.49) | collective-permute-done | bytes 524320 | tf_op jit(solution)/shard_map/ppermute | solution.py:816
  453.2 5.3 shard_map.393.refs_7_
  464.2 4.9 fusion.108
  469.1 3.7 add_convert_fusion.2.refs_2_
  472.9 4.1 fusion.109
  479.2 9.3 %convert_add_fusion.2.refs_1_ = f32[704,2048]{1,0:T(8,128)} fusion(bf16[704,2048]{1,0:T(8,128)(2,1)} %shard_map.395, bf16[1024,704]{1,0:T(8,128)(2,1)} %shard_map.394, bf16[1024,2048]{1,0:T(8,128)(2,1)} %get-tuple-element.209), kind=kOutput, calls=%fused_computation.2 | convolution fusion | flops 2955673600 | bytes 14286848 | tf_op jit(solution)/shard_map/dot_general | solution.py:89
  488.5 9.3 %convert_add_fusion.1.refs_1_ = f32[704,2048]{1,0:T(8,128)} fusion(bf16[704,2048]{1,0:T(8,128)(2,1)} %shard_map.397, bf16[1024,704]{1,0:T(8,128)(2,1)} %shard_map.396, bf16[1024,2048]{1,0:T(8,128)(2,1)} %get-tuple-element.209), kind=kOutput, calls=%fused_computation.1 | convolution fusion | flops 2955673600 | bytes 14286848 | tf_op jit(solution)/shard_map/dot_general | solution.py:89
  507.9 54.5 %shard_map.400 = (f32[2048,1408]{1,0:T(8,128)}, f32[2048,1408]{1,0:T(8,128)}, f32[1408,2048]{1,0:T(8,128)}) custom-call(bf16[2048,2048]{1,0:T(8,128)(2,1)} %shard_map.389.refs_0_, bf16[2048,2048]{1,0:T(8,128)(2,1)} %collective-permute-done.55.refs_1_, bf16[2048,2048]{1,0:T(8,128)(2,1)} %shard_map.390.refs_2_, ...), custom_call_target="tpu_custom_call" | custom-call | tf_op jit(solution)/shard_map/pallas_call | solution.py:474
  571.6 5.5 shard_map.414.refs_1_.refs_7_
  604.0 4.9 shard_map.420
  610.2 3.4 collective-permute-start.75
  615.3 54.7 %shard_map.421 = (f32[2048,1408]{1,0:T(8,128)}, f32[2048,1408]{1,0:T(8,128)}, f32[1408,2048]{1,0:T(8,128)}) custom-call(bf16[2048,2048]{1,0:T(8,128)(2,1)} %shard_map.389.refs_0_, bf16[2048,2048]{1,0:T(8,128)(2,1)} %collective-permute-done.55.refs_1_, ...), custom_call_target="tpu_custom_call", output_to_operand_aliasing={{0}: (9, {}), {1}: (10, {}), {2}: (11, {})} | custom-call | tf_op jit(solution)/shard_map/pallas_call | solution.py:474
  689.2 54.3 %shard_map.434 = (f32[2048,1408]{1,0:T(8,128)}, f32[2048,1408]{1,0:T(8,128)}, f32[1408,2048]{1,0:T(8,128)}) custom-call(bf16[2048,2048]{1,0:T(8,128)(2,1)} %shard_map.389.refs_0_, bf16[2048,2048]{1,0:T(8,128)(2,1)} %collective-permute-done.55.refs_1_, ...), custom_call_target="tpu_custom_call", output_to_operand_aliasing={{0}: (10, {}), {1}: (11, {}), {2}: (12, {})} | custom-call | tf_op jit(solution)/shard_map/pallas_call | solution.py:474
  764.7 4.6 fusion.25
  770.9 46.2 %shard_map.444 = (f32[2048,1408]{1,0:T(8,128)}, f32[2048,1408]{1,0:T(8,128)}, f32[1408,2048]{1,0:T(8,128)}) custom-call(bf16[2048,2048]{1,0:T(8,128)(2,1)} %shard_map.389.refs_0_, bf16[2048,2048]{1,0:T(8,128)(2,1)} %collective-permute-done.55.refs_1_, ...), custom_call_target="tpu_custom_call", output_to_operand_aliasing={{0}: (10, {}), {1}: (11, {}), {2}: (12, {})} | custom-call | tf_op jit(solution)/shard_map/pallas_call | solution.py:474
  817.9 14.9 %collective-permute-done.84.refs_0_ = bf16[128,2048]{1,0:T(8,128)(2,1)S(1)} collective-permute-done((bf16[128,2048]{1,0:T(8,128)(2,1)}, bf16[128,2048]{1,0:T(8,128)(2,1)S(1)}, u32[]{:S(2)}, u32[]{:S(2)}) %collective-permute-start.84) | collective-permute-done | bytes 524320 | tf_op jit(solution)/shard_map/ppermute | solution.py:816
  851.9 4.4 shard_map.462.refs_1_
  857.5 6.3 convert_add_fusion.refs_2_
  866.2 4.1 shard_map.464.refs_1_
  870.2 5.0 collective-permute-done.90.refs_0_
  875.5 9.7 %shard_map.471 = (f32[256,4096]{1,0:T(8,128)}, f32[1024,1536]{1,0:T(8,128)}, f32[576,1024]{1,0:T(8,128)}, f32[1024,64]{1,0:T(8,128)}) custom-call(s32[2]{0:T(128)} %pad_add_fusion.1.refs_0_, bf16[512,1536]{1,0:T(8,128)(2,1)} %maximum_select_fusion.1.refs_1_, bf16[512,1536]{1,0:T(8,128)(2,1)} %shard_map.467.refs_2_, ...), custom_call_target="tpu_custom_call" | custom-call | tf_op jit(solution)/shard_map/pallas_call | solution.py:676
  (907 shorter events, 286.5 us)
Async XLA Ops:
  7.2 180.5 %all-gather.4.cloned.1.call-start = ((), (), s32[]{:S(2)}) async-start(), calls=%async_computation.3 | async-start | bytes 8912896 | tf_op jit(solution)/shard_map/all_gather | solution.py:1161
  7.9 554.5 %reduce-scatter.4.cloned.1.call-start = ((), (), s32[]{:S(2)}) async-start(), calls=%async_computation.4 | async-start | bytes 1310720 | tf_op jit(solution)/shard_map/reduce_scatter | solution.py:1452
  8.0 58.8 %collective-permute-start.17 = (bf16[128,2048]{1,0:T(8,128)(2,1)}, bf16[128,2048]{1,0:T(8,128)(2,1)}, u32[]{:S(2)}, u32[]{:S(2)}) collective-permute-start(bf16[128,2048]{1,0:T(8,128)(2,1)} %param.24), channel_id=1, source_target_pairs={{0,1},{1,0},{2,3},{3,2},{4,5},{5,4},{6,7},{7,6},{8,9},{9,8},{10,11... | collective-permute-start | bytes 1572872 | tf_op jit(solution)/shard_map/ppermute | solution.py:1056
  30.0 41.0 %collective-permute-start.9 = (bf16[1024,16]{0,1:T(8,128)(2,1)S(1)}, bf16[1024,16]{0,1:T(8,128)(2,1)S(1)}, u32[]{:S(2)}, u32[]{:S(2)}) collective-permute-start(bf16[1024,16]{0,1:T(8,128)(2,1)S(1)} %copy-done.179), channel_id=1, source_target_pairs={{0,1},{1,0},{2,3},{3,2},{4,5},{5,4},{6,7},{7,6},{8,9},{9,8},{10,11... | collective-permute-start | bytes 98312 | tf_op jit(solution)/shard_map/ppermute | solution.py:1056
  36.6 56.9 %collective-permute-start.14 = (bf16[704,2048]{1,0:T(8,128)(2,1)S(1)}, bf16[704,2048]{1,0:T(8,128)(2,1)}, u32[]{:S(2)}, u32[]{:S(2)}) collective-permute-start(bf16[704,2048]{1,0:T(8,128)(2,1)S(1)} %bitcast.101), channel_id=1, source_target_pairs={{0,1},{1,0},{2,3},{3,2},{4,5},{5,4},{6,7},{7,6},{8,9},{9,8},{10,11... | collective-permute-start | bytes 8650760 | tf_op jit(solution)/shard_map/ppermute | solution.py:1056
  39.9 54.1 %collective-permute-start.15 = (bf16[704,2048]{1,0:T(8,128)(2,1)}, bf16[704,2048]{1,0:T(8,128)(2,1)}, u32[]{:S(2)}, u32[]{:S(2)}) collective-permute-start(bf16[704,2048]{1,0:T(8,128)(2,1)} %bitcast.8.refs_7_.refs_8_.refs_5_.refs_6_), channel_id=1, source_target_pairs={{0,1},{1,0},{2,3},{3,2},{4,5},{5,4},{6,7},{7,6},{8,9},{9,8},{10,11... | collective-permute-start | bytes 8650760 | tf_op jit(solution)/shard_map/ppermute | solution.py:1056
  75.9 46.4 %collective-permute-start.19 = (bf16[128,2176]{1,0:T(8,128)(2,1)}, bf16[128,2176]{1,0:T(8,128)(2,1)S(1)}, u32[]{:S(2)}, u32[]{:S(2)}) collective-permute-start(bf16[128,2176]{1,0:T(8,128)(2,1)} %concatenate.221.refs_1_), channel_id=1, source_target_pairs={{0,24},{8,0},{16,8},{24,16},{1,25},{9,1},{17,9},{25,17},{2,26},{10... | collective-permute-start | bytes 1671176 | tf_op jit(solution)/shard_map/ppermute | solution.py:816
  76.3 54.6 %collective-permute-start.18 = (bf16[128,2176]{1,0:T(8,128)(2,1)}, bf16[128,2176]{1,0:T(8,128)(2,1)}, u32[]{:S(2)}, u32[]{:S(2)}) collective-permute-start(bf16[128,2176]{1,0:T(8,128)(2,1)} %concatenate.221.refs_1_), channel_id=1, source_target_pairs={{0,8},{8,16},{16,24},{24,0},{1,9},{9,17},{17,25},{25,1},{2,10},{10... | collective-permute-start | bytes 1671176 | tf_op jit(solution)/shard_map/ppermute | solution.py:816
  94.0 41.5 %collective-permute-start.12 = (bf16[128,2176]{1,0:T(8,128)(2,1)}, bf16[128,2176]{1,0:T(8,128)(2,1)S(1)}, u32[]{:S(2)}, u32[]{:S(2)}) collective-permute-start(bf16[128,2176]{1,0:T(8,128)(2,1)} %concatenate.221.refs_1_), channel_id=1, source_target_pairs={{0,4},{2,6},{4,0},{6,2},{8,12},{10,14},{12,8},{14,10},{16,20},{18,... | collective-permute-start | bytes 1671176 | tf_op jit(solution)/shard_map/ppermute | solution.py:825
  95.5 41.6 %collective-permute-start.13 = (bf16[128,2176]{1,0:T(8,128)(2,1)}, bf16[128,2176]{1,0:T(8,128)(2,1)S(1)}, u32[]{:S(2)}, u32[]{:S(2)}) collective-permute-start(bf16[128,2176]{1,0:T(8,128)(2,1)} %concatenate.221.refs_1_), channel_id=1, source_target_pairs={{0,6},{2,4},{4,2},{6,0},{8,14},{10,12},{12,10},{14,8},{16,22},{18,... | collective-permute-start | bytes 1671176 | tf_op jit(solution)/shard_map/ppermute | solution.py:825
  122.2 44.1 %collective-permute-start.10 = (bf16[128,2176]{1,0:T(8,128)(2,1)}, bf16[128,2176]{1,0:T(8,128)(2,1)S(1)}, u32[]{:S(2)}, u32[]{:S(2)}) collective-permute-start(bf16[128,2176]{1,0:T(8,128)(2,1)} %concatenate.221.refs_1_), channel_id=1, source_target_pairs={{0,16},{8,24},{16,0},{24,8},{1,17},{9,25},{17,1},{25,9},{2,18},{10... | collective-permute-start | bytes 1671176 | tf_op jit(solution)/shard_map/ppermute | solution.py:816
  133.5 40.2 %collective-permute-start.21 = (bf16[128,2176]{1,0:T(8,128)(2,1)}, bf16[128,2176]{1,0:T(8,128)(2,1)}, u32[]{:S(2)}, u32[]{:S(2)}) collective-permute-start(bf16[128,2176]{1,0:T(8,128)(2,1)} %shard_map.341.refs_12_.refs_1_), channel_id=1, source_target_pairs={{0,2},{2,0},{4,6},{6,4},{8,10},{10,8},{12,14},{14,12},{16,18},{18,... | collective-permute-start | bytes 1671176 | tf_op jit(solution)/shard_map/ppermute | solution.py:825
  170.7 41.1 %collective-permute-start.50 = (bf16[128,2816]{1,0:T(8,128)(2,1)}, bf16[128,2816]{1,0:T(8,128)(2,1)}, u32[]{:S(2)}, u32[]{:S(2)}) collective-permute-start(bf16[128,2816]{1,0:T(8,128)(2,1)} %pad_maximum_fusion.11), channel_id=1, source_target_pairs={{0,1},{1,0},{2,3},{3,2},{4,5},{5,4},{6,7},{7,6},{8,9},{9,8},{10,11... | collective-permute-start | bytes 2162696 | tf_op jit(solution)/shard_map/ppermute | solution.py:1056
  173.7 44.3 %collective-permute-start.26 = (bf16[256,2176]{1,0:T(8,128)(2,1)}, bf16[256,2176]{1,0:T(8,128)(2,1)}, u32[]{:S(2)}, u32[]{:S(2)}) collective-permute-start(bf16[256,2176]{1,0:T(8,128)(2,1)} %pad_maximum_fusion.5.refs_1_), channel_id=1, source_target_pairs={{0,4},{4,0},{1,5},{5,1},{2,6},{6,2},{3,7},{7,3},{8,12},{12,8},{9,1... | collective-permute-start | bytes 3342344 | tf_op jit(solution)/shard_map/ppermute | solution.py:816
  208.9 58.8 %collective-permute-start.27 = (bf16[128,2176]{1,0:T(8,128)(2,1)}, bf16[128,2176]{1,0:T(8,128)(2,1)S(1)}, u32[]{:S(2)}, u32[]{:S(2)}) collective-permute-start(bf16[128,2176]{1,0:T(8,128)(2,1)} %get-tuple-element.172), channel_id=1, source_target_pairs={{0,2},{2,0},{4,6},{6,4},{8,10},{10,8},{12,14},{14,12},{16,18},{18,... | collective-permute-start | bytes 1671176 | tf_op jit(solution)/shard_map/ppermute | solution.py:825
  210.3 58.8 %collective-permute-start.28 = (bf16[128,2176]{1,0:T(8,128)(2,1)}, bf16[128,2176]{1,0:T(8,128)(2,1)S(1)}, u32[]{:S(2)}, u32[]{:S(2)}) collective-permute-start(bf16[128,2176]{1,0:T(8,128)(2,1)} %get-tuple-element.184), channel_id=1, source_target_pairs={{0,4},{2,6},{4,0},{6,2},{8,12},{10,14},{12,8},{14,10},{16,20},{18,... | collective-permute-start | bytes 1671176 | tf_op jit(solution)/shard_map/ppermute | solution.py:825
  211.8 58.2 %collective-permute-start.29 = (bf16[128,2176]{1,0:T(8,128)(2,1)}, bf16[128,2176]{1,0:T(8,128)(2,1)}, u32[]{:S(2)}, u32[]{:S(2)}) collective-permute-start(bf16[128,2176]{1,0:T(8,128)(2,1)} %get-tuple-element.185), channel_id=1, source_target_pairs={{0,6},{2,4},{4,2},{6,0},{8,14},{10,12},{12,10},{14,8},{16,22},{18,... | collective-permute-start | bytes 1671176 | tf_op jit(solution)/shard_map/ppermute | solution.py:825
  297.2 64.3 %collective-permute-start.41 = (bf16[128,2176]{1,0:T(8,128)(2,1)}, bf16[128,2176]{1,0:T(8,128)(2,1)S(1)}, u32[]{:S(2)}, u32[]{:S(2)}) collective-permute-start(bf16[128,2176]{1,0:T(8,128)(2,1)} %add_convert_fusion.7.refs_14_), channel_id=1, source_target_pairs={{0,16},{8,24},{16,0},{24,8},{1,17},{9,25},{17,1},{25,9},{2,18},{10... | collective-permute-start | bytes 1671176 | tf_op jit(solution)/shard_map/ppermute | solution.py:816
  339.9 42.8 %collective-permute-start.44 = (bf16[704,2048]{1,0:T(8,128)(2,1)}, bf16[704,2048]{1,0:T(8,128)(2,1)}, u32[]{:S(2)}, u32[]{:S(2)}) collective-permute-start(bf16[704,2048]{1,0:T(8,128)(2,1)} %convolution_convert_fusion.1.refs_1_), channel_id=1, source_target_pairs={{0,1},{1,0},{2,3},{3,2},{4,5},{5,4},{6,7},{7,6},{8,9},{9,8},{10,11... | collective-permute-start | bytes 8650760 | tf_op jit(solution)/shard_map/ppermute | solution.py:1056
  342.5 41.7 %collective-permute-start.43 = (bf16[704,2048]{1,0:T(8,128)(2,1)}, bf16[704,2048]{1,0:T(8,128)(2,1)}, u32[]{:S(2)}, u32[]{:S(2)}) collective-permute-start(bf16[704,2048]{1,0:T(8,128)(2,1)} %convolution_convert_fusion.2.refs_1_), channel_id=1, source_target_pairs={{0,1},{1,0},{2,3},{3,2},{4,5},{5,4},{6,7},{7,6},{8,9},{9,8},{10,11... | collective-permute-start | bytes 8650760 | tf_op jit(solution)/shard_map/ppermute | solution.py:1056
  371.7 58.6 %collective-permute-start.53 = (bf16[256,704]{1,0:T(8,128)(2,1)}, bf16[256,704]{1,0:T(8,128)(2,1)S(1)}, u32[]{:S(2)}, u32[]{:S(2)}) collective-permute-start(bf16[256,704]{1,0:T(8,128)(2,1)} %pad_maximum_fusion.20), channel_id=1, source_target_pairs={{0,6},{2,4},{4,2},{6,0},{8,14},{10,12},{12,10},{14,8},{16,22},{18,... | collective-permute-start | bytes 1081352 | tf_op jit(solution)/shard_map/ppermute | solution.py:825
  378.0 53.1 %collective-permute-start.52 = (bf16[256,704]{1,0:T(8,128)(2,1)}, bf16[256,704]{1,0:T(8,128)(2,1)S(1)}, u32[]{:S(2)}, u32[]{:S(2)}) collective-permute-start(bf16[256,704]{1,0:T(8,128)(2,1)} %pad_maximum_fusion.19), channel_id=1, source_target_pairs={{0,4},{2,6},{4,0},{6,2},{8,12},{10,14},{12,8},{14,10},{16,20},{18,... | collective-permute-start | bytes 1081352 | tf_op jit(solution)/shard_map/ppermute | solution.py:825
  384.8 121.6 %collective-permute-start.56 = (bf16[2048,2048]{1,0:T(8,128)(2,1)}, bf16[2048,2048]{1,0:T(8,128)(2,1)}, u32[]{:S(2)}, u32[]{:S(2)}) collective-permute-start(bf16[2048,2048]{1,0:T(8,128)(2,1)} %shard_map.390.refs_2_), channel_id=1, source_target_pairs={{0,1},{1,0},{2,3},{3,2},{4,5},{5,4},{6,7},{7,6},{8,9},{9,8},{10,11... | collective-permute-start | bytes 25165832 | tf_op jit(solution)/shard_map/ppermute | solution.py:1056
  398.2 108.6 %collective-permute-start.55 = (bf16[2048,2048]{1,0:T(8,128)(2,1)}, bf16[2048,2048]{1,0:T(8,128)(2,1)}, u32[]{:S(2)}, u32[]{:S(2)}) collective-permute-start(bf16[2048,2048]{1,0:T(8,128)(2,1)} %shard_map.389.refs_0_), channel_id=1, source_target_pairs={{0,1},{1,0},{2,3},{3,2},{4,5},{5,4},{6,7},{7,6},{8,9},{9,8},{10,11... | collective-permute-start | bytes 25165832 | tf_op jit(solution)/shard_map/ppermute | solution.py:1056
  458.5 105.7 %reduce-scatter.6.cloned.1.call-start = ((), (), s32[]{:S(2)}) async-start(), calls=%async_computation.5 | async-start | bytes 2621440 | tf_op jit(solution)/shard_map/reduce_scatter | solution.py:1417
  472.8 199.5 %reduce-scatter.8.cloned.1.call-start = ((), (), s32[]{:S(2)}) async-start(), calls=%async_computation.6 | async-start | bytes 1474560 | tf_op jit(solution)/shard_map/reduce_scatter | solution.py:1482
  500.7 61.8 %collective-permute-start.66 = (bf16[256,1536]{1,0:T(8,128)(2,1)}, bf16[256,1536]{1,0:T(8,128)(2,1)S(1)}, u32[]{:S(2)}, u32[]{:S(2)}) collective-permute-start(bf16[256,1536]{1,0:T(8,128)(2,1)} %pad_maximum_fusion.10.refs_10_.refs_0_), channel_id=1, source_target_pairs={{0,2},{2,0},{1,3},{3,1},{4,6},{6,4},{5,7},{7,5},{8,10},{10,8},{9,1... | collective-permute-start | bytes 2359304 | tf_op jit(solution)/shard_map/ppermute | solution.py:816
  503.8 59.5 %collective-permute-start.65 = (bf16[256,1536]{1,0:T(8,128)(2,1)}, bf16[256,1536]{1,0:T(8,128)(2,1)}, u32[]{:S(2)}, u32[]{:S(2)}) collective-permute-start(bf16[256,1536]{1,0:T(8,128)(2,1)} %pad_maximum_fusion.9.refs_9_.refs_0_), channel_id=1, source_target_pairs={{0,4},{4,0},{1,5},{5,1},{2,6},{6,2},{3,7},{7,3},{8,12},{12,8},{9,1... | collective-permute-start | bytes 2359304 | tf_op jit(solution)/shard_map/ppermute | solution.py:816
  504.4 59.0 %collective-permute-start.64 = (bf16[128,2176]{1,0:T(8,128)(2,1)S(1)}, bf16[128,2176]{1,0:T(8,128)(2,1)S(1)}, u32[]{:S(2)}, u32[]{:S(2)}) collective-permute-start(bf16[128,2176]{1,0:T(8,128)(2,1)S(1)} %pad.8.refs_8_.refs_0_), channel_id=1, source_target_pairs={{0,6},{2,4},{4,2},{6,0},{8,14},{10,12},{12,10},{14,8},{16,22},{18,... | collective-permute-start | bytes 1671176 | tf_op jit(solution)/shard_map/ppermute | solution.py:825
  506.4 57.8 %collective-permute-start.63 = (bf16[128,2176]{1,0:T(8,128)(2,1)S(1)}, bf16[128,2176]{1,0:T(8,128)(2,1)}, u32[]{:S(2)}, u32[]{:S(2)}) collective-permute-start(bf16[128,2176]{1,0:T(8,128)(2,1)S(1)} %pad.8.refs_8_.refs_0_), channel_id=1, source_target_pairs={{0,4},{2,6},{4,0},{6,2},{8,12},{10,14},{12,8},{14,10},{16,20},{18,... | collective-permute-start | bytes 1671176 | tf_op jit(solution)/shard_map/ppermute | solution.py:825
  506.8 57.4 %collective-permute-start.62 = (bf16[128,2176]{1,0:T(8,128)(2,1)S(1)}, bf16[128,2176]{1,0:T(8,128)(2,1)}, u32[]{:S(2)}, u32[]{:S(2)}) collective-permute-start(bf16[128,2176]{1,0:T(8,128)(2,1)S(1)} %pad.8.refs_8_.refs_0_), channel_id=1, source_target_pairs={{0,2},{2,0},{4,6},{6,4},{8,10},{10,8},{12,14},{14,12},{16,18},{18,... | collective-permute-start | bytes 1671176 | tf_op jit(solution)/shard_map/ppermute | solution.py:825
  577.1 174.7 %all-gather.6.cloned.1.call-start = ((), (), s32[]{:S(2)}) async-start(), calls=%async_computation.7 | async-start | bytes 4456448 | tf_op jit(solution)/shard_map/all_gather | solution.py:1458
  579.0 284.9 %all-gather.8.cloned.1.call-start = ((), (), s32[]{:S(2)}) async-start(), calls=%async_computation.8 | async-start | bytes 5013504 | tf_op jit(solution)/shard_map/all_gather | solution.py:1498
  601.0 71.3 %collective-permute-start.77 = (bf16[512,2048]{1,0:T(8,128)(2,1)}, bf16[512,2048]{1,0:T(8,128)(2,1)}, u32[]{:S(2)}, u32[]{:S(2)}) collective-permute-start(bf16[512,2048]{1,0:T(8,128)(2,1)} %shard_map.425), channel_id=1, source_target_pairs={{0,2},{2,0},{1,3},{3,1},{4,6},{6,4},{5,7},{7,5},{8,10},{10,8},{9,1... | collective-permute-start | bytes 6291464 | tf_op jit(solution)/shard_map/ppermute | solution.py:816
  602.1 70.2 %collective-permute-start.78 = (bf16[512,2048]{1,0:T(8,128)(2,1)}, bf16[512,2048]{1,0:T(8,128)(2,1)}, u32[]{:S(2)}, u32[]{:S(2)}) collective-permute-start(bf16[512,2048]{1,0:T(8,128)(2,1)} %shard_map.427), channel_id=1, source_target_pairs={{0,4},{4,0},{1,5},{5,1},{2,6},{6,2},{3,7},{7,3},{8,12},{12,8},{9,1... | collective-permute-start | bytes 6291464 | tf_op jit(solution)/shard_map/ppermute | solution.py:816
  609.8 60.3 %collective-permute-start.76 = (bf16[64,3200]{1,0:T(8,128)(2,1)S(1)}, bf16[64,3200]{1,0:T(8,128)(2,1)S(1)}, u32[]{:S(2)}, u32[]{:S(2)}) collective-permute-start(bf16[64,3200]{1,0:T(8,128)(2,1)S(1)} %get-tuple-element.355), channel_id=1, source_target_pairs={{0,24},{8,0},{16,8},{24,16},{1,25},{9,1},{17,9},{25,17},{2,26},{10... | collective-permute-start | bytes 1228808 | tf_op jit(solution)/shard_map/ppermute | solution.py:816
  610.2 60.6 %collective-permute-start.75 = (bf16[64,3200]{1,0:T(8,128)(2,1)S(1)}, bf16[64,3200]{1,0:T(8,128)(2,1)S(1)}, u32[]{:S(2)}, u32[]{:S(2)}) collective-permute-start(bf16[64,3200]{1,0:T(8,128)(2,1)S(1)} %get-tuple-element.356), channel_id=1, source_target_pairs={{0,16},{8,24},{16,0},{24,8},{1,17},{9,25},{17,1},{25,9},{2,18},{10... | collective-permute-start | bytes 1228808 | tf_op jit(solution)/shard_map/ppermute | solution.py:816
  613.6 57.9 %collective-permute-start.74 = (bf16[64,3200]{1,0:T(8,128)(2,1)S(1)}, bf16[64,3200]{1,0:T(8,128)(2,1)S(1)}, u32[]{:S(2)}, u32[]{:S(2)}) collective-permute-start(bf16[64,3200]{1,0:T(8,128)(2,1)S(1)} %get-tuple-element.357), channel_id=1, source_target_pairs={{0,8},{8,16},{16,24},{24,0},{1,9},{9,17},{17,25},{25,1},{2,10},{10... | collective-permute-start | bytes 1228808 | tf_op jit(solution)/shard_map/ppermute | solution.py:816
  674.8 68.7 %collective-permute-start.81 = (bf16[64,3200]{1,0:T(8,128)(2,1)S(1)}, bf16[64,3200]{1,0:T(8,128)(2,1)}, u32[]{:S(2)}, u32[]{:S(2)}) collective-permute-start(bf16[64,3200]{1,0:T(8,128)(2,1)S(1)} %add_convert_fusion.9.refs_9_.refs_0_), channel_id=1, source_target_pairs={{0,24},{8,0},{16,8},{24,16},{1,25},{9,1},{17,9},{25,17},{2,26},{10... | collective-permute-start | bytes 1228808 | tf_op jit(solution)/shard_map/ppermute | solution.py:816
  675.9 69.5 %collective-permute-start.80 = (bf16[64,3200]{1,0:T(8,128)(2,1)S(1)}, bf16[64,3200]{1,0:T(8,128)(2,1)S(1)}, u32[]{:S(2)}, u32[]{:S(2)}) collective-permute-start(bf16[64,3200]{1,0:T(8,128)(2,1)S(1)} %add_convert_fusion.9.refs_9_.refs_0_), channel_id=1, source_target_pairs={{0,16},{8,24},{16,0},{24,8},{1,17},{9,25},{17,1},{25,9},{2,18},{10... | collective-permute-start | bytes 1228808 | tf_op jit(solution)/shard_map/ppermute | solution.py:816
  677.7 68.4 %collective-permute-start.79 = (bf16[64,3200]{1,0:T(8,128)(2,1)S(1)}, bf16[64,3200]{1,0:T(8,128)(2,1)S(1)}, u32[]{:S(2)}, u32[]{:S(2)}) collective-permute-start(bf16[64,3200]{1,0:T(8,128)(2,1)S(1)} %add_convert_fusion.9.refs_9_.refs_0_), channel_id=1, source_target_pairs={{0,8},{8,16},{16,24},{24,0},{1,9},{9,17},{17,25},{25,1},{2,10},{10... | collective-permute-start | bytes 1228808 | tf_op jit(solution)/shard_map/ppermute | solution.py:816
  683.1 66.7 %collective-permute-start.82 = (bf16[256,2048]{1,0:T(8,128)(2,1)}, bf16[256,2048]{1,0:T(8,128)(2,1)S(1)}, u32[]{:S(2)}, u32[]{:S(2)}) collective-permute-start(bf16[256,2048]{1,0:T(8,128)(2,1)} %get-tuple-element.351), channel_id=1, source_target_pairs={{0,4},{4,0},{1,5},{5,1},{2,6},{6,2},{3,7},{7,3},{8,12},{12,8},{9,1... | collective-permute-start | bytes 3145736 | tf_op jit(solution)/shard_map/ppermute | solution.py:816
  688.2 62.6 %collective-permute-start.83 = (bf16[256,2048]{1,0:T(8,128)(2,1)}, bf16[256,2048]{1,0:T(8,128)(2,1)S(1)}, u32[]{:S(2)}, u32[]{:S(2)}) collective-permute-start(bf16[256,2048]{1,0:T(8,128)(2,1)} %get-tuple-element.354), channel_id=1, source_target_pairs={{0,2},{2,0},{1,3},{3,1},{4,6},{6,4},{5,7},{7,5},{8,10},{10,8},{9,1... | collective-permute-start | bytes 3145736 | tf_op jit(solution)/shard_map/ppermute | solution.py:816
  755.7 61.4 %collective-permute-start.87 = (bf16[128,2048]{1,0:T(8,128)(2,1)S(1)}, bf16[128,2048]{1,0:T(8,128)(2,1)S(1)}, u32[]{:S(2)}, u32[]{:S(2)}) collective-permute-start(bf16[128,2048]{1,0:T(8,128)(2,1)S(1)} %get-tuple-element.359), channel_id=1, source_target_pairs={{0,16},{8,24},{16,0},{24,8},{1,17},{9,25},{17,1},{25,9},{2,18},{10... | collective-permute-start | bytes 1572872 | tf_op jit(solution)/shard_map/ppermute | solution.py:816
  759.2 73.7 %collective-permute-start.84 = (bf16[128,2048]{1,0:T(8,128)(2,1)}, bf16[128,2048]{1,0:T(8,128)(2,1)S(1)}, u32[]{:S(2)}, u32[]{:S(2)}) collective-permute-start(bf16[128,2048]{1,0:T(8,128)(2,1)} %get-tuple-element.361), channel_id=1, source_target_pairs={{0,24},{8,0},{16,8},{24,16},{1,25},{9,1},{17,9},{25,17},{2,26},{10... | collective-permute-start | bytes 1572872 | tf_op jit(solution)/shard_map/ppermute | solution.py:816
  762.3 71.5 %collective-permute-start.86 = (bf16[256,1664]{1,0:T(8,128)(2,1)S(1)}, bf16[256,1664]{1,0:T(8,128)(2,1)S(1)}, u32[]{:S(2)}, u32[]{:S(2)}) collective-permute-start(bf16[256,1664]{1,0:T(8,128)(2,1)S(1)} %dynamic-slice.14.refs_8_.refs_0_), channel_id=1, source_target_pairs={{0,4},{4,0},{1,5},{5,1},{2,6},{6,2},{3,7},{7,3},{8,12},{12,8},{9,1... | collective-permute-start | bytes 2555912 | tf_op jit(solution)/shard_map/ppermute | solution.py:816
  763.5 70.3 %collective-permute-start.85 = (bf16[256,1536]{1,0:T(8,128)(2,1)S(1)}, bf16[256,1536]{1,0:T(8,128)(2,1)}, u32[]{:S(2)}, u32[]{:S(2)}) collective-permute-start(bf16[256,1536]{1,0:T(8,128)(2,1)S(1)} %constant_dynamic-slice_fusion.9.refs_7_.refs_0_), channel_id=1, source_target_pairs={{0,2},{2,0},{1,3},{3,1},{4,6},{6,4},{5,7},{7,5},{8,10},{10,8},{9,1... | collective-permute-start | bytes 2359304 | tf_op jit(solution)/shard_map/ppermute | solution.py:816
  764.5 69.3 %collective-permute-start.88 = (bf16[128,2048]{1,0:T(8,128)(2,1)}, bf16[128,2048]{1,0:T(8,128)(2,1)}, u32[]{:S(2)}, u32[]{:S(2)}) collective-permute-start(bf16[128,2048]{1,0:T(8,128)(2,1)} %get-tuple-element.360), channel_id=1, source_target_pairs={{0,8},{8,16},{16,24},{24,0},{1,9},{9,17},{17,25},{25,1},{2,10},{10... | collective-permute-start | bytes 1572872 | tf_op jit(solution)/shard_map/ppermute | solution.py:816
  (269 other events, 2101.3 us)
Sparse Core Ops, SparseCore 0:
  10.8 151.7 all-gather.3
  458.7 26.7 reduce-scatter.3
  489.2 58.9 reduce-scatter.5
  577.2 28.9 reduce-scatter.7
  608.9 112.9 all-gather.5
  724.5 110.9 all-gather.7

commit v5 on v4

--- a/solution.py
+++ b/solution.py
@@ -1281,7 +1281,7 @@
     fillers = [
         lambda waits: others_part(1, [others_part(0, waits)]),
         lambda waits: others_part(2, waits),
-        lambda waits: own_part(1, [own_part(0, waits)]),
+        lambda waits: own_part(1, waits),
     ]
     mark = sh_back
     backs = [None] * turns
@@ -1405,8 +1405,9 @@
         score_scale,
         [v[0] for v in heads_line],
     )
-    heads_line = [hold(v, grad_query) for v in heads_line]
-    lefts = hold(lefts, grad_query)
+    mark = own_part(0, [grad_query])
+    heads_line = [hold(v, mark) for v in heads_line]
+    lefts = hold(lefts, mark)
     there = [v for line in [*heads_line, lefts] for v in line[1:]]
     grad_query = tie(grad_query, *there)
     heads_all = [cores.spread(v) for v in chips.stack_done(heads_line, grad_query)]

time: 913 us -> 900 us (0.986)
    unnamed x450 -> x430, local copies, waits for them, and re-layouts: 63.3 us -> 68 us
  transfers between devices with their start and end apart: 97 -> 97, of which waited for: 20 -> 23; matrix products, arithmetic and copies ran while one was open for 26% -> 25% of each run, Pallas kernels for 42% -> 43%
where the time goes in v5:
time: 900 us; the launch traced here: 889 us
  Pallas kernels  396 us (44%)
  matrix products  112 us (12%)
  waiting for transfers between devices  101 us (11%)
  local copies, waits for them, and re-layouts  100 us (11%)
  starting transfers between devices  82.9 us (9%)
  other arithmetic  78.9 us (9%)
  between operations  17.4 us (2%)
    pallas_call x4, Pallas kernels, run_shared(): pl.pallas_call(functools.partial(shared_kernel, parts, tiles, start, widt...  210 us
    ppermute x35, waiting for transfers between devices, along(): lax.ppermute(value, self.names[axis], [(i, (i + by) % n) for i in range(n)])  86.4 us
    unnamed x430, local copies, waits for them, and re-layouts  68 us
    pallas_call x4, Pallas kernels, run_experts_back(): pl.pallas_call(functools.partial(expert_back_kernel, len(blocks), len(res...  67.9 us
    pallas_call x4, Pallas kernels, run_experts(): pl.pallas_call(functools.partial(expert_kernel, len(blocks), tok, pieces,...  54 us
    dot_general x6, matrix products, t_dot(): lax.dot_general(left, right, (((0,), (0,)), ((), ())), preferred_element_...  47.3 us
    ppermute x35, starting transfers between devices, along(): lax.ppermute(value, self.names[axis], [(i, (i + by) % n) for i in range(n)])  43.6 us
    ppermute x27, starting transfers between devices, offset_by(): return lax.ppermute(value, self.names, out)  33.6 us
  transfers between devices with their start and end apart: 97, of which 23 were waited for; matrix products, arithmetic and copies ran while one was open for 25% of the time, Pallas kernels for 43%

profile of v5, /device:TPU:18, one launch (start us, length us, event | category | flops | bytes accessed | tf_op | source)
XLA Modules:
  0.0 888.7 jit_solution(11331490779702077662)
XLA Ops:
  34.9 3.2 convolution_add_fusion.refs_0_
  38.3 14.0 %shard_map.340 = (bf16[128,2048]{1,0:T(8,128)(2,1)S(1)}, bf16[128,2048]{1,0:T(8,128)(2,1)S(1)}, bf16[128,1024]{1,0:T(8,128)(2,1)S(1)}, bf16[128,8192]{1,0:T(8,12...) custom-call(f32[128,3072]{1,0:T(8,128)S(1)} %convolution_add_fusion.refs_0_, ...), custom_call_target="tpu_custom_call" | custom-call | tf_op jit(solution)/shard_map/pallas_call | solution.py:595
  57.3 4.0 multiply_reduce_fusion.2
  63.5 4.0 fusion.20
  74.4 5.0 fusion.31
  79.4 5.3 fusion.30
  84.8 5.2 fusion.26
  93.5 24.9 %collective-permute-done.19.refs_0_ = bf16[128,2176]{1,0:T(8,128)(2,1)} collective-permute-done((bf16[128,2176]{1,0:T(8,128)(2,1)}, bf16[128,2176]{1,0:T(8,128)(2,1)}, u32[]{:S(2)}, u32[]{:S(2)}) %collective-permute-start.19) | collective-permute-done | bytes 557088 | tf_op jit(solution)/shard_map/ppermute | solution.py:816
  120.5 3.2 convolution_add_fusion.1.refs_1_.refs_11_
  131.1 13.6 %shard_map.343 = (bf16[16,128]{1,0:T(8,128)(2,1)}, bf16[1024,2048]{1,0:T(8,128)(2,1)}, bf16[2048,2048]{1,0:T(8,128)(2,1)}, f32[1024,1408]{1,0:T(8,128)}, f32[102...) custom-call(s32[17]{0:T(128)} %pad_add_fusion.refs_0_, ...), custom_call_target="tpu_custom_call" | custom-call | tf_op jit(solution)/shard_map/pallas_call | solution.py:212
  144.7 21.2 %collective-permute-done.10.refs_0_ = bf16[128,2176]{1,0:T(8,128)(2,1)S(1)} collective-permute-done((bf16[128,2176]{1,0:T(8,128)(2,1)}, bf16[128,2176]{1,0:T(8,128)(2,1)S(1)}, u32[]{:S(2)}, u32[]{:S(2)}) %collective-permute-start.10) | collective-permute-done | bytes 557088 | tf_op jit(solution)/shard_map/ppermute | solution.py:816
  173.8 13.4 %shard_map.345 = (bf16[16,128]{1,0:T(8,128)(2,1)}, bf16[1024,2048]{1,0:T(8,128)(2,1)}, bf16[2048,2048]{1,0:T(8,128)(2,1)}, f32[1024,1408]{1,0:T(8,128)}, f32[102...) custom-call(s32[17]{0:T(128)} %pad_add_fusion.refs_0_, ...), custom_call_target="tpu_custom_call", output_to_operand_aliasing={{1}: (14, {}), {2}: (15, {}), {3}: (16, {}), {4}: (17, {}),... | custom-call | tf_op jit(solution)/shard_map/pallas_call | solution.py:212
  187.3 16.8 %shard_map.346 = (bf16[128,2176]{1,0:T(8,128)(2,1)}, bf16[128,2176]{1,0:T(8,128)(2,1)}, bf16[128,2176]{1,0:T(8,128)(2,1)}, bf16[128,2176]{1,0:T(8,128)(2,1)}, bf...) custom-call(s32[17]{0:T(128)} %pad_add_fusion.refs_0_, ...), custom_call_target="tpu_custom_call" | custom-call | tf_op jit(solution)/shard_map/pallas_call | solution.py:356
  217.4 13.5 %shard_map.349 = (bf16[16,128]{1,0:T(8,128)(2,1)}, bf16[1024,2048]{1,0:T(8,128)(2,1)}, bf16[2048,2048]{1,0:T(8,128)(2,1)}, f32[1024,1408]{1,0:T(8,128)}, f32[102...) custom-call(s32[17]{0:T(128)} %pad_add_fusion.refs_0_, ...), custom_call_target="tpu_custom_call", output_to_operand_aliasing={{1}: (11, {}), {2}: (12, {}), {3}: (13, {}), {4}: (14, {}),... | custom-call | tf_op jit(solution)/shard_map/pallas_call | solution.py:212
  230.9 3.4 collective-permute-done.24.refs_2_
  234.3 13.5 %shard_map.350 = (bf16[16,128]{1,0:T(8,128)(2,1)}, bf16[1024,2048]{1,0:T(8,128)(2,1)}, bf16[2048,2048]{1,0:T(8,128)(2,1)}, f32[1024,1408]{1,0:T(8,128)}, f32[102...) custom-call(s32[17]{0:T(128)} %pad_add_fusion.refs_0_, ...), custom_call_target="tpu_custom_call", output_to_operand_aliasing={{1}: (10, {}), {2}: (11, {}), {3}: (12, {}), {4}: (13, {}),... | custom-call | tf_op jit(solution)/shard_map/pallas_call | solution.py:212
  247.7 17.0 %shard_map.351 = (bf16[128,2176]{1,0:T(8,128)(2,1)}, bf16[128,2176]{1,0:T(8,128)(2,1)}, bf16[128,2176]{1,0:T(8,128)(2,1)}, bf16[128,2176]{1,0:T(8,128)(2,1)}, bf...) custom-call(s32[17]{0:T(128)} %pad_add_fusion.refs_0_, ...), custom_call_target="tpu_custom_call", output_to_operand_aliasing={{4}: (14, {}), {5}: (15, {}), {6}: (16, {}), {7}: (17, {}),... | custom-call | tf_op jit(solution)/shard_map/pallas_call | solution.py:356
  271.9 17.3 %shard_map.355 = (bf16[128,2176]{1,0:T(8,128)(2,1)}, bf16[128,2176]{1,0:T(8,128)(2,1)}, bf16[128,2176]{1,0:T(8,128)(2,1)}, bf16[128,2176]{1,0:T(8,128)(2,1)}, bf...) custom-call(s32[17]{0:T(128)} %pad_add_fusion.refs_0_, ...), custom_call_target="tpu_custom_call", output_to_operand_aliasing={{4}: (17, {}), {5}: (18, {}), {6}: (19, {}), {7}: (20, {}),... | custom-call | tf_op jit(solution)/shard_map/pallas_call | solution.py:356
  296.2 3.0 collective-permute-start.41
  299.2 16.8 %shard_map.359 = (bf16[128,2176]{1,0:T(8,128)(2,1)}, bf16[128,2176]{1,0:T(8,128)(2,1)}, bf16[128,2176]{1,0:T(8,128)(2,1)}, bf16[128,2176]{1,0:T(8,128)(2,1)}, bf...) custom-call(s32[17]{0:T(128)} %pad_add_fusion.refs_0_, ...), custom_call_target="tpu_custom_call", output_to_operand_aliasing={{4}: (15, {}), {5}: (16, {}), {6}: (17, {}), {7}: (18, {}),... | custom-call | tf_op jit(solution)/shard_map/pallas_call | solution.py:356
  324.3 7.4 convolution_convert_fusion.2.refs_1_
  331.8 7.4 convolution_convert_fusion.1.refs_1_
  346.0 7.4 convolution_convert_fusion.refs_1_
  362.8 7.9 collective-permute-done.40.refs_0_
  370.7 3.3 collective-permute-start.53
  385.1 4.0 fusion.106
  391.6 5.5 collective-permute-done.47.refs_0_
  408.5 16.6 %shard_map.378 = (bf16[128,3072]{1,0:T(8,128)(2,1)S(1)}, bf16[256,4096]{1,0:T(8,128)(2,1)S(1)}, bf16[256,4096]{1,0:T(8,128)(2,1)S(1)}, f32[256,512]{1,0:T(8,128)S(1)}, f32[256,64]{1,0:T(8,128)S(1)}) custom-call(bf16[128,2048]{1,0:T(8,128)(2,1)S(1)} %copy-done.15, bf16[256,4096]{1,0:T(8,128)(2,1)S(1)} %copy-done.11, bf16[256,4096]{1,0:T(8,128)(2,1)S(1)} %copy-done.13, ...), custom_call_target="tpu_custom_call" | custom-call | tf_op jit(solution)/shard_map/pallas_call | solution.py:619
  432.3 9.3 %convert_add_fusion.2.refs_1_ = f32[704,2048]{1,0:T(8,128)} fusion(bf16[704,2048]{1,0:T(8,128)(2,1)} %shard_map.380, bf16[1024,704]{1,0:T(8,128)(2,1)} %shard_map.379, bf16[1024,2048]{1,0:T(8,128)(2,1)} %get-tuple-element.209), kind=kOutput, calls=%fused_computation.2 | convolution fusion | flops 2955673600 | bytes 14286848 | tf_op jit(solution)/shard_map/dot_general | solution.py:89
  451.8 5.3 shard_map.395.refs_7_
  459.1 3.7 add_convert_fusion.2.refs_2_
  467.2 4.0 fusion.108
  471.3 4.1 fusion.109
  477.1 9.3 %convert_add_fusion.1.refs_1_ = f32[704,2048]{1,0:T(8,128)} fusion(bf16[704,2048]{1,0:T(8,128)(2,1)} %shard_map.397, bf16[1024,704]{1,0:T(8,128)(2,1)} %shard_map.396, bf16[1024,2048]{1,0:T(8,128)(2,1)} %get-tuple-element.209), kind=kOutput, calls=%fused_computation.1 | convolution fusion | flops 2955673600 | bytes 14286848 | tf_op jit(solution)/shard_map/dot_general | solution.py:89
  496.7 54.4 %shard_map.400 = (f32[2048,1408]{1,0:T(8,128)}, f32[2048,1408]{1,0:T(8,128)}, f32[1408,2048]{1,0:T(8,128)}) custom-call(bf16[2048,2048]{1,0:T(8,128)(2,1)} %shard_map.391.refs_0_, bf16[2048,2048]{1,0:T(8,128)(2,1)} %collective-permute-done.55.refs_1_, bf16[2048,2048]{1,0:T(8,128)(2,1)} %shard_map.392.refs_2_, ...), custom_call_target="tpu_custom_call" | custom-call | tf_op jit(solution)/shard_map/pallas_call | solution.py:474
  560.2 5.5 shard_map.414.refs_1_.refs_7_
  592.2 4.9 shard_map.420
  603.2 54.7 %shard_map.421 = (f32[2048,1408]{1,0:T(8,128)}, f32[2048,1408]{1,0:T(8,128)}, f32[1408,2048]{1,0:T(8,128)}) custom-call(bf16[2048,2048]{1,0:T(8,128)(2,1)} %shard_map.391.refs_0_, bf16[2048,2048]{1,0:T(8,128)(2,1)} %collective-permute-done.55.refs_1_, ...), custom_call_target="tpu_custom_call", output_to_operand_aliasing={{0}: (9, {}), {1}: (10, {}), {2}: (11, {})} | custom-call | tf_op jit(solution)/shard_map/pallas_call | solution.py:474
  677.0 54.3 %shard_map.434 = (f32[2048,1408]{1,0:T(8,128)}, f32[2048,1408]{1,0:T(8,128)}, f32[1408,2048]{1,0:T(8,128)}) custom-call(bf16[2048,2048]{1,0:T(8,128)(2,1)} %shard_map.391.refs_0_, bf16[2048,2048]{1,0:T(8,128)(2,1)} %collective-permute-done.55.refs_1_, ...), custom_call_target="tpu_custom_call", output_to_operand_aliasing={{0}: (10, {}), {1}: (11, {}), {2}: (12, {})} | custom-call | tf_op jit(solution)/shard_map/pallas_call | solution.py:474
  753.2 4.5 fusion.25
  759.5 46.2 %shard_map.444 = (f32[2048,1408]{1,0:T(8,128)}, f32[2048,1408]{1,0:T(8,128)}, f32[1408,2048]{1,0:T(8,128)}) custom-call(bf16[2048,2048]{1,0:T(8,128)(2,1)} %shard_map.391.refs_0_, bf16[2048,2048]{1,0:T(8,128)(2,1)} %collective-permute-done.55.refs_1_, ...), custom_call_target="tpu_custom_call", output_to_operand_aliasing={{0}: (10, {}), {1}: (11, {}), {2}: (12, {})} | custom-call | tf_op jit(solution)/shard_map/pallas_call | solution.py:474
  806.5 14.4 %collective-permute-done.84.refs_0_ = bf16[128,2048]{1,0:T(8,128)(2,1)S(1)} collective-permute-done((bf16[128,2048]{1,0:T(8,128)(2,1)}, bf16[128,2048]{1,0:T(8,128)(2,1)S(1)}, u32[]{:S(2)}, u32[]{:S(2)}) %collective-permute-start.84) | collective-permute-done | bytes 524320 | tf_op jit(solution)/shard_map/ppermute | solution.py:816
  835.2 3.1 fusion.19.refs_1_
  840.5 4.4 shard_map.462.refs_1_
  846.0 6.3 convert_add_fusion.refs_2_
  854.7 4.1 shard_map.464.refs_1_
  858.8 5.9 collective-permute-done.90.refs_0_
  865.8 9.7 %shard_map.471 = (f32[256,4096]{1,0:T(8,128)}, f32[1024,1536]{1,0:T(8,128)}, f32[576,1024]{1,0:T(8,128)}, f32[1024,64]{1,0:T(8,128)}) custom-call(s32[2]{0:T(128)} %pad_add_fusion.1.refs_0_, bf16[512,1536]{1,0:T(8,128)(2,1)} %maximum_select_fusion.1.refs_1_, bf16[512,1536]{1,0:T(8,128)(2,1)} %shard_map.467.refs_2_, ...), custom_call_target="tpu_custom_call" | custom-call | tf_op jit(solution)/shard_map/pallas_call | solution.py:676
  (887 shorter events, 285.3 us)
Async XLA Ops:
  7.2 180.1 %all-gather.4.cloned.1.call-start = ((), (), s32[]{:S(2)}) async-start(), calls=%async_computation.3 | async-start | bytes 8912896 | tf_op jit(solution)/shard_map/all_gather | solution.py:1161
  7.9 543.2 %reduce-scatter.4.cloned.1.call-start = ((), (), s32[]{:S(2)}) async-start(), calls=%async_computation.4 | async-start | bytes 1310720 | tf_op jit(solution)/shard_map/reduce_scatter | solution.py:1453
  8.0 55.0 %collective-permute-start.17 = (bf16[128,2048]{1,0:T(8,128)(2,1)}, bf16[128,2048]{1,0:T(8,128)(2,1)}, u32[]{:S(2)}, u32[]{:S(2)}) collective-permute-start(bf16[128,2048]{1,0:T(8,128)(2,1)} %param.24), channel_id=1, source_target_pairs={{0,1},{1,0},{2,3},{3,2},{4,5},{5,4},{6,7},{7,6},{8,9},{9,8},{10,11... | collective-permute-start | bytes 1572872 | tf_op jit(solution)/shard_map/ppermute | solution.py:1056
  34.5 55.4 %collective-permute-start.14 = (bf16[704,2048]{1,0:T(8,128)(2,1)S(1)}, bf16[704,2048]{1,0:T(8,128)(2,1)}, u32[]{:S(2)}, u32[]{:S(2)}) collective-permute-start(bf16[704,2048]{1,0:T(8,128)(2,1)S(1)} %bitcast.102), channel_id=1, source_target_pairs={{0,1},{1,0},{2,3},{3,2},{4,5},{5,4},{6,7},{7,6},{8,9},{9,8},{10,11... | collective-permute-start | bytes 8650760 | tf_op jit(solution)/shard_map/ppermute | solution.py:1056
  38.1 52.4 %collective-permute-start.15 = (bf16[704,2048]{1,0:T(8,128)(2,1)}, bf16[704,2048]{1,0:T(8,128)(2,1)}, u32[]{:S(2)}, u32[]{:S(2)}) collective-permute-start(bf16[704,2048]{1,0:T(8,128)(2,1)} %bitcast.8.refs_7_.refs_8_.refs_5_.refs_6_), channel_id=1, source_target_pairs={{0,1},{1,0},{2,3},{3,2},{4,5},{5,4},{6,7},{7,6},{8,9},{9,8},{10,11... | collective-permute-start | bytes 8650760 | tf_op jit(solution)/shard_map/ppermute | solution.py:1056
  72.2 46.2 %collective-permute-start.19 = (bf16[128,2176]{1,0:T(8,128)(2,1)}, bf16[128,2176]{1,0:T(8,128)(2,1)}, u32[]{:S(2)}, u32[]{:S(2)}) collective-permute-start(bf16[128,2176]{1,0:T(8,128)(2,1)} %concatenate.221.refs_1_), channel_id=1, source_target_pairs={{0,24},{8,0},{16,8},{24,16},{1,25},{9,1},{17,9},{25,17},{2,26},{10... | collective-permute-start | bytes 1671176 | tf_op jit(solution)/shard_map/ppermute | solution.py:816
  72.6 51.1 %collective-permute-start.18 = (bf16[128,2176]{1,0:T(8,128)(2,1)}, bf16[128,2176]{1,0:T(8,128)(2,1)}, u32[]{:S(2)}, u32[]{:S(2)}) collective-permute-start(bf16[128,2176]{1,0:T(8,128)(2,1)} %concatenate.221.refs_1_), channel_id=1, source_target_pairs={{0,8},{8,16},{16,24},{24,0},{1,9},{9,17},{17,25},{25,1},{2,10},{10... | collective-permute-start | bytes 1671176 | tf_op jit(solution)/shard_map/ppermute | solution.py:816
  118.4 47.5 %collective-permute-start.10 = (bf16[128,2176]{1,0:T(8,128)(2,1)}, bf16[128,2176]{1,0:T(8,128)(2,1)S(1)}, u32[]{:S(2)}, u32[]{:S(2)}) collective-permute-start(bf16[128,2176]{1,0:T(8,128)(2,1)} %concatenate.221.refs_1_), channel_id=1, source_target_pairs={{0,16},{8,24},{16,0},{24,8},{1,17},{9,25},{17,1},{25,9},{2,18},{10... | collective-permute-start | bytes 1671176 | tf_op jit(solution)/shard_map/ppermute | solution.py:816
  123.8 46.4 %collective-permute-start.25 = (bf16[128,2176]{1,0:T(8,128)(2,1)}, bf16[128,2176]{1,0:T(8,128)(2,1)S(1)}, u32[]{:S(2)}, u32[]{:S(2)}) collective-permute-start(bf16[128,2176]{1,0:T(8,128)(2,1)} %shard_map.342.refs_13_.refs_12_), channel_id=1, source_target_pairs={{0,2},{2,0},{1,3},{3,1},{4,6},{6,4},{5,7},{7,5},{8,10},{10,8},{9,1... | collective-permute-start | bytes 1671176 | tf_op jit(solution)/shard_map/ppermute | solution.py:816
  126.8 46.5 %collective-permute-start.21 = (bf16[128,2176]{1,0:T(8,128)(2,1)}, bf16[128,2176]{1,0:T(8,128)(2,1)}, u32[]{:S(2)}, u32[]{:S(2)}) collective-permute-start(bf16[128,2176]{1,0:T(8,128)(2,1)} %shard_map.341.refs_12_.refs_1_), channel_id=1, source_target_pairs={{0,2},{2,0},{4,6},{6,4},{8,10},{10,8},{12,14},{14,12},{16,18},{18,... | collective-permute-start | bytes 1671176 | tf_op jit(solution)/shard_map/ppermute | solution.py:825
  128.3 45.5 %collective-permute-start.22 = (bf16[128,2176]{1,0:T(8,128)(2,1)}, bf16[128,2176]{1,0:T(8,128)(2,1)}, u32[]{:S(2)}, u32[]{:S(2)}) collective-permute-start(bf16[128,2176]{1,0:T(8,128)(2,1)} %shard_map.341.refs_12_.refs_1_), channel_id=1, source_target_pairs={{0,4},{2,6},{4,0},{6,2},{8,12},{10,14},{12,8},{14,10},{16,20},{18,... | collective-permute-start | bytes 1671176 | tf_op jit(solution)/shard_map/ppermute | solution.py:825
  129.8 44.0 %collective-permute-start.23 = (bf16[128,2176]{1,0:T(8,128)(2,1)}, bf16[128,2176]{1,0:T(8,128)(2,1)}, u32[]{:S(2)}, u32[]{:S(2)}) collective-permute-start(bf16[128,2176]{1,0:T(8,128)(2,1)} %shard_map.341.refs_12_.refs_1_), channel_id=1, source_target_pairs={{0,6},{2,4},{4,2},{6,0},{8,14},{10,12},{12,10},{14,8},{16,22},{18,... | collective-permute-start | bytes 1671176 | tf_op jit(solution)/shard_map/ppermute | solution.py:825
  170.2 41.2 %collective-permute-start.50 = (bf16[128,2816]{1,0:T(8,128)(2,1)}, bf16[128,2816]{1,0:T(8,128)(2,1)}, u32[]{:S(2)}, u32[]{:S(2)}) collective-permute-start(bf16[128,2816]{1,0:T(8,128)(2,1)} %pad_maximum_fusion.11), channel_id=1, source_target_pairs={{0,1},{1,0},{2,3},{3,2},{4,5},{5,4},{6,7},{7,6},{8,9},{9,8},{10,11... | collective-permute-start | bytes 2162696 | tf_op jit(solution)/shard_map/ppermute | solution.py:1056
  173.3 44.1 %collective-permute-start.26 = (bf16[256,2176]{1,0:T(8,128)(2,1)}, bf16[256,2176]{1,0:T(8,128)(2,1)}, u32[]{:S(2)}, u32[]{:S(2)}) collective-permute-start(bf16[256,2176]{1,0:T(8,128)(2,1)} %pad_maximum_fusion.5.refs_1_), channel_id=1, source_target_pairs={{0,4},{4,0},{1,5},{5,1},{2,6},{6,2},{3,7},{7,3},{8,12},{12,8},{9,1... | collective-permute-start | bytes 3342344 | tf_op jit(solution)/shard_map/ppermute | solution.py:816
  208.3 58.5 %collective-permute-start.27 = (bf16[128,2176]{1,0:T(8,128)(2,1)S(1)}, bf16[128,2176]{1,0:T(8,128)(2,1)S(1)}, u32[]{:S(2)}, u32[]{:S(2)}) collective-permute-start(bf16[128,2176]{1,0:T(8,128)(2,1)S(1)} %copy-done.197), channel_id=1, source_target_pairs={{0,2},{2,0},{4,6},{6,4},{8,10},{10,8},{12,14},{14,12},{16,18},{18,... | collective-permute-start | bytes 1671176 | tf_op jit(solution)/shard_map/ppermute | solution.py:825
  209.8 58.5 %collective-permute-start.28 = (bf16[128,2176]{1,0:T(8,128)(2,1)}, bf16[128,2176]{1,0:T(8,128)(2,1)}, u32[]{:S(2)}, u32[]{:S(2)}) collective-permute-start(bf16[128,2176]{1,0:T(8,128)(2,1)} %get-tuple-element.184), channel_id=1, source_target_pairs={{0,4},{2,6},{4,0},{6,2},{8,12},{10,14},{12,8},{14,10},{16,20},{18,... | collective-permute-start | bytes 1671176 | tf_op jit(solution)/shard_map/ppermute | solution.py:825
  211.4 57.0 %collective-permute-start.29 = (bf16[128,2176]{1,0:T(8,128)(2,1)}, bf16[128,2176]{1,0:T(8,128)(2,1)}, u32[]{:S(2)}, u32[]{:S(2)}) collective-permute-start(bf16[128,2176]{1,0:T(8,128)(2,1)} %get-tuple-element.185), channel_id=1, source_target_pairs={{0,6},{2,4},{4,2},{6,0},{8,14},{10,12},{12,10},{14,8},{16,22},{18,... | collective-permute-start | bytes 1671176 | tf_op jit(solution)/shard_map/ppermute | solution.py:825
  296.2 63.7 %collective-permute-start.41 = (bf16[128,2176]{1,0:T(8,128)(2,1)}, bf16[128,2176]{1,0:T(8,128)(2,1)S(1)}, u32[]{:S(2)}, u32[]{:S(2)}) collective-permute-start(bf16[128,2176]{1,0:T(8,128)(2,1)} %add_convert_fusion.7.refs_14_), channel_id=1, source_target_pairs={{0,16},{8,24},{16,0},{24,8},{1,17},{9,25},{17,1},{25,9},{2,18},{10... | collective-permute-start | bytes 1671176 | tf_op jit(solution)/shard_map/ppermute | solution.py:816
  339.2 42.5 %collective-permute-start.44 = (bf16[704,2048]{1,0:T(8,128)(2,1)}, bf16[704,2048]{1,0:T(8,128)(2,1)}, u32[]{:S(2)}, u32[]{:S(2)}) collective-permute-start(bf16[704,2048]{1,0:T(8,128)(2,1)} %convolution_convert_fusion.1.refs_1_), channel_id=1, source_target_pairs={{0,1},{1,0},{2,3},{3,2},{4,5},{5,4},{6,7},{7,6},{8,9},{9,8},{10,11... | collective-permute-start | bytes 8650760 | tf_op jit(solution)/shard_map/ppermute | solution.py:1056
  370.7 58.6 %collective-permute-start.53 = (bf16[256,704]{1,0:T(8,128)(2,1)}, bf16[256,704]{1,0:T(8,128)(2,1)S(1)}, u32[]{:S(2)}, u32[]{:S(2)}) collective-permute-start(bf16[256,704]{1,0:T(8,128)(2,1)} %pad_maximum_fusion.20), channel_id=1, source_target_pairs={{0,6},{2,4},{4,2},{6,0},{8,14},{10,12},{12,10},{14,8},{16,22},{18,... | collective-permute-start | bytes 1081352 | tf_op jit(solution)/shard_map/ppermute | solution.py:825
  376.9 53.9 %collective-permute-start.52 = (bf16[256,704]{1,0:T(8,128)(2,1)}, bf16[256,704]{1,0:T(8,128)(2,1)S(1)}, u32[]{:S(2)}, u32[]{:S(2)}) collective-permute-start(bf16[256,704]{1,0:T(8,128)(2,1)} %pad_maximum_fusion.19), channel_id=1, source_target_pairs={{0,4},{2,6},{4,0},{6,2},{8,12},{10,14},{12,8},{14,10},{16,20},{18,... | collective-permute-start | bytes 1081352 | tf_op jit(solution)/shard_map/ppermute | solution.py:825
  381.7 59.9 %collective-permute-start.51 = (bf16[256,704]{1,0:T(8,128)(2,1)}, bf16[256,704]{1,0:T(8,128)(2,1)S(1)}, u32[]{:S(2)}, u32[]{:S(2)}) collective-permute-start(bf16[256,704]{1,0:T(8,128)(2,1)} %pad_maximum_fusion.18), channel_id=1, source_target_pairs={{0,2},{2,0},{4,6},{6,4},{8,10},{10,8},{12,14},{14,12},{16,18},{18,... | collective-permute-start | bytes 1081352 | tf_op jit(solution)/shard_map/ppermute | solution.py:825
  397.2 97.9 %collective-permute-start.56 = (bf16[2048,2048]{1,0:T(8,128)(2,1)}, bf16[2048,2048]{1,0:T(8,128)(2,1)}, u32[]{:S(2)}, u32[]{:S(2)}) collective-permute-start(bf16[2048,2048]{1,0:T(8,128)(2,1)} %shard_map.392.refs_2_), channel_id=1, source_target_pairs={{0,1},{1,0},{2,3},{3,2},{4,5},{5,4},{6,7},{7,6},{8,9},{9,8},{10,11... | collective-permute-start | bytes 25165832 | tf_op jit(solution)/shard_map/ppermute | solution.py:1056
  398.0 97.6 %collective-permute-start.55 = (bf16[2048,2048]{1,0:T(8,128)(2,1)}, bf16[2048,2048]{1,0:T(8,128)(2,1)}, u32[]{:S(2)}, u32[]{:S(2)}) collective-permute-start(bf16[2048,2048]{1,0:T(8,128)(2,1)} %shard_map.391.refs_0_), channel_id=1, source_target_pairs={{0,1},{1,0},{2,3},{3,2},{4,5},{5,4},{6,7},{7,6},{8,9},{9,8},{10,11... | collective-permute-start | bytes 25165832 | tf_op jit(solution)/shard_map/ppermute | solution.py:1056
  457.2 95.7 %reduce-scatter.6.cloned.1.call-start = ((), (), s32[]{:S(2)}) async-start(), calls=%async_computation.5 | async-start | bytes 2621440 | tf_op jit(solution)/shard_map/reduce_scatter | solution.py:1418
  462.8 197.5 %reduce-scatter.8.cloned.1.call-start = ((), (), s32[]{:S(2)}) async-start(), calls=%async_computation.6 | async-start | bytes 1474560 | tf_op jit(solution)/shard_map/reduce_scatter | solution.py:1483
  489.5 61.7 %collective-permute-start.66 = (bf16[256,1536]{1,0:T(8,128)(2,1)}, bf16[256,1536]{1,0:T(8,128)(2,1)S(1)}, u32[]{:S(2)}, u32[]{:S(2)}) collective-permute-start(bf16[256,1536]{1,0:T(8,128)(2,1)} %pad_maximum_fusion.10.refs_10_.refs_0_), channel_id=1, source_target_pairs={{0,2},{2,0},{1,3},{3,1},{4,6},{6,4},{5,7},{7,5},{8,10},{10,8},{9,1... | collective-permute-start | bytes 2359304 | tf_op jit(solution)/shard_map/ppermute | solution.py:816
  492.5 59.5 %collective-permute-start.65 = (bf16[256,1536]{1,0:T(8,128)(2,1)}, bf16[256,1536]{1,0:T(8,128)(2,1)}, u32[]{:S(2)}, u32[]{:S(2)}) collective-permute-start(bf16[256,1536]{1,0:T(8,128)(2,1)} %pad_maximum_fusion.9.refs_9_.refs_0_), channel_id=1, source_target_pairs={{0,4},{4,0},{1,5},{5,1},{2,6},{6,2},{3,7},{7,3},{8,12},{12,8},{9,1... | collective-permute-start | bytes 2359304 | tf_op jit(solution)/shard_map/ppermute | solution.py:816
  493.1 58.9 %collective-permute-start.64 = (bf16[128,2176]{1,0:T(8,128)(2,1)S(1)}, bf16[128,2176]{1,0:T(8,128)(2,1)S(1)}, u32[]{:S(2)}, u32[]{:S(2)}) collective-permute-start(bf16[128,2176]{1,0:T(8,128)(2,1)S(1)} %pad.8.refs_8_.refs_0_), channel_id=1, source_target_pairs={{0,6},{2,4},{4,2},{6,0},{8,14},{10,12},{12,10},{14,8},{16,22},{18,... | collective-permute-start | bytes 1671176 | tf_op jit(solution)/shard_map/ppermute | solution.py:825
  495.1 57.7 %collective-permute-start.63 = (bf16[128,2176]{1,0:T(8,128)(2,1)S(1)}, bf16[128,2176]{1,0:T(8,128)(2,1)}, u32[]{:S(2)}, u32[]{:S(2)}) collective-permute-start(bf16[128,2176]{1,0:T(8,128)(2,1)S(1)} %pad.8.refs_8_.refs_0_), channel_id=1, source_target_pairs={{0,4},{2,6},{4,0},{6,2},{8,12},{10,14},{12,8},{14,10},{16,20},{18,... | collective-permute-start | bytes 1671176 | tf_op jit(solution)/shard_map/ppermute | solution.py:825
  495.7 57.1 %collective-permute-start.62 = (bf16[128,2176]{1,0:T(8,128)(2,1)S(1)}, bf16[128,2176]{1,0:T(8,128)(2,1)}, u32[]{:S(2)}, u32[]{:S(2)}) collective-permute-start(bf16[128,2176]{1,0:T(8,128)(2,1)S(1)} %pad.8.refs_8_.refs_0_), channel_id=1, source_target_pairs={{0,2},{2,0},{4,6},{6,4},{8,10},{10,8},{12,14},{14,12},{16,18},{18,... | collective-permute-start | bytes 1671176 | tf_op jit(solution)/shard_map/ppermute | solution.py:825
  565.8 173.7 %all-gather.6.cloned.1.call-start = ((), (), s32[]{:S(2)}) async-start(), calls=%async_computation.7 | async-start | bytes 4456448 | tf_op jit(solution)/shard_map/all_gather | solution.py:1459
  567.6 284.8 %all-gather.8.cloned.1.call-start = ((), (), s32[]{:S(2)}) async-start(), calls=%async_computation.8 | async-start | bytes 5013504 | tf_op jit(solution)/shard_map/all_gather | solution.py:1499
  588.8 71.5 %collective-permute-start.77 = (bf16[512,2048]{1,0:T(8,128)(2,1)}, bf16[512,2048]{1,0:T(8,128)(2,1)}, u32[]{:S(2)}, u32[]{:S(2)}) collective-permute-start(bf16[512,2048]{1,0:T(8,128)(2,1)} %shard_map.425), channel_id=1, source_target_pairs={{0,2},{2,0},{1,3},{3,1},{4,6},{6,4},{5,7},{7,5},{8,10},{10,8},{9,1... | collective-permute-start | bytes 6291464 | tf_op jit(solution)/shard_map/ppermute | solution.py:816
  589.9 70.3 %collective-permute-start.78 = (bf16[512,2048]{1,0:T(8,128)(2,1)}, bf16[512,2048]{1,0:T(8,128)(2,1)}, u32[]{:S(2)}, u32[]{:S(2)}) collective-permute-start(bf16[512,2048]{1,0:T(8,128)(2,1)} %shard_map.427), channel_id=1, source_target_pairs={{0,4},{4,0},{1,5},{5,1},{2,6},{6,2},{3,7},{7,3},{8,12},{12,8},{9,1... | collective-permute-start | bytes 6291464 | tf_op jit(solution)/shard_map/ppermute | solution.py:816
  597.9 60.1 %collective-permute-start.76 = (bf16[64,3200]{1,0:T(8,128)(2,1)S(1)}, bf16[64,3200]{1,0:T(8,128)(2,1)S(1)}, u32[]{:S(2)}, u32[]{:S(2)}) collective-permute-start(bf16[64,3200]{1,0:T(8,128)(2,1)S(1)} %get-tuple-element.355), channel_id=1, source_target_pairs={{0,24},{8,0},{16,8},{24,16},{1,25},{9,1},{17,9},{25,17},{2,26},{10... | collective-permute-start | bytes 1228808 | tf_op jit(solution)/shard_map/ppermute | solution.py:816
  597.9 60.8 %collective-permute-start.75 = (bf16[64,3200]{1,0:T(8,128)(2,1)S(1)}, bf16[64,3200]{1,0:T(8,128)(2,1)S(1)}, u32[]{:S(2)}, u32[]{:S(2)}) collective-permute-start(bf16[64,3200]{1,0:T(8,128)(2,1)S(1)} %get-tuple-element.356), channel_id=1, source_target_pairs={{0,16},{8,24},{16,0},{24,8},{1,17},{9,25},{17,1},{25,9},{2,18},{10... | collective-permute-start | bytes 1228808 | tf_op jit(solution)/shard_map/ppermute | solution.py:816
  600.9 58.6 %collective-permute-start.74 = (bf16[64,3200]{1,0:T(8,128)(2,1)S(1)}, bf16[64,3200]{1,0:T(8,128)(2,1)S(1)}, u32[]{:S(2)}, u32[]{:S(2)}) collective-permute-start(bf16[64,3200]{1,0:T(8,128)(2,1)S(1)} %get-tuple-element.357), channel_id=1, source_target_pairs={{0,8},{8,16},{16,24},{24,0},{1,9},{9,17},{17,25},{25,1},{2,10},{10... | collective-permute-start | bytes 1228808 | tf_op jit(solution)/shard_map/ppermute | solution.py:816
  663.1 68.2 %collective-permute-start.81 = (bf16[64,3200]{1,0:T(8,128)(2,1)S(1)}, bf16[64,3200]{1,0:T(8,128)(2,1)}, u32[]{:S(2)}, u32[]{:S(2)}) collective-permute-start(bf16[64,3200]{1,0:T(8,128)(2,1)S(1)} %add_convert_fusion.9.refs_9_.refs_0_), channel_id=1, source_target_pairs={{0,24},{8,0},{16,8},{24,16},{1,25},{9,1},{17,9},{25,17},{2,26},{10... | collective-permute-start | bytes 1228808 | tf_op jit(solution)/shard_map/ppermute | solution.py:816
  663.5 69.6 %collective-permute-start.80 = (bf16[64,3200]{1,0:T(8,128)(2,1)S(1)}, bf16[64,3200]{1,0:T(8,128)(2,1)S(1)}, u32[]{:S(2)}, u32[]{:S(2)}) collective-permute-start(bf16[64,3200]{1,0:T(8,128)(2,1)S(1)} %add_convert_fusion.9.refs_9_.refs_0_), channel_id=1, source_target_pairs={{0,16},{8,24},{16,0},{24,8},{1,17},{9,25},{17,1},{25,9},{2,18},{10... | collective-permute-start | bytes 1228808 | tf_op jit(solution)/shard_map/ppermute | solution.py:816
  665.3 68.6 %collective-permute-start.79 = (bf16[64,3200]{1,0:T(8,128)(2,1)S(1)}, bf16[64,3200]{1,0:T(8,128)(2,1)S(1)}, u32[]{:S(2)}, u32[]{:S(2)}) collective-permute-start(bf16[64,3200]{1,0:T(8,128)(2,1)S(1)} %add_convert_fusion.9.refs_9_.refs_0_), channel_id=1, source_target_pairs={{0,8},{8,16},{16,24},{24,0},{1,9},{9,17},{17,25},{25,1},{2,10},{10... | collective-permute-start | bytes 1228808 | tf_op jit(solution)/shard_map/ppermute | solution.py:816
  671.0 66.6 %collective-permute-start.82 = (bf16[256,2048]{1,0:T(8,128)(2,1)}, bf16[256,2048]{1,0:T(8,128)(2,1)S(1)}, u32[]{:S(2)}, u32[]{:S(2)}) collective-permute-start(bf16[256,2048]{1,0:T(8,128)(2,1)} %get-tuple-element.351), channel_id=1, source_target_pairs={{0,4},{4,0},{1,5},{5,1},{2,6},{6,2},{3,7},{7,3},{8,12},{12,8},{9,1... | collective-permute-start | bytes 3145736 | tf_op jit(solution)/shard_map/ppermute | solution.py:816
  675.7 62.8 %collective-permute-start.83 = (bf16[256,2048]{1,0:T(8,128)(2,1)}, bf16[256,2048]{1,0:T(8,128)(2,1)S(1)}, u32[]{:S(2)}, u32[]{:S(2)}) collective-permute-start(bf16[256,2048]{1,0:T(8,128)(2,1)} %get-tuple-element.354), channel_id=1, source_target_pairs={{0,2},{2,0},{1,3},{3,1},{4,6},{6,4},{5,7},{7,5},{8,10},{10,8},{9,1... | collective-permute-start | bytes 3145736 | tf_op jit(solution)/shard_map/ppermute | solution.py:816
  743.4 62.3 %collective-permute-start.87 = (bf16[128,2048]{1,0:T(8,128)(2,1)S(1)}, bf16[128,2048]{1,0:T(8,128)(2,1)S(1)}, u32[]{:S(2)}, u32[]{:S(2)}) collective-permute-start(bf16[128,2048]{1,0:T(8,128)(2,1)S(1)} %get-tuple-element.359), channel_id=1, source_target_pairs={{0,16},{8,24},{16,0},{24,8},{1,17},{9,25},{17,1},{25,9},{2,18},{10... | collective-permute-start | bytes 1572872 | tf_op jit(solution)/shard_map/ppermute | solution.py:816
  747.7 73.2 %collective-permute-start.84 = (bf16[128,2048]{1,0:T(8,128)(2,1)}, bf16[128,2048]{1,0:T(8,128)(2,1)S(1)}, u32[]{:S(2)}, u32[]{:S(2)}) collective-permute-start(bf16[128,2048]{1,0:T(8,128)(2,1)} %get-tuple-element.361), channel_id=1, source_target_pairs={{0,24},{8,0},{16,8},{24,16},{1,25},{9,1},{17,9},{25,17},{2,26},{10... | collective-permute-start | bytes 1572872 | tf_op jit(solution)/shard_map/ppermute | solution.py:816
  750.0 72.1 %collective-permute-start.86 = (bf16[256,1664]{1,0:T(8,128)(2,1)S(1)}, bf16[256,1664]{1,0:T(8,128)(2,1)S(1)}, u32[]{:S(2)}, u32[]{:S(2)}) collective-permute-start(bf16[256,1664]{1,0:T(8,128)(2,1)S(1)} %dynamic-slice.14.refs_8_.refs_0_), channel_id=1, source_target_pairs={{0,4},{4,0},{1,5},{5,1},{2,6},{6,2},{3,7},{7,3},{8,12},{12,8},{9,1... | collective-permute-start | bytes 2555912 | tf_op jit(solution)/shard_map/ppermute | solution.py:816
  751.0 71.1 %collective-permute-start.85 = (bf16[256,1536]{1,0:T(8,128)(2,1)S(1)}, bf16[256,1536]{1,0:T(8,128)(2,1)}, u32[]{:S(2)}, u32[]{:S(2)}) collective-permute-start(bf16[256,1536]{1,0:T(8,128)(2,1)S(1)} %constant_dynamic-slice_fusion.9.refs_7_.refs_0_), channel_id=1, source_target_pairs={{0,2},{2,0},{1,3},{3,1},{4,6},{6,4},{5,7},{7,5},{8,10},{10,8},{9,1... | collective-permute-start | bytes 2359304 | tf_op jit(solution)/shard_map/ppermute | solution.py:816
  752.1 70.0 %collective-permute-start.88 = (bf16[128,2048]{1,0:T(8,128)(2,1)}, bf16[128,2048]{1,0:T(8,128)(2,1)}, u32[]{:S(2)}, u32[]{:S(2)}) collective-permute-start(bf16[128,2048]{1,0:T(8,128)(2,1)} %get-tuple-element.360), channel_id=1, source_target_pairs={{0,8},{8,16},{16,24},{24,0},{1,9},{9,17},{17,25},{25,1},{2,10},{10... | collective-permute-start | bytes 1572872 | tf_op jit(solution)/shard_map/ppermute | solution.py:816
  (259 other events, 1909.2 us)
Sparse Core Ops, SparseCore 0:
  10.8 154.0 all-gather.3
  457.3 26.4 reduce-scatter.3
  487.6 56.8 reduce-scatter.5
  565.9 28.6 reduce-scatter.7
  597.2 115.3 all-gather.5
  715.3 110.0 all-gather.7
